TPU v7x, 32 devices: a whole 2x2x4 slice. The times are simulated.
32 devices in a mesh: ctx: 16 (over z, y, x), head: 2 (over core).
Axes of the slice: x: 2, y: 2, z: 4, core: 2. Of those that a mesh axis runs over, the one named last changes fastest.
Arguments:
- tokens: bfloat16 [2048, 4096], P('ctx'), may hold values from -6 to 6
- norm_gain: float32 [4096], replicated, may hold values from 0.1 to 1.9
- w_query: bfloat16 [4096, 4096], P('ctx', 'head')
- w_key: bfloat16 [4096, 1024], P('ctx', 'head'), may hold values from -0.09375 to 0.09375
- w_value: bfloat16 [4096, 1024], P('ctx', 'head'), may hold values from -0.09375 to 0.09375
- w_out: bfloat16 [4096, 4096], P('head', 'ctx'), may hold values from -0.5 to 0.5
- doc_starts: int32 [16], replicated, may hold values from 0 to 2047, as said below
Outputs:
- block_out: bfloat16 [2048, 4096], P('ctx', 'head')
Inputs may be any that keep to these rules, and one draw needn't show every extreme that they name: doc_starts[0] is 0, the entries rise strictly, and the first document holds at least 1024 tokens.
All inputs are finite; a program needn't handle non-finite values.
Results may differ from a plain program's by a relative error of at most 0.02.
The roundings to bfloat16 on the way count: a program that leaves them out, or rounds other values in their place, can miss the bound.
Values may be sent and summed in bfloat16 or wider, within the bound.
No kernel may reach another device: no remote copies, remote signals or barrier semaphores. Data moves between devices by JAX's collectives and lax.ppermute only.
A program may use at most 128 MiB of HBM per device.

v0:
```python
import jax
import jax.numpy as jnp
from jax import lax
from jax.sharding import PartitionSpec as P

HD = 128


def shifted(block, axis, distance):
    devices = range(lax.axis_size(axis))
    route = [(i - distance, i) for i in devices if i - distance in devices]
    return lax.ppermute(block, axis, route)


def rotate_heads(values, positions):
    half = values.shape[-1] // 2
    freqs = 500000.0 ** (-(jnp.arange(half, dtype=jnp.float32) * 2.0 / values.shape[-1]))
    angles = positions.astype(jnp.float32)[:, None] * freqs[None, :]
    cosine = jnp.cos(angles)[:, None, :]
    sine = jnp.sin(angles)[:, None, :]
    lower = values[..., :half]
    upper = values[..., half:]
    return jnp.concatenate([lower * cosine - upper * sine, upper * cosine + lower * sine], axis=-1)


def document_of(positions, doc_starts):
    return jnp.sum((doc_starts[None, :] <= positions[:, None]).astype(jnp.int32), axis=1) - 1


def attend(running, kv_block, key_first, query_heads, query_pos, query_doc, doc_starts):
    highest, denominator, weighted = running
    key_count = kv_block.shape[1]
    kv_local = query_heads.shape[1]
    head_size = query_heads.shape[3]
    key_rows = kv_block[0].reshape(key_count, kv_local, head_size)
    value_rows = kv_block[1].reshape(key_count, kv_local, head_size)
    key_pos = key_first + jnp.arange(key_count, dtype=jnp.int32)
    key_doc = document_of(key_pos, doc_starts)

    def update(unused):
        scores = jnp.einsum(
            "qhgd,khd->hgqk", query_heads, key_rows, preferred_element_type=jnp.float32
        ) * head_size ** (-0.5)
        visible = (key_doc[None, :] == query_doc[:, None]) & (
            key_pos[None, :] <= query_pos[:, None]
        )
        scores = jnp.where(visible[None, None], scores, -1e30)
        new_highest = jnp.maximum(highest, jnp.max(scores, axis=-1))
        probs = jnp.where(visible[None, None], jnp.exp(scores - new_highest[..., None]), 0.0)
        rescale = jnp.exp(highest - new_highest)
        product = jnp.einsum(
            "hgqk,khd->hgqd",
            probs.astype(jnp.bfloat16),
            value_rows,
            preferred_element_type=jnp.float32,
        )
        return (
            new_highest,
            denominator * rescale + jnp.sum(probs, axis=-1),
            weighted * rescale[..., None] + product,
        )

    needed = (key_first >= 0) & (key_first <= query_pos[-1]) & (key_doc[-1] >= query_doc[0])
    return lax.cond(needed, update, lambda unused: running, 0)


def per_device(tokens, norm_gain, w_query, w_key, w_value, w_out, doc_starts):
    local_rows = tokens.shape[0]
    ctx_count = lax.axis_size("ctx")
    my_index = lax.axis_index("ctx")
    source = tokens.astype(jnp.float32)
    normed = (
        source * lax.rsqrt(jnp.mean(source * source, axis=1, keepdims=True) + 1e-05) * norm_gain
    ).astype(jnp.bfloat16)

    def add_rows(weight_rows):
        return jnp.dot(normed, weight_rows, preferred_element_type=jnp.float32)

    query_lin = add_rows(lax.all_gather(w_query, "ctx", axis=0, tiled=True))
    key_lin = add_rows(lax.all_gather(w_key, "ctx", axis=0, tiled=True))
    value_lin = add_rows(lax.all_gather(w_value, "ctx", axis=0, tiled=True))
    head_size = HD
    query_count = query_lin.shape[1] // head_size
    kv_local = key_lin.shape[1] // head_size
    groups = query_count // kv_local
    query_pos = my_index * local_rows + jnp.arange(local_rows, dtype=jnp.int32)
    query_doc = document_of(query_pos, doc_starts)
    query_heads = rotate_heads(
        query_lin.reshape(local_rows, query_count, head_size), query_pos
    ).astype(jnp.bfloat16)
    query_heads = query_heads.reshape(local_rows, kv_local, groups, head_size)
    key_proj = rotate_heads(key_lin.reshape(local_rows, kv_local, head_size), query_pos).astype(
        jnp.bfloat16
    )
    value_proj = value_lin.astype(jnp.bfloat16)
    kv_pair = jnp.stack([key_proj.reshape(local_rows, kv_local * head_size), value_proj])
    initial = (
        jnp.full((kv_local, groups, local_rows), -1e30, jnp.float32),
        jnp.zeros((kv_local, groups, local_rows), jnp.float32),
        jnp.zeros((kv_local, groups, local_rows, head_size), jnp.float32),
    )
    running = attend(
        initial, kv_pair, my_index * local_rows, query_heads, query_pos, query_doc, doc_starts
    )

    def cycle_turn(turn_index, carried):
        running_now, kv_block = carried
        kv_block = shifted(kv_block, "ctx", 1)
        anchor = my_index - turn_index
        return (
            attend(
                running_now,
                kv_block,
                anchor * local_rows,
                query_heads,
                query_pos,
                query_doc,
                doc_starts,
            ),
            kv_block,
        )

    final, unused_block = lax.fori_loop(1, ctx_count, cycle_turn, (running, kv_pair))
    mixed = final[2] / final[1][..., None]
    attended = (
        jnp.transpose(mixed, (2, 0, 1, 3))
        .reshape(local_rows, query_count * head_size)
        .astype(jnp.bfloat16)
    )
    partial_out = jnp.dot(
        attended,
        lax.all_gather(w_out, "ctx", axis=1, tiled=True),
        preferred_element_type=jnp.float32,
    )
    return lax.psum_scatter(
        partial_out.astype(jnp.bfloat16), "head", scatter_dimension=1, tiled=True
    )


def solution(mesh):
    placed = (
        P("ctx", None),
        P(),
        P("ctx", "head"),
        P("ctx", "head"),
        P("ctx", "head"),
        P("head", "ctx"),
        P(),
    )
    return jax.shard_map(
        per_device, mesh=mesh, in_specs=placed, out_specs=P("ctx", "head"), check_vma=False
    )
```

profile of v0, /device:TPU:1, one launch (start us, length us, event | category | flops | bytes accessed | tf_op | source)
XLA Modules:
  0.0 711.4 jit_solution(10069566770992349965)
XLA Ops:
  13.3 73.9 %all-gather.5.cloned.1.call-done = bf16[4096,512]{1,0:T(8,128)(2,1)} async-done(((bf16[256,512]{1,0:T(8,128)(2,1)}), bf16[4096,512]{1,0:T(8,128)(2,1)}) %all-gather.5.cloned.1.call-update) | async-done | bytes 4194320 | tf_op jit(solution)/shard_map/all_gather | solution.py:80
  87.2 2.9 fusion.27
  90.8 73.9 %all-gather.9.cloned.1.call-done = bf16[4096,512]{1,0:T(8,128)(2,1)} async-done(((bf16[256,512]{1,0:T(8,128)(2,1)}), bf16[4096,512]{1,0:T(8,128)(2,1)}) %all-gather.9.cloned.1.call-update) | async-done | bytes 4194320 | tf_op jit(solution)/shard_map/all_gather | solution.py:81
  164.6 2.9 convolution_convert_fusion.1
  167.8 190.7 %all-gather.7.cloned.1.call-done = bf16[4096,2048]{1,0:T(8,128)(2,1)} async-done(((bf16[256,2048]{1,0:T(8,128)(2,1)}), bf16[4096,2048]{1,0:T(8,128)(2,1)}) %all-gather.7.cloned.1.call-update) | async-done | bytes 16777232 | tf_op jit(solution)/shard_map/all_gather | solution.py:79
  358.5 8.2 %convolution_bitcast_fusion = f32[16,8,16,128]{3,1,2,0:T(8,128)S(1)} fusion(bf16[4096,2048]{1,0:T(8,128)(2,1)} %all-gather.7.cloned.1.call-done, bf16[128,4096]{1,0:T(8,128)(2,1)S(1)} %copy-done, f32[4096]{0:T(1024)S(1)} %copy-done.1, f32[128]{0:T(128)S(1)} %add_rsqrt_fusion), kind=kOutput, calls=%fused_computation.41 | convolution fusion | flops 2149580800 | bytes 18891264 | tf_op jit(solution)/shard_map/dot_general | solution.py:77
  368.0 4.1 conditional.2
  372.2 252.6 %while.21 = (s32[]{:T(128)}, f32[4,4,128]{2,1,0:T(4,128)}, f32[4,4,128]{2,1,0:T(4,128)S(1)}, f32[4,4,128,128]{3,2,1,0:T(8,128)S(1)}, bf16[2,128,512]{1,2,0:T(8,1...) while((s32[]{:T(128)}, f32[4,4,128]{2,1,0:T(4,128)}, ...), condition=%wide.region_12.13_spmd, body=%wide.region_6.12_spmd.sunk | while | flops 137160976 | bytes 8329667 | solution.py:123
  372.2 3.1 collective-permute-start
  377.9 7.8 %collective-permute-done = bf16[2,128,512]{1,2,0:T(8,128)(2,1)S(1)} collective-permute-done((bf16[2,128,512]{1,2,0:T(8,128)(2,1)S(1)}, bf16[2,128,512]{1,2,0:T(8,128)(2,1)S(1)}, u32[]{:S(2)}, u32[]{:S(2)}) %collective-permute-start) | collective-permute-done | bytes 262176 | tf_op jit(solution)/shard_map/while/body/eval_jaxpr/ppermute | solution.py:12
  385.8 7.6 %collective-permute-start = (bf16[2,128,512]{1,2,0:T(8,128)(2,1)S(1)}, bf16[2,128,512]{1,2,0:T(8,128)(2,1)S(1)}, u32[]{:S(2)}, u32[]{:S(2)}) collective-permute-start(bf16[2,128,512]{1,2,0:T(8,128)(2,1)S(1)} %get-tuple-element.495), channel_id=1, source_target_pairs={{0,2},{2,4},{4,6},{6,8},{8,10},{10,12},{12,14},{14,16},{16,18},{18... | collective-permute-start | bytes 786440 | tf_op jit(solution)/shard_map/while/body/eval_jaxpr/ppermute | solution.py:12
  398.1 4.2 collective-permute-start
  406.1 8.4 %collective-permute-start = (bf16[2,128,512]{1,2,0:T(8,128)(2,1)S(1)}, bf16[2,128,512]{1,2,0:T(8,128)(2,1)S(1)}, u32[]{:S(2)}, u32[]{:S(2)}) collective-permute-start(bf16[2,128,512]{1,2,0:T(8,128)(2,1)S(1)} %get-tuple-element.495), channel_id=1, source_target_pairs={{0,2},{2,4},{4,6},{6,8},{8,10},{10,12},{12,14},{14,16},{16,18},{18... | collective-permute-start | bytes 786440 | tf_op jit(solution)/shard_map/while/body/eval_jaxpr/ppermute | solution.py:12
  417.2 6.2 collective-permute-done
  423.5 6.1 collective-permute-start
  432.3 7.0 collective-permute-done
  439.3 8.8 %collective-permute-start = (bf16[2,128,512]{1,2,0:T(8,128)(2,1)S(1)}, bf16[2,128,512]{1,2,0:T(8,128)(2,1)S(1)}, u32[]{:S(2)}, u32[]{:S(2)}) collective-permute-start(bf16[2,128,512]{1,2,0:T(8,128)(2,1)S(1)} %get-tuple-element.495), channel_id=1, source_target_pairs={{0,2},{2,4},{4,6},{6,8},{8,10},{10,12},{12,14},{14,16},{16,18},{18... | collective-permute-start | bytes 786440 | tf_op jit(solution)/shard_map/while/body/eval_jaxpr/ppermute | solution.py:12
  451.4 4.7 collective-permute-start
  460.2 11.9 %collective-permute-start = (bf16[2,128,512]{1,2,0:T(8,128)(2,1)S(1)}, bf16[2,128,512]{1,2,0:T(8,128)(2,1)S(1)}, u32[]{:S(2)}, u32[]{:S(2)}) collective-permute-start(bf16[2,128,512]{1,2,0:T(8,128)(2,1)S(1)} %get-tuple-element.495), channel_id=1, source_target_pairs={{0,2},{2,4},{4,6},{6,8},{8,10},{10,12},{12,14},{14,16},{16,18},{18... | collective-permute-start | bytes 786440 | tf_op jit(solution)/shard_map/while/body/eval_jaxpr/ppermute | solution.py:12
  474.7 3.8 collective-permute-done
  478.6 15.5 %collective-permute-start = (bf16[2,128,512]{1,2,0:T(8,128)(2,1)S(1)}, bf16[2,128,512]{1,2,0:T(8,128)(2,1)S(1)}, u32[]{:S(2)}, u32[]{:S(2)}) collective-permute-start(bf16[2,128,512]{1,2,0:T(8,128)(2,1)S(1)} %get-tuple-element.495), channel_id=1, source_target_pairs={{0,2},{2,4},{4,6},{6,8},{8,10},{10,12},{12,14},{14,16},{16,18},{18... | collective-permute-start | bytes 786440 | tf_op jit(solution)/shard_map/while/body/eval_jaxpr/ppermute | solution.py:12
  496.8 7.1 collective-permute-done
  503.9 7.9 %collective-permute-start = (bf16[2,128,512]{1,2,0:T(8,128)(2,1)S(1)}, bf16[2,128,512]{1,2,0:T(8,128)(2,1)S(1)}, u32[]{:S(2)}, u32[]{:S(2)}) collective-permute-start(bf16[2,128,512]{1,2,0:T(8,128)(2,1)S(1)} %get-tuple-element.495), channel_id=1, source_target_pairs={{0,2},{2,4},{4,6},{6,8},{8,10},{10,12},{12,14},{14,16},{16,18},{18... | collective-permute-start | bytes 786440 | tf_op jit(solution)/shard_map/while/body/eval_jaxpr/ppermute | solution.py:12
  514.5 6.3 collective-permute-done
  520.8 11.1 %collective-permute-start = (bf16[2,128,512]{1,2,0:T(8,128)(2,1)S(1)}, bf16[2,128,512]{1,2,0:T(8,128)(2,1)S(1)}, u32[]{:S(2)}, u32[]{:S(2)}) collective-permute-start(bf16[2,128,512]{1,2,0:T(8,128)(2,1)S(1)} %get-tuple-element.495), channel_id=1, source_target_pairs={{0,2},{2,4},{4,6},{6,8},{8,10},{10,12},{12,14},{14,16},{16,18},{18... | collective-permute-start | bytes 786440 | tf_op jit(solution)/shard_map/while/body/eval_jaxpr/ppermute | solution.py:12
  534.6 2.6 collective-permute-done
  537.2 9.7 %collective-permute-start = (bf16[2,128,512]{1,2,0:T(8,128)(2,1)S(1)}, bf16[2,128,512]{1,2,0:T(8,128)(2,1)S(1)}, u32[]{:S(2)}, u32[]{:S(2)}) collective-permute-start(bf16[2,128,512]{1,2,0:T(8,128)(2,1)S(1)} %get-tuple-element.495), channel_id=1, source_target_pairs={{0,2},{2,4},{4,6},{6,8},{8,10},{10,12},{12,14},{14,16},{16,18},{18... | collective-permute-start | bytes 786440 | tf_op jit(solution)/shard_map/while/body/eval_jaxpr/ppermute | solution.py:12
  550.2 18.4 %collective-permute-start = (bf16[2,128,512]{1,2,0:T(8,128)(2,1)S(1)}, bf16[2,128,512]{1,2,0:T(8,128)(2,1)S(1)}, u32[]{:S(2)}, u32[]{:S(2)}) collective-permute-start(bf16[2,128,512]{1,2,0:T(8,128)(2,1)S(1)} %get-tuple-element.495), channel_id=1, source_target_pairs={{0,2},{2,4},{4,6},{6,8},{8,10},{10,12},{12,14},{14,16},{16,18},{18... | collective-permute-start | bytes 786440 | tf_op jit(solution)/shard_map/while/body/eval_jaxpr/ppermute | solution.py:12
  571.9 12.5 %collective-permute-start = (bf16[2,128,512]{1,2,0:T(8,128)(2,1)S(1)}, bf16[2,128,512]{1,2,0:T(8,128)(2,1)S(1)}, u32[]{:S(2)}, u32[]{:S(2)}) collective-permute-start(bf16[2,128,512]{1,2,0:T(8,128)(2,1)S(1)} %get-tuple-element.495), channel_id=1, source_target_pairs={{0,2},{2,4},{4,6},{6,8},{8,10},{10,12},{12,14},{14,16},{16,18},{18... | collective-permute-start | bytes 786440 | tf_op jit(solution)/shard_map/while/body/eval_jaxpr/ppermute | solution.py:12
  587.8 33.7 %collective-permute-start = (bf16[2,128,512]{1,2,0:T(8,128)(2,1)S(1)}, bf16[2,128,512]{1,2,0:T(8,128)(2,1)S(1)}, u32[]{:S(2)}, u32[]{:S(2)}) collective-permute-start(bf16[2,128,512]{1,2,0:T(8,128)(2,1)S(1)} %get-tuple-element.495), channel_id=1, source_target_pairs={{0,2},{2,4},{4,6},{6,8},{8,10},{10,12},{12,14},{14,16},{16,18},{18... | collective-permute-start | bytes 786440 | tf_op jit(solution)/shard_map/while/body/eval_jaxpr/ppermute | solution.py:12
  625.3 9.1 %convolution_convert_fusion = bf16[128,4096]{1,0:T(8,128)(2,1)} fusion(bf16[128,2048]{0,1:T(8,128)(2,1)S(1)} %bitcast.65, bf16[2048,4096]{1,0:T(8,128)(2,1)} %all-gather.11.cloned.1.call-done), kind=kOutput, calls=%fused_computation.35 | convolution fusion | flops 2148007936 | bytes 18350080 | tf_op jit(solution)/shard_map/dot_general | solution.py:130
  634.4 70.4 %reduce-scatter.2.cloned.1.call-done = bf16[128,2048]{1,0:T(8,128)(2,1)} async-done(((bf16[128,4096]{1,0:T(8,128)(2,1)}), bf16[128,2048]{1,0:T(8,128)(2,1)}) %reduce-scatter.2.cloned.1.call-update) | async-done | bytes 524304 | tf_op jit(solution)/shard_map/reduce_scatter | solution.py:135
  (176 shorter events, 39.7 us)
Async XLA Ops:
  6.5 4.1 copy-start.2
  6.5 6.1 copy-start
  6.5 80.6 %copy-start.1 = (f32[4096]{0:T(1024)S(1)}, f32[4096]{0:T(1024)}, u32[]{:S(2)}) copy-start(f32[4096]{0:T(1024)} %param.14) | copy-start | bytes 49156
  6.5 80.6 %all-gather.5.cloned.1.call-start = ((), (), s32[]{:S(2)}) async-start(), calls=%async_computation.1 | async-start | bytes 4456448 | tf_op jit(solution)/shard_map/all_gather | solution.py:80
  7.3 157.4 %all-gather.9.cloned.1.call-start = ((), (), s32[]{:S(2)}) async-start(), calls=%async_computation.3 | async-start | bytes 4456448 | tf_op jit(solution)/shard_map/all_gather | solution.py:81
  8.0 350.4 %all-gather.7.cloned.1.call-start = ((), (), s32[]{:S(2)}) async-start(), calls=%async_computation.2 | async-start | bytes 17825792 | tf_op jit(solution)/shard_map/all_gather | solution.py:79
  8.7 616.5 %all-gather.11.cloned.1.call-start = ((), (), s32[]{:S(2)}) async-start(), calls=%async_computation.4 | async-start | bytes 17825792 | tf_op jit(solution)/shard_map/all_gather | solution.py:132
  9.3 695.5 %reduce-scatter.2.cloned.1.call-start = ((), (), s32[]{:S(2)}) async-start(), calls=%async_computation.5 | async-start | bytes 1572864 | tf_op jit(solution)/shard_map/reduce_scatter | solution.py:135
  372.2 13.6 %collective-permute-start = (bf16[2,128,512]{1,2,0:T(8,128)(2,1)S(1)}, bf16[2,128,512]{1,2,0:T(8,128)(2,1)S(1)}, u32[]{:S(2)}, u32[]{:S(2)}) collective-permute-start(bf16[2,128,512]{1,2,0:T(8,128)(2,1)S(1)} %get-tuple-element.495), channel_id=1, source_target_pairs={{0,2},{2,4},{4,6},{6,8},{8,10},{10,12},{12,14},{14,16},{16,18},{18... | collective-permute-start | bytes 786440 | tf_op jit(solution)/shard_map/while/body/eval_jaxpr/ppermute | solution.py:12
  385.8 12.2 %collective-permute-start = (bf16[2,128,512]{1,2,0:T(8,128)(2,1)S(1)}, bf16[2,128,512]{1,2,0:T(8,128)(2,1)S(1)}, u32[]{:S(2)}, u32[]{:S(2)}) collective-permute-start(bf16[2,128,512]{1,2,0:T(8,128)(2,1)S(1)} %get-tuple-element.495), channel_id=1, source_target_pairs={{0,2},{2,4},{4,6},{6,8},{8,10},{10,12},{12,14},{14,16},{16,18},{18... | collective-permute-start | bytes 786440 | tf_op jit(solution)/shard_map/while/body/eval_jaxpr/ppermute | solution.py:12
  398.1 8.0 %collective-permute-start = (bf16[2,128,512]{1,2,0:T(8,128)(2,1)S(1)}, bf16[2,128,512]{1,2,0:T(8,128)(2,1)S(1)}, u32[]{:S(2)}, u32[]{:S(2)}) collective-permute-start(bf16[2,128,512]{1,2,0:T(8,128)(2,1)S(1)} %get-tuple-element.495), channel_id=1, source_target_pairs={{0,2},{2,4},{4,6},{6,8},{8,10},{10,12},{12,14},{14,16},{16,18},{18... | collective-permute-start | bytes 786440 | tf_op jit(solution)/shard_map/while/body/eval_jaxpr/ppermute | solution.py:12
  406.1 17.3 %collective-permute-start = (bf16[2,128,512]{1,2,0:T(8,128)(2,1)S(1)}, bf16[2,128,512]{1,2,0:T(8,128)(2,1)S(1)}, u32[]{:S(2)}, u32[]{:S(2)}) collective-permute-start(bf16[2,128,512]{1,2,0:T(8,128)(2,1)S(1)} %get-tuple-element.495), channel_id=1, source_target_pairs={{0,2},{2,4},{4,6},{6,8},{8,10},{10,12},{12,14},{14,16},{16,18},{18... | collective-permute-start | bytes 786440 | tf_op jit(solution)/shard_map/while/body/eval_jaxpr/ppermute | solution.py:12
  423.5 15.8 %collective-permute-start = (bf16[2,128,512]{1,2,0:T(8,128)(2,1)S(1)}, bf16[2,128,512]{1,2,0:T(8,128)(2,1)S(1)}, u32[]{:S(2)}, u32[]{:S(2)}) collective-permute-start(bf16[2,128,512]{1,2,0:T(8,128)(2,1)S(1)} %get-tuple-element.495), channel_id=1, source_target_pairs={{0,2},{2,4},{4,6},{6,8},{8,10},{10,12},{12,14},{14,16},{16,18},{18... | collective-permute-start | bytes 786440 | tf_op jit(solution)/shard_map/while/body/eval_jaxpr/ppermute | solution.py:12
  439.3 12.1 %collective-permute-start = (bf16[2,128,512]{1,2,0:T(8,128)(2,1)S(1)}, bf16[2,128,512]{1,2,0:T(8,128)(2,1)S(1)}, u32[]{:S(2)}, u32[]{:S(2)}) collective-permute-start(bf16[2,128,512]{1,2,0:T(8,128)(2,1)S(1)} %get-tuple-element.495), channel_id=1, source_target_pairs={{0,2},{2,4},{4,6},{6,8},{8,10},{10,12},{12,14},{14,16},{16,18},{18... | collective-permute-start | bytes 786440 | tf_op jit(solution)/shard_map/while/body/eval_jaxpr/ppermute | solution.py:12
  451.4 8.7 %collective-permute-start = (bf16[2,128,512]{1,2,0:T(8,128)(2,1)S(1)}, bf16[2,128,512]{1,2,0:T(8,128)(2,1)S(1)}, u32[]{:S(2)}, u32[]{:S(2)}) collective-permute-start(bf16[2,128,512]{1,2,0:T(8,128)(2,1)S(1)} %get-tuple-element.495), channel_id=1, source_target_pairs={{0,2},{2,4},{4,6},{6,8},{8,10},{10,12},{12,14},{14,16},{16,18},{18... | collective-permute-start | bytes 786440 | tf_op jit(solution)/shard_map/while/body/eval_jaxpr/ppermute | solution.py:12
  460.2 18.3 %collective-permute-start = (bf16[2,128,512]{1,2,0:T(8,128)(2,1)S(1)}, bf16[2,128,512]{1,2,0:T(8,128)(2,1)S(1)}, u32[]{:S(2)}, u32[]{:S(2)}) collective-permute-start(bf16[2,128,512]{1,2,0:T(8,128)(2,1)S(1)} %get-tuple-element.495), channel_id=1, source_target_pairs={{0,2},{2,4},{4,6},{6,8},{8,10},{10,12},{12,14},{14,16},{16,18},{18... | collective-permute-start | bytes 786440 | tf_op jit(solution)/shard_map/while/body/eval_jaxpr/ppermute | solution.py:12
  478.6 25.3 %collective-permute-start = (bf16[2,128,512]{1,2,0:T(8,128)(2,1)S(1)}, bf16[2,128,512]{1,2,0:T(8,128)(2,1)S(1)}, u32[]{:S(2)}, u32[]{:S(2)}) collective-permute-start(bf16[2,128,512]{1,2,0:T(8,128)(2,1)S(1)} %get-tuple-element.495), channel_id=1, source_target_pairs={{0,2},{2,4},{4,6},{6,8},{8,10},{10,12},{12,14},{14,16},{16,18},{18... | collective-permute-start | bytes 786440 | tf_op jit(solution)/shard_map/while/body/eval_jaxpr/ppermute | solution.py:12
  503.9 16.9 %collective-permute-start = (bf16[2,128,512]{1,2,0:T(8,128)(2,1)S(1)}, bf16[2,128,512]{1,2,0:T(8,128)(2,1)S(1)}, u32[]{:S(2)}, u32[]{:S(2)}) collective-permute-start(bf16[2,128,512]{1,2,0:T(8,128)(2,1)S(1)} %get-tuple-element.495), channel_id=1, source_target_pairs={{0,2},{2,4},{4,6},{6,8},{8,10},{10,12},{12,14},{14,16},{16,18},{18... | collective-permute-start | bytes 786440 | tf_op jit(solution)/shard_map/while/body/eval_jaxpr/ppermute | solution.py:12
  520.8 16.3 %collective-permute-start = (bf16[2,128,512]{1,2,0:T(8,128)(2,1)S(1)}, bf16[2,128,512]{1,2,0:T(8,128)(2,1)S(1)}, u32[]{:S(2)}, u32[]{:S(2)}) collective-permute-start(bf16[2,128,512]{1,2,0:T(8,128)(2,1)S(1)} %get-tuple-element.495), channel_id=1, source_target_pairs={{0,2},{2,4},{4,6},{6,8},{8,10},{10,12},{12,14},{14,16},{16,18},{18... | collective-permute-start | bytes 786440 | tf_op jit(solution)/shard_map/while/body/eval_jaxpr/ppermute | solution.py:12
  537.2 13.0 %collective-permute-start = (bf16[2,128,512]{1,2,0:T(8,128)(2,1)S(1)}, bf16[2,128,512]{1,2,0:T(8,128)(2,1)S(1)}, u32[]{:S(2)}, u32[]{:S(2)}) collective-permute-start(bf16[2,128,512]{1,2,0:T(8,128)(2,1)S(1)} %get-tuple-element.495), channel_id=1, source_target_pairs={{0,2},{2,4},{4,6},{6,8},{8,10},{10,12},{12,14},{14,16},{16,18},{18... | collective-permute-start | bytes 786440 | tf_op jit(solution)/shard_map/while/body/eval_jaxpr/ppermute | solution.py:12
  550.2 21.7 %collective-permute-start = (bf16[2,128,512]{1,2,0:T(8,128)(2,1)S(1)}, bf16[2,128,512]{1,2,0:T(8,128)(2,1)S(1)}, u32[]{:S(2)}, u32[]{:S(2)}) collective-permute-start(bf16[2,128,512]{1,2,0:T(8,128)(2,1)S(1)} %get-tuple-element.495), channel_id=1, source_target_pairs={{0,2},{2,4},{4,6},{6,8},{8,10},{10,12},{12,14},{14,16},{16,18},{18... | collective-permute-start | bytes 786440 | tf_op jit(solution)/shard_map/while/body/eval_jaxpr/ppermute | solution.py:12
  571.9 15.8 %collective-permute-start = (bf16[2,128,512]{1,2,0:T(8,128)(2,1)S(1)}, bf16[2,128,512]{1,2,0:T(8,128)(2,1)S(1)}, u32[]{:S(2)}, u32[]{:S(2)}) collective-permute-start(bf16[2,128,512]{1,2,0:T(8,128)(2,1)S(1)} %get-tuple-element.495), channel_id=1, source_target_pairs={{0,2},{2,4},{4,6},{6,8},{8,10},{10,12},{12,14},{14,16},{16,18},{18... | collective-permute-start | bytes 786440 | tf_op jit(solution)/shard_map/while/body/eval_jaxpr/ppermute | solution.py:12
  587.8 37.0 %collective-permute-start = (bf16[2,128,512]{1,2,0:T(8,128)(2,1)S(1)}, bf16[2,128,512]{1,2,0:T(8,128)(2,1)S(1)}, u32[]{:S(2)}, u32[]{:S(2)}) collective-permute-start(bf16[2,128,512]{1,2,0:T(8,128)(2,1)S(1)} %get-tuple-element.495), channel_id=1, source_target_pairs={{0,2},{2,4},{4,6},{6,8},{8,10},{10,12},{12,14},{14,16},{16,18},{18... | collective-permute-start | bytes 786440 | tf_op jit(solution)/shard_map/while/body/eval_jaxpr/ppermute | solution.py:12
Sparse Core Ops, SparseCore 0:
  10.1 76.9 all-gather.4
  89.9 74.6 all-gather.8
  167.4 190.9 all-gather.6
  361.0 251.8 all-gather.10
  634.6 70.2 reduce-scatter.1
where the time goes:
time: 714 us; the launch traced here: 711 us
  waiting for transfers between devices  460 us (64%)
  starting transfers between devices  164 us (23%)
  matrix products  24.7 us (3%)
  local copies, waits for them, and re-layouts  22 us (3%)
  loops' own time  19.9 us (3%)
  between operations  15.2 us (2%)
    all_gather x1, waiting for transfers between devices, per_device(): query_lin = add_rows(lax.all_gather(w_query, 'ctx', axis=0, tiled=True))  191 us
    ppermute x15, starting transfers between devices, shifted(): return lax.ppermute(block, axis, route)  164 us
    all_gather x1, waiting for transfers between devices, per_device(): key_lin = add_rows(lax.all_gather(w_key, 'ctx', axis=0, tiled=True))  73.9 us
    all_gather x1, waiting for transfers between devices, per_device(): value_lin = add_rows(lax.all_gather(w_value, 'ctx', axis=0, tiled=True))  73.9 us
    reduce_scatter x1, waiting for transfers between devices, per_device(): lax.psum_scatter(partial_out.astype(jnp.bfloat16), 'head', scatter_dimens...  70.4 us
    ppermute x15, waiting for transfers between devices, shifted(): return lax.ppermute(block, axis, route)  48.5 us
    another operation x1, loops' own time, per_device(): lax.fori_loop(1, ctx_count, cycle_turn, (running, kv_pair))  19.6 us
  transfers between devices with their start and end apart: 20, of which 19 were waited for; matrix products, arithmetic and copies ran while one was open for 6% of the time, Pallas kernels for 0%

commit v1 on v0

v1 whole, which is shorter than its diff:
```python
import functools

import jax
import jax.numpy as jnp
from jax import lax
from jax.experimental import pallas as pl
from jax.experimental.pallas import tpu as pltpu
from jax.sharding import Mesh
from jax.sharding import PartitionSpec as P

HD = 128
HALF = HD // 2


def rotary_tables(positions):
    freqs = 500000.0 ** (-(jnp.arange(HALF, dtype=jnp.float32) * 2.0 / HD))
    angles = positions.astype(jnp.float32)[:, None] * freqs[None, :]
    cosine = jnp.cos(angles)
    sine = jnp.sin(angles)
    return (
        jnp.concatenate([cosine, cosine], axis=1),
        jnp.concatenate([-sine, sine], axis=1),
    )


def rotate(values, cosine, sine):
    swapped = jnp.concatenate([values[:, HALF:], values[:, :HALF]], axis=1)
    return values * cosine + swapped * sine


def attention_kernel(blocks, n_query, n_kv, *refs):
    query_refs = refs[:n_query]
    cos_ref, sin_ref, qpos_ref, qstart_ref, kpos_ref = refs[n_query : n_query + 5]
    kv_refs = refs[n_query + 5 : n_query + 5 + n_kv]
    out_ref, rotated, bias = refs[n_query + 5 + n_kv :]
    heads, tokens, _ = rotated.shape
    cosine = cos_ref[...]
    sine = sin_ref[...]
    for h in range(heads):
        lanes = pl.ds(h * HD, HD)
        total = query_refs[0][:, lanes].astype(jnp.float32)
        for ref in query_refs[1:]:
            total = total + ref[:, lanes].astype(jnp.float32)
        turned = total * cosine + pltpu.roll(total, HALF, 1) * sine
        rotated[h] = turned.astype(jnp.bfloat16)
    rows = tokens // blocks
    kv_rows = kv_refs[0].shape[0]
    scale = HD**-0.5
    for j in range(blocks):
        first = j * rows
        length = kv_rows * (j + 1) // blocks
        qpos = qpos_ref[pl.ds(first, rows), :]
        qstart = qstart_ref[pl.ds(first, rows), :]
        for d in range(n_kv):
            kpos = kpos_ref[pl.ds(d, 1), pl.ds(0, length)]
            visible = (kpos <= qpos) & (kpos >= qstart)
            bias[:, pl.ds(d * length, length)] = jnp.where(visible, 0.0, -jnp.inf)

        def one_head(h, unused):
            query = rotated[h, pl.ds(first, rows), :]
            scores = []
            for d in range(n_kv):
                part = lax.dot_general(
                    query,
                    kv_refs[d][pl.ds(0, length), pl.ds(0, HD)],
                    (((1,), (1,)), ((), ())),
                    preferred_element_type=jnp.float32,
                )
                scores.append(part + bias[:, pl.ds(d * length, length)])
            highest = functools.reduce(
                jnp.maximum, [jnp.max(s, axis=1, keepdims=True) for s in scores]
            )
            denominator = 0.0
            mixed = 0.0
            for d in range(n_kv):
                probs = jnp.exp((scores[d] - highest) * scale)
                denominator = denominator + jnp.sum(probs, axis=1, keepdims=True)
                mixed = mixed + jnp.dot(
                    probs.astype(jnp.bfloat16),
                    kv_refs[d][pl.ds(0, length), pl.ds(HD, HD)],
                    preferred_element_type=jnp.float32,
                )
            lanes = pl.ds(pl.multiple_of(h * HD, HD), HD)
            out_ref[pl.ds(first, rows), lanes] = (mixed / denominator).astype(jnp.bfloat16)
            return unused

        lax.fori_loop(0, heads, one_head, 0)


def attention(query_parts, cosine, sine, qpos, qstart, kpos, kv_parts, blocks):
    tokens, width = query_parts[0].shape
    heads = width // HD
    keys = sum(part.shape[0] for part in kv_parts)
    return pl.pallas_call(
        functools.partial(attention_kernel, blocks, len(query_parts), len(kv_parts)),
        out_shape=jax.ShapeDtypeStruct((tokens, width), jnp.bfloat16),
        scratch_shapes=[
            pltpu.VMEM((heads, tokens, HD), jnp.bfloat16),
            pltpu.VMEM((tokens // blocks, keys), jnp.float32),
        ],
        compiler_params=pltpu.CompilerParams(vmem_limit_bytes=48 * 1024 * 1024),
        cost_estimate=pl.CostEstimate(
            flops=4 * tokens * width * keys,
            bytes_accessed=keys * 4 * HD + 4 * tokens * width,
            transcendentals=tokens * heads * keys,
        ),
    )(*query_parts, cosine, sine, qpos, qstart, kpos, *kv_parts)


def project_kernel(attended_ref, weight_ref, out_ref):
    parts, _, depth = attended_ref.shape
    total = 0.0
    for part in range(parts):
        total = total + jnp.dot(
            attended_ref[part],
            weight_ref[0, pl.ds(part * depth, depth), :],
            preferred_element_type=jnp.float32,
        )
    out_ref[...] = total.astype(jnp.bfloat16)


def project(attended, weight):
    parts, tokens, depth = attended.shape
    blocks, rows, width = weight.shape
    return pl.pallas_call(
        project_kernel,
        grid=(blocks,),
        out_shape=jax.ShapeDtypeStruct((tokens, blocks * width), jnp.bfloat16),
        in_specs=[
            pl.BlockSpec((parts, tokens, depth), lambda i: (0, 0, 0)),
            pl.BlockSpec((1, rows, width), lambda i: (i, 0, 0)),
        ],
        out_specs=pl.BlockSpec((tokens, width), lambda i: (0, i)),
        compiler_params=pltpu.CompilerParams(vmem_limit_bytes=48 * 1024 * 1024),
        cost_estimate=pl.CostEstimate(
            flops=2 * tokens * rows * blocks * width,
            bytes_accessed=2 * (rows * blocks * width + tokens * (rows + blocks * width)),
            transcendentals=0,
        ),
    )(attended, weight)


def cyclic(count, distance):
    return [(i, (i + distance) % count) for i in range(count)]


def per_device(tokens, norm_gain, w_query, w_key, w_value, w_out, doc_starts):
    rows, features = tokens.shape
    n_hi = lax.axis_size("hi")
    n_lo = lax.axis_size("lo")
    hi = lax.axis_index("hi")
    lo = lax.axis_index("lo")
    depth = features // n_hi
    kv_local = w_key.shape[1] // HD

    w_pair = jnp.concatenate(
        [
            w_key.reshape(w_key.shape[0], kv_local, HD),
            w_value.reshape(w_value.shape[0], kv_local, HD),
        ],
        axis=2,
    ).reshape(w_key.shape[0], 2 * w_key.shape[1])
    pair_rows = lax.all_gather(w_pair, "lo", axis=0, tiled=True)
    query_rows = lax.all_gather(w_query, "lo", axis=0, tiled=True)
    out_columns = lax.all_gather(w_out, "lo", axis=0) if n_hi > 1 else None

    source = tokens.astype(jnp.float32)
    normed = (
        source * lax.rsqrt(jnp.mean(source * source, axis=1, keepdims=True) + 1e-05) * norm_gain
    ).astype(jnp.bfloat16)

    own = lax.dynamic_slice_in_dim(normed, hi * depth, depth, 1)
    group_rows = n_hi * rows
    gathered = jnp.zeros((group_rows, depth), jnp.bfloat16)
    gathered = lax.dynamic_update_slice_in_dim(gathered, own, hi * rows, 0)
    for d in range(1, n_hi):
        there = lax.rem(hi + d, n_hi)
        piece = lax.dynamic_slice_in_dim(normed, there * depth, depth, 1)
        piece = lax.ppermute(piece, "hi", cyclic(n_hi, d))
        came_from = lax.rem(hi - d + n_hi, n_hi)
        gathered = lax.dynamic_update_slice_in_dim(gathered, piece, came_from * rows, 0)

    def split_sum(weight):
        product = jnp.dot(gathered, weight, preferred_element_type=jnp.float32).astype(
            jnp.bfloat16
        )
        width = weight.shape[1] // n_hi
        parts = [lax.dynamic_slice_in_dim(product, hi * width, width, 1)]
        for d in range(1, n_hi):
            there = lax.rem(hi + d, n_hi)
            piece = lax.dynamic_slice_in_dim(product, there * width, width, 1)
            parts.append(lax.ppermute(piece, "hi", cyclic(n_hi, d)))
        return parts

    row_index = jnp.arange(group_rows, dtype=jnp.int32)

    def positions_of(lo_index):
        return (row_index // rows * n_lo + lo_index) * rows + row_index % rows

    qpos = positions_of(lo)
    qstart = jnp.max(jnp.where(doc_starts[None, :] <= qpos[:, None], doc_starts[None, :], 0), axis=1)
    cosine, sine = rotary_tables(qpos)

    pair_sum = functools.reduce(
        jnp.add, [part.astype(jnp.float32) for part in split_sum(pair_rows)]
    )
    key_proj = rotate(pair_sum[:, :HD], cosine, sine).astype(jnp.bfloat16)
    kv_own = jnp.concatenate([key_proj, pair_sum[:, HD:].astype(jnp.bfloat16)], axis=1)
    if n_hi > 1:
        kv_parts = [kv_own]
        kpos = [qpos]
        for d in range(1, n_lo):
            kv_parts.append(lax.ppermute(kv_own, "lo", cyclic(n_lo, d)))
            kpos.append(positions_of(lax.rem(lo - d + n_lo, n_lo)))
        kpos = jnp.stack(kpos)
    else:
        kv_parts = [lax.all_gather(kv_own, "lo", axis=0, tiled=True)]
        kpos = jnp.arange(n_lo * rows, dtype=jnp.int32)[None, :]

    query_parts = split_sum(query_rows)
    attended = attention(
        query_parts, cosine, sine, qpos[:, None], qstart[:, None], kpos, kv_parts, n_hi
    )
    if n_hi == 1:
        wide = lax.all_gather(w_out, "lo", axis=1, tiled=True)
        partial_out = jnp.dot(attended, wide, preferred_element_type=jnp.float32)
        return lax.psum_scatter(
            partial_out.astype(jnp.bfloat16), "head", scatter_dimension=1, tiled=True
        )
    partial_out = project(lax.all_gather(attended, "hi", axis=0), out_columns)

    head = lax.axis_index("head")
    kept = group_rows // 2
    mine = lax.dynamic_slice_in_dim(partial_out, head * kept, kept, 0)
    theirs = lax.dynamic_slice_in_dim(partial_out, (1 - head) * kept, kept, 0)
    theirs = lax.ppermute(theirs, "head", [(0, 1), (1, 0)])
    summed = (mine.astype(jnp.float32) + theirs.astype(jnp.float32)).astype(jnp.bfloat16)
    arrived = []
    for e in range(2):
        block = lax.rem(hi + e, 2)
        piece = lax.dynamic_slice_in_dim(summed, block * rows, rows, 0)
        route = [
            (z * 2 + g, (2 * g + (z + e) % 2) * 2 + z // 2) for z in range(n_hi) for g in range(2)
        ]
        arrived.append(lax.ppermute(piece, ("hi", "head"), route))
    even = lax.rem(hi, 2) == 0
    return jnp.concatenate(
        [jnp.where(even, arrived[0], arrived[1]), jnp.where(even, arrived[1], arrived[0])], axis=1
    )


def solution(mesh):
    ctx = mesh.shape["ctx"]
    heads = mesh.shape["head"]
    both = ("hi", "lo")
    placed = (
        P(both, None),
        P(),
        P(both, "head"),
        P(both, "head"),
        P(both, "head"),
        P("head", both),
        P(),
    )

    def run(tokens, norm_gain, w_query, w_key, w_value, w_out, doc_starts):
        n_hi = w_key.shape[1] // HD // heads
        grid = Mesh(mesh.devices.reshape(n_hi, ctx // n_hi, heads), ("hi", "lo", "head"))
        return jax.shard_map(
            per_device, mesh=grid, in_specs=placed, out_specs=P(both, "head"), check_vma=False
        )(tokens, norm_gain, w_query, w_key, w_value, w_out, doc_starts)

    return run
```

time: 714 us -> 251 us (0.35)
  waiting for transfers between devices: 460 us -> 179 us
  starting transfers between devices: 164 us -> 21.3 us
  loops' own time: 19.9 us -> 0 us
  Pallas kernels: 0 us -> 17.4 us
  matrix products: 24.7 us -> 7.36 us
  local copies, waits for them, and re-layouts: 22 us -> 6.51 us
    all_gather x4, waiting for transfers between devices: 338 us -> 97.2 us  [the longest x1 48.8 us: per_device(): partial_out = project(lax.all_gather(attended, 'hi', axis=0), out_columns)]
    ppermute x15, starting transfers between devices: 164 us -> 21.1 us  [the longest x6 8.14 us: split_sum(): parts.append(lax.ppermute(piece, 'hi', cyclic(n_hi, d)))]
    reduce_scatter x1 -> x0, waiting for transfers between devices: 70.4 us -> none  [per_device(): lax.psum_scatter(partial_out.astype(jnp.bfloat16), 'head', scatter_dimens...]
    ppermute x15, waiting for transfers between devices: 48.5 us -> 80.6 us  [the longest x6 39.7 us: split_sum(): parts.append(lax.ppermute(piece, 'hi', cyclic(n_hi, d)))]
    slice x33 -> x2, local copies, waits for them, and re-layouts: 20.4 us -> 0.15 us  [the longest x1 0.13 us: rotate(): swapped = jnp.concatenate([values[:, HALF:], values[:, :HALF]], axis=1)]
    another operation x17 -> x0, loops' own time: 19.9 us -> none  [the longest x1 19.6 us: per_device(): lax.fori_loop(1, ctx_count, cycle_turn, (running, kv_pair))]
    dot_general x6 -> x2, matrix products: 24.7 us -> 7.36 us  [split_sum(): jnp.dot(gathered, weight, preferred_element_type=jnp.float32)]
    pallas_call x0 -> x2, Pallas kernels: none -> 17.4 us  [the longest x1 12.6 us: attention(): pl.pallas_call(functools.partial(attention_kernel, blocks, len(query_part...]
  transfers between devices with their start and end apart: 20 -> 19, of which waited for: 19 -> 13; matrix products, arithmetic and copies ran while one was open for 6% -> 5% of each run, Pallas kernels for 0% -> 5%
where the time goes in v1:
time: 251 us; the launch traced here: 250 us
  waiting for transfers between devices  179 us (71%)
  starting transfers between devices  21.3 us (8%)
  Pallas kernels  17.4 us (7%)
  between operations  13.4 us (5%)
  matrix products  7.36 us (3%)
  local copies, waits for them, and re-layouts  6.51 us (3%)
  other arithmetic  4.67 us (2%)
    all_gather x1, waiting for transfers between devices, per_device(): partial_out = project(lax.all_gather(attended, 'hi', axis=0), out_columns)  48.8 us
    ppermute x6, waiting for transfers between devices, split_sum(): parts.append(lax.ppermute(piece, 'hi', cyclic(n_hi, d)))  39.7 us
    all_gather x1, waiting for transfers between devices, per_device(): query_rows = lax.all_gather(w_query, 'lo', axis=0, tiled=True)  29.2 us
    ppermute x3, waiting for transfers between devices, per_device(): piece = lax.ppermute(piece, 'hi', cyclic(n_hi, d))  16.7 us
    all_gather x1, waiting for transfers between devices, per_device(): pair_rows = lax.all_gather(w_pair, 'lo', axis=0, tiled=True)  12.8 us
    ppermute x3, waiting for transfers between devices, per_device(): kv_parts.append(lax.ppermute(kv_own, 'lo', cyclic(n_lo, d)))  12.7 us
    pallas_call x1, Pallas kernels, attention(): pl.pallas_call(functools.partial(attention_kernel, blocks, len(query_part...  12.6 us
    ppermute x2, waiting for transfers between devices, per_device(): arrived.append(lax.ppermute(piece, ('hi', 'head'), route))  9.94 us
  transfers between devices with their start and end apart: 19, of which 13 were waited for; matrix products, arithmetic and copies ran while one was open for 5% of the time, Pallas kernels for 5%

profile of v1, /device:TPU:1, one launch (start us, length us, event | category | flops | bytes accessed | tf_op | source)
XLA Modules:
  0.0 249.8 jit_solution(18140814580204460979)
XLA Ops:
  6.5 1.0 reshape.182
  7.6 1.0 reshape.181
  12.2 2.2 collective-permute-start
  14.4 2.3 collective-permute-start.1
  16.7 1.1 collective-permute-start.2
  17.8 4.8 %collective-permute-done = bf16[128,1024]{1,0:T(8,128)(2,1)S(1)} collective-permute-done((bf16[128,1024]{1,0:T(8,128)(2,1)S(1)}, bf16[128,1024]{1,0:T(8,128)(2,1)S(1)}, u32[]{:S(2)}, u32[]{:S(2)}) %collective-permute-start) | collective-permute-done | bytes 262176 | tf_op jit(solution)/shard_map/ppermute | solution.py:179
  22.6 11.9 %collective-permute-done.1 = bf16[128,1024]{1,0:T(8,128)(2,1)S(1)} collective-permute-done((bf16[128,1024]{1,0:T(8,128)(2,1)S(1)}, bf16[128,1024]{1,0:T(8,128)(2,1)S(1)}, u32[]{:S(2)}, u32[]{:S(2)}) %collective-permute-start.1) | collective-permute-done | bytes 262176 | tf_op jit(solution)/shard_map/ppermute | solution.py:179
  34.5 12.8 %all-gather.9.cloned.1.call-done = bf16[1024,1024]{1,0:T(8,128)(2,1)} async-done(((bf16[256,1024]{1,0:T(8,128)(2,1)}), bf16[1024,1024]{1,0:T(8,128)(2,1)}) %all-gather.9.cloned.1.call-update) | async-done | bytes 2097168 | tf_op jit(solution)/shard_map/all_gather | solution.py:163
  47.3 2.8 %convolution_convert_fusion.1 = bf16[512,1024]{1,0:T(8,128)(2,1)S(1)} fusion(bf16[512,1024]{1,0:T(8,128)(2,1)S(1)} %constant_dynamic-update-slice_fusion, bf16[1024,1024]{1,0:T(8,128)(2,1)} %all-gather.9.cloned.1.call-done), kind=kOutput, calls=%fused_computation.6 | convolution fusion | flops 1074266112 | bytes 4194304 | tf_op jit(solution)/shard_map/dot_general | solution.py:184
  50.3 3.1 %collective-permute-start.8 = (bf16[512,256]{1,0:T(8,128)(2,1)S(1)}, bf16[512,256]{1,0:T(8,128)(2,1)S(1)}, u32[]{:S(2)}, u32[]{:S(2)}) collective-permute-start(bf16[512,256]{1,0:T(8,128)(2,1)S(1)} %get-tuple-element.12), channel_id=1, source_target_pairs={{0,24},{8,0},{16,8},{24,16},{1,25},{9,1},{17,9},{25,17},{2,26},{10... | collective-permute-start | bytes 786440 | tf_op jit(solution)/shard_map/ppermute | solution.py:192
  55.0 3.5 %collective-permute-done.8 = bf16[512,256]{1,0:T(8,128)(2,1)S(1)} collective-permute-done((bf16[512,256]{1,0:T(8,128)(2,1)S(1)}, bf16[512,256]{1,0:T(8,128)(2,1)S(1)}, u32[]{:S(2)}, u32[]{:S(2)}) %collective-permute-start.8) | collective-permute-done | bytes 262176 | tf_op jit(solution)/shard_map/ppermute | solution.py:192
  58.5 16.9 %collective-permute-done.7 = bf16[512,256]{1,0:T(8,128)(2,1)} collective-permute-done((bf16[512,256]{1,0:T(8,128)(2,1)S(1)}, bf16[512,256]{1,0:T(8,128)(2,1)}, u32[]{:S(2)}, u32[]{:S(2)}) %collective-permute-start.7) | collective-permute-done | bytes 262176 | tf_op jit(solution)/shard_map/ppermute | solution.py:192
  75.4 1.2 convert_add_fusion
  77.1 1.2 collective-permute-start.9
  78.3 29.2 %all-gather.7.cloned.1.call-done = bf16[1024,2048]{1,0:T(8,128)(2,1)} async-done(((bf16[256,2048]{1,0:T(8,128)(2,1)}), bf16[1024,2048]{1,0:T(8,128)(2,1)}) %all-gather.7.cloned.1.call-update) | async-done | bytes 4194320 | tf_op jit(solution)/shard_map/all_gather | solution.py:164
  107.5 4.5 %convolution_convert_fusion = bf16[512,2048]{1,0:T(8,128)(2,1)S(1)} fusion(bf16[512,1024]{1,0:T(8,128)(2,1)S(1)} %constant_dynamic-update-slice_fusion, bf16[1024,2048]{1,0:T(8,128)(2,1)} %all-gather.7.cloned.1.call-done), kind=kOutput, calls=%fused_computation | convolution fusion | flops 2148532224 | bytes 7340032 | tf_op jit(solution)/shard_map/dot_general | solution.py:184
  112.1 1.2 constant_dynamic-slice_fusion.6
  113.3 1.3 collective-permute-start.3
  115.4 2.4 collective-permute-start.5
  117.9 1.2 collective-permute-start.10
  119.7 11.2 %collective-permute-done.10.refs_11_ = bf16[512,256]{1,0:T(8,128)(2,1)} collective-permute-done((bf16[512,256]{1,0:T(8,128)(2,1)S(1)}, bf16[512,256]{1,0:T(8,128)(2,1)}, u32[]{:S(2)}, u32[]{:S(2)}) %collective-permute-start.10) | collective-permute-done | bytes 262176 | tf_op jit(solution)/shard_map/ppermute | solution.py:213
  130.9 1.5 collective-permute-done.11.refs_12_
  132.4 19.2 %collective-permute-done.4.refs_2_ = bf16[512,512]{1,0:T(8,128)(2,1)S(1)} collective-permute-done((bf16[512,512]{1,0:T(8,128)(2,1)}, bf16[512,512]{1,0:T(8,128)(2,1)S(1)}, u32[]{:S(2)}, u32[]{:S(2)}) %collective-permute-start.4) | collective-permute-done | bytes 524320 | tf_op jit(solution)/shard_map/ppermute | solution.py:192
  151.7 12.6 %shard_map.73 = bf16[512,512]{1,0:T(8,128)(2,1)} custom-call(bf16[512,512]{1,0:T(8,128)(2,1)S(1)} %get-tuple-element.10.refs_0_, bf16[512,512]{1,0:T(8,128)(2,1)S(1)} %collective-permute-done.3.refs_1_, bf16[512,512]{1,0:T(8,128)(2,1)S(1)} %collective-permute-done.4.refs_2_, bf16[512,512]{1,0:T(8,128)(2,1)S(1)} %collective-permute-done.5.refs_3_, ...), custom_call_target="tpu_custom_call" | custom-call | flops 2147483648 | bytes 2097152 | tf_op jit(solution)/shard_map/pallas_call | solution.py:94
  164.3 6.4 %all-gather.13.cloned.1.call-done = bf16[8192,256]{1,0:T(8,128)(2,1)} async-done(((bf16[2048,256]{1,0:T(8,128)(2,1)}), bf16[8192,256]{1,0:T(8,128)(2,1)}) %all-gather.13.cloned.1.call-update) | async-done | bytes 4194320 | tf_op jit(solution)/shard_map/all_gather | solution.py:165
  170.7 48.8 %all-gather.11.cloned.1.call-done = bf16[2048,512]{1,0:T(8,128)(2,1)} async-done(((bf16[512,512]{1,0:T(8,128)(2,1)}), bf16[2048,512]{1,0:T(8,128)(2,1)}) %all-gather.11.cloned.1.call-update) | async-done | bytes 2097168 | tf_op jit(solution)/shard_map/all_gather | solution.py:230
  219.6 1.6 copy-done
  221.2 4.7 %shard_map.74 = bf16[512,1024]{1,0:T(8,128)(2,1)S(1)} custom-call(bf16[4,512,512]{2,1,0:T(8,128)(2,1)S(1)} %bitcast.9, bf16[4,2048,256]{2,1,0:T(8,128)(2,1)} %bitcast.13), custom_call_target="tpu_custom_call" | custom-call | flops 2147483648 | bytes 7340032 | tf_op jit(solution)/shard_map/pallas_call | solution.py:125
  226.7 1.5 collective-permute-done.12
  228.5 3.0 %collective-permute-start.13 = (bf16[128,1024]{1,0:T(8,128)(2,1)S(1)}, bf16[128,1024]{1,0:T(8,128)(2,1)S(1)}, u32[]{:S(2)}, u32[]{:S(2)}) collective-permute-start(bf16[128,1024]{1,0:T(8,128)(2,1)S(1)} %get-tuple-element.20), channel_id=1, source_target_pairs={{0,0},{1,16},{8,8},{9,24},{16,1},{17,17},{24,9},{25,25},{2,2},{3,1... | collective-permute-start | bytes 786440 | tf_op jit(solution)/shard_map/ppermute | solution.py:245
  231.5 1.0 collective-permute-start.14
  232.5 9.9 %collective-permute-done.13 = bf16[128,1024]{1,0:T(8,128)(2,1)S(1)} collective-permute-done((bf16[128,1024]{1,0:T(8,128)(2,1)S(1)}, bf16[128,1024]{1,0:T(8,128)(2,1)S(1)}, u32[]{:S(2)}, u32[]{:S(2)}) %collective-permute-start.13) | collective-permute-done | bytes 262176 | tf_op jit(solution)/shard_map/ppermute | solution.py:245
  (55 shorter events, 9.1 us)
Async XLA Ops:
  6.5 40.8 %all-gather.9.cloned.1.call-start = ((), (), s32[]{:S(2)}) async-start(), calls=%async_computation.1 | async-start | bytes 2621440 | tf_op jit(solution)/shard_map/all_gather | solution.py:163
  8.9 2.5 copy-start.1
  9.8 1.9 copy-start.2
  9.8 97.7 %all-gather.7.cloned.1.call-start = ((), (), s32[]{:S(2)}) async-start(), calls=%async_computation | async-start | bytes 5242880 | tf_op jit(solution)/shard_map/all_gather | solution.py:164
  10.5 160.2 %all-gather.13.cloned.1.call-start = ((), (), s32[]{:S(2)}) async-start(), calls=%async_computation.3 | async-start | bytes 5242880 | tf_op jit(solution)/shard_map/all_gather | solution.py:165
  11.3 208.3 %all-gather.11.cloned.1.call-start = ((), (), s32[]{:S(2)}) async-start(), calls=%async_computation.2 | async-start | bytes 2621440 | tf_op jit(solution)/shard_map/all_gather | solution.py:230
  12.2 10.3 %collective-permute-start = (bf16[128,1024]{1,0:T(8,128)(2,1)S(1)}, bf16[128,1024]{1,0:T(8,128)(2,1)S(1)}, u32[]{:S(2)}, u32[]{:S(2)}) collective-permute-start(bf16[128,1024]{1,0:T(8,128)(2,1)S(1)} %get-tuple-element.16), channel_id=1, source_target_pairs={{0,8},{8,16},{16,24},{24,0},{1,9},{9,17},{17,25},{25,1},{2,10},{10... | collective-permute-start | bytes 786440 | tf_op jit(solution)/shard_map/ppermute | solution.py:179
  14.4 20.1 %collective-permute-start.1 = (bf16[128,1024]{1,0:T(8,128)(2,1)S(1)}, bf16[128,1024]{1,0:T(8,128)(2,1)S(1)}, u32[]{:S(2)}, u32[]{:S(2)}) collective-permute-start(bf16[128,1024]{1,0:T(8,128)(2,1)S(1)} %get-tuple-element.15), channel_id=1, source_target_pairs={{0,16},{8,24},{16,0},{24,8},{1,17},{9,25},{17,1},{25,9},{2,18},{10... | collective-permute-start | bytes 786440 | tf_op jit(solution)/shard_map/ppermute | solution.py:179
  16.7 17.8 %collective-permute-start.2 = (bf16[128,1024]{1,0:T(8,128)(2,1)S(1)}, bf16[128,1024]{1,0:T(8,128)(2,1)S(1)}, u32[]{:S(2)}, u32[]{:S(2)}) collective-permute-start(bf16[128,1024]{1,0:T(8,128)(2,1)S(1)} %get-tuple-element.14), channel_id=1, source_target_pairs={{0,24},{8,0},{16,8},{24,16},{1,25},{9,1},{17,9},{25,17},{2,26},{10... | collective-permute-start | bytes 786440 | tf_op jit(solution)/shard_map/ppermute | solution.py:179
  50.3 8.2 %collective-permute-start.8 = (bf16[512,256]{1,0:T(8,128)(2,1)S(1)}, bf16[512,256]{1,0:T(8,128)(2,1)S(1)}, u32[]{:S(2)}, u32[]{:S(2)}) collective-permute-start(bf16[512,256]{1,0:T(8,128)(2,1)S(1)} %get-tuple-element.12), channel_id=1, source_target_pairs={{0,24},{8,0},{16,8},{24,16},{1,25},{9,1},{17,9},{25,17},{2,26},{10... | collective-permute-start | bytes 786440 | tf_op jit(solution)/shard_map/ppermute | solution.py:192
  53.4 22.0 %collective-permute-start.7 = (bf16[512,256]{1,0:T(8,128)(2,1)S(1)}, bf16[512,256]{1,0:T(8,128)(2,1)}, u32[]{:S(2)}, u32[]{:S(2)}) collective-permute-start(bf16[512,256]{1,0:T(8,128)(2,1)S(1)} %get-tuple-element.13), channel_id=1, source_target_pairs={{0,16},{8,24},{16,0},{24,8},{1,17},{9,25},{17,1},{25,9},{2,18},{10... | collective-permute-start | bytes 786440 | tf_op jit(solution)/shard_map/ppermute | solution.py:192
  53.4 22.0 %collective-permute-start.6 = (bf16[512,256]{1,0:T(8,128)(2,1)S(1)}, bf16[512,256]{1,0:T(8,128)(2,1)}, u32[]{:S(2)}, u32[]{:S(2)}) collective-permute-start(bf16[512,256]{1,0:T(8,128)(2,1)S(1)} %get-tuple-element.11), channel_id=1, source_target_pairs={{0,8},{8,16},{16,24},{24,0},{1,9},{9,17},{17,25},{25,1},{2,10},{10... | collective-permute-start | bytes 786440 | tf_op jit(solution)/shard_map/ppermute | solution.py:192
  77.1 42.0 %collective-permute-start.9 = (bf16[512,256]{1,0:T(8,128)(2,1)S(1)}, bf16[512,256]{1,0:T(8,128)(2,1)S(1)}, u32[]{:S(2)}, u32[]{:S(2)}) collective-permute-start(bf16[512,256]{1,0:T(8,128)(2,1)S(1)} %pad_maximum_fusion.4.refs_9_), channel_id=1, source_target_pairs={{0,2},{2,4},{4,6},{6,0},{1,3},{3,5},{5,7},{7,1},{8,10},{10,12},{12... | collective-permute-start | bytes 786440 | tf_op jit(solution)/shard_map/ppermute | solution.py:213
  112.1 5.7 %copy-start.3 = (s32[16]{0:T(128)S(1)}, s32[16]{0:T(128)}, u32[]{:S(2)}) copy-start(s32[16]{0:T(128)} %param.13) | copy-start | bytes 196
  113.3 19.1 %collective-permute-start.3 = (bf16[512,512]{1,0:T(8,128)(2,1)}, bf16[512,512]{1,0:T(8,128)(2,1)S(1)}, u32[]{:S(2)}, u32[]{:S(2)}) collective-permute-start(bf16[512,512]{1,0:T(8,128)(2,1)} %get-tuple-element.9), channel_id=1, source_target_pairs={{0,8},{8,16},{16,24},{24,0},{1,9},{9,17},{17,25},{25,1},{2,10},{10... | collective-permute-start | bytes 1572872 | tf_op jit(solution)/shard_map/ppermute | solution.py:192
  114.6 37.1 %collective-permute-start.4 = (bf16[512,512]{1,0:T(8,128)(2,1)}, bf16[512,512]{1,0:T(8,128)(2,1)S(1)}, u32[]{:S(2)}, u32[]{:S(2)}) collective-permute-start(bf16[512,512]{1,0:T(8,128)(2,1)} %get-tuple-element.8), channel_id=1, source_target_pairs={{0,16},{8,24},{16,0},{24,8},{1,17},{9,25},{17,1},{25,9},{2,18},{10... | collective-permute-start | bytes 1572872 | tf_op jit(solution)/shard_map/ppermute | solution.py:192
  115.4 36.2 %collective-permute-start.5 = (bf16[512,512]{1,0:T(8,128)(2,1)}, bf16[512,512]{1,0:T(8,128)(2,1)S(1)}, u32[]{:S(2)}, u32[]{:S(2)}) collective-permute-start(bf16[512,512]{1,0:T(8,128)(2,1)} %get-tuple-element.7), channel_id=1, source_target_pairs={{0,24},{8,0},{16,8},{24,16},{1,25},{9,1},{17,9},{25,17},{2,26},{10... | collective-permute-start | bytes 1572872 | tf_op jit(solution)/shard_map/ppermute | solution.py:192
  117.9 13.0 %collective-permute-start.10 = (bf16[512,256]{1,0:T(8,128)(2,1)S(1)}, bf16[512,256]{1,0:T(8,128)(2,1)}, u32[]{:S(2)}, u32[]{:S(2)}) collective-permute-start(bf16[512,256]{1,0:T(8,128)(2,1)S(1)} %pad_maximum_fusion.4.refs_9_), channel_id=1, source_target_pairs={{0,4},{2,6},{4,0},{6,2},{1,5},{3,7},{5,1},{7,3},{8,12},{10,14},{12... | collective-permute-start | bytes 786440 | tf_op jit(solution)/shard_map/ppermute | solution.py:213
  119.1 13.3 %collective-permute-start.11 = (bf16[512,256]{1,0:T(8,128)(2,1)S(1)}, bf16[512,256]{1,0:T(8,128)(2,1)}, u32[]{:S(2)}, u32[]{:S(2)}) collective-permute-start(bf16[512,256]{1,0:T(8,128)(2,1)S(1)} %pad_maximum_fusion.4.refs_9_), channel_id=1, source_target_pairs={{0,6},{2,0},{4,2},{6,4},{1,7},{3,1},{5,3},{7,5},{8,14},{10,8},{12,... | collective-permute-start | bytes 786440 | tf_op jit(solution)/shard_map/ppermute | solution.py:213
  219.6 1.6 copy-start
  226.0 2.3 collective-permute-start.12
  228.5 13.9 %collective-permute-start.13 = (bf16[128,1024]{1,0:T(8,128)(2,1)S(1)}, bf16[128,1024]{1,0:T(8,128)(2,1)S(1)}, u32[]{:S(2)}, u32[]{:S(2)}) collective-permute-start(bf16[128,1024]{1,0:T(8,128)(2,1)S(1)} %get-tuple-element.20), channel_id=1, source_target_pairs={{0,0},{1,16},{8,8},{9,24},{16,1},{17,17},{24,9},{25,25},{2,2},{3,1... | collective-permute-start | bytes 786440 | tf_op jit(solution)/shard_map/ppermute | solution.py:245
  231.5 10.9 %collective-permute-start.14 = (bf16[128,1024]{1,0:T(8,128)(2,1)S(1)}, bf16[128,1024]{1,0:T(8,128)(2,1)S(1)}, u32[]{:S(2)}, u32[]{:S(2)}) collective-permute-start(bf16[128,1024]{1,0:T(8,128)(2,1)S(1)} %get-tuple-element.21), channel_id=1, source_target_pairs={{0,8},{1,24},{8,0},{9,16},{16,9},{17,25},{24,1},{25,17},{2,10},{3,... | collective-permute-start | bytes 786440 | tf_op jit(solution)/shard_map/ppermute | solution.py:245
Sparse Core Ops, SparseCore 0:
  9.9 37.3 all-gather.8
  49.2 58.3 all-gather.6
  109.4 61.3 all-gather.12
  172.2 47.3 all-gather.10

commit v2 on v1

v2 whole, which is shorter than its diff:
```python
import functools

import jax
import jax.numpy as jnp
from jax import lax
from jax.experimental import pallas as pl
from jax.experimental.pallas import tpu as pltpu
from jax.sharding import Mesh
from jax.sharding import PartitionSpec as P

HD = 128
HALF = HD // 2


def rotary_tables(positions):
    freqs = 500000.0 ** (-(jnp.arange(HALF, dtype=jnp.float32) * 2.0 / HD))
    angles = positions.astype(jnp.float32)[:, None] * freqs[None, :]
    cosine = jnp.cos(angles)
    sine = jnp.sin(angles)
    return (
        jnp.concatenate([cosine, cosine], axis=1),
        jnp.concatenate([-sine, sine], axis=1),
    )


def rotate(values, cosine, sine):
    swapped = jnp.concatenate([values[:, HALF:], values[:, :HALF]], axis=1)
    return values * cosine + swapped * sine


def attention_kernel(blocks, n_query, n_kv, *refs):
    query_refs = refs[:n_query]
    cos_ref, sin_ref, qpos_ref, qstart_ref, kpos_ref = refs[n_query : n_query + 5]
    kv_refs = refs[n_query + 5 : n_query + 5 + n_kv]
    out_ref, rotated, bias = refs[n_query + 5 + n_kv :]
    heads, tokens, _ = rotated.shape
    cosine = cos_ref[...]
    sine = sin_ref[...]
    for h in range(heads):
        lanes = pl.ds(h * HD, HD)
        total = query_refs[0][:, lanes].astype(jnp.float32)
        for ref in query_refs[1:]:
            total = total + ref[:, lanes].astype(jnp.float32)
        turned = total * cosine + pltpu.roll(total, HALF, 1) * sine
        rotated[h] = turned.astype(jnp.bfloat16)
    rows = tokens // blocks
    kv_rows = kv_refs[0].shape[0]
    scale = HD**-0.5
    for j in range(blocks):
        first = j * rows
        length = kv_rows * (j + 1) // blocks
        qpos = qpos_ref[pl.ds(first, rows), :]
        qstart = qstart_ref[pl.ds(first, rows), :]
        for d in range(n_kv):
            kpos = kpos_ref[pl.ds(d, 1), pl.ds(0, length)]
            visible = (kpos <= qpos) & (kpos >= qstart)
            bias[:, pl.ds(d * length, length)] = jnp.where(visible, 0.0, -jnp.inf)

        def one_head(h, unused):
            query = rotated[h, pl.ds(first, rows), :]
            scores = []
            for d in range(n_kv):
                part = lax.dot_general(
                    query,
                    kv_refs[d][pl.ds(0, length), pl.ds(0, HD)],
                    (((1,), (1,)), ((), ())),
                    preferred_element_type=jnp.float32,
                )
                scores.append(part + bias[:, pl.ds(d * length, length)])
            highest = functools.reduce(
                jnp.maximum, [jnp.max(s, axis=1, keepdims=True) for s in scores]
            )
            denominator = 0.0
            mixed = 0.0
            for d in range(n_kv):
                probs = jnp.exp((scores[d] - highest) * scale)
                denominator = denominator + jnp.sum(probs, axis=1, keepdims=True)
                mixed = mixed + jnp.dot(
                    probs.astype(jnp.bfloat16),
                    kv_refs[d][pl.ds(0, length), pl.ds(HD, HD)],
                    preferred_element_type=jnp.float32,
                )
            lanes = pl.ds(pl.multiple_of(h * HD, HD), HD)
            out_ref[pl.ds(first, rows), lanes] = (mixed / denominator).astype(jnp.bfloat16)
            return unused

        lax.fori_loop(0, heads, one_head, 0)


def attention(query_parts, cosine, sine, qpos, qstart, kpos, kv_parts, blocks):
    tokens, width = query_parts[0].shape
    heads = width // HD
    keys = sum(part.shape[0] for part in kv_parts)
    return pl.pallas_call(
        functools.partial(attention_kernel, blocks, len(query_parts), len(kv_parts)),
        out_shape=jax.ShapeDtypeStruct((tokens, width), jnp.bfloat16),
        scratch_shapes=[
            pltpu.VMEM((heads, tokens, HD), jnp.bfloat16),
            pltpu.VMEM((tokens // blocks, keys), jnp.float32),
        ],
        compiler_params=pltpu.CompilerParams(vmem_limit_bytes=20 * 1024 * 1024),
        cost_estimate=pl.CostEstimate(
            flops=4 * tokens * width * keys,
            bytes_accessed=keys * 4 * HD + 4 * tokens * width,
            transcendentals=tokens * heads * keys,
        ),
    )(*query_parts, cosine, sine, qpos, qstart, kpos, *kv_parts)


def project_kernel(place_ref, *refs):
    attended_refs = refs[:4]
    weight_refs = refs[4:8]
    total_refs = refs[8:-2]
    hi = place_ref[0]
    lo = place_ref[1]
    core = place_ref[2]
    depth = attended_refs[0].shape[1]
    width = weight_refs[0].shape[1]
    span = weight_refs[0].shape[0] // 4
    offset = place_ref[3]
    for side, out_ref in enumerate(refs[-2:]):
        kept = out_ref.shape[0]
        rows = pl.ds(pl.multiple_of(lax.rem(core + side, 2) * kept, kept), kept)
        for r, weight_ref in enumerate(weight_refs):
            columns = pl.ds(pl.multiple_of((lo ^ r) * width, width), width)
            total = total_refs[side][:, columns] if total_refs else 0.0
            for k, attended_ref in enumerate(attended_refs):
                first = lax.rem(hi - k + 4, 4) * span + offset
                total = total + jnp.dot(
                    attended_ref[rows, :],
                    weight_ref[pl.ds(pl.multiple_of(first, depth), depth), :],
                    preferred_element_type=jnp.float32,
                )
            out_ref[:, columns] = total.astype(out_ref.dtype)


def project(place, attended_parts, weights, totals, kind):
    tokens, depth = attended_parts[0].shape
    width = weights[0].shape[1]
    shape = jax.ShapeDtypeStruct((tokens // 2, 4 * width), kind)
    operands = (*attended_parts, *weights, *totals)
    return pl.pallas_call(
        project_kernel,
        in_specs=[pl.BlockSpec(memory_space=pltpu.SMEM)]
        + [pl.BlockSpec(memory_space=pltpu.VMEM)] * len(operands),
        out_shape=(shape, shape),
        compiler_params=pltpu.CompilerParams(vmem_limit_bytes=20 * 1024 * 1024),
        cost_estimate=pl.CostEstimate(
            flops=2 * tokens * 4 * depth * 4 * width,
            bytes_accessed=sum(x.size * x.dtype.itemsize for x in operands),
            transcendentals=0,
        ),
    )(place, *operands)


def cyclic(count, distance):
    return [(i, (i + distance) % count) for i in range(count)]


def normalised(tokens, norm_gain):
    source = tokens.astype(jnp.float32)
    return (
        source * lax.rsqrt(jnp.mean(source * source, axis=1, keepdims=True) + 1e-05) * norm_gain
    ).astype(jnp.bfloat16)


def document_start(positions, doc_starts):
    begun = doc_starts[None, :] <= positions[:, None]
    return jnp.max(jnp.where(begun, doc_starts[None, :], 0), axis=1)


def plain_device(tokens, norm_gain, w_query, w_key, w_value, w_out, doc_starts):
    rows = tokens.shape[0]
    count = lax.axis_size("ctx")
    normed = normalised(tokens, norm_gain)

    def project_with(weight):
        gathered = lax.all_gather(weight, "ctx", axis=0, tiled=True)
        return jnp.dot(normed, gathered, preferred_element_type=jnp.float32)

    qpos = lax.axis_index("ctx") * rows + jnp.arange(rows, dtype=jnp.int32)
    qstart = document_start(qpos, doc_starts)
    cosine, sine = rotary_tables(qpos)
    kpos = jnp.arange(count * rows, dtype=jnp.int32)[None, :]
    query = project_with(w_query)
    key = project_with(w_key)
    value = project_with(w_value).astype(jnp.bfloat16)
    kv_local = w_key.shape[1] // HD
    group = w_query.shape[1] // kv_local
    mixed = []
    for h in range(kv_local):
        lanes = slice(h * HD, (h + 1) * HD)
        turned = rotate(key[:, lanes], cosine, sine).astype(jnp.bfloat16)
        pair = jnp.concatenate([turned, value[:, lanes]], axis=1)
        pair = lax.all_gather(pair, "ctx", axis=0, tiled=True)
        part = query[:, h * group : (h + 1) * group]
        mixed.append(
            attention([part], cosine, sine, qpos[:, None], qstart[:, None], kpos, [pair], 1)
        )
    attended = jnp.concatenate(mixed, axis=1)
    wide = lax.all_gather(w_out, "ctx", axis=1, tiled=True)
    partial_out = jnp.dot(attended, wide, preferred_element_type=jnp.float32)
    return lax.psum_scatter(
        partial_out.astype(jnp.bfloat16), "head", scatter_dimension=1, tiled=True
    )


def after(value, *earlier):
    return lax.optimization_barrier((value, *earlier))[0]


def beside(value, bit):
    return lax.ppermute(value, "lo", [(i, i ^ bit) for i in range(4)])


def across(from_one, from_two):
    half = from_one.shape[0] // 2
    return beside(from_two[:half], 1), beside(from_one[half:], 2)


def line_device(tokens, norm_gain, w_query, w_key, w_value, w_out, doc_starts):
    rows, features = tokens.shape
    hi = lax.axis_index("hi")
    lo = lax.axis_index("lo")
    core = lax.axis_index("head")
    depth = features // 4
    share = depth // 4
    group_rows = 4 * rows
    heads = w_query.shape[1] // 4

    w_pair = jnp.concatenate([w_key, w_value], axis=1)
    half = heads // 2
    w_halves = [
        jnp.concatenate(
            [w_query[:, z * heads + c * half : z * heads + (c + 1) * half] for z in range(4)],
            axis=1,
        )
        for c in range(2)
    ]

    def spread(pieces):
        return [pieces[0]] + [lax.ppermute(pieces[d], "hi", cyclic(4, d)) for d in range(1, 4)]

    pair_one, pair_two = beside(w_pair, 1), beside(w_pair, 2)
    w_a = after(w_halves[0], pair_one, pair_two)
    pair_cross = across(pair_one, pair_two)
    a_one, a_two = beside(w_a, 1), beside(w_a, 2)
    w_b = after(w_halves[1], a_one, a_two)
    a_cross = across(a_one, a_two)
    b_one, b_two = beside(w_b, 1), beside(w_b, 2)
    b_cross = across(b_one, b_two)
    w_o = after(w_out, *b_cross)
    o_one, o_two = beside(w_o, 1), beside(w_o, 2)
    o_cross = jnp.concatenate(across(o_one, o_two), axis=0)

    normed = normalised(tokens, norm_gain)
    pieces = []
    for d in range(4):
        first = lax.rem(hi + d, 4) * depth
        pieces.append(
            jnp.concatenate(
                [
                    lax.dynamic_slice_in_dim(normed, first + (lo ^ r) * share, share, 1)
                    for r in range(4)
                ],
                axis=1,
            )
        )
    gathered = jnp.zeros((group_rows, depth), jnp.bfloat16)
    for d, piece in enumerate(spread(pieces)):
        gathered = lax.dynamic_update_slice_in_dim(
            gathered, piece, lax.rem(hi - d + 4, 4) * rows, 0
        )

    def product(own, one, two, cross):
        total = jnp.dot(gathered[:, :share], own, preferred_element_type=jnp.float32)
        place = share
        for weight in (one, two, *cross):
            depth_here = weight.shape[0]
            total = total + jnp.dot(
                gathered[:, place : place + depth_here],
                weight,
                preferred_element_type=jnp.float32,
            )
            place += depth_here
        return total.astype(jnp.bfloat16)

    row_index = jnp.arange(group_rows, dtype=jnp.int32)

    def positions_of(lo_index):
        return (row_index // rows * 4 + lo_index) * rows + row_index % rows

    qpos = positions_of(lo)
    qstart = document_start(qpos, doc_starts)
    cosine, sine = rotary_tables(qpos)
    kpos = jnp.stack([positions_of(lo ^ r) for r in range(4)])

    pair_product = product(w_pair, pair_one, pair_two, pair_cross)
    kv_width = w_key.shape[1]
    pieces = []
    for d in range(4):
        first = lax.rem(hi + d, 4) * HD
        pieces.append(
            jnp.concatenate(
                [
                    lax.dynamic_slice_in_dim(pair_product, first, HD, 1),
                    lax.dynamic_slice_in_dim(pair_product, first + kv_width, HD, 1),
                ],
                axis=1,
            )
        )
    pair_sum = functools.reduce(jnp.add, [part.astype(jnp.float32) for part in spread(pieces)])
    key_proj = rotate(pair_sum[:, :HD], cosine, sine).astype(jnp.bfloat16)
    kv_own = jnp.concatenate([key_proj, pair_sum[:, HD:].astype(jnp.bfloat16)], axis=1)
    kv_parts = [kv_own] + [
        lax.ppermute(kv_own, "lo", [(i, i ^ r) for i in range(4)]) for r in range(1, 4)
    ]

    place = jnp.stack([hi, lo, core])
    totals = ()
    kinds = (jnp.float32, jnp.bfloat16)
    chunks = [(w_a, a_one, a_two, a_cross), (w_b, b_one, b_two, b_cross)]
    for c, chunk in enumerate(chunks):
        query = product(*chunk)
        query_parts = spread(
            [lax.dynamic_slice_in_dim(query, lax.rem(hi + d, 4) * half, half, 1) for d in range(4)]
        )
        attended = attention(
            query_parts, cosine, sine, qpos[:, None], qstart[:, None], kpos, kv_parts, 4
        )
        attended_parts = [attended] + [
            lax.ppermute(attended, "hi", cyclic(4, d)) for d in range(1, 4)
        ]
        where = jnp.concatenate([place, jnp.full((1,), c * half, jnp.int32)])
        totals = project(where, attended_parts, (w_o, o_one, o_two, o_cross), totals, kinds[c])

    mine, theirs = totals
    theirs = lax.ppermute(theirs, "head", [(0, 1), (1, 0)])
    summed = (mine.astype(jnp.float32) + theirs.astype(jnp.float32)).astype(jnp.bfloat16)
    arrived = []
    for e in range(2):
        block = lax.rem(hi + e, 2)
        piece = lax.dynamic_slice_in_dim(summed, block * rows, rows, 0)
        route = [(z * 2 + g, (2 * g + (z + e) % 2) * 2 + z // 2) for z in range(4) for g in range(2)]
        arrived.append(lax.ppermute(piece, ("hi", "head"), route))
    even = lax.rem(hi, 2) == 0
    return jnp.concatenate(
        [jnp.where(even, arrived[0], arrived[1]), jnp.where(even, arrived[1], arrived[0])], axis=1
    )


def solution(mesh):
    ctx = mesh.shape["ctx"]
    heads = mesh.shape["head"]

    def run(tokens, norm_gain, w_query, w_key, w_value, w_out, doc_starts):
        lines = w_key.shape[1] // HD // heads
        if (ctx, heads, lines) == (16, 2, 4):
            both = ("hi", "lo")
            grid = Mesh(mesh.devices.reshape(4, 4, 2), ("hi", "lo", "head"))
            body = line_device
        else:
            both, grid, body = "ctx", mesh, plain_device
        placed = (
            P(both, None),
            P(),
            P(both, "head"),
            P(both, "head"),
            P(both, "head"),
            P("head", both),
            P(),
        )
        return jax.shard_map(
            body, mesh=grid, in_specs=placed, out_specs=P(both, "head"), check_vma=False
        )(tokens, norm_gain, w_query, w_key, w_value, w_out, doc_starts)

    return run
```

time: 251 us -> 239 us (0.952)
  waiting for transfers between devices: 179 us -> 102 us
  starting transfers between devices: 21.3 us -> 80.7 us
  between operations: 13.4 us -> 0.84 us
  other arithmetic: 4.67 us -> 11.2 us
  local copies, waits for them, and re-layouts: 6.51 us -> 12.9 us
  matrix products: 7.36 us -> 12.1 us
    all_gather x4 -> x0, waiting for transfers between devices: 97.2 us -> none  [the longest x1 48.8 us: per_device(): partial_out = project(lax.all_gather(attended, 'hi', axis=0), out_columns)]
    ppermute x15 -> x40, starting transfers between devices: 21.1 us -> 80.7 us  [the longest x12 34.3 us: spread(): lax.ppermute(pieces[d], 'hi', cyclic(4, d))]
    ppermute x15 -> x40, waiting for transfers between devices: 80.6 us -> 102 us  [the longest x12 41.3 us: spread(): lax.ppermute(pieces[d], 'hi', cyclic(4, d))]
    dot_general x2 -> x15, matrix products: 7.36 us -> 12.1 us  [the longest x12 9.37 us: product(): jnp.dot(gathered[:, place:place + depth_here], weight, preferred_element_...]
    concatenate x3 -> x12, other arithmetic: 1.14 us -> 4.09 us  [the longest x3 2.18 us: line_device(): jnp.concatenate([lax.dynamic_slice_in_dim(normed, first + (lo ^ r) * shar...]
    dynamic_update_slice x3, local copies, waits for them, and re-layouts: 0.07 us -> 2.92 us  [line_device(): lax.dynamic_update_slice_in_dim(gathered, piece, lax.rem(hi - d + 4, 4) *...]
    pallas_call x1 -> x2, Pallas kernels: 12.6 us -> 13.8 us  [attention(): pl.pallas_call(functools.partial(attention_kernel, blocks, len(query_part...]
  transfers between devices with their start and end apart: 19 -> 40, of which waited for: 13 -> 15; matrix products, arithmetic and copies ran while one was open for 5% -> 12% of each run, Pallas kernels for 5% -> 7%
where the time goes in v2:
time: 239 us; the launch traced here: 238 us
  waiting for transfers between devices  102 us (43%)
  starting transfers between devices  80.7 us (34%)
  Pallas kernels  18.4 us (8%)
  local copies, waits for them, and re-layouts  12.9 us (5%)
  matrix products  12.1 us (5%)
  other arithmetic  11.2 us (5%)
    ppermute x12, waiting for transfers between devices, spread(): lax.ppermute(pieces[d], 'hi', cyclic(4, d))  41.3 us
    ppermute x16, waiting for transfers between devices, beside(): return lax.ppermute(value, 'lo', [(i, i ^ bit) for i in range(4)])  36.2 us
    ppermute x12, starting transfers between devices, spread(): lax.ppermute(pieces[d], 'hi', cyclic(4, d))  34.3 us
    ppermute x6, starting transfers between devices, line_device(): lax.ppermute(attended, 'hi', cyclic(4, d))  20.8 us
    ppermute x6, waiting for transfers between devices, line_device(): lax.ppermute(attended, 'hi', cyclic(4, d))  15.5 us
    pallas_call x2, Pallas kernels, attention(): pl.pallas_call(functools.partial(attention_kernel, blocks, len(query_part...  13.8 us
    ppermute x16, starting transfers between devices, beside(): return lax.ppermute(value, 'lo', [(i, i ^ bit) for i in range(4)])  12.9 us
    dot_general x12, matrix products, product(): jnp.dot(gathered[:, place:place + depth_here], weight, preferred_element_...  9.37 us
  transfers between devices with their start and end apart: 40, of which 15 were waited for; matrix products, arithmetic and copies ran while one was open for 12% of the time, Pallas kernels for 7%

profile of v2, /device:TPU:1, one launch (start us, length us, event | category | flops | bytes accessed | tf_op | source)
XLA Modules:
  0.0 237.7 jit_solution(8936747544065340468)
XLA Ops:
  3.4 2.0 collective-permute-start.3
  12.3 2.3 collective-permute-start.1
  17.3 1.9 fusion.52
  20.7 11.2 %collective-permute-done.1 = bf16[128,1024]{1,0:T(8,128)(2,1)} collective-permute-done((bf16[128,1024]{1,0:T(8,128)(2,1)}, bf16[128,1024]{1,0:T(8,128)(2,1)}, u32[]{:S(2)}, u32[]{:S(2)}) %collective-permute-start.1) | collective-permute-done | bytes 262176 | tf_op jit(solution)/shard_map/ppermute | solution.py:242
  42.2 12.1 %collective-permute-done.14 = bf16[128,1024]{1,0:T(8,128)(2,1)S(1)} collective-permute-done((bf16[128,1024]{1,0:T(8,128)(2,1)S(1)}, bf16[128,1024]{1,0:T(8,128)(2,1)S(1)}, u32[]{:S(2)}, u32[]{:S(2)}) %collective-permute-start.14) | collective-permute-done | bytes 262176 | tf_op jit(solution)/shard_map/ppermute | solution.py:213
  55.7 3.7 %collective-permute-start.18 = (bf16[512,256]{1,0:T(8,128)(2,1)S(1)}, bf16[512,256]{1,0:T(8,128)(2,1)S(1)}, u32[]{:S(2)}, u32[]{:S(2)}) collective-permute-start(bf16[512,256]{1,0:T(8,128)(2,1)S(1)} %pad_maximum_fusion.10), channel_id=1, source_target_pairs={{0,24},{8,0},{16,8},{24,16},{1,25},{9,1},{17,9},{25,17},{2,26},{10... | collective-permute-start | bytes 786440 | tf_op jit(solution)/shard_map/ppermute | solution.py:242
  59.4 2.6 %collective-permute-start.17 = (bf16[512,256]{1,0:T(8,128)(2,1)S(1)}, bf16[512,256]{1,0:T(8,128)(2,1)S(1)}, u32[]{:S(2)}, u32[]{:S(2)}) collective-permute-start(bf16[512,256]{1,0:T(8,128)(2,1)S(1)} %pad_maximum_fusion.9), channel_id=1, source_target_pairs={{0,16},{8,24},{16,0},{24,8},{1,17},{9,25},{17,1},{25,9},{2,18},{10... | collective-permute-start | bytes 786440 | tf_op jit(solution)/shard_map/ppermute | solution.py:242
  63.6 2.4 %collective-permute-done.18 = bf16[512,256]{1,0:T(8,128)(2,1)S(1)} collective-permute-done((bf16[512,256]{1,0:T(8,128)(2,1)S(1)}, bf16[512,256]{1,0:T(8,128)(2,1)S(1)}, u32[]{:S(2)}, u32[]{:S(2)}) %collective-permute-start.18) | collective-permute-done | bytes 262176 | tf_op jit(solution)/shard_map/ppermute | solution.py:242
  66.0 17.7 %collective-permute-done.17 = bf16[512,256]{1,0:T(8,128)(2,1)S(1)} collective-permute-done((bf16[512,256]{1,0:T(8,128)(2,1)S(1)}, bf16[512,256]{1,0:T(8,128)(2,1)S(1)}, u32[]{:S(2)}, u32[]{:S(2)}) %collective-permute-start.17) | collective-permute-done | bytes 262176 | tf_op jit(solution)/shard_map/ppermute | solution.py:242
  88.5 8.7 %collective-permute-done.29 = bf16[128,1024]{1,0:T(8,128)(2,1)S(1)} collective-permute-done((bf16[128,1024]{1,0:T(8,128)(2,1)S(1)}, bf16[128,1024]{1,0:T(8,128)(2,1)S(1)}, u32[]{:S(2)}, u32[]{:S(2)}) %collective-permute-start.29) | collective-permute-done | bytes 262176 | tf_op jit(solution)/shard_map/ppermute | solution.py:213
  97.8 4.6 %collective-permute-done.30 = bf16[128,1024]{1,0:T(8,128)(2,1)S(1)} collective-permute-done((bf16[128,1024]{1,0:T(8,128)(2,1)S(1)}, bf16[128,1024]{1,0:T(8,128)(2,1)S(1)}, u32[]{:S(2)}, u32[]{:S(2)}) %collective-permute-start.30) | collective-permute-done | bytes 262176 | tf_op jit(solution)/shard_map/ppermute | solution.py:213
  107.3 3.3 %collective-permute-done.9 = bf16[128,1024]{1,0:T(8,128)(2,1)S(1)} collective-permute-done((bf16[128,1024]{1,0:T(8,128)(2,1)S(1)}, bf16[128,1024]{1,0:T(8,128)(2,1)S(1)}, u32[]{:S(2)}, u32[]{:S(2)}) %collective-permute-start.9) | collective-permute-done | bytes 262176 | tf_op jit(solution)/shard_map/ppermute | solution.py:213
  115.0 7.4 %collective-permute-start.31 = (bf16[512,256]{1,0:T(8,128)(2,1)}, bf16[512,256]{1,0:T(8,128)(2,1)}, u32[]{:S(2)}, u32[]{:S(2)}) collective-permute-start(bf16[512,256]{1,0:T(8,128)(2,1)} %get-tuple-element.25), channel_id=1, source_target_pairs={{0,8},{8,16},{16,24},{24,0},{1,9},{9,17},{17,25},{25,1},{2,10},{10... | collective-permute-start | bytes 786440 | tf_op jit(solution)/shard_map/ppermute | solution.py:242
  123.9 2.0 collective-permute-start.32
  126.0 6.5 %collective-permute-done.25.refs_5_ = bf16[2048,256]{1,0:T(8,128)(2,1)S(1)} collective-permute-done((bf16[2048,256]{1,0:T(8,128)(2,1)S(1)}, bf16[2048,256]{1,0:T(8,128)(2,1)S(1)}, u32[]{:S(2)}, u32[]{:S(2)}) %collective-permute-start.25) | collective-permute-done | bytes 1048608 | tf_op jit(solution)/shard_map/ppermute | solution.py:213
  132.5 6.2 %collective-permute-start.33 = (bf16[512,256]{1,0:T(8,128)(2,1)}, bf16[512,256]{1,0:T(8,128)(2,1)}, u32[]{:S(2)}, u32[]{:S(2)}) collective-permute-start(bf16[512,256]{1,0:T(8,128)(2,1)} %get-tuple-element.23), channel_id=1, source_target_pairs={{0,24},{8,0},{16,8},{24,16},{1,25},{9,1},{17,9},{25,17},{2,26},{10... | collective-permute-start | bytes 786440 | tf_op jit(solution)/shard_map/ppermute | solution.py:242
  139.6 3.2 %collective-permute-start.11 = (bf16[512,256]{1,0:T(8,128)(2,1)}, bf16[512,256]{1,0:T(8,128)(2,1)}, u32[]{:S(2)}, u32[]{:S(2)}) collective-permute-start(bf16[512,256]{1,0:T(8,128)(2,1)} %get-tuple-element.37), channel_id=1, source_target_pairs={{0,8},{8,16},{16,24},{24,0},{1,9},{9,17},{17,25},{25,1},{2,10},{10... | collective-permute-start | bytes 786440 | tf_op jit(solution)/shard_map/ppermute | solution.py:242
  144.8 3.4 %collective-permute-start.12 = (bf16[512,256]{1,0:T(8,128)(2,1)S(1)}, bf16[512,256]{1,0:T(8,128)(2,1)S(1)}, u32[]{:S(2)}, u32[]{:S(2)}) collective-permute-start(bf16[512,256]{1,0:T(8,128)(2,1)S(1)} %copy-done.18), channel_id=1, source_target_pairs={{0,16},{8,24},{16,0},{24,8},{1,17},{9,25},{17,1},{25,9},{2,18},{10... | collective-permute-start | bytes 786440 | tf_op jit(solution)/shard_map/ppermute | solution.py:242
  149.2 7.0 %shard_map.74.refs_0_ = bf16[512,256]{1,0:T(8,128)(2,1)S(1)} custom-call(bf16[512,256]{1,0:T(8,128)(2,1)S(1)} %copy-done.3, bf16[512,256]{1,0:T(8,128)(2,1)} %collective-permute-done.31.refs_1_, bf16[512,256]{1,0:T(8,128)(2,1)} %collective-permute-done.32.refs_2_, bf16[512,256]{1,0:T(8,128)(2,1)} %collective-permute-done.33.refs_3_, ...), custom_call_target="tpu_custom_call" | custom-call | flops 1073741824 | bytes 1572864 | tf_op jit(solution)/shard_map/pallas_call | solution.py:94
  156.9 9.9 %collective-permute-done.12.refs_2_ = bf16[512,256]{1,0:T(8,128)(2,1)S(1)} collective-permute-done((bf16[512,256]{1,0:T(8,128)(2,1)S(1)}, bf16[512,256]{1,0:T(8,128)(2,1)S(1)}, u32[]{:S(2)}, u32[]{:S(2)}) %collective-permute-start.12) | collective-permute-done | bytes 262176 | tf_op jit(solution)/shard_map/ppermute | solution.py:242
  166.7 8.1 %collective-permute-start.36 = (bf16[512,256]{1,0:T(8,128)(2,1)S(1)}, bf16[512,256]{1,0:T(8,128)(2,1)S(1)}, u32[]{:S(2)}, u32[]{:S(2)}) collective-permute-start(bf16[512,256]{1,0:T(8,128)(2,1)S(1)} %shard_map.74.refs_0_), channel_id=1, source_target_pairs={{0,24},{8,0},{16,8},{24,16},{1,25},{9,1},{17,9},{25,17},{2,26},{10... | collective-permute-start | bytes 786440 | tf_op jit(solution)/shard_map/ppermute | solution.py:332
  174.8 6.8 %shard_map.73.refs_0_ = bf16[512,256]{1,0:T(8,128)(2,1)S(1)} custom-call(bf16[512,256]{1,0:T(8,128)(2,1)S(1)} %copy-done.4, bf16[512,256]{1,0:T(8,128)(2,1)} %collective-permute-done.11.refs_1_, bf16[512,256]{1,0:T(8,128)(2,1)S(1)} %collective-permute-done.12.refs_2_, bf16[512,256]{1,0:T(8,128)(2,1)S(1)} %collective-permute-done.13.refs_3_, ...), custom_call_target="tpu_custom_call" | custom-call | flops 1073741824 | bytes 1572864 | tf_op jit(solution)/shard_map/pallas_call | solution.py:94
  181.7 8.6 %collective-permute-start.22 = (bf16[512,256]{1,0:T(8,128)(2,1)S(1)}, bf16[512,256]{1,0:T(8,128)(2,1)S(1)}, u32[]{:S(2)}, u32[]{:S(2)}) collective-permute-start(bf16[512,256]{1,0:T(8,128)(2,1)S(1)} %shard_map.73.refs_0_), channel_id=1, source_target_pairs={{0,8},{8,16},{16,24},{24,0},{1,9},{9,17},{17,25},{25,1},{2,10},{10... | collective-permute-start | bytes 786440 | tf_op jit(solution)/shard_map/ppermute | solution.py:332
  191.6 2.3 collective-permute-start.24
  193.9 4.5 %collective-permute-done.36.refs_3_ = bf16[512,256]{1,0:T(8,128)(2,1)S(1)} collective-permute-done((bf16[512,256]{1,0:T(8,128)(2,1)S(1)}, bf16[512,256]{1,0:T(8,128)(2,1)S(1)}, u32[]{:S(2)}, u32[]{:S(2)}) %collective-permute-start.36) | collective-permute-done | bytes 262176 | tf_op jit(solution)/shard_map/ppermute | solution.py:332
  200.3 11.0 %collective-permute-done.23.refs_2_ = bf16[512,256]{1,0:T(8,128)(2,1)S(1)} collective-permute-done((bf16[512,256]{1,0:T(8,128)(2,1)S(1)}, bf16[512,256]{1,0:T(8,128)(2,1)S(1)}, u32[]{:S(2)}, u32[]{:S(2)}) %collective-permute-start.23) | collective-permute-done | bytes 262176 | tf_op jit(solution)/shard_map/ppermute | solution.py:332
  211.2 2.7 %shard_map.76 = (bf16[256,1024]{1,0:T(8,128)(2,1)S(1)}, bf16[256,1024]{1,0:T(8,128)(2,1)}) custom-call(s32[4]{0:T(128)S(1)} %pad_add_fusion.1.place_ref, bf16[512,256]{1,0:T(8,128)(2,1)S(1)} %shard_map.73.refs_0_, bf16[512,256]{1,0:T(8,128)(2,1)S(1)} %collective-permute-done.22.refs_1_, bf16[512,256]{1,0:T(8,128)(2,1)S(1)} %collective-permute-done.23.refs_2_, ...), custom_call_target="tpu_custom_call" | custom-call | flops 1073741824 | bytes 7340032 | tf_op jit(solution)/shard_map/pallas_call | solution.py:142
  214.7 3.4 %collective-permute-start.37 = (bf16[256,1024]{1,0:T(8,128)(2,1)}, bf16[256,1024]{1,0:T(8,128)(2,1)S(1)}, u32[]{:S(2)}, u32[]{:S(2)}) collective-permute-start(bf16[256,1024]{1,0:T(8,128)(2,1)} %get-tuple-element.18), channel_id=1, source_target_pairs={{0,1},{1,0},{2,3},{3,2},{4,5},{5,4},{6,7},{7,6},{8,9},{9,8},{10,11... | collective-permute-start | bytes 1572872 | tf_op jit(solution)/shard_map/ppermute | solution.py:338
  221.2 5.6 %collective-permute-start.38 = (bf16[128,1024]{1,0:T(8,128)(2,1)S(1)}, bf16[128,1024]{1,0:T(8,128)(2,1)S(1)}, u32[]{:S(2)}, u32[]{:S(2)}) collective-permute-start(bf16[128,1024]{1,0:T(8,128)(2,1)S(1)} %get-tuple-element.65), channel_id=1, source_target_pairs={{0,0},{1,16},{8,8},{9,24},{16,1},{17,17},{24,9},{25,25},{2,2},{3,1... | collective-permute-start | bytes 786440 | tf_op jit(solution)/shard_map/ppermute | solution.py:345
  226.7 3.2 %collective-permute-start.39 = (bf16[128,1024]{1,0:T(8,128)(2,1)S(1)}, bf16[128,1024]{1,0:T(8,128)(2,1)S(1)}, u32[]{:S(2)}, u32[]{:S(2)}) collective-permute-start(bf16[128,1024]{1,0:T(8,128)(2,1)S(1)} %get-tuple-element.66), channel_id=1, source_target_pairs={{0,8},{1,24},{8,0},{9,16},{16,9},{17,25},{24,1},{25,17},{2,10},{3,... | collective-permute-start | bytes 786440 | tf_op jit(solution)/shard_map/ppermute | solution.py:345
  229.9 2.5 %collective-permute-done.38 = bf16[128,1024]{1,0:T(8,128)(2,1)S(1)} collective-permute-done((bf16[128,1024]{1,0:T(8,128)(2,1)S(1)}, bf16[128,1024]{1,0:T(8,128)(2,1)S(1)}, u32[]{:S(2)}, u32[]{:S(2)}) %collective-permute-start.38) | collective-permute-done | bytes 262176 | tf_op jit(solution)/shard_map/ppermute | solution.py:345
  232.4 4.3 %collective-permute-done.39 = bf16[128,1024]{1,0:T(8,128)(2,1)S(1)} collective-permute-done((bf16[128,1024]{1,0:T(8,128)(2,1)S(1)}, bf16[128,1024]{1,0:T(8,128)(2,1)S(1)}, u32[]{:S(2)}, u32[]{:S(2)}) %collective-permute-start.39) | collective-permute-done | bytes 262176 | tf_op jit(solution)/shard_map/ppermute | solution.py:345
  (166 shorter events, 55.6 us)
Async XLA Ops:
  3.4 32.3 %collective-permute-start.3 = (bf16[256,1024]{1,0:T(8,128)(2,1)}, bf16[256,1024]{1,0:T(8,128)(2,1)S(1)}, u32[]{:S(2)}, u32[]{:S(2)}) collective-permute-start(bf16[256,1024]{1,0:T(8,128)(2,1)} %constant_dynamic-update-slice_fusion), channel_id=1, source_target_pairs={{0,2},{2,0},{4,6},{6,4},{1,3},{3,1},{5,7},{7,5},{8,10},{10,8},{12,... | collective-permute-start | bytes 1572872 | tf_op jit(solution)/shard_map/ppermute | solution.py:213
  5.5 30.3 %collective-permute-start.4 = (bf16[256,1024]{1,0:T(8,128)(2,1)}, bf16[256,1024]{1,0:T(8,128)(2,1)}, u32[]{:S(2)}, u32[]{:S(2)}) collective-permute-start(bf16[256,1024]{1,0:T(8,128)(2,1)} %constant_dynamic-update-slice_fusion), channel_id=1, source_target_pairs={{0,4},{2,6},{4,0},{6,2},{1,5},{3,7},{5,1},{7,3},{8,12},{10,14},{12... | collective-permute-start | bytes 1572872 | tf_op jit(solution)/shard_map/ppermute | solution.py:213
  12.3 19.6 %collective-permute-start.1 = (bf16[128,1024]{1,0:T(8,128)(2,1)}, bf16[128,1024]{1,0:T(8,128)(2,1)}, u32[]{:S(2)}, u32[]{:S(2)}) collective-permute-start(bf16[128,1024]{1,0:T(8,128)(2,1)} %pad_maximum_fusion.4), channel_id=1, source_target_pairs={{0,16},{8,24},{16,0},{24,8},{1,17},{9,25},{17,1},{25,9},{2,18},{10... | collective-permute-start | bytes 786440 | tf_op jit(solution)/shard_map/ppermute | solution.py:242
  15.3 17.6 %collective-permute-start.2 = (bf16[128,1024]{1,0:T(8,128)(2,1)}, bf16[128,1024]{1,0:T(8,128)(2,1)}, u32[]{:S(2)}, u32[]{:S(2)}) collective-permute-start(bf16[128,1024]{1,0:T(8,128)(2,1)} %pad_maximum_fusion.5), channel_id=1, source_target_pairs={{0,24},{8,0},{16,8},{24,16},{1,25},{9,1},{17,9},{25,17},{2,26},{10... | collective-permute-start | bytes 786440 | tf_op jit(solution)/shard_map/ppermute | solution.py:242
  35.8 26.4 %collective-permute-start.5 = (bf16[256,1024]{1,0:T(8,128)(2,1)S(1)}, bf16[256,1024]{1,0:T(8,128)(2,1)S(1)}, u32[]{:S(2)}, u32[]{:S(2)}) collective-permute-start(bf16[256,1024]{1,0:T(8,128)(2,1)S(1)} %pad_maximum_fusion.1), channel_id=1, source_target_pairs={{0,2},{2,0},{4,6},{6,4},{1,3},{3,1},{5,7},{7,5},{8,10},{10,8},{12,... | collective-permute-start | bytes 1572872 | tf_op jit(solution)/shard_map/ppermute | solution.py:213
  36.1 26.1 %collective-permute-start.6 = (bf16[256,1024]{1,0:T(8,128)(2,1)S(1)}, bf16[256,1024]{1,0:T(8,128)(2,1)S(1)}, u32[]{:S(2)}, u32[]{:S(2)}) collective-permute-start(bf16[256,1024]{1,0:T(8,128)(2,1)S(1)} %pad_maximum_fusion.1), channel_id=1, source_target_pairs={{0,4},{2,6},{4,0},{6,2},{1,5},{3,7},{5,1},{7,3},{8,12},{10,14},{12... | collective-permute-start | bytes 1572872 | tf_op jit(solution)/shard_map/ppermute | solution.py:213
  37.7 16.6 %collective-permute-start.14 = (bf16[128,1024]{1,0:T(8,128)(2,1)S(1)}, bf16[128,1024]{1,0:T(8,128)(2,1)S(1)}, u32[]{:S(2)}, u32[]{:S(2)}) collective-permute-start(bf16[128,1024]{1,0:T(8,128)(2,1)S(1)} %slice.120), channel_id=1, source_target_pairs={{0,2},{2,0},{4,6},{6,4},{1,3},{3,1},{5,7},{7,5},{8,10},{10,8},{12,... | collective-permute-start | bytes 786440 | tf_op jit(solution)/shard_map/ppermute | solution.py:213
  39.0 15.7 %collective-permute-start.15 = (bf16[128,1024]{1,0:T(8,128)(2,1)S(1)}, bf16[128,1024]{1,0:T(8,128)(2,1)S(1)}, u32[]{:S(2)}, u32[]{:S(2)}) collective-permute-start(bf16[128,1024]{1,0:T(8,128)(2,1)S(1)} %slice.121), channel_id=1, source_target_pairs={{0,4},{2,6},{4,0},{6,2},{1,5},{3,7},{5,1},{7,3},{8,12},{10,14},{12... | collective-permute-start | bytes 786440 | tf_op jit(solution)/shard_map/ppermute | solution.py:213
  59.4 24.4 %collective-permute-start.17 = (bf16[512,256]{1,0:T(8,128)(2,1)S(1)}, bf16[512,256]{1,0:T(8,128)(2,1)S(1)}, u32[]{:S(2)}, u32[]{:S(2)}) collective-permute-start(bf16[512,256]{1,0:T(8,128)(2,1)S(1)} %pad_maximum_fusion.9), channel_id=1, source_target_pairs={{0,16},{8,24},{16,0},{24,8},{1,17},{9,25},{17,1},{25,9},{2,18},{10... | collective-permute-start | bytes 786440 | tf_op jit(solution)/shard_map/ppermute | solution.py:242
  62.1 21.7 %collective-permute-start.16 = (bf16[512,256]{1,0:T(8,128)(2,1)S(1)}, bf16[512,256]{1,0:T(8,128)(2,1)S(1)}, u32[]{:S(2)}, u32[]{:S(2)}) collective-permute-start(bf16[512,256]{1,0:T(8,128)(2,1)S(1)} %pad_maximum_fusion.8), channel_id=1, source_target_pairs={{0,8},{8,16},{16,24},{24,0},{1,9},{9,17},{17,25},{25,1},{2,10},{10... | collective-permute-start | bytes 786440 | tf_op jit(solution)/shard_map/ppermute | solution.py:242
  62.1 41.9 %collective-permute-start.8 = (bf16[256,1024]{1,0:T(8,128)(2,1)S(1)}, bf16[256,1024]{1,0:T(8,128)(2,1)S(1)}, u32[]{:S(2)}, u32[]{:S(2)}) collective-permute-start(bf16[256,1024]{1,0:T(8,128)(2,1)S(1)} %pad_maximum_fusion), channel_id=1, source_target_pairs={{0,4},{2,6},{4,0},{6,2},{1,5},{3,7},{5,1},{7,3},{8,12},{10,14},{12... | collective-permute-start | bytes 1572872 | tf_op jit(solution)/shard_map/ppermute | solution.py:213
  62.4 43.1 %collective-permute-start.7 = (bf16[256,1024]{1,0:T(8,128)(2,1)S(1)}, bf16[256,1024]{1,0:T(8,128)(2,1)S(1)}, u32[]{:S(2)}, u32[]{:S(2)}) collective-permute-start(bf16[256,1024]{1,0:T(8,128)(2,1)S(1)} %pad_maximum_fusion), channel_id=1, source_target_pairs={{0,2},{2,0},{4,6},{6,4},{1,3},{3,1},{5,7},{7,5},{8,10},{10,8},{12,... | collective-permute-start | bytes 1572872 | tf_op jit(solution)/shard_map/ppermute | solution.py:213
  85.8 29.2 %collective-permute-start.19 = (bf16[512,256]{1,0:T(8,128)(2,1)}, bf16[512,256]{1,0:T(8,128)(2,1)S(1)}, u32[]{:S(2)}, u32[]{:S(2)}) collective-permute-start(bf16[512,256]{1,0:T(8,128)(2,1)} %pad_maximum_fusion.11.refs_9_), channel_id=1, source_target_pairs={{0,2},{2,0},{4,6},{6,4},{1,3},{3,1},{5,7},{7,5},{8,10},{10,8},{12,... | collective-permute-start | bytes 786440 | tf_op jit(solution)/shard_map/ppermute | solution.py:316
  86.2 37.7 %collective-permute-start.20 = (bf16[512,256]{1,0:T(8,128)(2,1)}, bf16[512,256]{1,0:T(8,128)(2,1)S(1)}, u32[]{:S(2)}, u32[]{:S(2)}) collective-permute-start(bf16[512,256]{1,0:T(8,128)(2,1)} %pad_maximum_fusion.11.refs_9_), channel_id=1, source_target_pairs={{0,4},{2,6},{4,0},{6,2},{1,5},{3,7},{5,1},{7,3},{8,12},{10,14},{12... | collective-permute-start | bytes 786440 | tf_op jit(solution)/shard_map/ppermute | solution.py:316
  102.4 41.5 %collective-permute-start.21 = (bf16[512,256]{1,0:T(8,128)(2,1)}, bf16[512,256]{1,0:T(8,128)(2,1)}, u32[]{:S(2)}, u32[]{:S(2)}) collective-permute-start(bf16[512,256]{1,0:T(8,128)(2,1)} %pad_maximum_fusion.11.refs_9_), channel_id=1, source_target_pairs={{0,6},{2,4},{4,2},{6,0},{1,7},{3,5},{5,3},{7,1},{8,14},{10,12},{12... | collective-permute-start | bytes 786440 | tf_op jit(solution)/shard_map/ppermute | solution.py:316
  111.7 20.8 %collective-permute-start.25 = (bf16[2048,256]{1,0:T(8,128)(2,1)S(1)}, bf16[2048,256]{1,0:T(8,128)(2,1)S(1)}, u32[]{:S(2)}, u32[]{:S(2)}) collective-permute-start(bf16[2048,256]{1,0:T(8,128)(2,1)S(1)} %copy-done), channel_id=1, source_target_pairs={{0,2},{2,0},{4,6},{6,4},{1,3},{3,1},{5,7},{7,5},{8,10},{10,8},{12,... | collective-permute-start | bytes 3145736 | tf_op jit(solution)/shard_map/ppermute | solution.py:213
  112.1 27.6 %collective-permute-start.26 = (bf16[2048,256]{1,0:T(8,128)(2,1)S(1)}, bf16[2048,256]{1,0:T(8,128)(2,1)S(1)}, u32[]{:S(2)}, u32[]{:S(2)}) collective-permute-start(bf16[2048,256]{1,0:T(8,128)(2,1)S(1)} %copy-done), channel_id=1, source_target_pairs={{0,4},{2,6},{4,0},{6,2},{1,5},{3,7},{5,1},{7,3},{8,12},{10,14},{12... | collective-permute-start | bytes 3145736 | tf_op jit(solution)/shard_map/ppermute | solution.py:213
  115.0 29.7 %collective-permute-start.31 = (bf16[512,256]{1,0:T(8,128)(2,1)}, bf16[512,256]{1,0:T(8,128)(2,1)}, u32[]{:S(2)}, u32[]{:S(2)}) collective-permute-start(bf16[512,256]{1,0:T(8,128)(2,1)} %get-tuple-element.25), channel_id=1, source_target_pairs={{0,8},{8,16},{16,24},{24,0},{1,9},{9,17},{17,25},{25,1},{2,10},{10... | collective-permute-start | bytes 786440 | tf_op jit(solution)/shard_map/ppermute | solution.py:242
  123.9 20.8 %collective-permute-start.32 = (bf16[512,256]{1,0:T(8,128)(2,1)}, bf16[512,256]{1,0:T(8,128)(2,1)}, u32[]{:S(2)}, u32[]{:S(2)}) collective-permute-start(bf16[512,256]{1,0:T(8,128)(2,1)} %get-tuple-element.24), channel_id=1, source_target_pairs={{0,16},{8,24},{16,0},{24,8},{1,17},{9,25},{17,1},{25,9},{2,18},{10... | collective-permute-start | bytes 786440 | tf_op jit(solution)/shard_map/ppermute | solution.py:242
  132.5 15.8 %collective-permute-start.33 = (bf16[512,256]{1,0:T(8,128)(2,1)}, bf16[512,256]{1,0:T(8,128)(2,1)}, u32[]{:S(2)}, u32[]{:S(2)}) collective-permute-start(bf16[512,256]{1,0:T(8,128)(2,1)} %get-tuple-element.23), channel_id=1, source_target_pairs={{0,24},{8,0},{16,8},{24,16},{1,25},{9,1},{17,9},{25,17},{2,26},{10... | collective-permute-start | bytes 786440 | tf_op jit(solution)/shard_map/ppermute | solution.py:242
  139.6 16.5 %collective-permute-start.11 = (bf16[512,256]{1,0:T(8,128)(2,1)}, bf16[512,256]{1,0:T(8,128)(2,1)}, u32[]{:S(2)}, u32[]{:S(2)}) collective-permute-start(bf16[512,256]{1,0:T(8,128)(2,1)} %get-tuple-element.37), channel_id=1, source_target_pairs={{0,8},{8,16},{16,24},{24,0},{1,9},{9,17},{17,25},{25,1},{2,10},{10... | collective-permute-start | bytes 786440 | tf_op jit(solution)/shard_map/ppermute | solution.py:242
  143.9 46.4 %collective-permute-start.27 = (bf16[1024,256]{1,0:T(8,128)(2,1)S(1)}, bf16[1024,256]{1,0:T(8,128)(2,1)S(1)}, u32[]{:S(2)}, u32[]{:S(2)}) collective-permute-start(bf16[1024,256]{1,0:T(8,128)(2,1)S(1)} %slice.126), channel_id=1, source_target_pairs={{0,2},{2,0},{4,6},{6,4},{1,3},{3,1},{5,7},{7,5},{8,10},{10,8},{12,... | collective-permute-start | bytes 1572872 | tf_op jit(solution)/shard_map/ppermute | solution.py:213
  144.7 46.9 %collective-permute-start.28 = (bf16[1024,256]{1,0:T(8,128)(2,1)S(1)}, bf16[1024,256]{1,0:T(8,128)(2,1)S(1)}, u32[]{:S(2)}, u32[]{:S(2)}) collective-permute-start(bf16[1024,256]{1,0:T(8,128)(2,1)S(1)} %slice.127), channel_id=1, source_target_pairs={{0,4},{2,6},{4,0},{6,2},{1,5},{3,7},{5,1},{7,3},{8,12},{10,14},{12... | collective-permute-start | bytes 1572872 | tf_op jit(solution)/shard_map/ppermute | solution.py:213
  144.8 22.0 %collective-permute-start.12 = (bf16[512,256]{1,0:T(8,128)(2,1)S(1)}, bf16[512,256]{1,0:T(8,128)(2,1)S(1)}, u32[]{:S(2)}, u32[]{:S(2)}) collective-permute-start(bf16[512,256]{1,0:T(8,128)(2,1)S(1)} %copy-done.18), channel_id=1, source_target_pairs={{0,16},{8,24},{16,0},{24,8},{1,17},{9,25},{17,1},{25,9},{2,18},{10... | collective-permute-start | bytes 786440 | tf_op jit(solution)/shard_map/ppermute | solution.py:242
  148.2 18.5 %collective-permute-start.13 = (bf16[512,256]{1,0:T(8,128)(2,1)S(1)}, bf16[512,256]{1,0:T(8,128)(2,1)S(1)}, u32[]{:S(2)}, u32[]{:S(2)}) collective-permute-start(bf16[512,256]{1,0:T(8,128)(2,1)S(1)} %copy-done.17), channel_id=1, source_target_pairs={{0,24},{8,0},{16,8},{24,16},{1,25},{9,1},{17,9},{25,17},{2,26},{10... | collective-permute-start | bytes 786440 | tf_op jit(solution)/shard_map/ppermute | solution.py:242
  156.2 25.5 %collective-permute-start.34 = (bf16[512,256]{1,0:T(8,128)(2,1)S(1)}, bf16[512,256]{1,0:T(8,128)(2,1)S(1)}, u32[]{:S(2)}, u32[]{:S(2)}) collective-permute-start(bf16[512,256]{1,0:T(8,128)(2,1)S(1)} %shard_map.74.refs_0_), channel_id=1, source_target_pairs={{0,8},{8,16},{16,24},{24,0},{1,9},{9,17},{17,25},{25,1},{2,10},{10... | collective-permute-start | bytes 786440 | tf_op jit(solution)/shard_map/ppermute | solution.py:332
  166.7 27.2 %collective-permute-start.35 = (bf16[512,256]{1,0:T(8,128)(2,1)S(1)}, bf16[512,256]{1,0:T(8,128)(2,1)S(1)}, u32[]{:S(2)}, u32[]{:S(2)}) collective-permute-start(bf16[512,256]{1,0:T(8,128)(2,1)S(1)} %shard_map.74.refs_0_), channel_id=1, source_target_pairs={{0,16},{8,24},{16,0},{24,8},{1,17},{9,25},{17,1},{25,9},{2,18},{10... | collective-permute-start | bytes 786440 | tf_op jit(solution)/shard_map/ppermute | solution.py:332
  166.7 31.7 %collective-permute-start.36 = (bf16[512,256]{1,0:T(8,128)(2,1)S(1)}, bf16[512,256]{1,0:T(8,128)(2,1)S(1)}, u32[]{:S(2)}, u32[]{:S(2)}) collective-permute-start(bf16[512,256]{1,0:T(8,128)(2,1)S(1)} %shard_map.74.refs_0_), channel_id=1, source_target_pairs={{0,24},{8,0},{16,8},{24,16},{1,25},{9,1},{17,9},{25,17},{2,26},{10... | collective-permute-start | bytes 786440 | tf_op jit(solution)/shard_map/ppermute | solution.py:332
  181.7 18.6 %collective-permute-start.22 = (bf16[512,256]{1,0:T(8,128)(2,1)S(1)}, bf16[512,256]{1,0:T(8,128)(2,1)S(1)}, u32[]{:S(2)}, u32[]{:S(2)}) collective-permute-start(bf16[512,256]{1,0:T(8,128)(2,1)S(1)} %shard_map.73.refs_0_), channel_id=1, source_target_pairs={{0,8},{8,16},{16,24},{24,0},{1,9},{9,17},{17,25},{25,1},{2,10},{10... | collective-permute-start | bytes 786440 | tf_op jit(solution)/shard_map/ppermute | solution.py:332
  190.3 20.9 %collective-permute-start.23 = (bf16[512,256]{1,0:T(8,128)(2,1)S(1)}, bf16[512,256]{1,0:T(8,128)(2,1)S(1)}, u32[]{:S(2)}, u32[]{:S(2)}) collective-permute-start(bf16[512,256]{1,0:T(8,128)(2,1)S(1)} %shard_map.73.refs_0_), channel_id=1, source_target_pairs={{0,16},{8,24},{16,0},{24,8},{1,17},{9,25},{17,1},{25,9},{2,18},{10... | collective-permute-start | bytes 786440 | tf_op jit(solution)/shard_map/ppermute | solution.py:332
  191.6 19.7 %collective-permute-start.24 = (bf16[512,256]{1,0:T(8,128)(2,1)S(1)}, bf16[512,256]{1,0:T(8,128)(2,1)S(1)}, u32[]{:S(2)}, u32[]{:S(2)}) collective-permute-start(bf16[512,256]{1,0:T(8,128)(2,1)S(1)} %shard_map.73.refs_0_), channel_id=1, source_target_pairs={{0,24},{8,0},{16,8},{24,16},{1,25},{9,1},{17,9},{25,17},{2,26},{10... | collective-permute-start | bytes 786440 | tf_op jit(solution)/shard_map/ppermute | solution.py:332
  221.2 11.3 %collective-permute-start.38 = (bf16[128,1024]{1,0:T(8,128)(2,1)S(1)}, bf16[128,1024]{1,0:T(8,128)(2,1)S(1)}, u32[]{:S(2)}, u32[]{:S(2)}) collective-permute-start(bf16[128,1024]{1,0:T(8,128)(2,1)S(1)} %get-tuple-element.65), channel_id=1, source_target_pairs={{0,0},{1,16},{8,8},{9,24},{16,1},{17,17},{24,9},{25,25},{2,2},{3,1... | collective-permute-start | bytes 786440 | tf_op jit(solution)/shard_map/ppermute | solution.py:345
  (31 other events, 334.7 us)

commit v3 on v2

v3 whole, which is shorter than its diff:
```python
import functools

import jax
import jax.numpy as jnp
from jax import lax
from jax.experimental import pallas as pl
from jax.experimental.pallas import tpu as pltpu
from jax.sharding import Mesh
from jax.sharding import PartitionSpec as P

HD = 128
HALF = HD // 2
MIB = 1024 * 1024


def local_kernel(body, out_shape, operands, flops, scratch=(), exps=0):
    size = sum(x.size * x.dtype.itemsize for x in operands)
    return pl.pallas_call(
        body,
        in_specs=[pl.BlockSpec(memory_space=pltpu.SMEM)]
        + [pl.BlockSpec(memory_space=pltpu.VMEM)] * (len(operands) - 1),
        out_shape=out_shape,
        scratch_shapes=scratch,
        compiler_params=pltpu.CompilerParams(vmem_limit_bytes=20 * MIB),
        cost_estimate=pl.CostEstimate(flops=flops, bytes_accessed=size, transcendentals=exps),
    )(*operands)


def rotary_tables(positions):
    freqs = 500000.0 ** (-(jnp.arange(HALF, dtype=jnp.float32) * 2.0 / HD))
    angles = positions.astype(jnp.float32)[:, None] * freqs[None, :]
    cosine = jnp.cos(angles)
    sine = jnp.sin(angles)
    return (
        jnp.concatenate([cosine, cosine], axis=1),
        jnp.concatenate([-sine, sine], axis=1),
    )


def summed_lanes(parts_ref, lanes):
    total = parts_ref[0, :, lanes].astype(jnp.float32)
    for part in range(1, parts_ref.shape[0]):
        total = total + parts_ref[part, :, lanes].astype(jnp.float32)
    return total


def rotated(values, cos_ref, sin_ref):
    return values * cos_ref[...] + pltpu.roll(values, HALF, 1) * sin_ref[...]


def pair_kernel(unused_ref, cos_ref, sin_ref, parts, out_ref):
    key = rotated(summed_lanes(parts, pl.ds(0, HD)), cos_ref, sin_ref)
    out_ref[:, pl.ds(0, HD)] = key.astype(jnp.bfloat16)
    out_ref[:, pl.ds(HD, HD)] = summed_lanes(parts, pl.ds(HD, HD)).astype(jnp.bfloat16)


def finish_pair(cosine, sine, parts):
    operands = (jnp.zeros((1,), jnp.int32), cosine, sine, parts)
    shape = jax.ShapeDtypeStruct(parts.shape[1:], jnp.bfloat16)
    return local_kernel(pair_kernel, shape, operands, 8 * parts.size)


def attention_kernel(blocks, stride, n_kv, place_ref, cos_ref, sin_ref, query_ref, *refs):
    kv_refs = refs[:n_kv]
    out_ref, turned, bias = refs[n_kv:]
    heads, tokens, _ = turned.shape
    for h in range(heads):
        total = summed_lanes(query_ref, pl.ds(h * HD, HD))
        turned[h] = rotated(total, cos_ref, sin_ref).astype(jnp.bfloat16)
    rows = tokens // blocks
    kv_rows = kv_refs[0].shape[0] // blocks
    documents = place_ref.shape[0] - 1 - n_kv
    scale = HD**-0.5
    for j in range(blocks):
        first = j * rows
        length = kv_rows * (j + 1)
        qpos = lax.broadcasted_iota(jnp.int32, (rows, HD), 0) + (place_ref[0] + j * stride)
        qstart = jnp.zeros_like(qpos)
        for i in range(documents):
            start = place_ref[1 + n_kv + i]
            qstart = jnp.where(qpos >= start, start, qstart)
        span = qpos - qstart
        for d in range(n_kv):
            for b in range(j + 1):
                for c in range(0, kv_rows, HD):
                    kpos = lax.broadcasted_iota(jnp.int32, (rows, HD), 1) + (
                        place_ref[1 + d] + (b * stride + c)
                    )
                    back = qpos - kpos
                    visible = (back >= 0) & (back <= span)
                    bias[:, pl.ds(d * length + b * kv_rows + c, HD)] = jnp.where(
                        visible, 0.0, -jnp.inf
                    )

        def one_head(h, unused):
            query = turned[h, pl.ds(first, rows), :]
            scores = []
            for d in range(n_kv):
                part = lax.dot_general(
                    query,
                    kv_refs[d][pl.ds(0, length), pl.ds(0, HD)],
                    (((1,), (1,)), ((), ())),
                    preferred_element_type=jnp.float32,
                )
                scores.append(part + bias[:, pl.ds(d * length, length)])
            highest = functools.reduce(
                jnp.maximum, [jnp.max(s, axis=1, keepdims=True) for s in scores]
            )
            denominator = 0.0
            mixed = 0.0
            for d in range(n_kv):
                probs = jnp.exp((scores[d] - highest) * scale)
                denominator = denominator + jnp.sum(probs, axis=1, keepdims=True)
                mixed = mixed + jnp.dot(
                    probs.astype(jnp.bfloat16),
                    kv_refs[d][pl.ds(0, length), pl.ds(HD, HD)],
                    preferred_element_type=jnp.float32,
                )
            lanes = pl.ds(pl.multiple_of(h * HD, HD), HD)
            out_ref[pl.ds(first, rows), lanes] = (mixed / denominator).astype(jnp.bfloat16)
            return unused

        lax.fori_loop(0, heads, one_head, 0)


def attention(place, cosine, sine, query_parts, kv_parts, blocks, stride):
    _, tokens, width = query_parts.shape
    heads = width // HD
    keys = sum(part.shape[0] for part in kv_parts)
    return local_kernel(
        functools.partial(attention_kernel, blocks, stride, len(kv_parts)),
        jax.ShapeDtypeStruct((tokens, width), jnp.bfloat16),
        (place, cosine, sine, query_parts, *kv_parts),
        4 * tokens * width * keys,
        [
            pltpu.VMEM((heads, tokens, HD), jnp.bfloat16),
            pltpu.VMEM((tokens // blocks, keys), jnp.float32),
        ],
        tokens * heads * keys,
    )


def product_kernel(groups, place_ref, token_ref, *refs):
    weight_refs = refs[:4]
    out_ref = refs[-1]
    lo = place_ref[1]
    share = weight_refs[0].shape[0] // groups
    width = weight_refs[0].shape[1] // 4
    for d in range(4):
        columns = pl.ds(d * width, width)
        for g in range(groups):
            total = 0.0
            for r in range(4):
                features = pl.ds(pl.multiple_of((lo ^ r) * share, share), share)
                total = total + jnp.dot(
                    token_ref[:, features],
                    weight_refs[r][pl.ds(g * share, share), columns],
                    preferred_element_type=jnp.float32,
                )
            out_ref[d, :, pl.ds(g * width, width)] = total.astype(jnp.bfloat16)


def product(place, line_tokens, weights, groups):
    count, depth = line_tokens.shape
    width = groups * weights[0].shape[1] // 4
    return local_kernel(
        functools.partial(product_kernel, groups),
        jax.ShapeDtypeStruct((4, count, width), jnp.bfloat16),
        (place, line_tokens, *weights),
        2 * count * depth * 4 * width,
    )


def project_kernel(place_ref, *refs):
    attended_refs = refs[:4]
    weight_refs = refs[4:8]
    total_refs = refs[8:-2]
    hi = place_ref[0]
    lo = place_ref[1]
    core = place_ref[2]
    offset = place_ref[3]
    depth = attended_refs[0].shape[1]
    width = weight_refs[0].shape[1]
    span = weight_refs[0].shape[0] // 4
    for side, out_ref in enumerate(refs[-2:]):
        kept = out_ref.shape[0]
        rows = pl.ds(pl.multiple_of(lax.rem(core + side, 2) * kept, kept), kept)
        for r, weight_ref in enumerate(weight_refs):
            columns = pl.ds(pl.multiple_of((lo ^ r) * width, width), width)
            total = total_refs[side][:, columns] if total_refs else 0.0
            for k, attended_ref in enumerate(attended_refs):
                first = lax.rem(hi - k + 4, 4) * span + offset
                total = total + jnp.dot(
                    attended_ref[rows, :],
                    weight_ref[pl.ds(pl.multiple_of(first, depth), depth), :],
                    preferred_element_type=jnp.float32,
                )
            out_ref[:, columns] = total.astype(out_ref.dtype)


def project(place, attended_parts, weights, totals, kind):
    tokens, depth = attended_parts[0].shape
    width = weights[0].shape[1]
    shape = jax.ShapeDtypeStruct((tokens // 2, 4 * width), kind)
    return local_kernel(
        project_kernel,
        (shape, shape),
        (place, *attended_parts, *weights, *totals),
        2 * tokens * 4 * depth * 4 * width,
    )


def normalised(tokens, norm_gain):
    source = tokens.astype(jnp.float32)
    return (
        source * lax.rsqrt(jnp.mean(source * source, axis=1, keepdims=True) + 1e-05) * norm_gain
    ).astype(jnp.bfloat16)


def plain_device(tokens, norm_gain, w_query, w_key, w_value, w_out, doc_starts):
    rows = tokens.shape[0]
    first = lax.axis_index("ctx") * rows
    normed = normalised(tokens, norm_gain)

    def project_with(weight):
        gathered = lax.all_gather(weight, "ctx", axis=0, tiled=True)
        total = jnp.dot(normed, gathered, preferred_element_type=jnp.float32)
        return total.astype(jnp.bfloat16)

    cosine, sine = rotary_tables(first + jnp.arange(rows, dtype=jnp.int32))
    place = jnp.concatenate([jnp.stack([first, jnp.zeros_like(first)]), doc_starts])
    query = project_with(w_query)
    key = project_with(w_key)
    value = project_with(w_value)
    kv_local = w_key.shape[1] // HD
    group = w_query.shape[1] // kv_local
    mixed = []
    for h in range(kv_local):
        lanes = slice(h * HD, (h + 1) * HD)
        pair = jnp.concatenate([key[:, lanes], value[:, lanes]], axis=1)
        pair = lax.all_gather(finish_pair(cosine, sine, pair[None]), "ctx", axis=0, tiled=True)
        part = query[:, h * group : (h + 1) * group]
        mixed.append(attention(place, cosine, sine, part[None], [pair], 1, 0))
    attended = jnp.concatenate(mixed, axis=1)
    wide = lax.all_gather(w_out, "ctx", axis=1, tiled=True)
    partial_out = jnp.dot(attended, wide, preferred_element_type=jnp.float32)
    return lax.psum_scatter(
        partial_out.astype(jnp.bfloat16), "head", scatter_dimension=1, tiled=True
    )


def after(value, *earlier):
    return lax.optimization_barrier((value, *earlier))[0]


def square(block):
    return [block] + [
        lax.ppermute(block, "lo", [(i, i ^ r) for i in range(4)]) for r in range(1, 4)
    ]


def along_line(pieces):
    return lax.all_to_all(pieces, "hi", 0, 0, tiled=True)


def round_line(block):
    return [block] + [
        lax.ppermute(block, "hi", [(i, (i + d) % 4) for i in range(4)]) for d in range(1, 4)
    ]


def line_device(tokens, norm_gain, w_query, w_key, w_value, w_out, doc_starts):
    rows, features = tokens.shape
    hi = lax.axis_index("hi")
    lo = lax.axis_index("lo")
    core = lax.axis_index("head")
    depth = features // 4
    heads = w_query.shape[1] // 4
    half = heads // 2
    place = jnp.stack([hi, lo, core])

    pair_blocks = square(jnp.concatenate([w_key, w_value], axis=0))
    stage = pair_blocks[1:]
    query_blocks = []
    for c in range(2):
        columns = [
            w_query[:, z * heads + c * half : z * heads + (c + 1) * half] for z in range(4)
        ]
        query_blocks.append(square(after(jnp.concatenate(columns, axis=1), *stage)))
        stage = query_blocks[-1][1:]
    out_blocks = square(after(w_out, *stage))

    normed = normalised(tokens, norm_gain)
    pieces = jnp.stack([normed[:, d * depth : (d + 1) * depth] for d in range(4)])
    line_tokens = along_line(pieces).reshape(4 * rows, depth)

    row_index = jnp.arange(4 * rows, dtype=jnp.int32)
    cosine, sine = rotary_tables((row_index // rows * 4 + lo) * rows + row_index % rows)
    kv_parts = square(
        finish_pair(
            cosine, sine, along_line(product(place, line_tokens, pair_blocks, 2))
        )
    )

    firsts = jnp.stack([lo, lo, lo ^ 1, lo ^ 2, lo ^ 3]) * rows
    seen = jnp.concatenate([firsts, doc_starts])
    totals = ()
    kinds = (jnp.float32, jnp.bfloat16)
    for c in range(2):
        query_parts = along_line(product(place, line_tokens, query_blocks[c], 1))
        attended = attention(seen, cosine, sine, query_parts, kv_parts, 4, 4 * rows)
        where = jnp.concatenate([place, jnp.full((1,), c * half, jnp.int32)])
        totals = project(where, round_line(attended), out_blocks, totals, kinds[c])

    mine, theirs = totals
    theirs = lax.ppermute(theirs, "head", [(0, 1), (1, 0)])
    summed = (mine.astype(jnp.float32) + theirs.astype(jnp.float32)).astype(jnp.bfloat16)
    arrived = []
    for e in range(2):
        block = lax.rem(hi + e, 2)
        piece = lax.dynamic_slice_in_dim(summed, block * rows, rows, 0)
        route = [(z * 2 + g, (2 * g + (z + e) % 2) * 2 + z // 2) for z in range(4) for g in range(2)]
        arrived.append(lax.ppermute(piece, ("hi", "head"), route))
    even = lax.rem(hi, 2) == 0
    return jnp.concatenate(
        [jnp.where(even, arrived[0], arrived[1]), jnp.where(even, arrived[1], arrived[0])], axis=1
    )


def solution(mesh):
    ctx = mesh.shape["ctx"]
    heads = mesh.shape["head"]

    def run(tokens, norm_gain, w_query, w_key, w_value, w_out, doc_starts):
        lines = w_key.shape[1] // HD // heads
        if (ctx, heads, lines) == (16, 2, 4):
            both = ("hi", "lo")
            grid = Mesh(mesh.devices.reshape(4, 4, 2), ("hi", "lo", "head"))
            body = line_device
        else:
            both, grid, body = "ctx", mesh, plain_device
        placed = (
            P(both, None),
            P(),
            P(both, "head"),
            P(both, "head"),
            P(both, "head"),
            P("head", both),
            P(),
        )
        return jax.shard_map(
            body, mesh=grid, in_specs=placed, out_specs=P(both, "head"), check_vma=False
        )(tokens, norm_gain, w_query, w_key, w_value, w_out, doc_starts)

    return run
```

time: 239 us -> 257 us (1.075)
  waiting for transfers between devices: 102 us -> 154 us
  starting transfers between devices: 80.7 us -> 48.6 us
  Pallas kernels: 18.4 us -> 31 us
  matrix products: 12.1 us -> 0 us
  other arithmetic: 11.2 us -> 8.45 us
    ppermute x37 -> x21, waiting for transfers between devices: 93 us -> 143 us  [the longest x15 121 us: square(): lax.ppermute(block, 'lo', [(i, i ^ r) for i in range(4)])]
    ppermute x37 -> x21, starting transfers between devices: 68.6 us -> 21.8 us  [the longest x15 14.6 us: square(): lax.ppermute(block, 'lo', [(i, i ^ r) for i in range(4)])]
    all_to_all x0 -> x4, starting transfers between devices: none -> 19.3 us  [along_line(): return lax.all_to_all(pieces, 'hi', 0, 0, tiled=True)]
    pallas_call x4 -> x8, Pallas kernels: 18.4 us -> 31 us  [local_kernel(): pl.pallas_call(body, in_specs=[pl.BlockSpec(memory_space=pltpu.SMEM)] + [...]
    dot_general x15 -> x0, matrix products: 12.1 us -> none  [the longest x12 9.37 us: product(): jnp.dot(gathered[:, place:place + depth_here], weight, preferred_element_...]
    unnamed x48 -> x49, local copies, waits for them, and re-layouts: 2.71 us -> 12 us
    ppermute x2, starting transfers between devices: 8.74 us -> 4.91 us  [line_device(): arrived.append(lax.ppermute(piece, ('hi', 'head'), route))]
    dynamic_slice x4 -> x0, local copies, waits for them, and re-layouts: 3.18 us -> none  [the longest x2 2.05 us: line_device(): lax.dynamic_slice_in_dim(query, lax.rem(hi + d, 4) * half, half, 1)]
  transfers between devices with their start and end apart: 40 -> 28, of which waited for: 15 -> 12; matrix products, arithmetic and copies ran while one was open for 12% -> 1% of each run, Pallas kernels for 7% -> 9%
where the time goes in v3:
time: 257 us; the launch traced here: 255 us
  waiting for transfers between devices  154 us (60%)
  starting transfers between devices  48.6 us (19%)
  Pallas kernels  31 us (12%)
  local copies, waits for them, and re-layouts  12.9 us (5%)
  other arithmetic  8.45 us (3%)
    ppermute x15, waiting for transfers between devices, square(): lax.ppermute(block, 'lo', [(i, i ^ r) for i in range(4)])  121 us
    pallas_call x8, Pallas kernels, local_kernel(): pl.pallas_call(body, in_specs=[pl.BlockSpec(memory_space=pltpu.SMEM)] + [...  31 us
    ppermute x6, waiting for transfers between devices, round_line(): lax.ppermute(block, 'hi', [(i, (i + d) % 4) for i in range(4)])  22.1 us
    all_to_all x4, starting transfers between devices, along_line(): return lax.all_to_all(pieces, 'hi', 0, 0, tiled=True)  19.3 us
    ppermute x15, starting transfers between devices, square(): lax.ppermute(block, 'lo', [(i, i ^ r) for i in range(4)])  14.6 us
    unnamed x49, local copies, waits for them, and re-layouts  12 us
    ppermute x2, waiting for transfers between devices, line_device(): arrived.append(lax.ppermute(piece, ('hi', 'head'), route))  9.41 us
    ppermute x6, starting transfers between devices, round_line(): lax.ppermute(block, 'hi', [(i, (i + d) % 4) for i in range(4)])  7.18 us
  transfers between devices with their start and end apart: 28, of which 12 were waited for; matrix products, arithmetic and copies ran while one was open for 1% of the time, Pallas kernels for 9%

profile of v3, /device:TPU:1, one launch (start us, length us, event | category | flops | bytes accessed | tf_op | source)
XLA Modules:
  0.0 255.4 jit_solution(16872668582157968085)
XLA Ops:
  0.0 1.6 fusion
  3.9 5.6 %all-to-all-start = ((bf16[4,128,1024]{2,1,0:T(8,128)(2,1)}), bf16[4,128,1024]{2,1,0:T(8,128)(2,1)S(1)}, u32[]{:S(2)}, u32[]{:S(2)}) async-start(bf16[4,128,1024]{2,1,0:T(8,128)(2,1)} %pad_maximum_fusion), calls=%async_computation | async-start | bytes 2097152 | tf_op jit(solution)/shard_map/all_to_all | solution.py:263
  9.6 2.2 collective-permute-start.2
  12.3 10.7 %collective-permute-done.2.refs_3_ = bf16[512,512]{1,0:T(8,128)(2,1)S(1)} collective-permute-done((bf16[512,512]{1,0:T(8,128)(2,1)S(1)}, bf16[512,512]{1,0:T(8,128)(2,1)S(1)}, u32[]{:S(2)}, u32[]{:S(2)}) %collective-permute-start.2) | collective-permute-done | bytes 524320 | tf_op jit(solution)/shard_map/ppermute | solution.py:258
  23.0 12.6 %collective-permute-done.1.refs_2_ = bf16[512,512]{1,0:T(8,128)(2,1)S(1)} collective-permute-done((bf16[512,512]{1,0:T(8,128)(2,1)S(1)}, bf16[512,512]{1,0:T(8,128)(2,1)S(1)}, u32[]{:S(2)}, u32[]{:S(2)}) %collective-permute-start.1) | collective-permute-done | bytes 524320 | tf_op jit(solution)/shard_map/ppermute | solution.py:258
  35.6 3.9 %shard_map.74 = bf16[4,512,256]{2,1,0:T(8,128)(2,1)} custom-call(s32[3]{0:T(128)S(1)} %pad_add_fusion.3.place_ref, bf16[512,1024]{1,0:T(8,128)(2,1)S(1)} %bitcast.15, bf16[512,512]{1,0:T(8,128)(2,1)S(1)} %constant_dynamic-update-slice_fusion.refs_0_, bf16[512,512]{1,0:T(8,128)(2,1)S(1)} %collective-permute-done.refs_1_, ...), custom_call_target="tpu_custom_call" | custom-call | flops 1073741824 | bytes 3145740 | tf_op jit(solution)/shard_map/pallas_call | solution.py:18
  39.5 4.7 %all-to-all-start.2 = ((bf16[4,512,256]{2,1,0:T(8,128)(2,1)}), bf16[4,512,256]{2,1,0:T(8,128)(2,1)S(1)}, u32[]{:S(2)}, u32[]{:S(2)}) async-start(bf16[4,512,256]{2,1,0:T(8,128)(2,1)} %shard_map.74), calls=%async_computation.2 | async-start | bytes 2097152 | tf_op jit(solution)/shard_map/all_to_all | solution.py:263
  45.7 1.7 collective-permute-start.4
  47.6 10.9 %collective-permute-done.5.refs_3_ = bf16[256,1024]{1,0:T(8,128)(2,1)S(1)} collective-permute-done((bf16[256,1024]{1,0:T(8,128)(2,1)S(1)}, bf16[256,1024]{1,0:T(8,128)(2,1)S(1)}, u32[]{:S(2)}, u32[]{:S(2)}) %collective-permute-start.5) | collective-permute-done | bytes 524320 | tf_op jit(solution)/shard_map/ppermute | solution.py:258
  58.5 12.5 %collective-permute-done.4.refs_2_ = bf16[256,1024]{1,0:T(8,128)(2,1)S(1)} collective-permute-done((bf16[256,1024]{1,0:T(8,128)(2,1)S(1)}, bf16[256,1024]{1,0:T(8,128)(2,1)S(1)}, u32[]{:S(2)}, u32[]{:S(2)}) %collective-permute-start.4) | collective-permute-done | bytes 524320 | tf_op jit(solution)/shard_map/ppermute | solution.py:258
  71.0 2.8 %shard_map.77 = bf16[4,512,256]{2,1,0:T(8,128)(2,1)} custom-call(s32[3]{0:T(128)S(1)} %pad_add_fusion.3.place_ref, bf16[512,1024]{1,0:T(8,128)(2,1)S(1)} %bitcast.16, bf16[256,1024]{1,0:T(8,128)(2,1)S(1)} %pad_maximum_fusion.2.refs_0_, bf16[256,1024]{1,0:T(8,128)(2,1)S(1)} %collective-permute-done.3.refs_1_, ...), custom_call_target="tpu_custom_call" | custom-call | flops 1073741824 | bytes 3145740 | tf_op jit(solution)/shard_map/pallas_call | solution.py:18
  73.8 4.5 %all-to-all-start.3 = ((bf16[4,512,256]{2,1,0:T(8,128)(2,1)}), bf16[4,512,256]{2,1,0:T(8,128)(2,1)S(1)}, u32[]{:S(2)}, u32[]{:S(2)}) async-start(bf16[4,512,256]{2,1,0:T(8,128)(2,1)} %shard_map.77), calls=%async_computation.3 | async-start | bytes 2097152 | tf_op jit(solution)/shard_map/all_to_all | solution.py:263
  80.1 1.7 collective-permute-start.7
  82.0 10.9 %collective-permute-done.8.refs_3_ = bf16[256,1024]{1,0:T(8,128)(2,1)S(1)} collective-permute-done((bf16[256,1024]{1,0:T(8,128)(2,1)S(1)}, bf16[256,1024]{1,0:T(8,128)(2,1)S(1)}, u32[]{:S(2)}, u32[]{:S(2)}) %collective-permute-start.8) | collective-permute-done | bytes 524320 | tf_op jit(solution)/shard_map/ppermute | solution.py:258
  92.9 12.5 %collective-permute-done.7.refs_2_ = bf16[256,1024]{1,0:T(8,128)(2,1)S(1)} collective-permute-done((bf16[256,1024]{1,0:T(8,128)(2,1)S(1)}, bf16[256,1024]{1,0:T(8,128)(2,1)S(1)}, u32[]{:S(2)}, u32[]{:S(2)}) %collective-permute-start.7) | collective-permute-done | bytes 524320 | tf_op jit(solution)/shard_map/ppermute | solution.py:258
  105.4 2.8 %shard_map.73 = bf16[4,512,256]{2,1,0:T(8,128)(2,1)} custom-call(s32[3]{0:T(128)S(1)} %pad_add_fusion.3.place_ref, bf16[512,1024]{1,0:T(8,128)(2,1)S(1)} %bitcast.17, bf16[256,1024]{1,0:T(8,128)(2,1)S(1)} %pad_maximum_fusion.1.refs_0_, bf16[256,1024]{1,0:T(8,128)(2,1)S(1)} %collective-permute-done.6.refs_1_, ...), custom_call_target="tpu_custom_call" | custom-call | flops 1073741824 | bytes 3145740 | tf_op jit(solution)/shard_map/pallas_call | solution.py:18
  109.2 4.5 %all-to-all-start.1 = ((bf16[4,512,256]{2,1,0:T(8,128)(2,1)}), bf16[4,512,256]{2,1,0:T(8,128)(2,1)}, u32[]{:S(2)}, u32[]{:S(2)}) async-start(bf16[4,512,256]{2,1,0:T(8,128)(2,1)} %shard_map.73), calls=%async_computation.1 | async-start | bytes 2097152 | tf_op jit(solution)/shard_map/all_to_all | solution.py:263
  115.5 1.7 collective-permute-start.16
  121.2 45.5 %collective-permute-done.11.refs_3_ = bf16[512,256]{1,0:T(8,128)(2,1)S(1)} collective-permute-done((bf16[512,256]{1,0:T(8,128)(2,1)}, bf16[512,256]{1,0:T(8,128)(2,1)S(1)}, u32[]{:S(2)}, u32[]{:S(2)}) %collective-permute-start.11) | collective-permute-done | bytes 262176 | tf_op jit(solution)/shard_map/ppermute | solution.py:258
  168.1 5.4 %collective-permute-done.10.refs_2_ = bf16[512,256]{1,0:T(8,128)(2,1)S(1)} collective-permute-done((bf16[512,256]{1,0:T(8,128)(2,1)}, bf16[512,256]{1,0:T(8,128)(2,1)S(1)}, u32[]{:S(2)}, u32[]{:S(2)}) %collective-permute-start.10) | collective-permute-done | bytes 262176 | tf_op jit(solution)/shard_map/ppermute | solution.py:258
  175.8 6.8 %shard_map.78.refs_0_ = bf16[512,256]{1,0:T(8,128)(2,1)S(1)} custom-call(s32[21]{0:T(128)S(1)} %pad_add_fusion.2.place_ref, f32[512,128]{1,0:T(8,128)S(1)} %get-tuple-element.40.cos_ref, f32[512,128]{1,0:T(8,128)S(1)} %copy-done.4, bf16[4,512,256]{2,1,0:T(8,128)(2,1)S(1)} %copy-done.2, bf16[512,256]{1,0:T(8,128)(2,1)} %shard_map.75.refs_0_, ...), custom_call_target="tpu_custom_call" | custom-call | flops 1073741824 | bytes 2621524 | tf_op jit(solution)/shard_map/pallas_call | solution.py:18
  183.4 3.3 %collective-permute-start.20 = (bf16[512,256]{1,0:T(8,128)(2,1)S(1)}, bf16[512,256]{1,0:T(8,128)(2,1)S(1)}, u32[]{:S(2)}, u32[]{:S(2)}) collective-permute-start(bf16[512,256]{1,0:T(8,128)(2,1)S(1)} %shard_map.78.refs_0_), channel_id=1, source_target_pairs={{0,24},{8,0},{16,8},{24,16},{1,25},{9,1},{17,9},{25,17},{2,26},{10... | collective-permute-start | bytes 786440 | tf_op jit(solution)/shard_map/ppermute | solution.py:268
  190.1 7.1 %shard_map.76.refs_0_ = bf16[512,256]{1,0:T(8,128)(2,1)S(1)} custom-call(s32[21]{0:T(128)S(1)} %pad_add_fusion.2.place_ref, f32[512,128]{1,0:T(8,128)S(1)} %get-tuple-element.40.cos_ref, f32[512,128]{1,0:T(8,128)S(1)} %copy-done.5, bf16[4,512,256]{2,1,0:T(8,128)(2,1)} %all-to-all-done.1.query_ref, bf16[512,256]{1,0:T(8,128)(2,1)} %shard_map.75.refs_0_, ...), custom_call_target="tpu_custom_call" | custom-call | flops 1073741824 | bytes 2621524 | tf_op jit(solution)/shard_map/pallas_call | solution.py:18
  197.2 3.0 %collective-permute-start.14 = (bf16[512,256]{1,0:T(8,128)(2,1)S(1)}, bf16[512,256]{1,0:T(8,128)(2,1)S(1)}, u32[]{:S(2)}, u32[]{:S(2)}) collective-permute-start(bf16[512,256]{1,0:T(8,128)(2,1)S(1)} %shard_map.76.refs_0_), channel_id=1, source_target_pairs={{0,24},{8,0},{16,8},{24,16},{1,25},{9,1},{17,9},{25,17},{2,26},{10... | collective-permute-start | bytes 786440 | tf_op jit(solution)/shard_map/ppermute | solution.py:268
  201.4 6.1 %collective-permute-done.19.refs_2_ = bf16[512,256]{1,0:T(8,128)(2,1)S(1)} collective-permute-done((bf16[512,256]{1,0:T(8,128)(2,1)S(1)}, bf16[512,256]{1,0:T(8,128)(2,1)S(1)}, u32[]{:S(2)}, u32[]{:S(2)}) %collective-permute-start.19) | collective-permute-done | bytes 262176 | tf_op jit(solution)/shard_map/ppermute | solution.py:268
  211.1 2.9 %shard_map.79 = (f32[256,1024]{1,0:T(8,128)S(1)}, f32[256,1024]{1,0:T(8,128)S(1)}) custom-call(s32[4]{0:T(128)S(1)} %get-tuple-element.19.place_ref, bf16[512,256]{1,0:T(8,128)(2,1)S(1)} %copy-done.8, bf16[512,256]{1,0:T(8,128)(2,1)} %collective-permute-done.18.refs_1_, bf16[512,256]{1,0:T(8,128)(2,1)S(1)} %copy-done.12, bf16[512,256]{1,0:T(8,128)(2,1)S(1)} %copy-done.10, ...), custom_call_target="tpu_custom_call" | custom-call | flops 1073741824 | bytes 5242896 | tf_op jit(solution)/shard_map/pallas_call | solution.py:18
  214.0 16.0 %collective-permute-done.13.refs_2_ = bf16[512,256]{1,0:T(8,128)(2,1)S(1)} collective-permute-done((bf16[512,256]{1,0:T(8,128)(2,1)S(1)}, bf16[512,256]{1,0:T(8,128)(2,1)S(1)}, u32[]{:S(2)}, u32[]{:S(2)}) %collective-permute-start.13) | collective-permute-done | bytes 262176 | tf_op jit(solution)/shard_map/ppermute | solution.py:268
  230.0 3.7 %shard_map.80 = (bf16[256,1024]{1,0:T(8,128)(2,1)S(1)}, bf16[256,1024]{1,0:T(8,128)(2,1)}) custom-call(s32[4]{0:T(128)S(1)} %pad_add_fusion.place_ref, bf16[512,256]{1,0:T(8,128)(2,1)S(1)} %shard_map.76.refs_0_, bf16[512,256]{1,0:T(8,128)(2,1)S(1)} %collective-permute-done.12.refs_1_, bf16[512,256]{1,0:T(8,128)(2,1)S(1)} %collective-permute-done.13.refs_2_, ...), custom_call_target="tpu_custom_call" | custom-call | flops 1073741824 | bytes 7340048 | tf_op jit(solution)/shard_map/pallas_call | solution.py:18
  234.5 2.6 %collective-permute-start.21 = (bf16[256,1024]{1,0:T(8,128)(2,1)}, bf16[256,1024]{1,0:T(8,128)(2,1)S(1)}, u32[]{:S(2)}, u32[]{:S(2)}) collective-permute-start(bf16[256,1024]{1,0:T(8,128)(2,1)} %get-tuple-element.18), channel_id=1, source_target_pairs={{0,1},{1,0},{2,3},{3,2},{4,5},{5,4},{6,7},{7,6},{8,9},{9,8},{10,11... | collective-permute-start | bytes 1572872 | tf_op jit(solution)/shard_map/ppermute | solution.py:316
  237.1 1.7 collective-permute-done.21
  240.2 4.7 %collective-permute-start.22 = (bf16[128,1024]{1,0:T(8,128)(2,1)S(1)}, bf16[128,1024]{1,0:T(8,128)(2,1)S(1)}, u32[]{:S(2)}, u32[]{:S(2)}) collective-permute-start(bf16[128,1024]{1,0:T(8,128)(2,1)S(1)} %get-tuple-element.35), channel_id=1, source_target_pairs={{0,0},{1,16},{8,8},{9,24},{16,1},{17,17},{24,9},{25,25},{2,2},{3,1... | collective-permute-start | bytes 786440 | tf_op jit(solution)/shard_map/ppermute | solution.py:323
  245.1 9.4 %collective-permute-done.22 = bf16[128,1024]{1,0:T(8,128)(2,1)S(1)} collective-permute-done((bf16[128,1024]{1,0:T(8,128)(2,1)S(1)}, bf16[128,1024]{1,0:T(8,128)(2,1)S(1)}, u32[]{:S(2)}, u32[]{:S(2)}) %collective-permute-start.22) | collective-permute-done | bytes 262176 | tf_op jit(solution)/shard_map/ppermute | solution.py:323
  (104 shorter events, 29.2 us)
Async XLA Ops:
  3.9 31.7 %all-to-all-start = ((bf16[4,128,1024]{2,1,0:T(8,128)(2,1)}), bf16[4,128,1024]{2,1,0:T(8,128)(2,1)S(1)}, u32[]{:S(2)}, u32[]{:S(2)}) async-start(bf16[4,128,1024]{2,1,0:T(8,128)(2,1)} %pad_maximum_fusion), calls=%async_computation | async-start | bytes 2097152 | tf_op jit(solution)/shard_map/all_to_all | solution.py:263
  9.6 13.5 %collective-permute-start.2 = (bf16[512,512]{1,0:T(8,128)(2,1)S(1)}, bf16[512,512]{1,0:T(8,128)(2,1)S(1)}, u32[]{:S(2)}, u32[]{:S(2)}) collective-permute-start(bf16[512,512]{1,0:T(8,128)(2,1)S(1)} %constant_dynamic-update-slice_fusion.refs_0_), channel_id=1, source_target_pairs={{0,6},{2,4},{4,2},{6,0},{1,7},{3,5},{5,3},{7,1},{8,14},{10,12},{12... | collective-permute-start | bytes 1572872 | tf_op jit(solution)/shard_map/ppermute | solution.py:258
  11.8 23.8 %collective-permute-start.1 = (bf16[512,512]{1,0:T(8,128)(2,1)S(1)}, bf16[512,512]{1,0:T(8,128)(2,1)S(1)}, u32[]{:S(2)}, u32[]{:S(2)}) collective-permute-start(bf16[512,512]{1,0:T(8,128)(2,1)S(1)} %constant_dynamic-update-slice_fusion.refs_0_), channel_id=1, source_target_pairs={{0,4},{2,6},{4,0},{6,2},{1,5},{3,7},{5,1},{7,3},{8,12},{10,14},{12... | collective-permute-start | bytes 1572872 | tf_op jit(solution)/shard_map/ppermute | solution.py:258
  12.0 23.6 %collective-permute-start = (bf16[512,512]{1,0:T(8,128)(2,1)S(1)}, bf16[512,512]{1,0:T(8,128)(2,1)S(1)}, u32[]{:S(2)}, u32[]{:S(2)}) collective-permute-start(bf16[512,512]{1,0:T(8,128)(2,1)S(1)} %constant_dynamic-update-slice_fusion.refs_0_), channel_id=1, source_target_pairs={{0,2},{2,0},{4,6},{6,4},{1,3},{3,1},{5,7},{7,5},{8,10},{10,8},{12,... | collective-permute-start | bytes 1572872 | tf_op jit(solution)/shard_map/ppermute | solution.py:258
  39.5 34.3 %all-to-all-start.2 = ((bf16[4,512,256]{2,1,0:T(8,128)(2,1)}), bf16[4,512,256]{2,1,0:T(8,128)(2,1)S(1)}, u32[]{:S(2)}, u32[]{:S(2)}) async-start(bf16[4,512,256]{2,1,0:T(8,128)(2,1)} %shard_map.74), calls=%async_computation.2 | async-start | bytes 2097152 | tf_op jit(solution)/shard_map/all_to_all | solution.py:263
  44.9 13.6 %collective-permute-start.5 = (bf16[256,1024]{1,0:T(8,128)(2,1)S(1)}, bf16[256,1024]{1,0:T(8,128)(2,1)S(1)}, u32[]{:S(2)}, u32[]{:S(2)}) collective-permute-start(bf16[256,1024]{1,0:T(8,128)(2,1)S(1)} %pad_maximum_fusion.2.refs_0_), channel_id=1, source_target_pairs={{0,6},{2,4},{4,2},{6,0},{1,7},{3,5},{5,3},{7,1},{8,14},{10,12},{12... | collective-permute-start | bytes 1572872 | tf_op jit(solution)/shard_map/ppermute | solution.py:258
  45.7 25.3 %collective-permute-start.4 = (bf16[256,1024]{1,0:T(8,128)(2,1)S(1)}, bf16[256,1024]{1,0:T(8,128)(2,1)S(1)}, u32[]{:S(2)}, u32[]{:S(2)}) collective-permute-start(bf16[256,1024]{1,0:T(8,128)(2,1)S(1)} %pad_maximum_fusion.2.refs_0_), channel_id=1, source_target_pairs={{0,4},{2,6},{4,0},{6,2},{1,5},{3,7},{5,1},{7,3},{8,12},{10,14},{12... | collective-permute-start | bytes 1572872 | tf_op jit(solution)/shard_map/ppermute | solution.py:258
  47.4 23.6 %collective-permute-start.3 = (bf16[256,1024]{1,0:T(8,128)(2,1)S(1)}, bf16[256,1024]{1,0:T(8,128)(2,1)S(1)}, u32[]{:S(2)}, u32[]{:S(2)}) collective-permute-start(bf16[256,1024]{1,0:T(8,128)(2,1)S(1)} %pad_maximum_fusion.2.refs_0_), channel_id=1, source_target_pairs={{0,2},{2,0},{4,6},{6,4},{1,3},{3,1},{5,7},{7,5},{8,10},{10,8},{12,... | collective-permute-start | bytes 1572872 | tf_op jit(solution)/shard_map/ppermute | solution.py:258
  73.8 34.3 %all-to-all-start.3 = ((bf16[4,512,256]{2,1,0:T(8,128)(2,1)}), bf16[4,512,256]{2,1,0:T(8,128)(2,1)S(1)}, u32[]{:S(2)}, u32[]{:S(2)}) async-start(bf16[4,512,256]{2,1,0:T(8,128)(2,1)} %shard_map.77), calls=%async_computation.3 | async-start | bytes 2097152 | tf_op jit(solution)/shard_map/all_to_all | solution.py:263
  79.3 13.6 %collective-permute-start.8 = (bf16[256,1024]{1,0:T(8,128)(2,1)S(1)}, bf16[256,1024]{1,0:T(8,128)(2,1)S(1)}, u32[]{:S(2)}, u32[]{:S(2)}) collective-permute-start(bf16[256,1024]{1,0:T(8,128)(2,1)S(1)} %pad_maximum_fusion.1.refs_0_), channel_id=1, source_target_pairs={{0,6},{2,4},{4,2},{6,0},{1,7},{3,5},{5,3},{7,1},{8,14},{10,12},{12... | collective-permute-start | bytes 1572872 | tf_op jit(solution)/shard_map/ppermute | solution.py:258
  80.1 25.3 %collective-permute-start.7 = (bf16[256,1024]{1,0:T(8,128)(2,1)S(1)}, bf16[256,1024]{1,0:T(8,128)(2,1)S(1)}, u32[]{:S(2)}, u32[]{:S(2)}) collective-permute-start(bf16[256,1024]{1,0:T(8,128)(2,1)S(1)} %pad_maximum_fusion.1.refs_0_), channel_id=1, source_target_pairs={{0,4},{2,6},{4,0},{6,2},{1,5},{3,7},{5,1},{7,3},{8,12},{10,14},{12... | collective-permute-start | bytes 1572872 | tf_op jit(solution)/shard_map/ppermute | solution.py:258
  81.8 23.6 %collective-permute-start.6 = (bf16[256,1024]{1,0:T(8,128)(2,1)S(1)}, bf16[256,1024]{1,0:T(8,128)(2,1)S(1)}, u32[]{:S(2)}, u32[]{:S(2)}) collective-permute-start(bf16[256,1024]{1,0:T(8,128)(2,1)S(1)} %pad_maximum_fusion.1.refs_0_), channel_id=1, source_target_pairs={{0,2},{2,0},{4,6},{6,4},{1,3},{3,1},{5,7},{7,5},{8,10},{10,8},{12,... | collective-permute-start | bytes 1572872 | tf_op jit(solution)/shard_map/ppermute | solution.py:258
  109.2 78.1 %all-to-all-start.1 = ((bf16[4,512,256]{2,1,0:T(8,128)(2,1)}), bf16[4,512,256]{2,1,0:T(8,128)(2,1)}, u32[]{:S(2)}, u32[]{:S(2)}) async-start(bf16[4,512,256]{2,1,0:T(8,128)(2,1)} %shard_map.73), calls=%async_computation.1 | async-start | bytes 2097152 | tf_op jit(solution)/shard_map/all_to_all | solution.py:263
  113.7 73.0 %collective-permute-start.17 = (bf16[2048,256]{1,0:T(8,128)(2,1)S(1)}, bf16[2048,256]{1,0:T(8,128)(2,1)S(1)}, u32[]{:S(2)}, u32[]{:S(2)}) collective-permute-start(bf16[2048,256]{1,0:T(8,128)(2,1)S(1)} %copy-done), channel_id=1, source_target_pairs={{0,6},{2,4},{4,2},{6,0},{1,7},{3,5},{5,3},{7,1},{8,14},{10,12},{12... | collective-permute-start | bytes 3145736 | tf_op jit(solution)/shard_map/ppermute | solution.py:258
  115.5 81.7 %collective-permute-start.16 = (bf16[2048,256]{1,0:T(8,128)(2,1)S(1)}, bf16[2048,256]{1,0:T(8,128)(2,1)}, u32[]{:S(2)}, u32[]{:S(2)}) collective-permute-start(bf16[2048,256]{1,0:T(8,128)(2,1)S(1)} %copy-done), channel_id=1, source_target_pairs={{0,4},{2,6},{4,0},{6,2},{1,5},{3,7},{5,1},{7,3},{8,12},{10,14},{12... | collective-permute-start | bytes 3145736 | tf_op jit(solution)/shard_map/ppermute | solution.py:258
  117.3 82.9 %collective-permute-start.15 = (bf16[2048,256]{1,0:T(8,128)(2,1)S(1)}, bf16[2048,256]{1,0:T(8,128)(2,1)}, u32[]{:S(2)}, u32[]{:S(2)}) collective-permute-start(bf16[2048,256]{1,0:T(8,128)(2,1)S(1)} %copy-done), channel_id=1, source_target_pairs={{0,2},{2,0},{4,6},{6,4},{1,3},{3,1},{5,7},{7,5},{8,10},{10,8},{12,... | collective-permute-start | bytes 3145736 | tf_op jit(solution)/shard_map/ppermute | solution.py:258
  117.7 50.3 %copy-start.23 = (s32[16]{0:T(128)S(1)}, s32[16]{0:T(128)}, u32[]{:S(2)}) copy-start(s32[16]{0:T(128)} %param.13) | copy-start | bytes 196
  118.7 48.0 %collective-permute-start.11 = (bf16[512,256]{1,0:T(8,128)(2,1)}, bf16[512,256]{1,0:T(8,128)(2,1)S(1)}, u32[]{:S(2)}, u32[]{:S(2)}) collective-permute-start(bf16[512,256]{1,0:T(8,128)(2,1)} %shard_map.75.refs_0_), channel_id=1, source_target_pairs={{0,6},{2,4},{4,2},{6,0},{1,7},{3,5},{5,3},{7,1},{8,14},{10,12},{12... | collective-permute-start | bytes 786440 | tf_op jit(solution)/shard_map/ppermute | solution.py:258
  119.8 53.7 %collective-permute-start.10 = (bf16[512,256]{1,0:T(8,128)(2,1)}, bf16[512,256]{1,0:T(8,128)(2,1)S(1)}, u32[]{:S(2)}, u32[]{:S(2)}) collective-permute-start(bf16[512,256]{1,0:T(8,128)(2,1)} %shard_map.75.refs_0_), channel_id=1, source_target_pairs={{0,4},{2,6},{4,0},{6,2},{1,5},{3,7},{5,1},{7,3},{8,12},{10,14},{12... | collective-permute-start | bytes 786440 | tf_op jit(solution)/shard_map/ppermute | solution.py:258
  166.7 6.8 %collective-permute-start.9 = (bf16[512,256]{1,0:T(8,128)(2,1)}, bf16[512,256]{1,0:T(8,128)(2,1)S(1)}, u32[]{:S(2)}, u32[]{:S(2)}) collective-permute-start(bf16[512,256]{1,0:T(8,128)(2,1)} %shard_map.75.refs_0_), channel_id=1, source_target_pairs={{0,2},{2,0},{4,6},{6,4},{1,3},{3,1},{5,7},{7,5},{8,10},{10,8},{12,... | collective-permute-start | bytes 786440 | tf_op jit(solution)/shard_map/ppermute | solution.py:258
  173.5 9.1 %copy-start.15 = (bf16[512,256]{1,0:T(8,128)(2,1)}, bf16[512,256]{1,0:T(8,128)(2,1)S(1)}, u32[]{:S(2)}) copy-start(bf16[512,256]{1,0:T(8,128)(2,1)S(1)} %collective-permute-done.10.refs_2_) | copy-start | bytes 786436
  175.8 11.5 %copy-start.5 = (f32[512,128]{1,0:T(8,128)S(1)}, f32[512,128]{1,0:T(8,128)}, u32[]{:S(2)}) copy-start(f32[512,128]{1,0:T(8,128)} %copy-done.3) | copy-start | bytes 786436
  183.4 13.8 %copy-start.7 = (bf16[512,256]{1,0:T(8,128)(2,1)}, bf16[512,256]{1,0:T(8,128)(2,1)S(1)}, u32[]{:S(2)}) copy-start(bf16[512,256]{1,0:T(8,128)(2,1)S(1)} %shard_map.78.refs_0_) | copy-start | bytes 786436
  183.4 17.2 %collective-permute-start.20 = (bf16[512,256]{1,0:T(8,128)(2,1)S(1)}, bf16[512,256]{1,0:T(8,128)(2,1)S(1)}, u32[]{:S(2)}, u32[]{:S(2)}) collective-permute-start(bf16[512,256]{1,0:T(8,128)(2,1)S(1)} %shard_map.78.refs_0_), channel_id=1, source_target_pairs={{0,24},{8,0},{16,8},{24,16},{1,25},{9,1},{17,9},{25,17},{2,26},{10... | collective-permute-start | bytes 786440 | tf_op jit(solution)/shard_map/ppermute | solution.py:268
  186.7 20.8 %collective-permute-start.19 = (bf16[512,256]{1,0:T(8,128)(2,1)S(1)}, bf16[512,256]{1,0:T(8,128)(2,1)S(1)}, u32[]{:S(2)}, u32[]{:S(2)}) collective-permute-start(bf16[512,256]{1,0:T(8,128)(2,1)S(1)} %shard_map.78.refs_0_), channel_id=1, source_target_pairs={{0,16},{8,24},{16,0},{24,8},{1,17},{9,25},{17,1},{25,9},{2,18},{10... | collective-permute-start | bytes 786440 | tf_op jit(solution)/shard_map/ppermute | solution.py:268
  186.7 21.5 %collective-permute-start.18 = (bf16[512,256]{1,0:T(8,128)(2,1)S(1)}, bf16[512,256]{1,0:T(8,128)(2,1)}, u32[]{:S(2)}, u32[]{:S(2)}) collective-permute-start(bf16[512,256]{1,0:T(8,128)(2,1)S(1)} %shard_map.78.refs_0_), channel_id=1, source_target_pairs={{0,8},{8,16},{16,24},{24,0},{1,9},{9,17},{17,25},{25,1},{2,10},{10... | collective-permute-start | bytes 786440 | tf_op jit(solution)/shard_map/ppermute | solution.py:268
  197.2 16.8 %collective-permute-start.14 = (bf16[512,256]{1,0:T(8,128)(2,1)S(1)}, bf16[512,256]{1,0:T(8,128)(2,1)S(1)}, u32[]{:S(2)}, u32[]{:S(2)}) collective-permute-start(bf16[512,256]{1,0:T(8,128)(2,1)S(1)} %shard_map.76.refs_0_), channel_id=1, source_target_pairs={{0,24},{8,0},{16,8},{24,16},{1,25},{9,1},{17,9},{25,17},{2,26},{10... | collective-permute-start | bytes 786440 | tf_op jit(solution)/shard_map/ppermute | solution.py:268
  200.2 29.8 %collective-permute-start.13 = (bf16[512,256]{1,0:T(8,128)(2,1)S(1)}, bf16[512,256]{1,0:T(8,128)(2,1)S(1)}, u32[]{:S(2)}, u32[]{:S(2)}) collective-permute-start(bf16[512,256]{1,0:T(8,128)(2,1)S(1)} %shard_map.76.refs_0_), channel_id=1, source_target_pairs={{0,16},{8,24},{16,0},{24,8},{1,17},{9,25},{17,1},{25,9},{2,18},{10... | collective-permute-start | bytes 786440 | tf_op jit(solution)/shard_map/ppermute | solution.py:268
  201.2 28.7 %collective-permute-start.12 = (bf16[512,256]{1,0:T(8,128)(2,1)S(1)}, bf16[512,256]{1,0:T(8,128)(2,1)S(1)}, u32[]{:S(2)}, u32[]{:S(2)}) collective-permute-start(bf16[512,256]{1,0:T(8,128)(2,1)S(1)} %shard_map.76.refs_0_), channel_id=1, source_target_pairs={{0,8},{8,16},{16,24},{24,0},{1,9},{9,17},{17,25},{25,1},{2,10},{10... | collective-permute-start | bytes 786440 | tf_op jit(solution)/shard_map/ppermute | solution.py:268
  234.5 4.4 %collective-permute-start.21 = (bf16[256,1024]{1,0:T(8,128)(2,1)}, bf16[256,1024]{1,0:T(8,128)(2,1)S(1)}, u32[]{:S(2)}, u32[]{:S(2)}) collective-permute-start(bf16[256,1024]{1,0:T(8,128)(2,1)} %get-tuple-element.18), channel_id=1, source_target_pairs={{0,1},{1,0},{2,3},{3,2},{4,5},{5,4},{6,7},{7,6},{8,9},{9,8},{10,11... | collective-permute-start | bytes 1572872 | tf_op jit(solution)/shard_map/ppermute | solution.py:316
  240.2 14.3 %collective-permute-start.22 = (bf16[128,1024]{1,0:T(8,128)(2,1)S(1)}, bf16[128,1024]{1,0:T(8,128)(2,1)S(1)}, u32[]{:S(2)}, u32[]{:S(2)}) collective-permute-start(bf16[128,1024]{1,0:T(8,128)(2,1)S(1)} %get-tuple-element.35), channel_id=1, source_target_pairs={{0,0},{1,16},{8,8},{9,24},{16,1},{17,17},{24,9},{25,25},{2,2},{3,1... | collective-permute-start | bytes 786440 | tf_op jit(solution)/shard_map/ppermute | solution.py:323
  244.8 9.7 %collective-permute-start.23 = (bf16[128,1024]{1,0:T(8,128)(2,1)S(1)}, bf16[128,1024]{1,0:T(8,128)(2,1)S(1)}, u32[]{:S(2)}, u32[]{:S(2)}) collective-permute-start(bf16[128,1024]{1,0:T(8,128)(2,1)S(1)} %get-tuple-element.36), channel_id=1, source_target_pairs={{0,8},{1,24},{8,0},{9,16},{16,9},{17,25},{24,1},{25,17},{2,10},{3,... | collective-permute-start | bytes 786440 | tf_op jit(solution)/shard_map/ppermute | solution.py:323
  (20 other events, 42.7 us)

commit v4 on v3

--- a/solution.py
+++ b/solution.py
@@ -21,7 +21,7 @@
         + [pl.BlockSpec(memory_space=pltpu.VMEM)] * (len(operands) - 1),
         out_shape=out_shape,
         scratch_shapes=scratch,
-        compiler_params=pltpu.CompilerParams(vmem_limit_bytes=20 * MIB),
+        compiler_params=pltpu.CompilerParams(vmem_limit_bytes=12 * MIB),
         cost_estimate=pl.CostEstimate(flops=flops, bytes_accessed=size, transcendentals=exps),
     )(*operands)
 
@@ -141,7 +141,7 @@
 
 
 def product_kernel(groups, place_ref, token_ref, *refs):
-    weight_refs = refs[:4]
+    weight_refs = refs[:5]
     out_ref = refs[-1]
     lo = place_ref[1]
     share = weight_refs[0].shape[0] // groups
@@ -152,10 +152,14 @@
             total = 0.0
             for r in range(4):
                 features = pl.ds(pl.multiple_of((lo ^ r) * share, share), share)
+                if r < 3:
+                    weight = weight_refs[r][pl.ds(g * share, share), columns]
+                elif groups == 2:
+                    weight = weight_refs[3 + g][:, columns]
+                else:
+                    weight = jnp.concatenate([ref[:, columns] for ref in weight_refs[3:]], axis=0)
                 total = total + jnp.dot(
-                    token_ref[:, features],
-                    weight_refs[r][pl.ds(g * share, share), columns],
-                    preferred_element_type=jnp.float32,
+                    token_ref[:, features], weight, preferred_element_type=jnp.float32
                 )
             out_ref[d, :, pl.ds(g * width, width)] = total.astype(jnp.bfloat16)
 
@@ -253,10 +257,17 @@
     return lax.optimization_barrier((value, *earlier))[0]
 
 
-def square(block):
-    return [block] + [
-        lax.ppermute(block, "lo", [(i, i ^ r) for i in range(4)]) for r in range(1, 4)
-    ]
+def beside(block, r):
+    return lax.ppermute(block, "lo", [(i, i ^ r) for i in range(4)])
+
+
+def sides(block):
+    return [block, beside(block, 1), beside(block, 2)]
+
+
+def corner(blocks):
+    half = blocks[0].shape[0] // 2
+    return [*blocks, beside(blocks[2][:half], 1), beside(blocks[1][half:], 2)]
 
 
 def along_line(pieces):
@@ -279,16 +290,15 @@
     half = heads // 2
     place = jnp.stack([hi, lo, core])
 
-    pair_blocks = square(jnp.concatenate([w_key, w_value], axis=0))
-    stage = pair_blocks[1:]
+    stage = sides(jnp.concatenate([w_key, w_value], axis=0))
+    pair_blocks = corner(stage)
     query_blocks = []
     for c in range(2):
         columns = [
             w_query[:, z * heads + c * half : z * heads + (c + 1) * half] for z in range(4)
         ]
-        query_blocks.append(square(after(jnp.concatenate(columns, axis=1), *stage)))
-        stage = query_blocks[-1][1:]
-    out_blocks = square(after(w_out, *stage))
+        stage = sides(after(jnp.concatenate(columns, axis=1), *stage[1:]))
+        query_blocks.append(corner(stage))
 
     normed = normalised(tokens, norm_gain)
     pieces = jnp.stack([normed[:, d * depth : (d + 1) * depth] for d in range(4)])
@@ -296,11 +306,12 @@
 
     row_index = jnp.arange(4 * rows, dtype=jnp.int32)
     cosine, sine = rotary_tables((row_index // rows * 4 + lo) * rows + row_index % rows)
-    kv_parts = square(
-        finish_pair(
-            cosine, sine, along_line(product(place, line_tokens, pair_blocks, 2))
-        )
-    )
+    kv_own = finish_pair(
+        cosine, sine, along_line(product(place, line_tokens, pair_blocks, 2))
+    )
+    kv_parts = [kv_own] + [beside(kv_own, r) for r in range(1, 4)]
+    out_blocks = corner(sides(after(w_out, *query_blocks[1][3:], *kv_parts[1:])))
+    out_blocks[3:] = [jnp.concatenate(out_blocks[3:], axis=0)]
 
     firsts = jnp.stack([lo, lo, lo ^ 1, lo ^ 2, lo ^ 3]) * rows
     seen = jnp.concatenate([firsts, doc_starts])

time: 257 us -> 209 us (0.81)
  waiting for transfers between devices: 154 us -> 100 us
  starting transfers between devices: 48.6 us -> 55.7 us
    ppermute x15 -> x19, waiting for transfers between devices: 121 us -> 54.6 us  [beside(): return lax.ppermute(block, 'lo', [(i, i ^ r) for i in range(4)])]
    all_to_all x4, waiting for transfers between devices: 0.01 us -> 10.1 us  [along_line(): return lax.all_to_all(pieces, 'hi', 0, 0, tiled=True)]
    ppermute x15 -> x19, starting transfers between devices: 14.6 us -> 22.1 us  [beside(): return lax.ppermute(block, 'lo', [(i, i ^ r) for i in range(4)])]
    unnamed x49 -> x42, local copies, waits for them, and re-layouts: 12 us -> 7.85 us
  transfers between devices with their start and end apart: 28 -> 32, of which waited for: 12 -> 16; matrix products, arithmetic and copies ran while one was open for 1% -> 3% of each run, Pallas kernels for 9% -> 12%
where the time goes in v4:
time: 209 us; the launch traced here: 207 us
  waiting for transfers between devices  100 us (48%)
  starting transfers between devices  55.7 us (27%)
  Pallas kernels  30.5 us (15%)
  local copies, waits for them, and re-layouts  12.4 us (6%)
  other arithmetic  7.55 us (4%)
    ppermute x19, waiting for transfers between devices, beside(): return lax.ppermute(block, 'lo', [(i, i ^ r) for i in range(4)])  54.6 us
    pallas_call x8, Pallas kernels, local_kernel(): pl.pallas_call(body, in_specs=[pl.BlockSpec(memory_space=pltpu.SMEM)] + [...  30.5 us
    ppermute x6, waiting for transfers between devices, round_line(): lax.ppermute(block, 'hi', [(i, (i + d) % 4) for i in range(4)])  24.5 us
    ppermute x19, starting transfers between devices, beside(): return lax.ppermute(block, 'lo', [(i, i ^ r) for i in range(4)])  22.1 us
    all_to_all x4, starting transfers between devices, along_line(): return lax.all_to_all(pieces, 'hi', 0, 0, tiled=True)  17.7 us
    all_to_all x4, waiting for transfers between devices, along_line(): return lax.all_to_all(pieces, 'hi', 0, 0, tiled=True)  10.1 us
    ppermute x2, waiting for transfers between devices, line_device(): arrived.append(lax.ppermute(piece, ('hi', 'head'), route))  9.41 us
    unnamed x42, local copies, waits for them, and re-layouts  7.85 us
  transfers between devices with their start and end apart: 32, of which 16 were waited for; matrix products, arithmetic and copies ran while one was open for 3% of the time, Pallas kernels for 12%

profile of v4, /device:TPU:1, one launch (start us, length us, event | category | flops | bytes accessed | tf_op | source)
XLA Modules:
  0.0 206.8 jit_solution(14425445277377967284)
XLA Ops:
  0.0 1.6 fusion
  3.9 5.6 %all-to-all-start = ((bf16[4,128,1024]{2,1,0:T(8,128)(2,1)}), bf16[4,128,1024]{2,1,0:T(8,128)(2,1)S(1)}, u32[]{:S(2)}, u32[]{:S(2)}) async-start(bf16[4,128,1024]{2,1,0:T(8,128)(2,1)} %pad_maximum_fusion), calls=%async_computation | async-start | bytes 2097152 | tf_op jit(solution)/shard_map/all_to_all | solution.py:274
  12.1 10.0 %collective-permute-done.1.refs_2_ = bf16[512,512]{1,0:T(8,128)(2,1)S(1)} collective-permute-done((bf16[512,512]{1,0:T(8,128)(2,1)S(1)}, bf16[512,512]{1,0:T(8,128)(2,1)S(1)}, u32[]{:S(2)}, u32[]{:S(2)}) %collective-permute-start.1) | collective-permute-done | bytes 524320 | tf_op jit(solution)/shard_map/ppermute | solution.py:261
  25.4 2.7 %collective-permute-done.8.refs_3_ = bf16[256,512]{1,0:T(8,128)(2,1)S(1)} collective-permute-done((bf16[256,512]{1,0:T(8,128)(2,1)S(1)}, bf16[256,512]{1,0:T(8,128)(2,1)S(1)}, u32[]{:S(2)}, u32[]{:S(2)}) %collective-permute-start.8) | collective-permute-done | bytes 262176 | tf_op jit(solution)/shard_map/ppermute | solution.py:261
  28.1 1.9 collective-permute-done.9.refs_4_
  30.0 4.7 %all-to-all-done = bf16[4,128,1024]{2,1,0:T(8,128)(2,1)S(1)} async-done(((bf16[4,128,1024]{2,1,0:T(8,128)(2,1)}), bf16[4,128,1024]{2,1,0:T(8,128)(2,1)S(1)}, u32[]{:S(2)}, u32[]{:S(2)}) %all-to-all-start) | async-done | bytes 1048608 | tf_op jit(solution)/shard_map/all_to_all | solution.py:274
  34.7 3.9 %shard_map.74 = bf16[4,512,256]{2,1,0:T(8,128)(2,1)} custom-call(s32[3]{0:T(128)S(1)} %pad_add_fusion.3.place_ref, bf16[512,1024]{1,0:T(8,128)(2,1)S(1)} %bitcast.15, bf16[512,512]{1,0:T(8,128)(2,1)S(1)} %constant_dynamic-update-slice_fusion.refs_0_, bf16[512,512]{1,0:T(8,128)(2,1)S(1)} %collective-permute-done.refs_1_, ...), custom_call_target="tpu_custom_call" | custom-call | flops 1073741824 | bytes 3145740 | tf_op jit(solution)/shard_map/pallas_call | solution.py:18
  38.6 3.6 %all-to-all-start.2 = ((bf16[4,512,256]{2,1,0:T(8,128)(2,1)}), bf16[4,512,256]{2,1,0:T(8,128)(2,1)S(1)}, u32[]{:S(2)}, u32[]{:S(2)}) async-start(bf16[4,512,256]{2,1,0:T(8,128)(2,1)} %shard_map.74), calls=%async_computation.2 | async-start | bytes 2097152 | tf_op jit(solution)/shard_map/all_to_all | solution.py:274
  45.6 9.5 %collective-permute-done.3.refs_2_ = bf16[256,1024]{1,0:T(8,128)(2,1)S(1)} collective-permute-done((bf16[256,1024]{1,0:T(8,128)(2,1)S(1)}, bf16[256,1024]{1,0:T(8,128)(2,1)S(1)}, u32[]{:S(2)}, u32[]{:S(2)}) %collective-permute-start.3) | collective-permute-done | bytes 524320 | tf_op jit(solution)/shard_map/ppermute | solution.py:261
  57.7 3.7 %collective-permute-done.20.refs_3_ = bf16[128,1024]{1,0:T(8,128)(2,1)S(1)} collective-permute-done((bf16[128,1024]{1,0:T(8,128)(2,1)S(1)}, bf16[128,1024]{1,0:T(8,128)(2,1)S(1)}, u32[]{:S(2)}, u32[]{:S(2)}) %collective-permute-start.20) | collective-permute-done | bytes 262176 | tf_op jit(solution)/shard_map/ppermute | solution.py:261
  62.0 2.8 %shard_map.77 = bf16[4,512,256]{2,1,0:T(8,128)(2,1)} custom-call(s32[3]{0:T(128)S(1)} %pad_add_fusion.3.place_ref, bf16[512,1024]{1,0:T(8,128)(2,1)S(1)} %bitcast.16, bf16[256,1024]{1,0:T(8,128)(2,1)S(1)} %pad_maximum_fusion.2.refs_0_, bf16[256,1024]{1,0:T(8,128)(2,1)S(1)} %collective-permute-done.2.refs_1_, ...), custom_call_target="tpu_custom_call" | custom-call | flops 1073741824 | bytes 3145740 | tf_op jit(solution)/shard_map/pallas_call | solution.py:18
  64.9 2.6 %all-to-all-done.2.parts = bf16[4,512,256]{2,1,0:T(8,128)(2,1)S(1)} async-done(((bf16[4,512,256]{2,1,0:T(8,128)(2,1)}), bf16[4,512,256]{2,1,0:T(8,128)(2,1)S(1)}, u32[]{:S(2)}, u32[]{:S(2)}) %all-to-all-start.2) | async-done | bytes 1048608 | tf_op jit(solution)/shard_map/all_to_all | solution.py:274
  67.4 4.3 %all-to-all-start.3 = ((bf16[4,512,256]{2,1,0:T(8,128)(2,1)}), bf16[4,512,256]{2,1,0:T(8,128)(2,1)}, u32[]{:S(2)}, u32[]{:S(2)}) async-start(bf16[4,512,256]{2,1,0:T(8,128)(2,1)} %shard_map.77), calls=%async_computation.3 | async-start | bytes 2097152 | tf_op jit(solution)/shard_map/all_to_all | solution.py:274
  74.3 9.2 %collective-permute-done.5.refs_2_ = bf16[256,1024]{1,0:T(8,128)(2,1)S(1)} collective-permute-done((bf16[256,1024]{1,0:T(8,128)(2,1)S(1)}, bf16[256,1024]{1,0:T(8,128)(2,1)S(1)}, u32[]{:S(2)}, u32[]{:S(2)}) %collective-permute-start.5) | collective-permute-done | bytes 524320 | tf_op jit(solution)/shard_map/ppermute | solution.py:261
  84.9 1.7 collective-permute-start.7
  91.4 2.8 %shard_map.73 = bf16[4,512,256]{2,1,0:T(8,128)(2,1)} custom-call(s32[3]{0:T(128)S(1)} %pad_add_fusion.3.place_ref, bf16[512,1024]{1,0:T(8,128)(2,1)S(1)} %bitcast.17, bf16[256,1024]{1,0:T(8,128)(2,1)S(1)} %pad_maximum_fusion.1.refs_0_, bf16[256,1024]{1,0:T(8,128)(2,1)S(1)} %collective-permute-done.4.refs_1_, ...), custom_call_target="tpu_custom_call" | custom-call | flops 1073741824 | bytes 3145740 | tf_op jit(solution)/shard_map/pallas_call | solution.py:18
  94.2 2.8 %all-to-all-done.3.query_ref = bf16[4,512,256]{2,1,0:T(8,128)(2,1)} async-done(((bf16[4,512,256]{2,1,0:T(8,128)(2,1)}), bf16[4,512,256]{2,1,0:T(8,128)(2,1)}, u32[]{:S(2)}, u32[]{:S(2)}) %all-to-all-start.3) | async-done | bytes 1048608 | tf_op jit(solution)/shard_map/all_to_all | solution.py:274
  97.0 4.3 %all-to-all-start.1 = ((bf16[4,512,256]{2,1,0:T(8,128)(2,1)}), bf16[4,512,256]{2,1,0:T(8,128)(2,1)}, u32[]{:S(2)}, u32[]{:S(2)}) async-start(bf16[4,512,256]{2,1,0:T(8,128)(2,1)} %shard_map.73), calls=%async_computation.1 | async-start | bytes 2097152 | tf_op jit(solution)/shard_map/all_to_all | solution.py:274
  102.0 1.7 collective-permute-done.11.refs_2_
  106.9 15.3 %collective-permute-done.17.refs_6_ = bf16[2048,256]{1,0:T(8,128)(2,1)S(1)} collective-permute-done((bf16[2048,256]{1,0:T(8,128)(2,1)S(1)}, bf16[2048,256]{1,0:T(8,128)(2,1)S(1)}, u32[]{:S(2)}, u32[]{:S(2)}) %collective-permute-start.17) | collective-permute-done | bytes 1048608 | tf_op jit(solution)/shard_map/ppermute | solution.py:261
  123.9 2.2 %collective-permute-start.19 = (bf16[1024,256]{1,0:T(8,128)(2,1)}, bf16[1024,256]{1,0:T(8,128)(2,1)}, u32[]{:S(2)}, u32[]{:S(2)}) collective-permute-start(bf16[1024,256]{1,0:T(8,128)(2,1)} %slice.89), channel_id=1, source_target_pairs={{0,4},{2,6},{4,0},{6,2},{1,5},{3,7},{5,1},{7,3},{8,12},{10,14},{12... | collective-permute-start | bytes 1572872 | tf_op jit(solution)/shard_map/ppermute | solution.py:261
  126.2 7.8 %shard_map.78.refs_0_ = bf16[512,256]{1,0:T(8,128)(2,1)} custom-call(s32[21]{0:T(128)S(1)} %pad_add_fusion.2.place_ref, f32[512,128]{1,0:T(8,128)S(1)} %get-tuple-element.40.cos_ref, f32[512,128]{1,0:T(8,128)S(1)} %copy-done.2, bf16[4,512,256]{2,1,0:T(8,128)(2,1)} %all-to-all-done.3.query_ref, bf16[512,256]{1,0:T(8,128)(2,1)} %shard_map.75.refs_0_, ...), custom_call_target="tpu_custom_call" | custom-call | flops 1073741824 | bytes 2621524 | tf_op jit(solution)/shard_map/pallas_call | solution.py:18
  134.0 2.3 %collective-permute-start.24 = (bf16[512,256]{1,0:T(8,128)(2,1)}, bf16[512,256]{1,0:T(8,128)(2,1)}, u32[]{:S(2)}, u32[]{:S(2)}) collective-permute-start(bf16[512,256]{1,0:T(8,128)(2,1)} %shard_map.78.refs_0_), channel_id=1, source_target_pairs={{0,24},{8,0},{16,8},{24,16},{1,25},{9,1},{17,9},{25,17},{2,26},{10... | collective-permute-start | bytes 786440 | tf_op jit(solution)/shard_map/ppermute | solution.py:279
  140.9 7.1 %shard_map.76.refs_0_ = bf16[512,256]{1,0:T(8,128)(2,1)S(1)} custom-call(s32[21]{0:T(128)S(1)} %pad_add_fusion.2.place_ref, f32[512,128]{1,0:T(8,128)S(1)} %get-tuple-element.40.cos_ref, f32[512,128]{1,0:T(8,128)S(1)} %copy-done.3, bf16[4,512,256]{2,1,0:T(8,128)(2,1)} %all-to-all-done.1.query_ref, bf16[512,256]{1,0:T(8,128)(2,1)} %shard_map.75.refs_0_, ...), custom_call_target="tpu_custom_call" | custom-call | flops 1073741824 | bytes 2621524 | tf_op jit(solution)/shard_map/pallas_call | solution.py:18
  148.0 2.8 %collective-permute-start.15 = (bf16[512,256]{1,0:T(8,128)(2,1)S(1)}, bf16[512,256]{1,0:T(8,128)(2,1)S(1)}, u32[]{:S(2)}, u32[]{:S(2)}) collective-permute-start(bf16[512,256]{1,0:T(8,128)(2,1)S(1)} %shard_map.76.refs_0_), channel_id=1, source_target_pairs={{0,24},{8,0},{16,8},{24,16},{1,25},{9,1},{17,9},{25,17},{2,26},{10... | collective-permute-start | bytes 786440 | tf_op jit(solution)/shard_map/ppermute | solution.py:279
  153.4 2.5 %shard_map.79 = (f32[256,1024]{1,0:T(8,128)S(1)}, f32[256,1024]{1,0:T(8,128)S(1)}) custom-call(s32[4]{0:T(128)S(1)} %get-tuple-element.19.place_ref, bf16[512,256]{1,0:T(8,128)(2,1)} %shard_map.78.refs_0_, bf16[512,256]{1,0:T(8,128)(2,1)} %collective-permute-done.22.refs_1_, bf16[512,256]{1,0:T(8,128)(2,1)} %collective-permute-done.23.refs_2_, ...), custom_call_target="tpu_custom_call" | custom-call | flops 1073741824 | bytes 5242896 | tf_op jit(solution)/shard_map/pallas_call | solution.py:18
  156.9 23.4 %collective-permute-done.14.refs_2_ = bf16[512,256]{1,0:T(8,128)(2,1)S(1)} collective-permute-done((bf16[512,256]{1,0:T(8,128)(2,1)S(1)}, bf16[512,256]{1,0:T(8,128)(2,1)S(1)}, u32[]{:S(2)}, u32[]{:S(2)}) %collective-permute-start.14) | collective-permute-done | bytes 262176 | tf_op jit(solution)/shard_map/ppermute | solution.py:279
  180.3 2.7 %shard_map.80 = (bf16[256,1024]{1,0:T(8,128)(2,1)S(1)}, bf16[256,1024]{1,0:T(8,128)(2,1)}) custom-call(s32[4]{0:T(128)S(1)} %pad_add_fusion.place_ref, bf16[512,256]{1,0:T(8,128)(2,1)S(1)} %shard_map.76.refs_0_, bf16[512,256]{1,0:T(8,128)(2,1)S(1)} %collective-permute-done.13.refs_1_, bf16[512,256]{1,0:T(8,128)(2,1)S(1)} %collective-permute-done.14.refs_2_, ...), custom_call_target="tpu_custom_call" | custom-call | flops 1073741824 | bytes 7340048 | tf_op jit(solution)/shard_map/pallas_call | solution.py:18
  183.8 4.5 %collective-permute-start.25 = (bf16[256,1024]{1,0:T(8,128)(2,1)}, bf16[256,1024]{1,0:T(8,128)(2,1)S(1)}, u32[]{:S(2)}, u32[]{:S(2)}) collective-permute-start(bf16[256,1024]{1,0:T(8,128)(2,1)} %get-tuple-element.18), channel_id=1, source_target_pairs={{0,1},{1,0},{2,3},{3,2},{4,5},{5,4},{6,7},{7,6},{8,9},{9,8},{10,11... | collective-permute-start | bytes 1572872 | tf_op jit(solution)/shard_map/ppermute | solution.py:327
  188.4 1.7 collective-permute-done.25
  191.4 4.9 %collective-permute-start.26 = (bf16[128,1024]{1,0:T(8,128)(2,1)S(1)}, bf16[128,1024]{1,0:T(8,128)(2,1)S(1)}, u32[]{:S(2)}, u32[]{:S(2)}) collective-permute-start(bf16[128,1024]{1,0:T(8,128)(2,1)S(1)} %get-tuple-element.35), channel_id=1, source_target_pairs={{0,0},{1,16},{8,8},{9,24},{16,1},{17,17},{24,9},{25,25},{2,2},{3,1... | collective-permute-start | bytes 786440 | tf_op jit(solution)/shard_map/ppermute | solution.py:334
  196.5 9.4 %collective-permute-done.26 = bf16[128,1024]{1,0:T(8,128)(2,1)S(1)} collective-permute-done((bf16[128,1024]{1,0:T(8,128)(2,1)S(1)}, bf16[128,1024]{1,0:T(8,128)(2,1)S(1)}, u32[]{:S(2)}, u32[]{:S(2)}) %collective-permute-start.26) | collective-permute-done | bytes 262176 | tf_op jit(solution)/shard_map/ppermute | solution.py:334
  (114 shorter events, 40.5 us)
Async XLA Ops:
  3.9 30.8 %all-to-all-start = ((bf16[4,128,1024]{2,1,0:T(8,128)(2,1)}), bf16[4,128,1024]{2,1,0:T(8,128)(2,1)S(1)}, u32[]{:S(2)}, u32[]{:S(2)}) async-start(bf16[4,128,1024]{2,1,0:T(8,128)(2,1)} %pad_maximum_fusion), calls=%async_computation | async-start | bytes 2097152 | tf_op jit(solution)/shard_map/all_to_all | solution.py:274
  9.6 12.5 %collective-permute-start.1 = (bf16[512,512]{1,0:T(8,128)(2,1)S(1)}, bf16[512,512]{1,0:T(8,128)(2,1)S(1)}, u32[]{:S(2)}, u32[]{:S(2)}) collective-permute-start(bf16[512,512]{1,0:T(8,128)(2,1)S(1)} %constant_dynamic-update-slice_fusion.refs_0_), channel_id=1, source_target_pairs={{0,4},{2,6},{4,0},{6,2},{1,5},{3,7},{5,1},{7,3},{8,12},{10,14},{12... | collective-permute-start | bytes 1572872 | tf_op jit(solution)/shard_map/ppermute | solution.py:261
  10.9 12.5 %collective-permute-start = (bf16[512,512]{1,0:T(8,128)(2,1)S(1)}, bf16[512,512]{1,0:T(8,128)(2,1)S(1)}, u32[]{:S(2)}, u32[]{:S(2)}) collective-permute-start(bf16[512,512]{1,0:T(8,128)(2,1)S(1)} %constant_dynamic-update-slice_fusion.refs_0_), channel_id=1, source_target_pairs={{0,2},{2,0},{4,6},{6,4},{1,3},{3,1},{5,7},{7,5},{8,10},{10,8},{12,... | collective-permute-start | bytes 1572872 | tf_op jit(solution)/shard_map/ppermute | solution.py:261
  22.1 6.0 %collective-permute-start.8 = (bf16[256,512]{1,0:T(8,128)(2,1)S(1)}, bf16[256,512]{1,0:T(8,128)(2,1)S(1)}, u32[]{:S(2)}, u32[]{:S(2)}) collective-permute-start(bf16[256,512]{1,0:T(8,128)(2,1)S(1)} %slice.86), channel_id=1, source_target_pairs={{0,2},{2,0},{4,6},{6,4},{1,3},{3,1},{5,7},{7,5},{8,10},{10,8},{12,... | collective-permute-start | bytes 786440 | tf_op jit(solution)/shard_map/ppermute | solution.py:261
  24.1 5.9 %collective-permute-start.9 = (bf16[256,512]{1,0:T(8,128)(2,1)}, bf16[256,512]{1,0:T(8,128)(2,1)S(1)}, u32[]{:S(2)}, u32[]{:S(2)}) collective-permute-start(bf16[256,512]{1,0:T(8,128)(2,1)} %slice.87), channel_id=1, source_target_pairs={{0,4},{2,6},{4,0},{6,2},{1,5},{3,7},{5,1},{7,3},{8,12},{10,14},{12... | collective-permute-start | bytes 786440 | tf_op jit(solution)/shard_map/ppermute | solution.py:261
  38.6 28.8 %all-to-all-start.2 = ((bf16[4,512,256]{2,1,0:T(8,128)(2,1)}), bf16[4,512,256]{2,1,0:T(8,128)(2,1)S(1)}, u32[]{:S(2)}, u32[]{:S(2)}) async-start(bf16[4,512,256]{2,1,0:T(8,128)(2,1)} %shard_map.74), calls=%async_computation.2 | async-start | bytes 2097152 | tf_op jit(solution)/shard_map/all_to_all | solution.py:274
  43.0 12.0 %collective-permute-start.3 = (bf16[256,1024]{1,0:T(8,128)(2,1)S(1)}, bf16[256,1024]{1,0:T(8,128)(2,1)S(1)}, u32[]{:S(2)}, u32[]{:S(2)}) collective-permute-start(bf16[256,1024]{1,0:T(8,128)(2,1)S(1)} %pad_maximum_fusion.2.refs_0_), channel_id=1, source_target_pairs={{0,4},{2,6},{4,0},{6,2},{1,5},{3,7},{5,1},{7,3},{8,12},{10,14},{12... | collective-permute-start | bytes 1572872 | tf_op jit(solution)/shard_map/ppermute | solution.py:261
  44.4 12.0 %collective-permute-start.2 = (bf16[256,1024]{1,0:T(8,128)(2,1)S(1)}, bf16[256,1024]{1,0:T(8,128)(2,1)S(1)}, u32[]{:S(2)}, u32[]{:S(2)}) collective-permute-start(bf16[256,1024]{1,0:T(8,128)(2,1)S(1)} %pad_maximum_fusion.2.refs_0_), channel_id=1, source_target_pairs={{0,2},{2,0},{4,6},{6,4},{1,3},{3,1},{5,7},{7,5},{8,10},{10,8},{12,... | collective-permute-start | bytes 1572872 | tf_op jit(solution)/shard_map/ppermute | solution.py:261
  55.1 6.3 %collective-permute-start.20 = (bf16[128,1024]{1,0:T(8,128)(2,1)S(1)}, bf16[128,1024]{1,0:T(8,128)(2,1)S(1)}, u32[]{:S(2)}, u32[]{:S(2)}) collective-permute-start(bf16[128,1024]{1,0:T(8,128)(2,1)S(1)} %slice.90), channel_id=1, source_target_pairs={{0,2},{2,0},{4,6},{6,4},{1,3},{3,1},{5,7},{7,5},{8,10},{10,8},{12,... | collective-permute-start | bytes 786440 | tf_op jit(solution)/shard_map/ppermute | solution.py:261
  56.4 5.6 %collective-permute-start.21 = (bf16[128,1024]{1,0:T(8,128)(2,1)S(1)}, bf16[128,1024]{1,0:T(8,128)(2,1)S(1)}, u32[]{:S(2)}, u32[]{:S(2)}) collective-permute-start(bf16[128,1024]{1,0:T(8,128)(2,1)S(1)} %slice.91), channel_id=1, source_target_pairs={{0,4},{2,6},{4,0},{6,2},{1,5},{3,7},{5,1},{7,3},{8,12},{10,14},{12... | collective-permute-start | bytes 786440 | tf_op jit(solution)/shard_map/ppermute | solution.py:261
  67.4 29.5 %all-to-all-start.3 = ((bf16[4,512,256]{2,1,0:T(8,128)(2,1)}), bf16[4,512,256]{2,1,0:T(8,128)(2,1)}, u32[]{:S(2)}, u32[]{:S(2)}) async-start(bf16[4,512,256]{2,1,0:T(8,128)(2,1)} %shard_map.77), calls=%async_computation.3 | async-start | bytes 2097152 | tf_op jit(solution)/shard_map/all_to_all | solution.py:274
  71.8 11.8 %collective-permute-start.5 = (bf16[256,1024]{1,0:T(8,128)(2,1)S(1)}, bf16[256,1024]{1,0:T(8,128)(2,1)S(1)}, u32[]{:S(2)}, u32[]{:S(2)}) collective-permute-start(bf16[256,1024]{1,0:T(8,128)(2,1)S(1)} %pad_maximum_fusion.1.refs_0_), channel_id=1, source_target_pairs={{0,4},{2,6},{4,0},{6,2},{1,5},{3,7},{5,1},{7,3},{8,12},{10,14},{12... | collective-permute-start | bytes 1572872 | tf_op jit(solution)/shard_map/ppermute | solution.py:261
  73.1 11.8 %collective-permute-start.4 = (bf16[256,1024]{1,0:T(8,128)(2,1)S(1)}, bf16[256,1024]{1,0:T(8,128)(2,1)S(1)}, u32[]{:S(2)}, u32[]{:S(2)}) collective-permute-start(bf16[256,1024]{1,0:T(8,128)(2,1)S(1)} %pad_maximum_fusion.1.refs_0_), channel_id=1, source_target_pairs={{0,2},{2,0},{4,6},{6,4},{1,3},{3,1},{5,7},{7,5},{8,10},{10,8},{12,... | collective-permute-start | bytes 1572872 | tf_op jit(solution)/shard_map/ppermute | solution.py:261
  83.6 7.8 %collective-permute-start.6 = (bf16[128,1024]{1,0:T(8,128)(2,1)S(1)}, bf16[128,1024]{1,0:T(8,128)(2,1)S(1)}, u32[]{:S(2)}, u32[]{:S(2)}) collective-permute-start(bf16[128,1024]{1,0:T(8,128)(2,1)S(1)} %slice.84), channel_id=1, source_target_pairs={{0,2},{2,0},{4,6},{6,4},{1,3},{3,1},{5,7},{7,5},{8,10},{10,8},{12,... | collective-permute-start | bytes 786440 | tf_op jit(solution)/shard_map/ppermute | solution.py:261
  84.9 6.5 %collective-permute-start.7 = (bf16[128,1024]{1,0:T(8,128)(2,1)S(1)}, bf16[128,1024]{1,0:T(8,128)(2,1)S(1)}, u32[]{:S(2)}, u32[]{:S(2)}) collective-permute-start(bf16[128,1024]{1,0:T(8,128)(2,1)S(1)} %slice.85), channel_id=1, source_target_pairs={{0,4},{2,6},{4,0},{6,2},{1,5},{3,7},{5,1},{7,3},{8,12},{10,14},{12... | collective-permute-start | bytes 786440 | tf_op jit(solution)/shard_map/ppermute | solution.py:261
  88.7 12.6 %collective-permute-start.12 = (bf16[512,256]{1,0:T(8,128)(2,1)}, bf16[512,256]{1,0:T(8,128)(2,1)S(1)}, u32[]{:S(2)}, u32[]{:S(2)}) collective-permute-start(bf16[512,256]{1,0:T(8,128)(2,1)} %shard_map.75.refs_0_), channel_id=1, source_target_pairs={{0,6},{2,4},{4,2},{6,0},{1,7},{3,5},{5,3},{7,1},{8,14},{10,12},{12... | collective-permute-start | bytes 786440 | tf_op jit(solution)/shard_map/ppermute | solution.py:261
  89.5 14.2 %collective-permute-start.11 = (bf16[512,256]{1,0:T(8,128)(2,1)}, bf16[512,256]{1,0:T(8,128)(2,1)S(1)}, u32[]{:S(2)}, u32[]{:S(2)}) collective-permute-start(bf16[512,256]{1,0:T(8,128)(2,1)} %shard_map.75.refs_0_), channel_id=1, source_target_pairs={{0,4},{2,6},{4,0},{6,2},{1,5},{3,7},{5,1},{7,3},{8,12},{10,14},{12... | collective-permute-start | bytes 786440 | tf_op jit(solution)/shard_map/ppermute | solution.py:261
  90.0 14.3 %collective-permute-start.10 = (bf16[512,256]{1,0:T(8,128)(2,1)}, bf16[512,256]{1,0:T(8,128)(2,1)S(1)}, u32[]{:S(2)}, u32[]{:S(2)}) collective-permute-start(bf16[512,256]{1,0:T(8,128)(2,1)} %shard_map.75.refs_0_), channel_id=1, source_target_pairs={{0,2},{2,0},{4,6},{6,4},{1,3},{3,1},{5,7},{7,5},{8,10},{10,8},{12,... | collective-permute-start | bytes 786440 | tf_op jit(solution)/shard_map/ppermute | solution.py:261
  97.0 40.1 %all-to-all-start.1 = ((bf16[4,512,256]{2,1,0:T(8,128)(2,1)}), bf16[4,512,256]{2,1,0:T(8,128)(2,1)}, u32[]{:S(2)}, u32[]{:S(2)}) async-start(bf16[4,512,256]{2,1,0:T(8,128)(2,1)} %shard_map.73), calls=%async_computation.1 | async-start | bytes 2097152 | tf_op jit(solution)/shard_map/all_to_all | solution.py:274
  105.1 17.1 %collective-permute-start.17 = (bf16[2048,256]{1,0:T(8,128)(2,1)S(1)}, bf16[2048,256]{1,0:T(8,128)(2,1)S(1)}, u32[]{:S(2)}, u32[]{:S(2)}) collective-permute-start(bf16[2048,256]{1,0:T(8,128)(2,1)S(1)} %copy-done), channel_id=1, source_target_pairs={{0,4},{2,6},{4,0},{6,2},{1,5},{3,7},{5,1},{7,3},{8,12},{10,14},{12... | collective-permute-start | bytes 3145736 | tf_op jit(solution)/shard_map/ppermute | solution.py:261
  105.4 17.7 %collective-permute-start.16 = (bf16[2048,256]{1,0:T(8,128)(2,1)S(1)}, bf16[2048,256]{1,0:T(8,128)(2,1)S(1)}, u32[]{:S(2)}, u32[]{:S(2)}) collective-permute-start(bf16[2048,256]{1,0:T(8,128)(2,1)S(1)} %copy-done), channel_id=1, source_target_pairs={{0,2},{2,0},{4,6},{6,4},{1,3},{3,1},{5,7},{7,5},{8,10},{10,8},{12,... | collective-permute-start | bytes 3145736 | tf_op jit(solution)/shard_map/ppermute | solution.py:261
  123.0 27.8 %collective-permute-start.18 = (bf16[1024,256]{1,0:T(8,128)(2,1)}, bf16[1024,256]{1,0:T(8,128)(2,1)}, u32[]{:S(2)}, u32[]{:S(2)}) collective-permute-start(bf16[1024,256]{1,0:T(8,128)(2,1)} %slice.88), channel_id=1, source_target_pairs={{0,2},{2,0},{4,6},{6,4},{1,3},{3,1},{5,7},{7,5},{8,10},{10,8},{12,... | collective-permute-start | bytes 1572872 | tf_op jit(solution)/shard_map/ppermute | solution.py:261
  123.9 27.3 %collective-permute-start.19 = (bf16[1024,256]{1,0:T(8,128)(2,1)}, bf16[1024,256]{1,0:T(8,128)(2,1)}, u32[]{:S(2)}, u32[]{:S(2)}) collective-permute-start(bf16[1024,256]{1,0:T(8,128)(2,1)} %slice.89), channel_id=1, source_target_pairs={{0,4},{2,6},{4,0},{6,2},{1,5},{3,7},{5,1},{7,3},{8,12},{10,14},{12... | collective-permute-start | bytes 1572872 | tf_op jit(solution)/shard_map/ppermute | solution.py:261
  134.0 13.9 %collective-permute-start.24 = (bf16[512,256]{1,0:T(8,128)(2,1)}, bf16[512,256]{1,0:T(8,128)(2,1)}, u32[]{:S(2)}, u32[]{:S(2)}) collective-permute-start(bf16[512,256]{1,0:T(8,128)(2,1)} %shard_map.78.refs_0_), channel_id=1, source_target_pairs={{0,24},{8,0},{16,8},{24,16},{1,25},{9,1},{17,9},{25,17},{2,26},{10... | collective-permute-start | bytes 786440 | tf_op jit(solution)/shard_map/ppermute | solution.py:279
  136.4 17.0 %collective-permute-start.23 = (bf16[512,256]{1,0:T(8,128)(2,1)}, bf16[512,256]{1,0:T(8,128)(2,1)}, u32[]{:S(2)}, u32[]{:S(2)}) collective-permute-start(bf16[512,256]{1,0:T(8,128)(2,1)} %shard_map.78.refs_0_), channel_id=1, source_target_pairs={{0,16},{8,24},{16,0},{24,8},{1,17},{9,25},{17,1},{25,9},{2,18},{10... | collective-permute-start | bytes 786440 | tf_op jit(solution)/shard_map/ppermute | solution.py:279
  136.4 17.0 %collective-permute-start.22 = (bf16[512,256]{1,0:T(8,128)(2,1)}, bf16[512,256]{1,0:T(8,128)(2,1)}, u32[]{:S(2)}, u32[]{:S(2)}) collective-permute-start(bf16[512,256]{1,0:T(8,128)(2,1)} %shard_map.78.refs_0_), channel_id=1, source_target_pairs={{0,8},{8,16},{16,24},{24,0},{1,9},{9,17},{17,25},{25,1},{2,10},{10... | collective-permute-start | bytes 786440 | tf_op jit(solution)/shard_map/ppermute | solution.py:279
  148.0 9.0 %collective-permute-start.15 = (bf16[512,256]{1,0:T(8,128)(2,1)S(1)}, bf16[512,256]{1,0:T(8,128)(2,1)S(1)}, u32[]{:S(2)}, u32[]{:S(2)}) collective-permute-start(bf16[512,256]{1,0:T(8,128)(2,1)S(1)} %shard_map.76.refs_0_), channel_id=1, source_target_pairs={{0,24},{8,0},{16,8},{24,16},{1,25},{9,1},{17,9},{25,17},{2,26},{10... | collective-permute-start | bytes 786440 | tf_op jit(solution)/shard_map/ppermute | solution.py:279
  150.8 29.5 %collective-permute-start.14 = (bf16[512,256]{1,0:T(8,128)(2,1)S(1)}, bf16[512,256]{1,0:T(8,128)(2,1)S(1)}, u32[]{:S(2)}, u32[]{:S(2)}) collective-permute-start(bf16[512,256]{1,0:T(8,128)(2,1)S(1)} %shard_map.76.refs_0_), channel_id=1, source_target_pairs={{0,16},{8,24},{16,0},{24,8},{1,17},{9,25},{17,1},{25,9},{2,18},{10... | collective-permute-start | bytes 786440 | tf_op jit(solution)/shard_map/ppermute | solution.py:279
  151.2 29.1 %collective-permute-start.13 = (bf16[512,256]{1,0:T(8,128)(2,1)S(1)}, bf16[512,256]{1,0:T(8,128)(2,1)S(1)}, u32[]{:S(2)}, u32[]{:S(2)}) collective-permute-start(bf16[512,256]{1,0:T(8,128)(2,1)S(1)} %shard_map.76.refs_0_), channel_id=1, source_target_pairs={{0,8},{8,16},{16,24},{24,0},{1,9},{9,17},{17,25},{25,1},{2,10},{10... | collective-permute-start | bytes 786440 | tf_op jit(solution)/shard_map/ppermute | solution.py:279
  183.8 6.3 %collective-permute-start.25 = (bf16[256,1024]{1,0:T(8,128)(2,1)}, bf16[256,1024]{1,0:T(8,128)(2,1)S(1)}, u32[]{:S(2)}, u32[]{:S(2)}) collective-permute-start(bf16[256,1024]{1,0:T(8,128)(2,1)} %get-tuple-element.18), channel_id=1, source_target_pairs={{0,1},{1,0},{2,3},{3,2},{4,5},{5,4},{6,7},{7,6},{8,9},{9,8},{10,11... | collective-permute-start | bytes 1572872 | tf_op jit(solution)/shard_map/ppermute | solution.py:327
  191.4 14.6 %collective-permute-start.26 = (bf16[128,1024]{1,0:T(8,128)(2,1)S(1)}, bf16[128,1024]{1,0:T(8,128)(2,1)S(1)}, u32[]{:S(2)}, u32[]{:S(2)}) collective-permute-start(bf16[128,1024]{1,0:T(8,128)(2,1)S(1)} %get-tuple-element.35), channel_id=1, source_target_pairs={{0,0},{1,16},{8,8},{9,24},{16,1},{17,17},{24,9},{25,25},{2,2},{3,1... | collective-permute-start | bytes 786440 | tf_op jit(solution)/shard_map/ppermute | solution.py:334
  196.3 9.7 %collective-permute-start.27 = (bf16[128,1024]{1,0:T(8,128)(2,1)S(1)}, bf16[128,1024]{1,0:T(8,128)(2,1)S(1)}, u32[]{:S(2)}, u32[]{:S(2)}) collective-permute-start(bf16[128,1024]{1,0:T(8,128)(2,1)S(1)} %get-tuple-element.36), channel_id=1, source_target_pairs={{0,8},{1,24},{8,0},{9,16},{16,9},{17,25},{24,1},{25,17},{2,10},{3,... | collective-permute-start | bytes 786440 | tf_op jit(solution)/shard_map/ppermute | solution.py:334
  (20 other events, 141.1 us)

commit v5 on v4

--- a/solution.py
+++ b/solution.py
@@ -37,10 +37,10 @@
     )
 
 
-def summed_lanes(parts_ref, lanes):
-    total = parts_ref[0, :, lanes].astype(jnp.float32)
-    for part in range(1, parts_ref.shape[0]):
-        total = total + parts_ref[part, :, lanes].astype(jnp.float32)
+def summed_lanes(refs, lanes):
+    total = refs[0][:, lanes].astype(jnp.float32)
+    for ref in refs[1:]:
+        total = total + ref[:, lanes].astype(jnp.float32)
     return total
 
 
@@ -48,24 +48,26 @@
     return values * cos_ref[...] + pltpu.roll(values, HALF, 1) * sin_ref[...]
 
 
-def pair_kernel(unused_ref, cos_ref, sin_ref, parts, out_ref):
+def pair_kernel(unused_ref, cos_ref, sin_ref, *refs):
+    parts, out_ref = refs[:-1], refs[-1]
     key = rotated(summed_lanes(parts, pl.ds(0, HD)), cos_ref, sin_ref)
     out_ref[:, pl.ds(0, HD)] = key.astype(jnp.bfloat16)
     out_ref[:, pl.ds(HD, HD)] = summed_lanes(parts, pl.ds(HD, HD)).astype(jnp.bfloat16)
 
 
 def finish_pair(cosine, sine, parts):
-    operands = (jnp.zeros((1,), jnp.int32), cosine, sine, parts)
-    shape = jax.ShapeDtypeStruct(parts.shape[1:], jnp.bfloat16)
-    return local_kernel(pair_kernel, shape, operands, 8 * parts.size)
-
-
-def attention_kernel(blocks, stride, n_kv, place_ref, cos_ref, sin_ref, query_ref, *refs):
-    kv_refs = refs[:n_kv]
-    out_ref, turned, bias = refs[n_kv:]
+    operands = (jnp.zeros((1,), jnp.int32), cosine, sine, *parts)
+    shape = jax.ShapeDtypeStruct(parts[0].shape, jnp.bfloat16)
+    return local_kernel(pair_kernel, shape, operands, 8 * parts[0].size)
+
+
+def attention_kernel(blocks, stride, n_query, n_kv, place_ref, cos_ref, sin_ref, *refs):
+    query_refs = refs[:n_query]
+    kv_refs = refs[n_query : n_query + n_kv]
+    out_ref, turned, bias = refs[n_query + n_kv :]
     heads, tokens, _ = turned.shape
     for h in range(heads):
-        total = summed_lanes(query_ref, pl.ds(h * HD, HD))
+        total = summed_lanes(query_refs, pl.ds(h * HD, HD))
         turned[h] = rotated(total, cos_ref, sin_ref).astype(jnp.bfloat16)
     rows = tokens // blocks
     kv_rows = kv_refs[0].shape[0] // blocks
@@ -124,13 +126,13 @@
 
 
 def attention(place, cosine, sine, query_parts, kv_parts, blocks, stride):
-    _, tokens, width = query_parts.shape
+    tokens, width = query_parts[0].shape
     heads = width // HD
     keys = sum(part.shape[0] for part in kv_parts)
     return local_kernel(
-        functools.partial(attention_kernel, blocks, stride, len(kv_parts)),
+        functools.partial(attention_kernel, blocks, stride, len(query_parts), len(kv_parts)),
         jax.ShapeDtypeStruct((tokens, width), jnp.bfloat16),
-        (place, cosine, sine, query_parts, *kv_parts),
+        (place, cosine, sine, *query_parts, *kv_parts),
         4 * tokens * width * keys,
         [
             pltpu.VMEM((heads, tokens, HD), jnp.bfloat16),
@@ -140,77 +142,110 @@
     )
 
 
-def product_kernel(groups, place_ref, token_ref, *refs):
-    weight_refs = refs[:5]
-    out_ref = refs[-1]
+def product_kernel(features_of, weights_of, place_ref, *refs):
+    token_refs = refs[:4]
+    weight_refs = refs[4:-5]
+    out_refs = refs[-5:-1]
+    gathered = refs[-1]
+    hi = place_ref[0]
     lo = place_ref[1]
-    share = weight_refs[0].shape[0] // groups
-    width = weight_refs[0].shape[1] // 4
-    for d in range(4):
-        columns = pl.ds(d * width, width)
-        for g in range(groups):
+    rows = token_refs[0].shape[0]
+    for d, token_ref in enumerate(token_refs):
+        first = pl.multiple_of(lax.rem(hi - d + 4, 4) * rows, rows)
+        gathered[pl.ds(first, rows), :] = token_ref[...]
+    for d, out_ref in enumerate(out_refs):
+        there = lax.rem(hi + d, 4)
+        place = 0
+        for weights in weights_of(weight_refs, there):
             total = 0.0
-            for r in range(4):
-                features = pl.ds(pl.multiple_of((lo ^ r) * share, share), share)
-                if r < 3:
-                    weight = weight_refs[r][pl.ds(g * share, share), columns]
-                elif groups == 2:
-                    weight = weight_refs[3 + g][:, columns]
-                else:
-                    weight = jnp.concatenate([ref[:, columns] for ref in weight_refs[3:]], axis=0)
+            for r, weight in enumerate(weights):
                 total = total + jnp.dot(
-                    token_ref[:, features], weight, preferred_element_type=jnp.float32
+                    gathered[:, features_of(lo, r)], weight, preferred_element_type=jnp.float32
                 )
-            out_ref[d, :, pl.ds(g * width, width)] = total.astype(jnp.bfloat16)
-
-
-def product(place, line_tokens, weights, groups):
-    count, depth = line_tokens.shape
-    width = groups * weights[0].shape[1] // 4
+            width = total.shape[1]
+            out_ref[:, pl.ds(place, width)] = total.astype(jnp.bfloat16)
+            place += width
+
+
+def product(features_of, weights_of, place, token_parts, weights, width):
+    rows, depth = token_parts[0].shape
+    shape = jax.ShapeDtypeStruct((4 * rows, width), jnp.bfloat16)
     return local_kernel(
-        functools.partial(product_kernel, groups),
-        jax.ShapeDtypeStruct((4, count, width), jnp.bfloat16),
-        (place, line_tokens, *weights),
-        2 * count * depth * 4 * width,
-    )
+        functools.partial(product_kernel, features_of, weights_of),
+        (shape,) * 4,
+        (place, *token_parts, *weights),
+        2 * 4 * rows * depth * 4 * width,
+        [pltpu.VMEM((4 * rows, depth), jnp.bfloat16)],
+    )
+
+
+def pair_product(place, token_parts, weights):
+    share = weights[0].shape[0] // 2
+
+    def features_of(lo, r):
+        return pl.ds(pl.multiple_of((lo ^ r) * share, share), share)
+
+    def weights_of(refs, there):
+        columns = pl.ds(pl.multiple_of(there * HD, HD), HD)
+        return [
+            [ref[pl.ds(g * share, share), columns] for ref in refs[:3]] + [refs[3 + g][:, columns]]
+            for g in range(2)
+        ]
+
+    return product(features_of, weights_of, place, token_parts, weights, 2 * HD)
+
+
+def query_product(place, token_parts, weight, chunk, chunks):
+    share = weight.shape[1]
+    width = weight.shape[2] // 4 // chunks
+
+    def features_of(lo, r):
+        return pl.ds(r * share, share)
+
+    def weights_of(refs, there):
+        columns = pl.ds(pl.multiple_of((there * chunks + chunk) * width, width), width)
+        return [[refs[0][r, :, columns] for r in range(4)]]
+
+    return product(features_of, weights_of, place, token_parts, [weight], width)
 
 
 def project_kernel(place_ref, *refs):
-    attended_refs = refs[:4]
-    weight_refs = refs[4:8]
+    own, left, right, weight_ref = refs[0], refs[1:4], refs[4:7], refs[7]
     total_refs = refs[8:-2]
     hi = place_ref[0]
-    lo = place_ref[1]
-    core = place_ref[2]
-    offset = place_ref[3]
-    depth = attended_refs[0].shape[1]
-    width = weight_refs[0].shape[1]
-    span = weight_refs[0].shape[0] // 4
+    core = place_ref[1]
+    offset = place_ref[2]
+    depth = own.shape[1]
+    blocks, features, width = weight_ref.shape
+    span = features // 4
     for side, out_ref in enumerate(refs[-2:]):
         kept = out_ref.shape[0]
         rows = pl.ds(pl.multiple_of(lax.rem(core + side, 2) * kept, kept), kept)
-        for r, weight_ref in enumerate(weight_refs):
-            columns = pl.ds(pl.multiple_of((lo ^ r) * width, width), width)
+        attended = [own[rows, :]]
+        for k in range(1, 4):
+            attended.append(jnp.where(hi >= k, left[k - 1][rows, :], right[3 - k][rows, :]))
+        for r in range(blocks):
+            columns = pl.ds(r * width, width)
             total = total_refs[side][:, columns] if total_refs else 0.0
-            for k, attended_ref in enumerate(attended_refs):
+            for k in range(4):
                 first = lax.rem(hi - k + 4, 4) * span + offset
                 total = total + jnp.dot(
-                    attended_ref[rows, :],
-                    weight_ref[pl.ds(pl.multiple_of(first, depth), depth), :],
+                    attended[k],
+                    weight_ref[r, pl.ds(pl.multiple_of(first, depth), depth), :],
                     preferred_element_type=jnp.float32,
                 )
             out_ref[:, columns] = total.astype(out_ref.dtype)
 
 
-def project(place, attended_parts, weights, totals, kind):
+def project(place, attended_parts, weight, totals, kind):
     tokens, depth = attended_parts[0].shape
-    width = weights[0].shape[1]
-    shape = jax.ShapeDtypeStruct((tokens // 2, 4 * width), kind)
+    blocks, _, width = weight.shape
+    shape = jax.ShapeDtypeStruct((tokens // 2, blocks * width), kind)
     return local_kernel(
         project_kernel,
         (shape, shape),
-        (place, *attended_parts, *weights, *totals),
-        2 * tokens * 4 * depth * 4 * width,
+        (place, *attended_parts, weight, *totals),
+        2 * tokens * 4 * depth * blocks * width,
     )
 
 
@@ -242,9 +277,9 @@
     for h in range(kv_local):
         lanes = slice(h * HD, (h + 1) * HD)
         pair = jnp.concatenate([key[:, lanes], value[:, lanes]], axis=1)
-        pair = lax.all_gather(finish_pair(cosine, sine, pair[None]), "ctx", axis=0, tiled=True)
+        pair = lax.all_gather(finish_pair(cosine, sine, [pair]), "ctx", axis=0, tiled=True)
         part = query[:, h * group : (h + 1) * group]
-        mixed.append(attention(place, cosine, sine, part[None], [pair], 1, 0))
+        mixed.append(attention(place, cosine, sine, [part], [pair], 1, 0))
     attended = jnp.concatenate(mixed, axis=1)
     wide = lax.all_gather(w_out, "ctx", axis=1, tiled=True)
     partial_out = jnp.dot(attended, wide, preferred_element_type=jnp.float32)
@@ -253,10 +288,6 @@
     )
 
 
-def after(value, *earlier):
-    return lax.optimization_barrier((value, *earlier))[0]
-
-
 def beside(block, r):
     return lax.ppermute(block, "lo", [(i, i ^ r) for i in range(4)])
 
@@ -271,13 +302,21 @@
 
 
 def along_line(pieces):
-    return lax.all_to_all(pieces, "hi", 0, 0, tiled=True)
-
-
-def round_line(block):
-    return [block] + [
-        lax.ppermute(block, "hi", [(i, (i + d) % 4) for i in range(4)]) for d in range(1, 4)
+    return [pieces[0]] + [
+        lax.ppermute(pieces[d], "hi", [(i, (i + d) % 4) for i in range(4)]) for d in range(1, 4)
     ]
+
+
+def pass_on(block):
+    blocks = [block]
+    for step in (1, -1):
+        moving = block
+        for _ in range(3):
+            moving = lax.ppermute(
+                moving, "hi", [(i, i + step) for i in range(4) if 0 <= i + step < 4]
+            )
+            blocks.append(moving)
+    return blocks
 
 
 def line_device(tokens, norm_gain, w_query, w_key, w_value, w_out, doc_starts):
@@ -288,40 +327,33 @@
     depth = features // 4
     heads = w_query.shape[1] // 4
     half = heads // 2
-    place = jnp.stack([hi, lo, core])
-
-    stage = sides(jnp.concatenate([w_key, w_value], axis=0))
-    pair_blocks = corner(stage)
-    query_blocks = []
-    for c in range(2):
-        columns = [
-            w_query[:, z * heads + c * half : z * heads + (c + 1) * half] for z in range(4)
-        ]
-        stage = sides(after(jnp.concatenate(columns, axis=1), *stage[1:]))
-        query_blocks.append(corner(stage))
+    place = jnp.stack([hi, lo])
+
+    query_weight = lax.all_gather(w_query, "lo", axis=0)
+    out_weight = lax.all_gather(w_out, "lo", axis=0)
+    pair_weight = corner(sides(jnp.concatenate([w_key, w_value], axis=0)))
 
     normed = normalised(tokens, norm_gain)
-    pieces = jnp.stack([normed[:, d * depth : (d + 1) * depth] for d in range(4)])
-    line_tokens = along_line(pieces).reshape(4 * rows, depth)
+    token_parts = along_line(
+        [lax.dynamic_slice_in_dim(normed, lax.rem(hi + d, 4) * depth, depth, 1) for d in range(4)]
+    )
 
     row_index = jnp.arange(4 * rows, dtype=jnp.int32)
     cosine, sine = rotary_tables((row_index // rows * 4 + lo) * rows + row_index % rows)
     kv_own = finish_pair(
-        cosine, sine, along_line(product(place, line_tokens, pair_blocks, 2))
+        cosine, sine, along_line(pair_product(place, token_parts, pair_weight))
     )
     kv_parts = [kv_own] + [beside(kv_own, r) for r in range(1, 4)]
-    out_blocks = corner(sides(after(w_out, *query_blocks[1][3:], *kv_parts[1:])))
-    out_blocks[3:] = [jnp.concatenate(out_blocks[3:], axis=0)]
 
     firsts = jnp.stack([lo, lo, lo ^ 1, lo ^ 2, lo ^ 3]) * rows
     seen = jnp.concatenate([firsts, doc_starts])
     totals = ()
     kinds = (jnp.float32, jnp.bfloat16)
     for c in range(2):
-        query_parts = along_line(product(place, line_tokens, query_blocks[c], 1))
+        query_parts = along_line(query_product(place, token_parts, query_weight, c, 2))
         attended = attention(seen, cosine, sine, query_parts, kv_parts, 4, 4 * rows)
-        where = jnp.concatenate([place, jnp.full((1,), c * half, jnp.int32)])
-        totals = project(where, round_line(attended), out_blocks, totals, kinds[c])
+        where = jnp.stack([hi, core, jnp.full((), c * half, jnp.int32)])
+        totals = project(where, pass_on(attended), out_weight, totals, kinds[c])
 
     mine, theirs = totals
     theirs = lax.ppermute(theirs, "head", [(0, 1), (1, 0)])

time: 209 us -> 207 us (level)
  waiting for transfers between devices: 100 us -> 69.6 us
  starting transfers between devices: 55.7 us -> 84.9 us
  between operations: 0.31 us -> 13.8 us
  Pallas kernels: 30.5 us -> 23.7 us
  other arithmetic: 7.55 us -> 3.19 us
  local copies, waits for them, and re-layouts: 12.4 us -> 10.1 us
    ppermute x6 -> x24, starting transfers between devices: 6.18 us -> 65.3 us  [the longest x12 48.4 us: pass_on(): lax.ppermute(moving, 'hi', [(i, i + step) for i in range(4) if 0 <= i + s...]
    ppermute x19 -> x7, waiting for transfers between devices: 54.6 us -> 5.11 us  [beside(): return lax.ppermute(block, 'lo', [(i, i ^ r) for i in range(4)])]
    all_to_all x4 -> x0, starting transfers between devices: 17.7 us -> none  [along_line(): return lax.all_to_all(pieces, 'hi', 0, 0, tiled=True)]
    all_gather x0 -> x2, waiting for transfers between devices: none -> 17.5 us  [the longest x1 17.5 us: line_device(): query_weight = lax.all_gather(w_query, 'lo', axis=0)]
    ppermute x19 -> x7, starting transfers between devices: 22.1 us -> 8.52 us  [beside(): return lax.ppermute(block, 'lo', [(i, i ^ r) for i in range(4)])]
    ppermute x6 -> x24, waiting for transfers between devices: 24.5 us -> 34.9 us  [the longest x12 34 us: along_line(): lax.ppermute(pieces[d], 'hi', [(i, (i + d) % 4) for i in range(4)])]
    all_to_all x4 -> x0, waiting for transfers between devices: 10.1 us -> none  [along_line(): return lax.all_to_all(pieces, 'hi', 0, 0, tiled=True)]
    pallas_call x8, Pallas kernels: 30.5 us -> 23.7 us  [local_kernel(): pl.pallas_call(body, in_specs=[pl.BlockSpec(memory_space=pltpu.SMEM)] + [...]
  transfers between devices with their start and end apart: 32 -> 36, of which waited for: 16 -> 9; matrix products, arithmetic and copies ran while one was open for 3% -> 2% of each run, Pallas kernels for 12% -> 10%
where the time goes in v5:
time: 207 us; the launch traced here: 205 us
  starting transfers between devices  84.9 us (41%)
  waiting for transfers between devices  69.6 us (34%)
  Pallas kernels  23.7 us (11%)
  between operations  13.8 us (7%)
  local copies, waits for them, and re-layouts  10.1 us (5%)
  other arithmetic  3.19 us (2%)
    ppermute x12, starting transfers between devices, pass_on(): lax.ppermute(moving, 'hi', [(i, i + step) for i in range(4) if 0 <= i + s...  48.4 us
    ppermute x12, waiting for transfers between devices, along_line(): lax.ppermute(pieces[d], 'hi', [(i, (i + d) % 4) for i in range(4)])  34 us
    pallas_call x8, Pallas kernels, local_kernel(): pl.pallas_call(body, in_specs=[pl.BlockSpec(memory_space=pltpu.SMEM)] + [...  23.7 us
    all_gather x1, waiting for transfers between devices, line_device(): query_weight = lax.all_gather(w_query, 'lo', axis=0)  17.5 us
    ppermute x12, starting transfers between devices, along_line(): lax.ppermute(pieces[d], 'hi', [(i, (i + d) % 4) for i in range(4)])  16.9 us
    ppermute x2, waiting for transfers between devices, line_device(): arrived.append(lax.ppermute(piece, ('hi', 'head'), route))  9.12 us
    ppermute x7, starting transfers between devices, beside(): return lax.ppermute(block, 'lo', [(i, i ^ r) for i in range(4)])  8.52 us
    unnamed x23, local copies, waits for them, and re-layouts  7.64 us
  transfers between devices with their start and end apart: 36, of which 9 were waited for; matrix products, arithmetic and copies ran while one was open for 2% of the time, Pallas kernels for 10%

profile of v5, /device:TPU:1, one launch (start us, length us, event | category | flops | bytes accessed | tf_op | source)
XLA Modules:
  0.0 205.3 jit_solution(17939765937201552088)
XLA Ops:
  8.1 2.1 %collective-permute-start.7 = (bf16[512,512]{1,0:T(8,128)(2,1)S(1)}, bf16[512,512]{1,0:T(8,128)(2,1)S(1)}, u32[]{:S(2)}, u32[]{:S(2)}) collective-permute-start(bf16[512,512]{1,0:T(8,128)(2,1)S(1)} %constant_dynamic-update-slice_fusion.refs_4_), channel_id=1, source_target_pairs={{0,4},{2,6},{4,0},{6,2},{1,5},{3,7},{5,1},{7,3},{8,12},{10,14},{12... | collective-permute-start | bytes 1572872 | tf_op jit(solution)/shard_map/ppermute | solution.py:292
  13.0 3.3 %collective-permute-start.2 = (bf16[128,1024]{1,0:T(8,128)(2,1)}, bf16[128,1024]{1,0:T(8,128)(2,1)S(1)}, u32[]{:S(2)}, u32[]{:S(2)}) collective-permute-start(bf16[128,1024]{1,0:T(8,128)(2,1)} %get-tuple-element.37), channel_id=1, source_target_pairs={{0,24},{8,0},{16,8},{24,16},{1,25},{9,1},{17,9},{25,17},{2,26},{10... | collective-permute-start | bytes 786440 | tf_op jit(solution)/shard_map/ppermute | solution.py:306
  16.8 5.1 %collective-permute-done.7.refs_6_ = bf16[512,512]{1,0:T(8,128)(2,1)S(1)} collective-permute-done((bf16[512,512]{1,0:T(8,128)(2,1)S(1)}, bf16[512,512]{1,0:T(8,128)(2,1)S(1)}, u32[]{:S(2)}, u32[]{:S(2)}) %collective-permute-start.7) | collective-permute-done | bytes 524320 | tf_op jit(solution)/shard_map/ppermute | solution.py:292
  25.9 11.8 %collective-permute-done.1.refs_2_ = bf16[128,1024]{1,0:T(8,128)(2,1)S(1)} collective-permute-done((bf16[128,1024]{1,0:T(8,128)(2,1)}, bf16[128,1024]{1,0:T(8,128)(2,1)S(1)}, u32[]{:S(2)}, u32[]{:S(2)}) %collective-permute-start.1) | collective-permute-done | bytes 262176 | tf_op jit(solution)/shard_map/ppermute | solution.py:306
  37.7 2.9 %shard_map.74 = (bf16[512,256]{1,0:T(8,128)(2,1)S(1)}, bf16[512,256]{1,0:T(8,128)(2,1)S(1)}, bf16[512,256]{1,0:T(8,128)(2,1)S(1)}, bf16[512,256]{1,0:T(8,128)(2,1)S(1)}) custom-call(s32[2]{0:T(128)S(1)} %pad_add_fusion.3.place_ref, bf16[128,1024]{1,0:T(8,128)(2,1)S(1)} %get-tuple-element.40.refs_0_, bf16[128,1024]{1,0:T(8,128)(2,1)S(1)} %collective-permute-done.refs_1_, ...), custom_call_target="tpu_custom_call" | custom-call | flops 1073741824 | bytes 3145736 | tf_op jit(solution)/shard_map/pallas_call | solution.py:18
  40.6 1.5 collective-permute-start.10
  42.1 2.1 %collective-permute-start.11 = (bf16[512,256]{1,0:T(8,128)(2,1)S(1)}, bf16[512,256]{1,0:T(8,128)(2,1)S(1)}, u32[]{:S(2)}, u32[]{:S(2)}) collective-permute-start(bf16[512,256]{1,0:T(8,128)(2,1)S(1)} %get-tuple-element.27), channel_id=1, source_target_pairs={{0,16},{8,24},{16,0},{24,8},{1,17},{9,25},{17,1},{25,9},{2,18},{10... | collective-permute-start | bytes 786440 | tf_op jit(solution)/shard_map/ppermute | solution.py:306
  44.2 2.3 %collective-permute-start.12 = (bf16[512,256]{1,0:T(8,128)(2,1)S(1)}, bf16[512,256]{1,0:T(8,128)(2,1)S(1)}, u32[]{:S(2)}, u32[]{:S(2)}) collective-permute-start(bf16[512,256]{1,0:T(8,128)(2,1)S(1)} %get-tuple-element.28), channel_id=1, source_target_pairs={{0,24},{8,0},{16,8},{24,16},{1,25},{9,1},{17,9},{25,17},{2,26},{10... | collective-permute-start | bytes 786440 | tf_op jit(solution)/shard_map/ppermute | solution.py:306
  48.0 13.9 %collective-permute-done.11.refs_2_ = bf16[512,256]{1,0:T(8,128)(2,1)S(1)} collective-permute-done((bf16[512,256]{1,0:T(8,128)(2,1)S(1)}, bf16[512,256]{1,0:T(8,128)(2,1)S(1)}, u32[]{:S(2)}, u32[]{:S(2)}) %collective-permute-start.11) | collective-permute-done | bytes 262176 | tf_op jit(solution)/shard_map/ppermute | solution.py:306
  64.9 17.5 %all-gather.5.cloned.1.call-done = bf16[1024,2048]{1,0:T(8,128)(2,1)} async-done(((bf16[256,2048]{1,0:T(8,128)(2,1)}), bf16[1024,2048]{1,0:T(8,128)(2,1)}) %all-gather.5.cloned.1.call-update) | async-done | bytes 4194320 | tf_op jit(solution)/shard_map/all_gather | solution.py:332
  82.4 2.2 %copy-done.2 = bf16[1024,2048]{1,0:T(8,128)(2,1)S(1)} copy-done((bf16[1024,2048]{1,0:T(8,128)(2,1)S(1)}, bf16[1024,2048]{1,0:T(8,128)(2,1)}, u32[]{:S(2)}) %copy-start.2) | copy-done | bytes 4194328
  84.6 2.0 shard_map.77
  87.4 2.5 %copy-done.3 = bf16[1024,2048]{1,0:T(8,128)(2,1)S(1)} copy-done((bf16[1024,2048]{1,0:T(8,128)(2,1)S(1)}, bf16[1024,2048]{1,0:T(8,128)(2,1)}, u32[]{:S(2)}) %copy-start.3) | copy-done | bytes 4194328
  89.9 1.9 shard_map.73
  91.8 3.3 %collective-permute-start.24 = (bf16[512,256]{1,0:T(8,128)(2,1)S(1)}, bf16[512,256]{1,0:T(8,128)(2,1)S(1)}, u32[]{:S(2)}, u32[]{:S(2)}) collective-permute-start(bf16[512,256]{1,0:T(8,128)(2,1)S(1)} %get-tuple-element.32), channel_id=1, source_target_pairs={{0,24},{8,0},{16,8},{24,16},{1,25},{9,1},{17,9},{25,17},{2,26},{10... | collective-permute-start | bytes 786440 | tf_op jit(solution)/shard_map/ppermute | solution.py:306
  96.7 2.3 %collective-permute-start.5 = (bf16[512,256]{1,0:T(8,128)(2,1)S(1)}, bf16[512,256]{1,0:T(8,128)(2,1)S(1)}, u32[]{:S(2)}, u32[]{:S(2)}) collective-permute-start(bf16[512,256]{1,0:T(8,128)(2,1)S(1)} %get-tuple-element.24), channel_id=1, source_target_pairs={{0,24},{8,0},{16,8},{24,16},{1,25},{9,1},{17,9},{25,17},{2,26},{10... | collective-permute-start | bytes 786440 | tf_op jit(solution)/shard_map/ppermute | solution.py:306
  99.1 8.1 %collective-permute-done.23.refs_2_ = bf16[512,256]{1,0:T(8,128)(2,1)S(1)} collective-permute-done((bf16[512,256]{1,0:T(8,128)(2,1)}, bf16[512,256]{1,0:T(8,128)(2,1)S(1)}, u32[]{:S(2)}, u32[]{:S(2)}) %collective-permute-start.23) | collective-permute-done | bytes 262176 | tf_op jit(solution)/shard_map/ppermute | solution.py:306
  107.1 6.3 %shard_map.78.refs_0_ = bf16[512,256]{1,0:T(8,128)(2,1)S(1)} custom-call(s32[21]{0:T(128)S(1)} %pad_add_fusion.2.place_ref, f32[512,128]{1,0:T(8,128)S(1)} %get-tuple-element.48.cos_ref, f32[512,128]{1,0:T(8,128)S(1)} %get-tuple-element.49.sin_ref, bf16[512,256]{1,0:T(8,128)(2,1)S(1)} %get-tuple-element.29.refs_0_, ...), custom_call_target="tpu_custom_call" | custom-call | flops 1073741824 | bytes 2621524 | tf_op jit(solution)/shard_map/pallas_call | solution.py:18
  114.8 20.0 %collective-permute-start.25 = (bf16[512,256]{1,0:T(8,128)(2,1)S(1)}, bf16[512,256]{1,0:T(8,128)(2,1)S(1)}, u32[]{:S(2)}, u32[]{:S(2)}) collective-permute-start(bf16[512,256]{1,0:T(8,128)(2,1)S(1)} %shard_map.78.refs_0_), channel_id=1, source_target_pairs={{0,8},{8,16},{16,24},{1,9},{9,17},{17,25},{2,10},{10,18},{18,26},{... | collective-permute-start | bytes 786440 | tf_op jit(solution)/shard_map/ppermute | solution.py:315
  134.8 6.3 %shard_map.76.refs_0_ = bf16[512,256]{1,0:T(8,128)(2,1)S(1)} custom-call(s32[21]{0:T(128)S(1)} %pad_add_fusion.2.place_ref, f32[512,128]{1,0:T(8,128)S(1)} %get-tuple-element.48.cos_ref, f32[512,128]{1,0:T(8,128)S(1)} %get-tuple-element.49.sin_ref, bf16[512,256]{1,0:T(8,128)(2,1)S(1)} %get-tuple-element.21.refs_0_, ...), custom_call_target="tpu_custom_call" | custom-call | flops 1073741824 | bytes 2621524 | tf_op jit(solution)/shard_map/pallas_call | solution.py:18
  142.4 4.0 %collective-permute-start.16 = (bf16[512,256]{1,0:T(8,128)(2,1)S(1)}, bf16[512,256]{1,0:T(8,128)(2,1)S(1)}, u32[]{:S(2)}, u32[]{:S(2)}) collective-permute-start(bf16[512,256]{1,0:T(8,128)(2,1)S(1)} %shard_map.76.refs_0_), channel_id=1, source_target_pairs={{0,8},{8,16},{16,24},{1,9},{9,17},{17,25},{2,10},{10,18},{18,26},{... | collective-permute-start | bytes 786440 | tf_op jit(solution)/shard_map/ppermute | solution.py:315
  147.7 4.0 %collective-permute-start.26 = (bf16[512,256]{1,0:T(8,128)(2,1)S(1)}, bf16[512,256]{1,0:T(8,128)(2,1)S(1)}, u32[]{:S(2)}, u32[]{:S(2)}) collective-permute-start(bf16[512,256]{1,0:T(8,128)(2,1)S(1)} %collective-permute-done.25.refs_1_), channel_id=1, source_target_pairs={{0,8},{8,16},{16,24},{1,9},{9,17},{17,25},{2,10},{10,18},{18,26},{... | collective-permute-start | bytes 786440 | tf_op jit(solution)/shard_map/ppermute | solution.py:315
  153.1 4.0 %collective-permute-start.17 = (bf16[512,256]{1,0:T(8,128)(2,1)S(1)}, bf16[512,256]{1,0:T(8,128)(2,1)S(1)}, u32[]{:S(2)}, u32[]{:S(2)}) collective-permute-start(bf16[512,256]{1,0:T(8,128)(2,1)S(1)} %collective-permute-done.16.refs_1_), channel_id=1, source_target_pairs={{0,8},{8,16},{16,24},{1,9},{9,17},{17,25},{2,10},{10,18},{18,26},{... | collective-permute-start | bytes 786440 | tf_op jit(solution)/shard_map/ppermute | solution.py:315
  158.4 4.0 %collective-permute-start.27 = (bf16[512,256]{1,0:T(8,128)(2,1)S(1)}, bf16[512,256]{1,0:T(8,128)(2,1)S(1)}, u32[]{:S(2)}, u32[]{:S(2)}) collective-permute-start(bf16[512,256]{1,0:T(8,128)(2,1)S(1)} %collective-permute-done.26.refs_2_), channel_id=1, source_target_pairs={{0,8},{8,16},{16,24},{1,9},{9,17},{17,25},{2,10},{10,18},{18,26},{... | collective-permute-start | bytes 786440 | tf_op jit(solution)/shard_map/ppermute | solution.py:315
  163.7 4.7 %collective-permute-start.18 = (bf16[512,256]{1,0:T(8,128)(2,1)S(1)}, bf16[512,256]{1,0:T(8,128)(2,1)}, u32[]{:S(2)}, u32[]{:S(2)}) collective-permute-start(bf16[512,256]{1,0:T(8,128)(2,1)S(1)} %collective-permute-done.17.refs_2_), channel_id=1, source_target_pairs={{0,8},{8,16},{16,24},{1,9},{9,17},{17,25},{2,10},{10,18},{18,26},{... | collective-permute-start | bytes 786440 | tf_op jit(solution)/shard_map/ppermute | solution.py:315
  168.6 2.2 %copy-done = bf16[8192,256]{1,0:T(8,128)(2,1)S(1)} copy-done((bf16[8192,256]{1,0:T(8,128)(2,1)S(1)}, bf16[8192,256]{1,0:T(8,128)(2,1)}, u32[]{:S(2)}) %copy-start) | copy-done | bytes 4194328
  170.8 1.8 shard_map.79
  173.4 2.2 %shard_map.80 = (bf16[256,1024]{1,0:T(8,128)(2,1)S(1)}, bf16[256,1024]{1,0:T(8,128)(2,1)S(1)}) custom-call(s32[3]{0:T(128)S(1)} %pad_add_fusion.place_ref, bf16[512,256]{1,0:T(8,128)(2,1)S(1)} %shard_map.76.refs_0_, bf16[512,256]{1,0:T(8,128)(2,1)S(1)} %collective-permute-done.16.refs_1_, bf16[512,256]{1,0:T(8,128)(2,1)S(1)} %collective-permute-done.17.refs_2_, ...), custom_call_target="tpu_custom_call" | custom-call | flops 1073741824 | bytes 8126476 | tf_op jit(solution)/shard_map/pallas_call | solution.py:18
  175.6 4.9 %collective-permute-start.31 = (bf16[256,1024]{1,0:T(8,128)(2,1)S(1)}, bf16[256,1024]{1,0:T(8,128)(2,1)S(1)}, u32[]{:S(2)}, u32[]{:S(2)}) collective-permute-start(bf16[256,1024]{1,0:T(8,128)(2,1)S(1)} %get-tuple-element.36), channel_id=1, source_target_pairs={{0,1},{1,0},{2,3},{3,2},{4,5},{5,4},{6,7},{7,6},{8,9},{9,8},{10,11... | collective-permute-start | bytes 1572872 | tf_op jit(solution)/shard_map/ppermute | solution.py:359
  180.5 1.5 collective-permute-done.31
  182.3 5.6 %collective-permute-start.32 = (bf16[128,1024]{1,0:T(8,128)(2,1)S(1)}, bf16[128,1024]{1,0:T(8,128)(2,1)S(1)}, u32[]{:S(2)}, u32[]{:S(2)}) collective-permute-start(bf16[128,1024]{1,0:T(8,128)(2,1)S(1)} %get-tuple-element.43), channel_id=1, source_target_pairs={{0,0},{1,16},{8,8},{9,24},{16,1},{17,17},{24,9},{25,25},{2,2},{3,1... | collective-permute-start | bytes 786440 | tf_op jit(solution)/shard_map/ppermute | solution.py:366
  188.5 9.1 %collective-permute-done.32 = bf16[128,1024]{1,0:T(8,128)(2,1)S(1)} collective-permute-done((bf16[128,1024]{1,0:T(8,128)(2,1)S(1)}, bf16[128,1024]{1,0:T(8,128)(2,1)S(1)}, u32[]{:S(2)}, u32[]{:S(2)}) %collective-permute-start.32) | collective-permute-done | bytes 262176 | tf_op jit(solution)/shard_map/ppermute | solution.py:366
  (94 shorter events, 26.0 us)
Async XLA Ops:
  6.5 75.9 %all-gather.5.cloned.1.call-start = ((), (), s32[]{:S(2)}) async-start(), calls=%async_computation | async-start | bytes 5242880 | tf_op jit(solution)/shard_map/all_gather | solution.py:332
  7.3 161.3 %all-gather.7.cloned.1.call-start = ((), (), s32[]{:S(2)}) async-start(), calls=%async_computation.1 | async-start | bytes 5242880 | tf_op jit(solution)/shard_map/all_gather | solution.py:333
  8.1 13.8 %collective-permute-start.7 = (bf16[512,512]{1,0:T(8,128)(2,1)S(1)}, bf16[512,512]{1,0:T(8,128)(2,1)S(1)}, u32[]{:S(2)}, u32[]{:S(2)}) collective-permute-start(bf16[512,512]{1,0:T(8,128)(2,1)S(1)} %constant_dynamic-update-slice_fusion.refs_4_), channel_id=1, source_target_pairs={{0,4},{2,6},{4,0},{6,2},{1,5},{3,7},{5,1},{7,3},{8,12},{10,14},{12... | collective-permute-start | bytes 1572872 | tf_op jit(solution)/shard_map/ppermute | solution.py:292
  10.2 13.6 %collective-permute-start.6 = (bf16[512,512]{1,0:T(8,128)(2,1)S(1)}, bf16[512,512]{1,0:T(8,128)(2,1)S(1)}, u32[]{:S(2)}, u32[]{:S(2)}) collective-permute-start(bf16[512,512]{1,0:T(8,128)(2,1)S(1)} %constant_dynamic-update-slice_fusion.refs_4_), channel_id=1, source_target_pairs={{0,2},{2,0},{4,6},{6,4},{1,3},{3,1},{5,7},{7,5},{8,10},{10,8},{12,... | collective-permute-start | bytes 1572872 | tf_op jit(solution)/shard_map/ppermute | solution.py:292
  13.0 12.9 %collective-permute-start.2 = (bf16[128,1024]{1,0:T(8,128)(2,1)}, bf16[128,1024]{1,0:T(8,128)(2,1)S(1)}, u32[]{:S(2)}, u32[]{:S(2)}) collective-permute-start(bf16[128,1024]{1,0:T(8,128)(2,1)} %get-tuple-element.37), channel_id=1, source_target_pairs={{0,24},{8,0},{16,8},{24,16},{1,25},{9,1},{17,9},{25,17},{2,26},{10... | collective-permute-start | bytes 786440 | tf_op jit(solution)/shard_map/ppermute | solution.py:306
  16.3 21.3 %collective-permute-start.1 = (bf16[128,1024]{1,0:T(8,128)(2,1)}, bf16[128,1024]{1,0:T(8,128)(2,1)S(1)}, u32[]{:S(2)}, u32[]{:S(2)}) collective-permute-start(bf16[128,1024]{1,0:T(8,128)(2,1)} %get-tuple-element.38), channel_id=1, source_target_pairs={{0,16},{8,24},{16,0},{24,8},{1,17},{9,25},{17,1},{25,9},{2,18},{10... | collective-permute-start | bytes 786440 | tf_op jit(solution)/shard_map/ppermute | solution.py:306
  16.3 21.3 %collective-permute-start = (bf16[128,1024]{1,0:T(8,128)(2,1)S(1)}, bf16[128,1024]{1,0:T(8,128)(2,1)S(1)}, u32[]{:S(2)}, u32[]{:S(2)}) collective-permute-start(bf16[128,1024]{1,0:T(8,128)(2,1)S(1)} %get-tuple-element.39), channel_id=1, source_target_pairs={{0,8},{8,16},{16,24},{24,0},{1,9},{9,17},{17,25},{25,1},{2,10},{10... | collective-permute-start | bytes 786440 | tf_op jit(solution)/shard_map/ppermute | solution.py:306
  22.6 15.1 %collective-permute-start.8 = (bf16[256,512]{1,0:T(8,128)(2,1)}, bf16[256,512]{1,0:T(8,128)(2,1)S(1)}, u32[]{:S(2)}, u32[]{:S(2)}) collective-permute-start(bf16[256,512]{1,0:T(8,128)(2,1)} %slice.8), channel_id=1, source_target_pairs={{0,2},{2,0},{4,6},{6,4},{1,3},{3,1},{5,7},{7,5},{8,10},{10,8},{12,... | collective-permute-start | bytes 786440 | tf_op jit(solution)/shard_map/ppermute | solution.py:292
  24.6 13.1 %collective-permute-start.9 = (bf16[256,512]{1,0:T(8,128)(2,1)}, bf16[256,512]{1,0:T(8,128)(2,1)S(1)}, u32[]{:S(2)}, u32[]{:S(2)}) collective-permute-start(bf16[256,512]{1,0:T(8,128)(2,1)} %slice.9), channel_id=1, source_target_pairs={{0,4},{2,6},{4,0},{6,2},{1,5},{3,7},{5,1},{7,3},{8,12},{10,14},{12... | collective-permute-start | bytes 786440 | tf_op jit(solution)/shard_map/ppermute | solution.py:292
  42.1 19.8 %collective-permute-start.11 = (bf16[512,256]{1,0:T(8,128)(2,1)S(1)}, bf16[512,256]{1,0:T(8,128)(2,1)S(1)}, u32[]{:S(2)}, u32[]{:S(2)}) collective-permute-start(bf16[512,256]{1,0:T(8,128)(2,1)S(1)} %get-tuple-element.27), channel_id=1, source_target_pairs={{0,16},{8,24},{16,0},{24,8},{1,17},{9,25},{17,1},{25,9},{2,18},{10... | collective-permute-start | bytes 786440 | tf_op jit(solution)/shard_map/ppermute | solution.py:306
  44.2 17.7 %collective-permute-start.12 = (bf16[512,256]{1,0:T(8,128)(2,1)S(1)}, bf16[512,256]{1,0:T(8,128)(2,1)S(1)}, u32[]{:S(2)}, u32[]{:S(2)}) collective-permute-start(bf16[512,256]{1,0:T(8,128)(2,1)S(1)} %get-tuple-element.28), channel_id=1, source_target_pairs={{0,24},{8,0},{16,8},{24,16},{1,25},{9,1},{17,9},{25,17},{2,26},{10... | collective-permute-start | bytes 786440 | tf_op jit(solution)/shard_map/ppermute | solution.py:306
  62.1 29.7 %collective-permute-start.15 = (bf16[512,256]{1,0:T(8,128)(2,1)S(1)}, bf16[512,256]{1,0:T(8,128)(2,1)S(1)}, u32[]{:S(2)}, u32[]{:S(2)}) collective-permute-start(bf16[512,256]{1,0:T(8,128)(2,1)S(1)} %shard_map.75.refs_4_), channel_id=1, source_target_pairs={{0,6},{2,4},{4,2},{6,0},{1,7},{3,5},{5,3},{7,1},{8,14},{10,12},{12... | collective-permute-start | bytes 786440 | tf_op jit(solution)/shard_map/ppermute | solution.py:292
  63.1 32.1 %collective-permute-start.14 = (bf16[512,256]{1,0:T(8,128)(2,1)S(1)}, bf16[512,256]{1,0:T(8,128)(2,1)S(1)}, u32[]{:S(2)}, u32[]{:S(2)}) collective-permute-start(bf16[512,256]{1,0:T(8,128)(2,1)S(1)} %shard_map.75.refs_4_), channel_id=1, source_target_pairs={{0,4},{2,6},{4,0},{6,2},{1,5},{3,7},{5,1},{7,3},{8,12},{10,14},{12... | collective-permute-start | bytes 786440 | tf_op jit(solution)/shard_map/ppermute | solution.py:292
  64.4 31.1 %collective-permute-start.13 = (bf16[512,256]{1,0:T(8,128)(2,1)S(1)}, bf16[512,256]{1,0:T(8,128)(2,1)S(1)}, u32[]{:S(2)}, u32[]{:S(2)}) collective-permute-start(bf16[512,256]{1,0:T(8,128)(2,1)S(1)} %shard_map.75.refs_4_), channel_id=1, source_target_pairs={{0,2},{2,0},{4,6},{6,4},{1,3},{3,1},{5,7},{7,5},{8,10},{10,8},{12,... | collective-permute-start | bytes 786440 | tf_op jit(solution)/shard_map/ppermute | solution.py:292
  87.4 19.7 %collective-permute-start.23 = (bf16[512,256]{1,0:T(8,128)(2,1)}, bf16[512,256]{1,0:T(8,128)(2,1)S(1)}, u32[]{:S(2)}, u32[]{:S(2)}) collective-permute-start(bf16[512,256]{1,0:T(8,128)(2,1)} %copy-done.4), channel_id=1, source_target_pairs={{0,16},{8,24},{16,0},{24,8},{1,17},{9,25},{17,1},{25,9},{2,18},{10... | collective-permute-start | bytes 786440 | tf_op jit(solution)/shard_map/ppermute | solution.py:306
  91.8 15.3 %collective-permute-start.24 = (bf16[512,256]{1,0:T(8,128)(2,1)S(1)}, bf16[512,256]{1,0:T(8,128)(2,1)S(1)}, u32[]{:S(2)}, u32[]{:S(2)}) collective-permute-start(bf16[512,256]{1,0:T(8,128)(2,1)S(1)} %get-tuple-element.32), channel_id=1, source_target_pairs={{0,24},{8,0},{16,8},{24,16},{1,25},{9,1},{17,9},{25,17},{2,26},{10... | collective-permute-start | bytes 786440 | tf_op jit(solution)/shard_map/ppermute | solution.py:306
  95.1 39.6 %collective-permute-start.3 = (bf16[512,256]{1,0:T(8,128)(2,1)S(1)}, bf16[512,256]{1,0:T(8,128)(2,1)S(1)}, u32[]{:S(2)}, u32[]{:S(2)}) collective-permute-start(bf16[512,256]{1,0:T(8,128)(2,1)S(1)} %get-tuple-element.22), channel_id=1, source_target_pairs={{0,8},{8,16},{16,24},{24,0},{1,9},{9,17},{17,25},{25,1},{2,10},{10... | collective-permute-start | bytes 786440 | tf_op jit(solution)/shard_map/ppermute | solution.py:306
  95.5 39.3 %collective-permute-start.4 = (bf16[512,256]{1,0:T(8,128)(2,1)S(1)}, bf16[512,256]{1,0:T(8,128)(2,1)S(1)}, u32[]{:S(2)}, u32[]{:S(2)}) collective-permute-start(bf16[512,256]{1,0:T(8,128)(2,1)S(1)} %get-tuple-element.23), channel_id=1, source_target_pairs={{0,16},{8,24},{16,0},{24,8},{1,17},{9,25},{17,1},{25,9},{2,18},{10... | collective-permute-start | bytes 786440 | tf_op jit(solution)/shard_map/ppermute | solution.py:306
  96.7 38.1 %collective-permute-start.5 = (bf16[512,256]{1,0:T(8,128)(2,1)S(1)}, bf16[512,256]{1,0:T(8,128)(2,1)S(1)}, u32[]{:S(2)}, u32[]{:S(2)}) collective-permute-start(bf16[512,256]{1,0:T(8,128)(2,1)S(1)} %get-tuple-element.24), channel_id=1, source_target_pairs={{0,24},{8,0},{16,8},{24,16},{1,25},{9,1},{17,9},{25,17},{2,26},{10... | collective-permute-start | bytes 786440 | tf_op jit(solution)/shard_map/ppermute | solution.py:306
  113.5 32.9 %collective-permute-start.28 = (bf16[512,256]{1,0:T(8,128)(2,1)S(1)}, bf16[512,256]{1,0:T(8,128)(2,1)S(1)}, u32[]{:S(2)}, u32[]{:S(2)}) collective-permute-start(bf16[512,256]{1,0:T(8,128)(2,1)S(1)} %shard_map.78.refs_0_), channel_id=1, source_target_pairs={{8,0},{16,8},{24,16},{9,1},{17,9},{25,17},{10,2},{18,10},{26,18},{... | collective-permute-start | bytes 786440 | tf_op jit(solution)/shard_map/ppermute | solution.py:315
  114.8 33.0 %collective-permute-start.25 = (bf16[512,256]{1,0:T(8,128)(2,1)S(1)}, bf16[512,256]{1,0:T(8,128)(2,1)S(1)}, u32[]{:S(2)}, u32[]{:S(2)}) collective-permute-start(bf16[512,256]{1,0:T(8,128)(2,1)S(1)} %shard_map.78.refs_0_), channel_id=1, source_target_pairs={{0,8},{8,16},{16,24},{1,9},{9,17},{17,25},{2,10},{10,18},{18,26},{... | collective-permute-start | bytes 786440 | tf_op jit(solution)/shard_map/ppermute | solution.py:315
  141.1 10.6 %collective-permute-start.19 = (bf16[512,256]{1,0:T(8,128)(2,1)S(1)}, bf16[512,256]{1,0:T(8,128)(2,1)S(1)}, u32[]{:S(2)}, u32[]{:S(2)}) collective-permute-start(bf16[512,256]{1,0:T(8,128)(2,1)S(1)} %shard_map.76.refs_0_), channel_id=1, source_target_pairs={{8,0},{16,8},{24,16},{9,1},{17,9},{25,17},{10,2},{18,10},{26,18},{... | collective-permute-start | bytes 786440 | tf_op jit(solution)/shard_map/ppermute | solution.py:315
  142.4 10.7 %collective-permute-start.16 = (bf16[512,256]{1,0:T(8,128)(2,1)S(1)}, bf16[512,256]{1,0:T(8,128)(2,1)S(1)}, u32[]{:S(2)}, u32[]{:S(2)}) collective-permute-start(bf16[512,256]{1,0:T(8,128)(2,1)S(1)} %shard_map.76.refs_0_), channel_id=1, source_target_pairs={{0,8},{8,16},{16,24},{1,9},{9,17},{17,25},{2,10},{10,18},{18,26},{... | collective-permute-start | bytes 786440 | tf_op jit(solution)/shard_map/ppermute | solution.py:315
  146.4 10.7 %collective-permute-start.29 = (bf16[512,256]{1,0:T(8,128)(2,1)S(1)}, bf16[512,256]{1,0:T(8,128)(2,1)S(1)}, u32[]{:S(2)}, u32[]{:S(2)}) collective-permute-start(bf16[512,256]{1,0:T(8,128)(2,1)S(1)} %collective-permute-done.28.refs_4_), channel_id=1, source_target_pairs={{8,0},{16,8},{24,16},{9,1},{17,9},{25,17},{10,2},{18,10},{26,18},{... | collective-permute-start | bytes 786440 | tf_op jit(solution)/shard_map/ppermute | solution.py:315
  147.7 10.7 %collective-permute-start.26 = (bf16[512,256]{1,0:T(8,128)(2,1)S(1)}, bf16[512,256]{1,0:T(8,128)(2,1)S(1)}, u32[]{:S(2)}, u32[]{:S(2)}) collective-permute-start(bf16[512,256]{1,0:T(8,128)(2,1)S(1)} %collective-permute-done.25.refs_1_), channel_id=1, source_target_pairs={{0,8},{8,16},{16,24},{1,9},{9,17},{17,25},{2,10},{10,18},{18,26},{... | collective-permute-start | bytes 786440 | tf_op jit(solution)/shard_map/ppermute | solution.py:315
  151.7 10.7 %collective-permute-start.20 = (bf16[512,256]{1,0:T(8,128)(2,1)S(1)}, bf16[512,256]{1,0:T(8,128)(2,1)S(1)}, u32[]{:S(2)}, u32[]{:S(2)}) collective-permute-start(bf16[512,256]{1,0:T(8,128)(2,1)S(1)} %collective-permute-done.19.refs_4_), channel_id=1, source_target_pairs={{8,0},{16,8},{24,16},{9,1},{17,9},{25,17},{10,2},{18,10},{26,18},{... | collective-permute-start | bytes 786440 | tf_op jit(solution)/shard_map/ppermute | solution.py:315
  153.1 10.7 %collective-permute-start.17 = (bf16[512,256]{1,0:T(8,128)(2,1)S(1)}, bf16[512,256]{1,0:T(8,128)(2,1)S(1)}, u32[]{:S(2)}, u32[]{:S(2)}) collective-permute-start(bf16[512,256]{1,0:T(8,128)(2,1)S(1)} %collective-permute-done.16.refs_1_), channel_id=1, source_target_pairs={{0,8},{8,16},{16,24},{1,9},{9,17},{17,25},{2,10},{10,18},{18,26},{... | collective-permute-start | bytes 786440 | tf_op jit(solution)/shard_map/ppermute | solution.py:315
  157.1 11.5 %collective-permute-start.30 = (bf16[512,256]{1,0:T(8,128)(2,1)S(1)}, bf16[512,256]{1,0:T(8,128)(2,1)S(1)}, u32[]{:S(2)}, u32[]{:S(2)}) collective-permute-start(bf16[512,256]{1,0:T(8,128)(2,1)S(1)} %collective-permute-done.29.refs_5_), channel_id=1, source_target_pairs={{8,0},{16,8},{24,16},{9,1},{17,9},{25,17},{10,2},{18,10},{26,18},{... | collective-permute-start | bytes 786440 | tf_op jit(solution)/shard_map/ppermute | solution.py:315
  158.4 10.2 %collective-permute-start.27 = (bf16[512,256]{1,0:T(8,128)(2,1)S(1)}, bf16[512,256]{1,0:T(8,128)(2,1)S(1)}, u32[]{:S(2)}, u32[]{:S(2)}) collective-permute-start(bf16[512,256]{1,0:T(8,128)(2,1)S(1)} %collective-permute-done.26.refs_2_), channel_id=1, source_target_pairs={{0,8},{8,16},{16,24},{1,9},{9,17},{17,25},{2,10},{10,18},{18,26},{... | collective-permute-start | bytes 786440 | tf_op jit(solution)/shard_map/ppermute | solution.py:315
  162.4 10.2 %collective-permute-start.21 = (bf16[512,256]{1,0:T(8,128)(2,1)S(1)}, bf16[512,256]{1,0:T(8,128)(2,1)S(1)}, u32[]{:S(2)}, u32[]{:S(2)}) collective-permute-start(bf16[512,256]{1,0:T(8,128)(2,1)S(1)} %collective-permute-done.20.refs_5_), channel_id=1, source_target_pairs={{8,0},{16,8},{24,16},{9,1},{17,9},{25,17},{10,2},{18,10},{26,18},{... | collective-permute-start | bytes 786440 | tf_op jit(solution)/shard_map/ppermute | solution.py:315
  163.7 9.7 %collective-permute-start.18 = (bf16[512,256]{1,0:T(8,128)(2,1)S(1)}, bf16[512,256]{1,0:T(8,128)(2,1)}, u32[]{:S(2)}, u32[]{:S(2)}) collective-permute-start(bf16[512,256]{1,0:T(8,128)(2,1)S(1)} %collective-permute-done.17.refs_2_), channel_id=1, source_target_pairs={{0,8},{8,16},{16,24},{1,9},{9,17},{17,25},{2,10},{10,18},{18,26},{... | collective-permute-start | bytes 786440 | tf_op jit(solution)/shard_map/ppermute | solution.py:315
  182.3 15.2 %collective-permute-start.32 = (bf16[128,1024]{1,0:T(8,128)(2,1)S(1)}, bf16[128,1024]{1,0:T(8,128)(2,1)S(1)}, u32[]{:S(2)}, u32[]{:S(2)}) collective-permute-start(bf16[128,1024]{1,0:T(8,128)(2,1)S(1)} %get-tuple-element.43), channel_id=1, source_target_pairs={{0,0},{1,16},{8,8},{9,24},{16,1},{17,17},{24,9},{25,25},{2,2},{3,1... | collective-permute-start | bytes 786440 | tf_op jit(solution)/shard_map/ppermute | solution.py:366
  (15 other events, 69.1 us)
Sparse Core Ops, SparseCore 0:
  9.2 73.1 all-gather.4
  84.2 50.2 all-gather.6

commit v6 on v4

--- a/solution.py
+++ b/solution.py
@@ -37,10 +37,10 @@
     )
 
 
-def summed_lanes(parts_ref, lanes):
-    total = parts_ref[0, :, lanes].astype(jnp.float32)
-    for part in range(1, parts_ref.shape[0]):
-        total = total + parts_ref[part, :, lanes].astype(jnp.float32)
+def summed_lanes(refs, lanes):
+    total = refs[0][:, lanes].astype(jnp.float32)
+    for ref in refs[1:]:
+        total = total + ref[:, lanes].astype(jnp.float32)
     return total
 
 
@@ -48,24 +48,26 @@
     return values * cos_ref[...] + pltpu.roll(values, HALF, 1) * sin_ref[...]
 
 
-def pair_kernel(unused_ref, cos_ref, sin_ref, parts, out_ref):
+def pair_kernel(unused_ref, cos_ref, sin_ref, *refs):
+    parts, out_ref = refs[:-1], refs[-1]
     key = rotated(summed_lanes(parts, pl.ds(0, HD)), cos_ref, sin_ref)
     out_ref[:, pl.ds(0, HD)] = key.astype(jnp.bfloat16)
     out_ref[:, pl.ds(HD, HD)] = summed_lanes(parts, pl.ds(HD, HD)).astype(jnp.bfloat16)
 
 
 def finish_pair(cosine, sine, parts):
-    operands = (jnp.zeros((1,), jnp.int32), cosine, sine, parts)
-    shape = jax.ShapeDtypeStruct(parts.shape[1:], jnp.bfloat16)
-    return local_kernel(pair_kernel, shape, operands, 8 * parts.size)
-
-
-def attention_kernel(blocks, stride, n_kv, place_ref, cos_ref, sin_ref, query_ref, *refs):
-    kv_refs = refs[:n_kv]
-    out_ref, turned, bias = refs[n_kv:]
+    operands = (jnp.zeros((1,), jnp.int32), cosine, sine, *parts)
+    shape = jax.ShapeDtypeStruct(parts[0].shape, jnp.bfloat16)
+    return local_kernel(pair_kernel, shape, operands, 8 * parts[0].size)
+
+
+def attention_kernel(blocks, stride, n_query, n_kv, place_ref, cos_ref, sin_ref, *refs):
+    query_refs = refs[:n_query]
+    kv_refs = refs[n_query : n_query + n_kv]
+    out_ref, turned, bias = refs[n_query + n_kv :]
     heads, tokens, _ = turned.shape
     for h in range(heads):
-        total = summed_lanes(query_ref, pl.ds(h * HD, HD))
+        total = summed_lanes(query_refs, pl.ds(h * HD, HD))
         turned[h] = rotated(total, cos_ref, sin_ref).astype(jnp.bfloat16)
     rows = tokens // blocks
     kv_rows = kv_refs[0].shape[0] // blocks
@@ -124,13 +126,13 @@
 
 
 def attention(place, cosine, sine, query_parts, kv_parts, blocks, stride):
-    _, tokens, width = query_parts.shape
+    tokens, width = query_parts[0].shape
     heads = width // HD
     keys = sum(part.shape[0] for part in kv_parts)
     return local_kernel(
-        functools.partial(attention_kernel, blocks, stride, len(kv_parts)),
+        functools.partial(attention_kernel, blocks, stride, len(query_parts), len(kv_parts)),
         jax.ShapeDtypeStruct((tokens, width), jnp.bfloat16),
-        (place, cosine, sine, query_parts, *kv_parts),
+        (place, cosine, sine, *query_parts, *kv_parts),
         4 * tokens * width * keys,
         [
             pltpu.VMEM((heads, tokens, HD), jnp.bfloat16),
@@ -140,38 +142,43 @@
     )
 
 
-def product_kernel(groups, place_ref, token_ref, *refs):
-    weight_refs = refs[:5]
-    out_ref = refs[-1]
+def product_kernel(place_ref, *refs):
+    token_refs, weight_refs, out_refs, gathered = refs[:4], refs[4:9], refs[9:11], refs[11]
+    hi = place_ref[0]
     lo = place_ref[1]
-    share = weight_refs[0].shape[0] // groups
-    width = weight_refs[0].shape[1] // 4
-    for d in range(4):
-        columns = pl.ds(d * width, width)
-        for g in range(groups):
-            total = 0.0
+    rows = token_refs[0].shape[0]
+    share = weight_refs[3].shape[0]
+    for d, token_ref in enumerate(token_refs):
+        gathered[pl.ds(pl.multiple_of((hi ^ d) * rows, rows), rows), :] = token_ref[...]
+    for side, out_ref in enumerate(out_refs):
+        width = out_ref.shape[1]
+        columns = pl.ds(pl.multiple_of((lax.div(hi, 2) ^ side) * width, width), width)
+        total = 0.0
+        for part in range(2):
             for r in range(4):
-                features = pl.ds(pl.multiple_of((lo ^ r) * share, share), share)
                 if r < 3:
-                    weight = weight_refs[r][pl.ds(g * share, share), columns]
-                elif groups == 2:
-                    weight = weight_refs[3 + g][:, columns]
+                    weight = weight_refs[r][pl.ds(part * share, share), columns]
                 else:
-                    weight = jnp.concatenate([ref[:, columns] for ref in weight_refs[3:]], axis=0)
+                    weight = weight_refs[3 + part][:, columns]
+                block = (lax.rem(hi, 2) ^ part) * 4 + (lo ^ r)
                 total = total + jnp.dot(
-                    token_ref[:, features], weight, preferred_element_type=jnp.float32
+                    gathered[:, pl.ds(pl.multiple_of(block * share, share), share)],
+                    weight,
+                    preferred_element_type=jnp.float32,
                 )
-            out_ref[d, :, pl.ds(g * width, width)] = total.astype(jnp.bfloat16)
-
-
-def product(place, line_tokens, weights, groups):
-    count, depth = line_tokens.shape
-    width = groups * weights[0].shape[1] // 4
+        out_ref[...] = total.astype(jnp.bfloat16)
+
+
+def product(place, token_parts, weights):
+    rows, depth = token_parts[0].shape
+    width = weights[0].shape[1] // 2
+    shape = jax.ShapeDtypeStruct((4 * rows, width), jnp.bfloat16)
     return local_kernel(
-        functools.partial(product_kernel, groups),
-        jax.ShapeDtypeStruct((4, count, width), jnp.bfloat16),
-        (place, line_tokens, *weights),
-        2 * count * depth * 4 * width,
+        product_kernel,
+        (shape,) * 2,
+        (place, *token_parts, *weights),
+        2 * 4 * rows * depth * 2 * width,
+        [pltpu.VMEM((4 * rows, depth), jnp.bfloat16)],
     )
 
 
@@ -242,9 +249,9 @@
     for h in range(kv_local):
         lanes = slice(h * HD, (h + 1) * HD)
         pair = jnp.concatenate([key[:, lanes], value[:, lanes]], axis=1)
-        pair = lax.all_gather(finish_pair(cosine, sine, pair[None]), "ctx", axis=0, tiled=True)
+        pair = lax.all_gather(finish_pair(cosine, sine, [pair]), "ctx", axis=0, tiled=True)
         part = query[:, h * group : (h + 1) * group]
-        mixed.append(attention(place, cosine, sine, part[None], [pair], 1, 0))
+        mixed.append(attention(place, cosine, sine, [part], [pair], 1, 0))
     attended = jnp.concatenate(mixed, axis=1)
     wide = lax.all_gather(w_out, "ctx", axis=1, tiled=True)
     partial_out = jnp.dot(attended, wide, preferred_element_type=jnp.float32)
@@ -270,8 +277,8 @@
     return [*blocks, beside(blocks[2][:half], 1), beside(blocks[1][half:], 2)]
 
 
-def along_line(pieces):
-    return lax.all_to_all(pieces, "hi", 0, 0, tiled=True)
+def along(block, d):
+    return lax.ppermute(block, "hi", [(i, i ^ d) for i in range(4)])
 
 
 def round_line(block):
@@ -285,43 +292,65 @@
     hi = lax.axis_index("hi")
     lo = lax.axis_index("lo")
     core = lax.axis_index("head")
-    depth = features // 4
+    which_half = lax.div(hi, 2)
+    which = lax.rem(hi, 2)
+    depth = features // 2
     heads = w_query.shape[1] // 4
-    half = heads // 2
-    place = jnp.stack([hi, lo, core])
-
-    stage = sides(jnp.concatenate([w_key, w_value], axis=0))
-    pair_blocks = corner(stage)
-    query_blocks = []
-    for c in range(2):
-        columns = [
-            w_query[:, z * heads + c * half : z * heads + (c + 1) * half] for z in range(4)
-        ]
-        stage = sides(after(jnp.concatenate(columns, axis=1), *stage[1:]))
-        query_blocks.append(corner(stage))
+    width = heads // 2
+    place = jnp.stack([hi, lo])
+
+    def columns_for(chip, sources, width):
+        return jnp.concatenate(
+            [
+                lax.dynamic_slice_in_dim(w, (2 * z + chip) * step + first, width, 1)
+                for z in range(2)
+                for w, step, first in sources
+            ],
+            axis=1,
+        )
+
+    stage = ()
+    weights = []
+    for sources, size in (
+        ([(w_key, HD, 0), (w_value, HD, 0)], HD),
+        ([(w_query, heads, 0)], width),
+        ([(w_query, heads, width)], width),
+    ):
+        came = along(columns_for(1 - which, sources, size), 1)
+        both = jnp.concatenate([columns_for(which, sources, size), came], axis=0)
+        stage = sides(after(both, *stage) if stage else both)
+        weights.append(corner(stage))
+        stage = stage[1:]
 
     normed = normalised(tokens, norm_gain)
-    pieces = jnp.stack([normed[:, d * depth : (d + 1) * depth] for d in range(4)])
-    line_tokens = along_line(pieces).reshape(4 * rows, depth)
+    own = lax.dynamic_slice_in_dim(normed, which_half * depth, depth, 1)
+    other = along(lax.dynamic_slice_in_dim(normed, (1 - which_half) * depth, depth, 1), 2)
+    token_parts = [own, along(own, 1), other, along(other, 1)]
 
     row_index = jnp.arange(4 * rows, dtype=jnp.int32)
     cosine, sine = rotary_tables((row_index // rows * 4 + lo) * rows + row_index % rows)
-    kv_own = finish_pair(
-        cosine, sine, along_line(product(place, line_tokens, pair_blocks, 2))
-    )
+
+    def summed_parts(weight):
+        kept, sent = product(place, token_parts, weight)
+        return [kept, along(sent, 2)]
+
+    kv_own = finish_pair(cosine, sine, summed_parts(weights[0]))
     kv_parts = [kv_own] + [beside(kv_own, r) for r in range(1, 4)]
-    out_blocks = corner(sides(after(w_out, *query_blocks[1][3:], *kv_parts[1:])))
-    out_blocks[3:] = [jnp.concatenate(out_blocks[3:], axis=0)]
 
     firsts = jnp.stack([lo, lo, lo ^ 1, lo ^ 2, lo ^ 3]) * rows
     seen = jnp.concatenate([firsts, doc_starts])
+    out_sides = sides(after(w_out, *weights[2][3:], *kv_parts[1:]))
+    attended = [
+        attention(seen, cosine, sine, summed_parts(weight), kv_parts, 4, 4 * rows)
+        for weight in weights[1:]
+    ]
+    out_sides[1:] = lax.optimization_barrier((*out_sides[1:], attended[0]))[:2]
+    out_blocks = corner(out_sides)
+    out_blocks[3:] = [jnp.concatenate(out_blocks[3:], axis=0)]
     totals = ()
-    kinds = (jnp.float32, jnp.bfloat16)
-    for c in range(2):
-        query_parts = along_line(product(place, line_tokens, query_blocks[c], 1))
-        attended = attention(seen, cosine, sine, query_parts, kv_parts, 4, 4 * rows)
-        where = jnp.concatenate([place, jnp.full((1,), c * half, jnp.int32)])
-        totals = project(where, round_line(attended), out_blocks, totals, kinds[c])
+    for c, kind in enumerate((jnp.float32, jnp.bfloat16)):
+        where = jnp.stack([hi, lo, core, jnp.full((), c * width, jnp.int32)])
+        totals = project(where, round_line(attended[c]), out_blocks, totals, kind)
 
     mine, theirs = totals
     theirs = lax.ppermute(theirs, "head", [(0, 1), (1, 0)])

time: 209 us -> 234 us (1.12)
  waiting for transfers between devices: 100 us -> 132 us
  Pallas kernels: 30.5 us -> 26 us
  starting transfers between devices: 55.7 us -> 53.1 us
    ppermute x0 -> x9, waiting for transfers between devices: none -> 54.3 us  [along(): return lax.ppermute(block, 'hi', [(i, i ^ d) for i in range(4)])]
    all_to_all x4 -> x0, starting transfers between devices: 17.7 us -> none  [along_line(): return lax.all_to_all(pieces, 'hi', 0, 0, tiled=True)]
    ppermute x0 -> x9, starting transfers between devices: none -> 11.7 us  [along(): return lax.ppermute(block, 'hi', [(i, i ^ d) for i in range(4)])]
    ppermute x6, starting transfers between devices: 6.18 us -> 17.7 us  [round_line(): lax.ppermute(block, 'hi', [(i, (i + d) % 4) for i in range(4)])]
    ppermute x19, waiting for transfers between devices: 54.6 us -> 43.8 us  [beside(): return lax.ppermute(block, 'lo', [(i, i ^ r) for i in range(4)])]
    all_to_all x4 -> x0, waiting for transfers between devices: 10.1 us -> none  [along_line(): return lax.all_to_all(pieces, 'hi', 0, 0, tiled=True)]
    pallas_call x8, Pallas kernels: 30.5 us -> 26 us  [local_kernel(): pl.pallas_call(body, in_specs=[pl.BlockSpec(memory_space=pltpu.SMEM)] + [...]
    ppermute x1, starting transfers between devices: 4.53 us -> 0.96 us  [line_device(): theirs = lax.ppermute(theirs, 'head', [(0, 1), (1, 0)])]
  transfers between devices with their start and end apart: 32 -> 37, of which waited for: 16 -> 23; matrix products, arithmetic and copies ran while one was open for 3% -> 5% of each run, Pallas kernels for 12% -> 10%
where the time goes in v6:
time: 234 us; the launch traced here: 232 us
  waiting for transfers between devices  132 us (56%)
  starting transfers between devices  53.1 us (23%)
  Pallas kernels  26 us (11%)
  local copies, waits for them, and re-layouts  13.9 us (6%)
  other arithmetic  6.68 us (3%)
    ppermute x9, waiting for transfers between devices, along(): return lax.ppermute(block, 'hi', [(i, i ^ d) for i in range(4)])  54.3 us
    ppermute x19, waiting for transfers between devices, beside(): return lax.ppermute(block, 'lo', [(i, i ^ r) for i in range(4)])  43.8 us
    pallas_call x8, Pallas kernels, local_kernel(): pl.pallas_call(body, in_specs=[pl.BlockSpec(memory_space=pltpu.SMEM)] + [...  26 us
    ppermute x6, waiting for transfers between devices, round_line(): lax.ppermute(block, 'hi', [(i, (i + d) % 4) for i in range(4)])  21.6 us
    ppermute x19, starting transfers between devices, beside(): return lax.ppermute(block, 'lo', [(i, i ^ r) for i in range(4)])  20.4 us
    ppermute x6, starting transfers between devices, round_line(): lax.ppermute(block, 'hi', [(i, (i + d) % 4) for i in range(4)])  17.7 us
    ppermute x9, starting transfers between devices, along(): return lax.ppermute(block, 'hi', [(i, i ^ d) for i in range(4)])  11.7 us
    ppermute x2, waiting for transfers between devices, line_device(): arrived.append(lax.ppermute(piece, ('hi', 'head'), route))  10.7 us
  transfers between devices with their start and end apart: 37, of which 23 were waited for; matrix products, arithmetic and copies ran while one was open for 5% of the time, Pallas kernels for 10%

profile of v6, /device:TPU:1, one launch (start us, length us, event | category | flops | bytes accessed | tf_op | source)
XLA Modules:
  0.0 232.4 jit_solution(11122851786744110606)
XLA Ops:
  1.2 2.2 collective-permute-start.5
  5.5 4.0 %collective-permute-done.5 = bf16[256,512]{1,0:T(8,128)(2,1)S(1)} collective-permute-done((bf16[256,512]{1,0:T(8,128)(2,1)S(1)}, bf16[256,512]{1,0:T(8,128)(2,1)S(1)}, u32[]{:S(2)}, u32[]{:S(2)}) %collective-permute-start.5) | collective-permute-done | bytes 262176 | tf_op jit(solution)/shard_map/ppermute | solution.py:281
  12.4 2.4 %collective-permute-start.1 = (bf16[128,2048]{1,0:T(8,128)(2,1)S(1)}, bf16[128,2048]{1,0:T(8,128)(2,1)S(1)}, u32[]{:S(2)}, u32[]{:S(2)}) collective-permute-start(bf16[128,2048]{1,0:T(8,128)(2,1)S(1)} %get-tuple-element.45), channel_id=1, source_target_pairs={{0,16},{8,24},{16,0},{24,8},{1,17},{9,25},{17,1},{25,9},{2,18},{10... | collective-permute-start | bytes 1572872 | tf_op jit(solution)/shard_map/ppermute | solution.py:281
  16.2 4.9 %collective-permute-done.7.refs_6_ = bf16[512,512]{1,0:T(8,128)(2,1)S(1)} collective-permute-done((bf16[512,512]{1,0:T(8,128)(2,1)S(1)}, bf16[512,512]{1,0:T(8,128)(2,1)S(1)}, u32[]{:S(2)}, u32[]{:S(2)}) %collective-permute-start.7) | collective-permute-done | bytes 524320 | tf_op jit(solution)/shard_map/ppermute | solution.py:268
  24.9 11.5 %collective-permute-done.1.refs_2_ = bf16[128,2048]{1,0:T(8,128)(2,1)S(1)} collective-permute-done((bf16[128,2048]{1,0:T(8,128)(2,1)S(1)}, bf16[128,2048]{1,0:T(8,128)(2,1)S(1)}, u32[]{:S(2)}, u32[]{:S(2)}) %collective-permute-start.1) | collective-permute-done | bytes 524320 | tf_op jit(solution)/shard_map/ppermute | solution.py:281
  36.4 2.5 %collective-permute-start.2 = (bf16[128,2048]{1,0:T(8,128)(2,1)S(1)}, bf16[128,2048]{1,0:T(8,128)(2,1)S(1)}, u32[]{:S(2)}, u32[]{:S(2)}) collective-permute-start(bf16[128,2048]{1,0:T(8,128)(2,1)S(1)} %collective-permute-done.1.refs_2_), channel_id=1, source_target_pairs={{0,8},{8,0},{16,24},{24,16},{1,9},{9,1},{17,25},{25,17},{2,10},{10... | collective-permute-start | bytes 1572872 | tf_op jit(solution)/shard_map/ppermute | solution.py:281
  40.9 6.9 %collective-permute-done.3 = bf16[256,512]{1,0:T(8,128)(2,1)} collective-permute-done((bf16[256,512]{1,0:T(8,128)(2,1)}, bf16[256,512]{1,0:T(8,128)(2,1)}, u32[]{:S(2)}, u32[]{:S(2)}) %collective-permute-start.3) | collective-permute-done | bytes 262176 | tf_op jit(solution)/shard_map/ppermute | solution.py:281
  53.5 5.5 %collective-permute-done.2.refs_3_ = bf16[128,2048]{1,0:T(8,128)(2,1)S(1)} collective-permute-done((bf16[128,2048]{1,0:T(8,128)(2,1)S(1)}, bf16[128,2048]{1,0:T(8,128)(2,1)S(1)}, u32[]{:S(2)}, u32[]{:S(2)}) %collective-permute-start.2) | collective-permute-done | bytes 524320 | tf_op jit(solution)/shard_map/ppermute | solution.py:281
  59.0 2.6 %shard_map.74 = (bf16[512,256]{1,0:T(8,128)(2,1)S(1)}, bf16[512,256]{1,0:T(8,128)(2,1)S(1)}) custom-call(s32[2]{0:T(128)S(1)} %pad_add_fusion.3.place_ref, bf16[128,2048]{1,0:T(8,128)(2,1)S(1)} %get-tuple-element.46.refs_0_, bf16[128,2048]{1,0:T(8,128)(2,1)S(1)} %collective-permute-done.refs_1_, bf16[128,2048]{1,0:T(8,128)(2,1)S(1)} %collective-permute-done.1.refs_2_, ...), custom_call_target="tpu_custom_call" | custom-call | flops 1073741824 | bytes 4194312 | tf_op jit(solution)/shard_map/pallas_call | solution.py:18
  61.7 3.5 %collective-permute-start.17 = (bf16[512,256]{1,0:T(8,128)(2,1)S(1)}, bf16[512,256]{1,0:T(8,128)(2,1)S(1)}, u32[]{:S(2)}, u32[]{:S(2)}) collective-permute-start(bf16[512,256]{1,0:T(8,128)(2,1)S(1)} %get-tuple-element.25), channel_id=1, source_target_pairs={{0,16},{8,24},{16,0},{24,8},{1,17},{9,25},{17,1},{25,9},{2,18},{10... | collective-permute-start | bytes 786440 | tf_op jit(solution)/shard_map/ppermute | solution.py:281
  66.4 9.2 %collective-permute-done.17.refs_1_ = bf16[512,256]{1,0:T(8,128)(2,1)S(1)} collective-permute-done((bf16[512,256]{1,0:T(8,128)(2,1)S(1)}, bf16[512,256]{1,0:T(8,128)(2,1)S(1)}, u32[]{:S(2)}, u32[]{:S(2)}) %collective-permute-start.17) | collective-permute-done | bytes 262176 | tf_op jit(solution)/shard_map/ppermute | solution.py:281
  76.1 2.4 %collective-permute-start.18 = (bf16[512,256]{1,0:T(8,128)(2,1)S(1)}, bf16[512,256]{1,0:T(8,128)(2,1)S(1)}, u32[]{:S(2)}, u32[]{:S(2)}) collective-permute-start(bf16[512,256]{1,0:T(8,128)(2,1)S(1)} %shard_map.75.refs_2_), channel_id=1, source_target_pairs={{0,2},{2,0},{4,6},{6,4},{1,3},{3,1},{5,7},{7,5},{8,10},{10,8},{12,... | collective-permute-start | bytes 786440 | tf_op jit(solution)/shard_map/ppermute | solution.py:268
  79.0 3.0 %collective-permute-done.20.refs_5_ = bf16[512,256]{1,0:T(8,128)(2,1)S(1)} collective-permute-done((bf16[512,256]{1,0:T(8,128)(2,1)S(1)}, bf16[512,256]{1,0:T(8,128)(2,1)S(1)}, u32[]{:S(2)}, u32[]{:S(2)}) %collective-permute-start.20) | collective-permute-done | bytes 262176 | tf_op jit(solution)/shard_map/ppermute | solution.py:268
  82.8 6.1 %collective-permute-done.19.refs_4_ = bf16[512,256]{1,0:T(8,128)(2,1)S(1)} collective-permute-done((bf16[512,256]{1,0:T(8,128)(2,1)S(1)}, bf16[512,256]{1,0:T(8,128)(2,1)S(1)}, u32[]{:S(2)}, u32[]{:S(2)}) %collective-permute-start.19) | collective-permute-done | bytes 262176 | tf_op jit(solution)/shard_map/ppermute | solution.py:268
  90.3 2.1 collective-permute-done.12.refs_7_
  92.3 2.1 collective-permute-done.13.refs_8_
  99.9 22.5 %collective-permute-done.26.refs_7_ = bf16[256,512]{1,0:T(8,128)(2,1)} collective-permute-done((bf16[256,512]{1,0:T(8,128)(2,1)}, bf16[256,512]{1,0:T(8,128)(2,1)}, u32[]{:S(2)}, u32[]{:S(2)}) %collective-permute-start.26) | collective-permute-done | bytes 262176 | tf_op jit(solution)/shard_map/ppermute | solution.py:268
  127.9 2.7 %shard_map.77 = (bf16[512,256]{1,0:T(8,128)(2,1)S(1)}, bf16[512,256]{1,0:T(8,128)(2,1)S(1)}) custom-call(s32[2]{0:T(128)S(1)} %pad_add_fusion.3.place_ref, bf16[128,2048]{1,0:T(8,128)(2,1)S(1)} %get-tuple-element.46.refs_0_, bf16[128,2048]{1,0:T(8,128)(2,1)S(1)} %copy-done.1, bf16[128,2048]{1,0:T(8,128)(2,1)S(1)} %collective-permute-done.1.refs_2_, ...), custom_call_target="tpu_custom_call" | custom-call | flops 1073741824 | bytes 4194312 | tf_op jit(solution)/shard_map/pallas_call | solution.py:18
  130.7 6.0 %collective-permute-done.28.refs_1_ = bf16[512,256]{1,0:T(8,128)(2,1)S(1)} collective-permute-done((bf16[512,256]{1,0:T(8,128)(2,1)S(1)}, bf16[512,256]{1,0:T(8,128)(2,1)S(1)}, u32[]{:S(2)}, u32[]{:S(2)}) %collective-permute-start.28) | collective-permute-done | bytes 262176 | tf_op jit(solution)/shard_map/ppermute | solution.py:281
  136.8 6.4 %shard_map.78.refs_0_ = bf16[512,256]{1,0:T(8,128)(2,1)S(1)} custom-call(s32[21]{0:T(128)S(1)} %pad_add_fusion.2.place_ref, f32[512,128]{1,0:T(8,128)S(1)} %get-tuple-element.62.cos_ref, f32[512,128]{1,0:T(8,128)S(1)} %copy-done.22, bf16[512,256]{1,0:T(8,128)(2,1)S(1)} %get-tuple-element.27.refs_0_, bf16[512,256]{1,0:T(8,128)(2,1)S(1)} %collective-permute-done.28.refs_1_, ...), custom_call_target="tpu_custom_call" | custom-call | flops 1073741824 | bytes 2097236 | tf_op jit(solution)/shard_map/pallas_call | solution.py:18
  144.3 6.5 %collective-permute-start.30 = (bf16[1024,256]{1,0:T(8,128)(2,1)S(1)}, bf16[1024,256]{1,0:T(8,128)(2,1)S(1)}, u32[]{:S(2)}, u32[]{:S(2)}) collective-permute-start(bf16[1024,256]{1,0:T(8,128)(2,1)S(1)} %slice.31), channel_id=1, source_target_pairs={{0,4},{2,6},{4,0},{6,2},{1,5},{3,7},{5,1},{7,3},{8,12},{10,14},{12... | collective-permute-start | bytes 1572872 | tf_op jit(solution)/shard_map/ppermute | solution.py:268
  152.9 2.8 %collective-permute-start.33 = (bf16[512,256]{1,0:T(8,128)(2,1)S(1)}, bf16[512,256]{1,0:T(8,128)(2,1)S(1)}, u32[]{:S(2)}, u32[]{:S(2)}) collective-permute-start(bf16[512,256]{1,0:T(8,128)(2,1)S(1)} %shard_map.78.refs_0_), channel_id=1, source_target_pairs={{0,24},{8,0},{16,8},{24,16},{1,25},{9,1},{17,9},{25,17},{2,26},{10... | collective-permute-start | bytes 786440 | tf_op jit(solution)/shard_map/ppermute | solution.py:286
  157.2 10.9 %collective-permute-done.14.refs_1_ = bf16[512,256]{1,0:T(8,128)(2,1)S(1)} collective-permute-done((bf16[512,256]{1,0:T(8,128)(2,1)S(1)}, bf16[512,256]{1,0:T(8,128)(2,1)S(1)}, u32[]{:S(2)}, u32[]{:S(2)}) %collective-permute-start.14) | collective-permute-done | bytes 262176 | tf_op jit(solution)/shard_map/ppermute | solution.py:281
  168.0 8.8 %collective-permute-start.31 = (bf16[512,256]{1,0:T(8,128)(2,1)S(1)}, bf16[512,256]{1,0:T(8,128)(2,1)S(1)}, u32[]{:S(2)}, u32[]{:S(2)}) collective-permute-start(bf16[512,256]{1,0:T(8,128)(2,1)S(1)} %shard_map.78.refs_0_), channel_id=1, source_target_pairs={{0,8},{8,16},{16,24},{24,0},{1,9},{9,17},{17,25},{25,1},{2,10},{10... | collective-permute-start | bytes 786440 | tf_op jit(solution)/shard_map/ppermute | solution.py:286
  176.9 6.3 %shard_map.76.refs_0_ = bf16[512,256]{1,0:T(8,128)(2,1)S(1)} custom-call(s32[21]{0:T(128)S(1)} %pad_add_fusion.2.place_ref, f32[512,128]{1,0:T(8,128)S(1)} %get-tuple-element.62.cos_ref, f32[512,128]{1,0:T(8,128)S(1)} %copy-done.22, bf16[512,256]{1,0:T(8,128)(2,1)S(1)} %get-tuple-element.22.refs_0_, bf16[512,256]{1,0:T(8,128)(2,1)S(1)} %collective-permute-done.14.refs_1_, ...), custom_call_target="tpu_custom_call" | custom-call | flops 1073741824 | bytes 2097236 | tf_op jit(solution)/shard_map/pallas_call | solution.py:18
  183.2 2.9 %collective-permute-start.23 = (bf16[512,256]{1,0:T(8,128)(2,1)S(1)}, bf16[512,256]{1,0:T(8,128)(2,1)S(1)}, u32[]{:S(2)}, u32[]{:S(2)}) collective-permute-start(bf16[512,256]{1,0:T(8,128)(2,1)S(1)} %shard_map.76.refs_0_), channel_id=1, source_target_pairs={{0,24},{8,0},{16,8},{24,16},{1,25},{9,1},{17,9},{25,17},{2,26},{10... | collective-permute-start | bytes 786440 | tf_op jit(solution)/shard_map/ppermute | solution.py:286
  189.7 2.5 %shard_map.79 = (f32[256,1024]{1,0:T(8,128)S(1)}, f32[256,1024]{1,0:T(8,128)S(1)}) custom-call(s32[4]{0:T(128)S(1)} %get-tuple-element.35.place_ref, bf16[512,256]{1,0:T(8,128)(2,1)S(1)} %shard_map.78.refs_0_, bf16[512,256]{1,0:T(8,128)(2,1)S(1)} %collective-permute-done.31.refs_1_, bf16[512,256]{1,0:T(8,128)(2,1)S(1)} %collective-permute-done.32.refs_2_, ...), custom_call_target="tpu_custom_call" | custom-call | flops 1073741824 | bytes 5242896 | tf_op jit(solution)/shard_map/pallas_call | solution.py:18
  192.2 3.5 %collective-permute-done.23.refs_3_ = bf16[512,256]{1,0:T(8,128)(2,1)S(1)} collective-permute-done((bf16[512,256]{1,0:T(8,128)(2,1)S(1)}, bf16[512,256]{1,0:T(8,128)(2,1)S(1)}, u32[]{:S(2)}, u32[]{:S(2)}) %collective-permute-start.23) | collective-permute-done | bytes 262176 | tf_op jit(solution)/shard_map/ppermute | solution.py:286
  195.7 16.4 %collective-permute-done.22.refs_2_ = bf16[512,256]{1,0:T(8,128)(2,1)S(1)} collective-permute-done((bf16[512,256]{1,0:T(8,128)(2,1)S(1)}, bf16[512,256]{1,0:T(8,128)(2,1)S(1)}, u32[]{:S(2)}, u32[]{:S(2)}) %collective-permute-start.22) | collective-permute-done | bytes 262176 | tf_op jit(solution)/shard_map/ppermute | solution.py:286
  212.1 3.4 %shard_map.80 = (bf16[256,1024]{1,0:T(8,128)(2,1)S(1)}, bf16[256,1024]{1,0:T(8,128)(2,1)}) custom-call(s32[4]{0:T(128)S(1)} %pad_add_fusion.place_ref, bf16[512,256]{1,0:T(8,128)(2,1)S(1)} %shard_map.76.refs_0_, bf16[512,256]{1,0:T(8,128)(2,1)S(1)} %collective-permute-done.21.refs_1_, bf16[512,256]{1,0:T(8,128)(2,1)S(1)} %collective-permute-done.22.refs_2_, ...), custom_call_target="tpu_custom_call" | custom-call | flops 1073741824 | bytes 7340048 | tf_op jit(solution)/shard_map/pallas_call | solution.py:18
  218.5 2.1 collective-permute-start.35
  220.9 10.7 %collective-permute-done.35 = bf16[128,1024]{1,0:T(8,128)(2,1)S(1)} collective-permute-done((bf16[128,1024]{1,0:T(8,128)(2,1)S(1)}, bf16[128,1024]{1,0:T(8,128)(2,1)S(1)}, u32[]{:S(2)}, u32[]{:S(2)}) %collective-permute-start.35) | collective-permute-done | bytes 262176 | tf_op jit(solution)/shard_map/ppermute | solution.py:363
  (170 shorter events, 46.6 us)
Async XLA Ops:
  1.2 8.2 %collective-permute-start.5 = (bf16[256,512]{1,0:T(8,128)(2,1)S(1)}, bf16[256,512]{1,0:T(8,128)(2,1)S(1)}, u32[]{:S(2)}, u32[]{:S(2)}) collective-permute-start(bf16[256,512]{1,0:T(8,128)(2,1)S(1)} %pad_maximum_fusion.8), channel_id=1, source_target_pairs={{0,8},{8,0},{16,24},{24,16},{1,9},{9,1},{17,25},{25,17},{2,10},{10... | collective-permute-start | bytes 786440 | tf_op jit(solution)/shard_map/ppermute | solution.py:281
  5.0 10.2 %collective-permute-start.4 = (bf16[256,512]{1,0:T(8,128)(2,1)}, bf16[256,512]{1,0:T(8,128)(2,1)}, u32[]{:S(2)}, u32[]{:S(2)}) collective-permute-start(bf16[256,512]{1,0:T(8,128)(2,1)} %pad_maximum_fusion.7), channel_id=1, source_target_pairs={{0,8},{8,0},{16,24},{24,16},{1,9},{9,1},{17,25},{25,17},{2,10},{10... | collective-permute-start | bytes 786440 | tf_op jit(solution)/shard_map/ppermute | solution.py:281
  9.5 11.5 %collective-permute-start.7 = (bf16[512,512]{1,0:T(8,128)(2,1)S(1)}, bf16[512,512]{1,0:T(8,128)(2,1)S(1)}, u32[]{:S(2)}, u32[]{:S(2)}) collective-permute-start(bf16[512,512]{1,0:T(8,128)(2,1)S(1)} %pad_maximum_fusion.2.refs_4_), channel_id=1, source_target_pairs={{0,4},{2,6},{4,0},{6,2},{1,5},{3,7},{5,1},{7,3},{8,12},{10,14},{12... | collective-permute-start | bytes 1572872 | tf_op jit(solution)/shard_map/ppermute | solution.py:268
  10.7 10.5 %collective-permute-start.6 = (bf16[512,512]{1,0:T(8,128)(2,1)S(1)}, bf16[512,512]{1,0:T(8,128)(2,1)}, u32[]{:S(2)}, u32[]{:S(2)}) collective-permute-start(bf16[512,512]{1,0:T(8,128)(2,1)S(1)} %pad_maximum_fusion.2.refs_4_), channel_id=1, source_target_pairs={{0,2},{2,0},{4,6},{6,4},{1,3},{3,1},{5,7},{7,5},{8,10},{10,8},{12,... | collective-permute-start | bytes 1572872 | tf_op jit(solution)/shard_map/ppermute | solution.py:268
  12.4 24.0 %collective-permute-start.1 = (bf16[128,2048]{1,0:T(8,128)(2,1)S(1)}, bf16[128,2048]{1,0:T(8,128)(2,1)S(1)}, u32[]{:S(2)}, u32[]{:S(2)}) collective-permute-start(bf16[128,2048]{1,0:T(8,128)(2,1)S(1)} %get-tuple-element.45), channel_id=1, source_target_pairs={{0,16},{8,24},{16,0},{24,8},{1,17},{9,25},{17,1},{25,9},{2,18},{10... | collective-permute-start | bytes 1572872 | tf_op jit(solution)/shard_map/ppermute | solution.py:281
  21.2 26.6 %collective-permute-start.9 = (bf16[512,512]{1,0:T(8,128)(2,1)S(1)}, bf16[512,512]{1,0:T(8,128)(2,1)S(1)}, u32[]{:S(2)}, u32[]{:S(2)}) collective-permute-start(bf16[512,512]{1,0:T(8,128)(2,1)S(1)} %pad_maximum_fusion.1.refs_4_), channel_id=1, source_target_pairs={{0,4},{2,6},{4,0},{6,2},{1,5},{3,7},{5,1},{7,3},{8,12},{10,14},{12... | collective-permute-start | bytes 1572872 | tf_op jit(solution)/shard_map/ppermute | solution.py:268
  22.2 28.3 %collective-permute-start = (bf16[128,2048]{1,0:T(8,128)(2,1)S(1)}, bf16[128,2048]{1,0:T(8,128)(2,1)S(1)}, u32[]{:S(2)}, u32[]{:S(2)}) collective-permute-start(bf16[128,2048]{1,0:T(8,128)(2,1)S(1)} %get-tuple-element.46.refs_0_), channel_id=1, source_target_pairs={{0,8},{8,0},{16,24},{24,16},{1,9},{9,1},{17,25},{25,17},{2,10},{10... | collective-permute-start | bytes 1572872 | tf_op jit(solution)/shard_map/ppermute | solution.py:281
  22.8 26.8 %collective-permute-start.8 = (bf16[512,512]{1,0:T(8,128)(2,1)S(1)}, bf16[512,512]{1,0:T(8,128)(2,1)}, u32[]{:S(2)}, u32[]{:S(2)}) collective-permute-start(bf16[512,512]{1,0:T(8,128)(2,1)S(1)} %pad_maximum_fusion.1.refs_4_), channel_id=1, source_target_pairs={{0,2},{2,0},{4,6},{6,4},{1,3},{3,1},{5,7},{7,5},{8,10},{10,8},{12,... | collective-permute-start | bytes 1572872 | tf_op jit(solution)/shard_map/ppermute | solution.py:268
  24.8 23.1 %collective-permute-start.3 = (bf16[256,512]{1,0:T(8,128)(2,1)}, bf16[256,512]{1,0:T(8,128)(2,1)}, u32[]{:S(2)}, u32[]{:S(2)}) collective-permute-start(bf16[256,512]{1,0:T(8,128)(2,1)} %pad_maximum_fusion.6), channel_id=1, source_target_pairs={{0,8},{8,0},{16,24},{24,16},{1,9},{9,1},{17,25},{25,17},{2,10},{10... | collective-permute-start | bytes 786440 | tf_op jit(solution)/shard_map/ppermute | solution.py:281
  36.4 22.7 %collective-permute-start.2 = (bf16[128,2048]{1,0:T(8,128)(2,1)S(1)}, bf16[128,2048]{1,0:T(8,128)(2,1)S(1)}, u32[]{:S(2)}, u32[]{:S(2)}) collective-permute-start(bf16[128,2048]{1,0:T(8,128)(2,1)S(1)} %collective-permute-done.1.refs_2_), channel_id=1, source_target_pairs={{0,8},{8,0},{16,24},{24,16},{1,9},{9,1},{17,25},{25,17},{2,10},{10... | collective-permute-start | bytes 1572872 | tf_op jit(solution)/shard_map/ppermute | solution.py:281
  49.6 28.9 %collective-permute-start.11 = (bf16[512,512]{1,0:T(8,128)(2,1)S(1)}, bf16[512,512]{1,0:T(8,128)(2,1)S(1)}, u32[]{:S(2)}, u32[]{:S(2)}) collective-permute-start(bf16[512,512]{1,0:T(8,128)(2,1)S(1)} %pad_maximum_fusion.refs_4_), channel_id=1, source_target_pairs={{0,4},{2,6},{4,0},{6,2},{1,5},{3,7},{5,1},{7,3},{8,12},{10,14},{12... | collective-permute-start | bytes 1572872 | tf_op jit(solution)/shard_map/ppermute | solution.py:268
  50.5 28.1 %collective-permute-start.10 = (bf16[512,512]{1,0:T(8,128)(2,1)S(1)}, bf16[512,512]{1,0:T(8,128)(2,1)S(1)}, u32[]{:S(2)}, u32[]{:S(2)}) collective-permute-start(bf16[512,512]{1,0:T(8,128)(2,1)S(1)} %pad_maximum_fusion.refs_4_), channel_id=1, source_target_pairs={{0,2},{2,0},{4,6},{6,4},{1,3},{3,1},{5,7},{7,5},{8,10},{10,8},{12,... | collective-permute-start | bytes 1572872 | tf_op jit(solution)/shard_map/ppermute | solution.py:268
  61.7 13.9 %collective-permute-start.17 = (bf16[512,256]{1,0:T(8,128)(2,1)S(1)}, bf16[512,256]{1,0:T(8,128)(2,1)S(1)}, u32[]{:S(2)}, u32[]{:S(2)}) collective-permute-start(bf16[512,256]{1,0:T(8,128)(2,1)S(1)} %get-tuple-element.25), channel_id=1, source_target_pairs={{0,16},{8,24},{16,0},{24,8},{1,17},{9,25},{17,1},{25,9},{2,18},{10... | collective-permute-start | bytes 786440 | tf_op jit(solution)/shard_map/ppermute | solution.py:281
  75.8 13.0 %collective-permute-start.19 = (bf16[512,256]{1,0:T(8,128)(2,1)S(1)}, bf16[512,256]{1,0:T(8,128)(2,1)S(1)}, u32[]{:S(2)}, u32[]{:S(2)}) collective-permute-start(bf16[512,256]{1,0:T(8,128)(2,1)S(1)} %shard_map.75.refs_2_), channel_id=1, source_target_pairs={{0,4},{2,6},{4,0},{6,2},{1,5},{3,7},{5,1},{7,3},{8,12},{10,14},{12... | collective-permute-start | bytes 786440 | tf_op jit(solution)/shard_map/ppermute | solution.py:268
  76.1 13.5 %collective-permute-start.18 = (bf16[512,256]{1,0:T(8,128)(2,1)S(1)}, bf16[512,256]{1,0:T(8,128)(2,1)S(1)}, u32[]{:S(2)}, u32[]{:S(2)}) collective-permute-start(bf16[512,256]{1,0:T(8,128)(2,1)S(1)} %shard_map.75.refs_2_), channel_id=1, source_target_pairs={{0,2},{2,0},{4,6},{6,4},{1,3},{3,1},{5,7},{7,5},{8,10},{10,8},{12,... | collective-permute-start | bytes 786440 | tf_op jit(solution)/shard_map/ppermute | solution.py:268
  78.5 13.8 %collective-permute-start.12 = (bf16[256,512]{1,0:T(8,128)(2,1)S(1)}, bf16[256,512]{1,0:T(8,128)(2,1)S(1)}, u32[]{:S(2)}, u32[]{:S(2)}) collective-permute-start(bf16[256,512]{1,0:T(8,128)(2,1)S(1)} %slice.32), channel_id=1, source_target_pairs={{0,2},{2,0},{4,6},{6,4},{1,3},{3,1},{5,7},{7,5},{8,10},{10,8},{12,... | collective-permute-start | bytes 786440 | tf_op jit(solution)/shard_map/ppermute | solution.py:268
  78.6 15.8 %collective-permute-start.13 = (bf16[256,512]{1,0:T(8,128)(2,1)S(1)}, bf16[256,512]{1,0:T(8,128)(2,1)S(1)}, u32[]{:S(2)}, u32[]{:S(2)}) collective-permute-start(bf16[256,512]{1,0:T(8,128)(2,1)S(1)} %slice.33), channel_id=1, source_target_pairs={{0,4},{2,6},{4,0},{6,2},{1,5},{3,7},{5,1},{7,3},{8,12},{10,14},{12... | collective-permute-start | bytes 786440 | tf_op jit(solution)/shard_map/ppermute | solution.py:268
  94.5 48.7 %collective-permute-start.25 = (bf16[2048,256]{1,0:T(8,128)(2,1)}, bf16[2048,256]{1,0:T(8,128)(2,1)S(1)}, u32[]{:S(2)}, u32[]{:S(2)}) collective-permute-start(bf16[2048,256]{1,0:T(8,128)(2,1)} %refs_4_.1), channel_id=1, source_target_pairs={{0,4},{2,6},{4,0},{6,2},{1,5},{3,7},{5,1},{7,3},{8,12},{10,14},{12... | collective-permute-start | bytes 3145736 | tf_op jit(solution)/shard_map/ppermute | solution.py:268
  94.5 48.7 %collective-permute-start.24 = (bf16[2048,256]{1,0:T(8,128)(2,1)}, bf16[2048,256]{1,0:T(8,128)(2,1)S(1)}, u32[]{:S(2)}, u32[]{:S(2)}) collective-permute-start(bf16[2048,256]{1,0:T(8,128)(2,1)} %refs_4_.1), channel_id=1, source_target_pairs={{0,2},{2,0},{4,6},{6,4},{1,3},{3,1},{5,7},{7,5},{8,10},{10,8},{12,... | collective-permute-start | bytes 3145736 | tf_op jit(solution)/shard_map/ppermute | solution.py:268
  96.3 26.0 %collective-permute-start.26 = (bf16[256,512]{1,0:T(8,128)(2,1)}, bf16[256,512]{1,0:T(8,128)(2,1)}, u32[]{:S(2)}, u32[]{:S(2)}) collective-permute-start(bf16[256,512]{1,0:T(8,128)(2,1)} %slice.36), channel_id=1, source_target_pairs={{0,2},{2,0},{4,6},{6,4},{1,3},{3,1},{5,7},{7,5},{8,10},{10,8},{12,... | collective-permute-start | bytes 786440 | tf_op jit(solution)/shard_map/ppermute | solution.py:268
  98.4 25.3 %collective-permute-start.27 = (bf16[256,512]{1,0:T(8,128)(2,1)}, bf16[256,512]{1,0:T(8,128)(2,1)}, u32[]{:S(2)}, u32[]{:S(2)}) collective-permute-start(bf16[256,512]{1,0:T(8,128)(2,1)} %slice.37), channel_id=1, source_target_pairs={{0,4},{2,6},{4,0},{6,2},{1,5},{3,7},{5,1},{7,3},{8,12},{10,14},{12... | collective-permute-start | bytes 786440 | tf_op jit(solution)/shard_map/ppermute | solution.py:268
  143.3 42.8 %collective-permute-start.29 = (bf16[1024,256]{1,0:T(8,128)(2,1)S(1)}, bf16[1024,256]{1,0:T(8,128)(2,1)S(1)}, u32[]{:S(2)}, u32[]{:S(2)}) collective-permute-start(bf16[1024,256]{1,0:T(8,128)(2,1)S(1)} %slice.30), channel_id=1, source_target_pairs={{0,2},{2,0},{4,6},{6,4},{1,3},{3,1},{5,7},{7,5},{8,10},{10,8},{12,... | collective-permute-start | bytes 1572872 | tf_op jit(solution)/shard_map/ppermute | solution.py:268
  144.3 42.2 %collective-permute-start.30 = (bf16[1024,256]{1,0:T(8,128)(2,1)S(1)}, bf16[1024,256]{1,0:T(8,128)(2,1)S(1)}, u32[]{:S(2)}, u32[]{:S(2)}) collective-permute-start(bf16[1024,256]{1,0:T(8,128)(2,1)S(1)} %slice.31), channel_id=1, source_target_pairs={{0,4},{2,6},{4,0},{6,2},{1,5},{3,7},{5,1},{7,3},{8,12},{10,14},{12... | collective-permute-start | bytes 1572872 | tf_op jit(solution)/shard_map/ppermute | solution.py:268
  152.7 15.3 %collective-permute-start.14 = (bf16[512,256]{1,0:T(8,128)(2,1)S(1)}, bf16[512,256]{1,0:T(8,128)(2,1)S(1)}, u32[]{:S(2)}, u32[]{:S(2)}) collective-permute-start(bf16[512,256]{1,0:T(8,128)(2,1)S(1)} %get-tuple-element.23), channel_id=1, source_target_pairs={{0,16},{8,24},{16,0},{24,8},{1,17},{9,25},{17,1},{25,9},{2,18},{10... | collective-permute-start | bytes 786440 | tf_op jit(solution)/shard_map/ppermute | solution.py:281
  152.9 30.3 %collective-permute-start.33 = (bf16[512,256]{1,0:T(8,128)(2,1)S(1)}, bf16[512,256]{1,0:T(8,128)(2,1)S(1)}, u32[]{:S(2)}, u32[]{:S(2)}) collective-permute-start(bf16[512,256]{1,0:T(8,128)(2,1)S(1)} %shard_map.78.refs_0_), channel_id=1, source_target_pairs={{0,24},{8,0},{16,8},{24,16},{1,25},{9,1},{17,9},{25,17},{2,26},{10... | collective-permute-start | bytes 786440 | tf_op jit(solution)/shard_map/ppermute | solution.py:286
  155.7 33.9 %collective-permute-start.32 = (bf16[512,256]{1,0:T(8,128)(2,1)S(1)}, bf16[512,256]{1,0:T(8,128)(2,1)S(1)}, u32[]{:S(2)}, u32[]{:S(2)}) collective-permute-start(bf16[512,256]{1,0:T(8,128)(2,1)S(1)} %shard_map.78.refs_0_), channel_id=1, source_target_pairs={{0,16},{8,24},{16,0},{24,8},{1,17},{9,25},{17,1},{25,9},{2,18},{10... | collective-permute-start | bytes 786440 | tf_op jit(solution)/shard_map/ppermute | solution.py:286
  168.0 21.6 %collective-permute-start.31 = (bf16[512,256]{1,0:T(8,128)(2,1)S(1)}, bf16[512,256]{1,0:T(8,128)(2,1)S(1)}, u32[]{:S(2)}, u32[]{:S(2)}) collective-permute-start(bf16[512,256]{1,0:T(8,128)(2,1)S(1)} %shard_map.78.refs_0_), channel_id=1, source_target_pairs={{0,8},{8,16},{16,24},{24,0},{1,9},{9,17},{17,25},{25,1},{2,10},{10... | collective-permute-start | bytes 786440 | tf_op jit(solution)/shard_map/ppermute | solution.py:286
  183.2 12.4 %collective-permute-start.23 = (bf16[512,256]{1,0:T(8,128)(2,1)S(1)}, bf16[512,256]{1,0:T(8,128)(2,1)S(1)}, u32[]{:S(2)}, u32[]{:S(2)}) collective-permute-start(bf16[512,256]{1,0:T(8,128)(2,1)S(1)} %shard_map.76.refs_0_), channel_id=1, source_target_pairs={{0,24},{8,0},{16,8},{24,16},{1,25},{9,1},{17,9},{25,17},{2,26},{10... | collective-permute-start | bytes 786440 | tf_op jit(solution)/shard_map/ppermute | solution.py:286
  186.1 26.0 %collective-permute-start.22 = (bf16[512,256]{1,0:T(8,128)(2,1)S(1)}, bf16[512,256]{1,0:T(8,128)(2,1)S(1)}, u32[]{:S(2)}, u32[]{:S(2)}) collective-permute-start(bf16[512,256]{1,0:T(8,128)(2,1)S(1)} %shard_map.76.refs_0_), channel_id=1, source_target_pairs={{0,16},{8,24},{16,0},{24,8},{1,17},{9,25},{17,1},{25,9},{2,18},{10... | collective-permute-start | bytes 786440 | tf_op jit(solution)/shard_map/ppermute | solution.py:286
  186.5 25.6 %collective-permute-start.21 = (bf16[512,256]{1,0:T(8,128)(2,1)S(1)}, bf16[512,256]{1,0:T(8,128)(2,1)S(1)}, u32[]{:S(2)}, u32[]{:S(2)}) collective-permute-start(bf16[512,256]{1,0:T(8,128)(2,1)S(1)} %shard_map.76.refs_0_), channel_id=1, source_target_pairs={{0,8},{8,16},{16,24},{24,0},{1,9},{9,17},{17,25},{25,1},{2,10},{10... | collective-permute-start | bytes 786440 | tf_op jit(solution)/shard_map/ppermute | solution.py:286
  218.5 13.1 %collective-permute-start.35 = (bf16[128,1024]{1,0:T(8,128)(2,1)S(1)}, bf16[128,1024]{1,0:T(8,128)(2,1)S(1)}, u32[]{:S(2)}, u32[]{:S(2)}) collective-permute-start(bf16[128,1024]{1,0:T(8,128)(2,1)S(1)} %get-tuple-element.49), channel_id=1, source_target_pairs={{0,0},{1,16},{8,8},{9,24},{16,1},{17,17},{24,9},{25,25},{2,2},{3,1... | collective-permute-start | bytes 786440 | tf_op jit(solution)/shard_map/ppermute | solution.py:363
  220.6 10.9 %collective-permute-start.36 = (bf16[128,1024]{1,0:T(8,128)(2,1)S(1)}, bf16[128,1024]{1,0:T(8,128)(2,1)S(1)}, u32[]{:S(2)}, u32[]{:S(2)}) collective-permute-start(bf16[128,1024]{1,0:T(8,128)(2,1)S(1)} %get-tuple-element.50), channel_id=1, source_target_pairs={{0,8},{1,24},{8,0},{9,16},{16,9},{17,25},{24,1},{25,17},{2,10},{3,... | collective-permute-start | bytes 786440 | tf_op jit(solution)/shard_map/ppermute | solution.py:363
  (47 other events, 414.1 us)

commit v7 on v6

--- a/solution.py
+++ b/solution.py
@@ -133,7 +133,7 @@
         functools.partial(attention_kernel, blocks, stride, len(query_parts), len(kv_parts)),
         jax.ShapeDtypeStruct((tokens, width), jnp.bfloat16),
         (place, cosine, sine, *query_parts, *kv_parts),
-        4 * tokens * width * keys,
+        32 * tokens * width * keys,
         [
             pltpu.VMEM((heads, tokens, HD), jnp.bfloat16),
             pltpu.VMEM((tokens // blocks, keys), jnp.float32),
@@ -152,7 +152,8 @@
         gathered[pl.ds(pl.multiple_of((hi ^ d) * rows, rows), rows), :] = token_ref[...]
     for side, out_ref in enumerate(out_refs):
         width = out_ref.shape[1]
-        columns = pl.ds(pl.multiple_of((lax.div(hi, 2) ^ side) * width, width), width)
+        first = (lax.div(hi, 2) ^ side) * place_ref[2] + place_ref[3]
+        columns = pl.ds(pl.multiple_of(first, width), width)
         total = 0.0
         for part in range(2):
             for r in range(4):
@@ -169,9 +170,11 @@
         out_ref[...] = total.astype(jnp.bfloat16)
 
 
-def product(place, token_parts, weights):
+def product(hi, lo, token_parts, weights, chunk, chunks):
     rows, depth = token_parts[0].shape
-    width = weights[0].shape[1] // 2
+    step = weights[0].shape[1] // 2
+    width = step // chunks
+    place = jnp.stack([hi, lo, jnp.full((), step, jnp.int32), jnp.full((), chunk * width, jnp.int32)])
     shape = jax.ShapeDtypeStruct((4 * rows, width), jnp.bfloat16)
     return local_kernel(
         product_kernel,
@@ -297,25 +300,20 @@
     depth = features // 2
     heads = w_query.shape[1] // 4
     width = heads // 2
-    place = jnp.stack([hi, lo])
 
     def columns_for(chip, sources, width):
         return jnp.concatenate(
             [
-                lax.dynamic_slice_in_dim(w, (2 * z + chip) * step + first, width, 1)
+                lax.dynamic_slice_in_dim(w, (2 * z + chip) * width, width, 1)
                 for z in range(2)
-                for w, step, first in sources
+                for w in sources
             ],
             axis=1,
         )
 
     stage = ()
     weights = []
-    for sources, size in (
-        ([(w_key, HD, 0), (w_value, HD, 0)], HD),
-        ([(w_query, heads, 0)], width),
-        ([(w_query, heads, width)], width),
-    ):
+    for sources, size in (((w_key, w_value), HD), ((w_query,), heads)):
         came = along(columns_for(1 - which, sources, size), 1)
         both = jnp.concatenate([columns_for(which, sources, size), came], axis=0)
         stage = sides(after(both, *stage) if stage else both)
@@ -330,21 +328,20 @@
     row_index = jnp.arange(4 * rows, dtype=jnp.int32)
     cosine, sine = rotary_tables((row_index // rows * 4 + lo) * rows + row_index % rows)
 
-    def summed_parts(weight):
-        kept, sent = product(place, token_parts, weight)
-        return [kept, along(sent, 2)]
-
-    kv_own = finish_pair(cosine, sine, summed_parts(weights[0]))
+    kept, sent = product(hi, lo, token_parts, weights[0], 0, 1)
+    kv_own = finish_pair(cosine, sine, [kept, along(sent, 2)])
     kv_parts = [kv_own] + [beside(kv_own, r) for r in range(1, 4)]
 
     firsts = jnp.stack([lo, lo, lo ^ 1, lo ^ 2, lo ^ 3]) * rows
     seen = jnp.concatenate([firsts, doc_starts])
-    out_sides = sides(after(w_out, *weights[2][3:], *kv_parts[1:]))
+    out_sides = sides(after(w_out, *weights[1][3:], *kv_parts[1:]))
+    products = [product(hi, lo, token_parts, weights[1], c, 2) for c in range(2)]
+    products[0] = (after(products[0][0], products[1][0]), products[0][1])
     attended = [
-        attention(seen, cosine, sine, summed_parts(weight), kv_parts, 4, 4 * rows)
-        for weight in weights[1:]
+        attention(seen, cosine, sine, [kept, along(sent, 2)], kv_parts, 4, 4 * rows)
+        for kept, sent in products
     ]
-    out_sides[1:] = lax.optimization_barrier((*out_sides[1:], attended[0]))[:2]
+    out_sides[1:] = lax.optimization_barrier((*out_sides[1:], attended[1]))[:2]
     out_blocks = corner(out_sides)
     out_blocks[3:] = [jnp.concatenate(out_blocks[3:], axis=0)]
     totals = ()

time: 234 us -> 205 us (0.88)
  starting transfers between devices: 53.1 us -> 36.2 us
  waiting for transfers between devices: 132 us -> 120 us
    ppermute x19 -> x15, waiting for transfers between devices: 43.8 us -> 21.2 us  [beside(): return lax.ppermute(block, 'lo', [(i, i ^ r) for i in range(4)])]
    ppermute x6, waiting for transfers between devices: 21.6 us -> 36.5 us  [round_line(): lax.ppermute(block, 'hi', [(i, (i + d) % 4) for i in range(4)])]
    ppermute x6, starting transfers between devices: 17.7 us -> 6.18 us  [round_line(): lax.ppermute(block, 'hi', [(i, (i + d) % 4) for i in range(4)])]
    ppermute x19 -> x15, starting transfers between devices: 20.4 us -> 13 us  [beside(): return lax.ppermute(block, 'lo', [(i, i ^ r) for i in range(4)])]
    ppermute x2, starting transfers between devices: 2.37 us -> 5.62 us  [line_device(): arrived.append(lax.ppermute(piece, ('hi', 'head'), route))]
    unnamed x85 -> x25, local copies, waits for them, and re-layouts: 7.14 us -> 4.54 us
    ppermute x9 -> x8, waiting for transfers between devices: 54.3 us -> 51.8 us  [along(): return lax.ppermute(block, 'hi', [(i, i ^ d) for i in range(4)])]
    ppermute x9 -> x8, starting transfers between devices: 11.7 us -> 9.4 us  [along(): return lax.ppermute(block, 'hi', [(i, i ^ d) for i in range(4)])]
  transfers between devices with their start and end apart: 37 -> 32, of which waited for: 23 -> 15; matrix products, arithmetic and copies ran while one was open for 5% -> 6% of each run, Pallas kernels for 10% -> 13%
where the time goes in v7:
time: 205 us; the launch traced here: 203 us
  waiting for transfers between devices  120 us (59%)
  starting transfers between devices  36.2 us (18%)
  Pallas kernels  28 us (14%)
  local copies, waits for them, and re-layouts  13.7 us (7%)
  other arithmetic  4.39 us (2%)
    ppermute x8, waiting for transfers between devices, along(): return lax.ppermute(block, 'hi', [(i, i ^ d) for i in range(4)])  51.8 us
    ppermute x6, waiting for transfers between devices, round_line(): lax.ppermute(block, 'hi', [(i, (i + d) % 4) for i in range(4)])  36.5 us
    pallas_call x8, Pallas kernels, local_kernel(): pl.pallas_call(body, in_specs=[pl.BlockSpec(memory_space=pltpu.SMEM)] + [...  28 us
    ppermute x15, waiting for transfers between devices, beside(): return lax.ppermute(block, 'lo', [(i, i ^ r) for i in range(4)])  21.2 us
    ppermute x15, starting transfers between devices, beside(): return lax.ppermute(block, 'lo', [(i, i ^ r) for i in range(4)])  13 us
    ppermute x2, waiting for transfers between devices, line_device(): arrived.append(lax.ppermute(piece, ('hi', 'head'), route))  9.42 us
    ppermute x8, starting transfers between devices, along(): return lax.ppermute(block, 'hi', [(i, i ^ d) for i in range(4)])  9.4 us
    ppermute x6, starting transfers between devices, round_line(): lax.ppermute(block, 'hi', [(i, (i + d) % 4) for i in range(4)])  6.18 us
  transfers between devices with their start and end apart: 32, of which 15 were waited for; matrix products, arithmetic and copies ran while one was open for 6% of the time, Pallas kernels for 13%

profile of v7, /device:TPU:1, one launch (start us, length us, event | category | flops | bytes accessed | tf_op | source)
XLA Modules:
  0.0 203.1 jit_solution(13535788498077137302)
XLA Ops:
  1.2 2.2 %collective-permute-start.4 = (bf16[256,512]{1,0:T(8,128)(2,1)S(1)}, bf16[256,512]{1,0:T(8,128)(2,1)S(1)}, u32[]{:S(2)}, u32[]{:S(2)}) collective-permute-start(bf16[256,512]{1,0:T(8,128)(2,1)S(1)} %pad_maximum_fusion.6), channel_id=1, source_target_pairs={{0,8},{8,0},{16,24},{24,16},{1,9},{9,1},{17,25},{25,17},{2,10},{10... | collective-permute-start | bytes 786440 | tf_op jit(solution)/shard_map/ppermute | solution.py:284
  5.8 3.7 %collective-permute-done.4 = bf16[256,512]{1,0:T(8,128)(2,1)S(1)} collective-permute-done((bf16[256,512]{1,0:T(8,128)(2,1)S(1)}, bf16[256,512]{1,0:T(8,128)(2,1)S(1)}, u32[]{:S(2)}, u32[]{:S(2)}) %collective-permute-start.4) | collective-permute-done | bytes 262176 | tf_op jit(solution)/shard_map/ppermute | solution.py:284
  13.1 2.3 %collective-permute-start.1 = (bf16[128,2048]{1,0:T(8,128)(2,1)}, bf16[128,2048]{1,0:T(8,128)(2,1)S(1)}, u32[]{:S(2)}, u32[]{:S(2)}) collective-permute-start(bf16[128,2048]{1,0:T(8,128)(2,1)} %get-tuple-element.41), channel_id=1, source_target_pairs={{0,16},{8,24},{16,0},{24,8},{1,17},{9,25},{17,1},{25,9},{2,18},{10... | collective-permute-start | bytes 1572872 | tf_op jit(solution)/shard_map/ppermute | solution.py:284
  15.5 12.2 %collective-permute-done.3 = bf16[256,1024]{1,0:T(8,128)(2,1)} collective-permute-done((bf16[256,1024]{1,0:T(8,128)(2,1)S(1)}, bf16[256,1024]{1,0:T(8,128)(2,1)}, u32[]{:S(2)}, u32[]{:S(2)}) %collective-permute-start.3) | collective-permute-done | bytes 524320 | tf_op jit(solution)/shard_map/ppermute | solution.py:284
  29.6 2.1 %collective-permute-start.8 = (bf16[512,1024]{1,0:T(8,128)(2,1)S(1)}, bf16[512,1024]{1,0:T(8,128)(2,1)S(1)}, u32[]{:S(2)}, u32[]{:S(2)}) collective-permute-start(bf16[512,1024]{1,0:T(8,128)(2,1)S(1)} %pad_maximum_fusion.refs_4_), channel_id=1, source_target_pairs={{0,4},{2,6},{4,0},{6,2},{1,5},{3,7},{5,1},{7,3},{8,12},{10,14},{12... | collective-permute-start | bytes 3145736 | tf_op jit(solution)/shard_map/ppermute | solution.py:271
  31.7 2.0 collective-permute-start.7
  33.7 2.0 %collective-permute-done.1.refs_2_ = bf16[128,2048]{1,0:T(8,128)(2,1)S(1)} collective-permute-done((bf16[128,2048]{1,0:T(8,128)(2,1)}, bf16[128,2048]{1,0:T(8,128)(2,1)S(1)}, u32[]{:S(2)}, u32[]{:S(2)}) %collective-permute-start.1) | collective-permute-done | bytes 524320 | tf_op jit(solution)/shard_map/ppermute | solution.py:284
  36.6 1.7 slice.26
  38.4 1.7 slice.27
  40.1 10.7 %collective-permute-done.refs_1_ = bf16[128,2048]{1,0:T(8,128)(2,1)} collective-permute-done((bf16[128,2048]{1,0:T(8,128)(2,1)S(1)}, bf16[128,2048]{1,0:T(8,128)(2,1)}, u32[]{:S(2)}, u32[]{:S(2)}) %collective-permute-start) | collective-permute-done | bytes 524320 | tf_op jit(solution)/shard_map/ppermute | solution.py:284
  51.0 10.0 %collective-permute-done.12.refs_7_ = bf16[256,512]{1,0:T(8,128)(2,1)S(1)} collective-permute-done((bf16[256,512]{1,0:T(8,128)(2,1)}, bf16[256,512]{1,0:T(8,128)(2,1)S(1)}, u32[]{:S(2)}, u32[]{:S(2)}) %collective-permute-start.12) | collective-permute-done | bytes 262176 | tf_op jit(solution)/shard_map/ppermute | solution.py:271
  64.0 2.8 %shard_map.74 = (bf16[512,256]{1,0:T(8,128)(2,1)S(1)}, bf16[512,256]{1,0:T(8,128)(2,1)S(1)}) custom-call(s32[4]{0:T(128)S(1)} %get-tuple-element.59.place_ref, bf16[128,2048]{1,0:T(8,128)(2,1)S(1)} %get-tuple-element.42.refs_0_, bf16[128,2048]{1,0:T(8,128)(2,1)} %collective-permute-done.refs_1_, bf16[128,2048]{1,0:T(8,128)(2,1)S(1)} %collective-permute-done.1.refs_2_, ...), custom_call_target="tpu_custom_call" | custom-call | flops 1073741824 | bytes 4194320 | tf_op jit(solution)/shard_map/pallas_call | solution.py:18
  69.3 1.9 slice.25
  72.4 8.3 %collective-permute-done.14.refs_1_ = bf16[512,256]{1,0:T(8,128)(2,1)S(1)} collective-permute-done((bf16[512,256]{1,0:T(8,128)(2,1)S(1)}, bf16[512,256]{1,0:T(8,128)(2,1)S(1)}, u32[]{:S(2)}, u32[]{:S(2)}) %collective-permute-start.14) | collective-permute-done | bytes 262176 | tf_op jit(solution)/shard_map/ppermute | solution.py:284
  84.9 4.8 %collective-permute-done.17.refs_5_ = bf16[512,256]{1,0:T(8,128)(2,1)} collective-permute-done((bf16[512,256]{1,0:T(8,128)(2,1)}, bf16[512,256]{1,0:T(8,128)(2,1)}, u32[]{:S(2)}, u32[]{:S(2)}) %collective-permute-start.17) | collective-permute-done | bytes 262176 | tf_op jit(solution)/shard_map/ppermute | solution.py:271
  89.8 6.3 %collective-permute-done.16.refs_4_ = bf16[512,256]{1,0:T(8,128)(2,1)} collective-permute-done((bf16[512,256]{1,0:T(8,128)(2,1)}, bf16[512,256]{1,0:T(8,128)(2,1)}, u32[]{:S(2)}, u32[]{:S(2)}) %collective-permute-start.16) | collective-permute-done | bytes 262176 | tf_op jit(solution)/shard_map/ppermute | solution.py:271
  98.2 3.2 %shard_map.73 = (bf16[512,256]{1,0:T(8,128)(2,1)S(1)}, bf16[512,256]{1,0:T(8,128)(2,1)S(1)}) custom-call(s32[4]{0:T(128)S(1)} %get-tuple-element.60.place_ref, bf16[128,2048]{1,0:T(8,128)(2,1)S(1)} %get-tuple-element.42.refs_0_, bf16[128,2048]{1,0:T(8,128)(2,1)} %collective-permute-done.refs_1_, bf16[128,2048]{1,0:T(8,128)(2,1)S(1)} %collective-permute-done.1.refs_2_, ...), custom_call_target="tpu_custom_call" | custom-call | flops 1073741824 | bytes 6291472 | tf_op jit(solution)/shard_map/pallas_call | solution.py:18
  101.6 3.3 %shard_map.77 = (bf16[512,256]{1,0:T(8,128)(2,1)S(1)}, bf16[512,256]{1,0:T(8,128)(2,1)S(1)}) custom-call(s32[4]{0:T(128)S(1)} %get-tuple-element.35.place_ref, bf16[128,2048]{1,0:T(8,128)(2,1)S(1)} %get-tuple-element.42.refs_0_, bf16[128,2048]{1,0:T(8,128)(2,1)} %collective-permute-done.refs_1_, bf16[128,2048]{1,0:T(8,128)(2,1)S(1)} %collective-permute-done.1.refs_2_, ...), custom_call_target="tpu_custom_call" | custom-call | flops 1073741824 | bytes 6291472 | tf_op jit(solution)/shard_map/pallas_call | solution.py:18
  104.9 2.4 %collective-permute-start.25 = (bf16[512,256]{1,0:T(8,128)(2,1)S(1)}, bf16[512,256]{1,0:T(8,128)(2,1)S(1)}, u32[]{:S(2)}, u32[]{:S(2)}) collective-permute-start(bf16[512,256]{1,0:T(8,128)(2,1)S(1)} %get-tuple-element.30), channel_id=1, source_target_pairs={{0,16},{8,24},{16,0},{24,8},{1,17},{9,25},{17,1},{25,9},{2,18},{10... | collective-permute-start | bytes 786440 | tf_op jit(solution)/shard_map/ppermute | solution.py:284
  107.3 14.1 %collective-permute-done.11.refs_1_ = bf16[512,256]{1,0:T(8,128)(2,1)S(1)} collective-permute-done((bf16[512,256]{1,0:T(8,128)(2,1)S(1)}, bf16[512,256]{1,0:T(8,128)(2,1)S(1)}, u32[]{:S(2)}, u32[]{:S(2)}) %collective-permute-start.11) | collective-permute-done | bytes 262176 | tf_op jit(solution)/shard_map/ppermute | solution.py:284
  121.3 7.1 %shard_map.76.refs_0_ = bf16[512,256]{1,0:T(8,128)(2,1)S(1)} custom-call(s32[21]{0:T(128)S(1)} %pad_add_fusion.7.place_ref, f32[512,128]{1,0:T(8,128)S(1)} %get-tuple-element.62.cos_ref, f32[512,128]{1,0:T(8,128)S(1)} %copy-done.6, bf16[512,256]{1,0:T(8,128)(2,1)S(1)} %get-tuple-element.21.refs_0_, bf16[512,256]{1,0:T(8,128)(2,1)S(1)} %collective-permute-done.11.refs_1_, ...), custom_call_target="tpu_custom_call" | custom-call | flops 8589934592 | bytes 2097236 | tf_op jit(solution)/shard_map/pallas_call | solution.py:18
  129.9 7.0 %shard_map.78.refs_0_ = bf16[512,256]{1,0:T(8,128)(2,1)S(1)} custom-call(s32[21]{0:T(128)S(1)} %pad_add_fusion.7.place_ref, f32[512,128]{1,0:T(8,128)S(1)} %get-tuple-element.62.cos_ref, f32[512,128]{1,0:T(8,128)S(1)} %copy-done.6, bf16[512,256]{1,0:T(8,128)(2,1)S(1)} %get-tuple-element.29.refs_0_, bf16[512,256]{1,0:T(8,128)(2,1)S(1)} %collective-permute-done.25.refs_1_, ...), custom_call_target="tpu_custom_call" | custom-call | flops 8589934592 | bytes 2097236 | tf_op jit(solution)/shard_map/pallas_call | solution.py:18
  138.8 4.3 %collective-permute-done.28.refs_3_ = bf16[512,256]{1,0:T(8,128)(2,1)S(1)} collective-permute-done((bf16[512,256]{1,0:T(8,128)(2,1)S(1)}, bf16[512,256]{1,0:T(8,128)(2,1)S(1)}, u32[]{:S(2)}, u32[]{:S(2)}) %collective-permute-start.28) | collective-permute-done | bytes 262176 | tf_op jit(solution)/shard_map/ppermute | solution.py:289
  143.0 4.0 %collective-permute-start.20 = (bf16[512,256]{1,0:T(8,128)(2,1)S(1)}, bf16[512,256]{1,0:T(8,128)(2,1)S(1)}, u32[]{:S(2)}, u32[]{:S(2)}) collective-permute-start(bf16[512,256]{1,0:T(8,128)(2,1)S(1)} %shard_map.76.refs_0_), channel_id=1, source_target_pairs={{0,24},{8,0},{16,8},{24,16},{1,25},{9,1},{17,9},{25,17},{2,26},{10... | collective-permute-start | bytes 786440 | tf_op jit(solution)/shard_map/ppermute | solution.py:289
  147.4 11.5 %collective-permute-done.27.refs_2_ = bf16[512,256]{1,0:T(8,128)(2,1)S(1)} collective-permute-done((bf16[512,256]{1,0:T(8,128)(2,1)S(1)}, bf16[512,256]{1,0:T(8,128)(2,1)S(1)}, u32[]{:S(2)}, u32[]{:S(2)}) %collective-permute-start.27) | collective-permute-done | bytes 262176 | tf_op jit(solution)/shard_map/ppermute | solution.py:289
  159.0 1.8 shard_map.79
  160.8 20.6 %collective-permute-done.19.refs_2_ = bf16[512,256]{1,0:T(8,128)(2,1)S(1)} collective-permute-done((bf16[512,256]{1,0:T(8,128)(2,1)S(1)}, bf16[512,256]{1,0:T(8,128)(2,1)S(1)}, u32[]{:S(2)}, u32[]{:S(2)}) %collective-permute-start.19) | collective-permute-done | bytes 262176 | tf_op jit(solution)/shard_map/ppermute | solution.py:289
  181.4 1.9 shard_map.80
  183.3 2.0 collective-permute-start.29
  185.4 1.5 collective-permute-done.29
  187.2 5.4 %collective-permute-start.30 = (bf16[128,1024]{1,0:T(8,128)(2,1)S(1)}, bf16[128,1024]{1,0:T(8,128)(2,1)S(1)}, u32[]{:S(2)}, u32[]{:S(2)}) collective-permute-start(bf16[128,1024]{1,0:T(8,128)(2,1)S(1)} %get-tuple-element.45), channel_id=1, source_target_pairs={{0,0},{1,16},{8,8},{9,24},{16,1},{17,17},{24,9},{25,25},{2,2},{3,1... | collective-permute-start | bytes 786440 | tf_op jit(solution)/shard_map/ppermute | solution.py:360
  192.8 9.4 %collective-permute-done.30 = bf16[128,1024]{1,0:T(8,128)(2,1)S(1)} collective-permute-done((bf16[128,1024]{1,0:T(8,128)(2,1)S(1)}, bf16[128,1024]{1,0:T(8,128)(2,1)S(1)}, u32[]{:S(2)}, u32[]{:S(2)}) %collective-permute-start.30) | collective-permute-done | bytes 262176 | tf_op jit(solution)/shard_map/ppermute | solution.py:360
  (95 shorter events, 28.5 us)
Async XLA Ops:
  1.2 8.2 %collective-permute-start.4 = (bf16[256,512]{1,0:T(8,128)(2,1)S(1)}, bf16[256,512]{1,0:T(8,128)(2,1)S(1)}, u32[]{:S(2)}, u32[]{:S(2)}) collective-permute-start(bf16[256,512]{1,0:T(8,128)(2,1)S(1)} %pad_maximum_fusion.6), channel_id=1, source_target_pairs={{0,8},{8,0},{16,24},{24,16},{1,9},{9,1},{17,25},{25,17},{2,10},{10... | collective-permute-start | bytes 786440 | tf_op jit(solution)/shard_map/ppermute | solution.py:284
  4.3 23.3 %collective-permute-start.3 = (bf16[256,1024]{1,0:T(8,128)(2,1)S(1)}, bf16[256,1024]{1,0:T(8,128)(2,1)}, u32[]{:S(2)}, u32[]{:S(2)}) collective-permute-start(bf16[256,1024]{1,0:T(8,128)(2,1)S(1)} %pad_maximum_fusion.1), channel_id=1, source_target_pairs={{0,8},{8,0},{16,24},{24,16},{1,9},{9,1},{17,25},{25,17},{2,10},{10... | collective-permute-start | bytes 1572872 | tf_op jit(solution)/shard_map/ppermute | solution.py:284
  9.5 19.3 %collective-permute-start.6 = (bf16[512,512]{1,0:T(8,128)(2,1)S(1)}, bf16[512,512]{1,0:T(8,128)(2,1)S(1)}, u32[]{:S(2)}, u32[]{:S(2)}) collective-permute-start(bf16[512,512]{1,0:T(8,128)(2,1)S(1)} %pad_maximum_fusion.2.refs_4_), channel_id=1, source_target_pairs={{0,4},{2,6},{4,0},{6,2},{1,5},{3,7},{5,1},{7,3},{8,12},{10,14},{12... | collective-permute-start | bytes 1572872 | tf_op jit(solution)/shard_map/ppermute | solution.py:271
  10.7 18.9 %collective-permute-start.5 = (bf16[512,512]{1,0:T(8,128)(2,1)S(1)}, bf16[512,512]{1,0:T(8,128)(2,1)}, u32[]{:S(2)}, u32[]{:S(2)}) collective-permute-start(bf16[512,512]{1,0:T(8,128)(2,1)S(1)} %pad_maximum_fusion.2.refs_4_), channel_id=1, source_target_pairs={{0,2},{2,0},{4,6},{6,4},{1,3},{3,1},{5,7},{7,5},{8,10},{10,8},{12,... | collective-permute-start | bytes 1572872 | tf_op jit(solution)/shard_map/ppermute | solution.py:271
  13.1 22.6 %collective-permute-start.1 = (bf16[128,2048]{1,0:T(8,128)(2,1)}, bf16[128,2048]{1,0:T(8,128)(2,1)S(1)}, u32[]{:S(2)}, u32[]{:S(2)}) collective-permute-start(bf16[128,2048]{1,0:T(8,128)(2,1)} %get-tuple-element.41), channel_id=1, source_target_pairs={{0,16},{8,24},{16,0},{24,8},{1,17},{9,25},{17,1},{25,9},{2,18},{10... | collective-permute-start | bytes 1572872 | tf_op jit(solution)/shard_map/ppermute | solution.py:284
  29.6 38.6 %collective-permute-start.8 = (bf16[512,1024]{1,0:T(8,128)(2,1)S(1)}, bf16[512,1024]{1,0:T(8,128)(2,1)S(1)}, u32[]{:S(2)}, u32[]{:S(2)}) collective-permute-start(bf16[512,1024]{1,0:T(8,128)(2,1)S(1)} %pad_maximum_fusion.refs_4_), channel_id=1, source_target_pairs={{0,4},{2,6},{4,0},{6,2},{1,5},{3,7},{5,1},{7,3},{8,12},{10,14},{12... | collective-permute-start | bytes 3145736 | tf_op jit(solution)/shard_map/ppermute | solution.py:271
  31.7 37.6 %collective-permute-start.7 = (bf16[512,1024]{1,0:T(8,128)(2,1)S(1)}, bf16[512,1024]{1,0:T(8,128)(2,1)}, u32[]{:S(2)}, u32[]{:S(2)}) collective-permute-start(bf16[512,1024]{1,0:T(8,128)(2,1)S(1)} %pad_maximum_fusion.refs_4_), channel_id=1, source_target_pairs={{0,2},{2,0},{4,6},{6,4},{1,3},{3,1},{5,7},{7,5},{8,10},{10,8},{12,... | collective-permute-start | bytes 3145736 | tf_op jit(solution)/shard_map/ppermute | solution.py:271
  33.7 17.0 %collective-permute-start = (bf16[128,2048]{1,0:T(8,128)(2,1)S(1)}, bf16[128,2048]{1,0:T(8,128)(2,1)}, u32[]{:S(2)}, u32[]{:S(2)}) collective-permute-start(bf16[128,2048]{1,0:T(8,128)(2,1)S(1)} %get-tuple-element.42.refs_0_), channel_id=1, source_target_pairs={{0,8},{8,0},{16,24},{24,16},{1,9},{9,1},{17,25},{25,17},{2,10},{10... | collective-permute-start | bytes 1572872 | tf_op jit(solution)/shard_map/ppermute | solution.py:284
  35.7 26.2 %collective-permute-start.2 = (bf16[128,2048]{1,0:T(8,128)(2,1)S(1)}, bf16[128,2048]{1,0:T(8,128)(2,1)}, u32[]{:S(2)}, u32[]{:S(2)}) collective-permute-start(bf16[128,2048]{1,0:T(8,128)(2,1)S(1)} %collective-permute-done.1.refs_2_), channel_id=1, source_target_pairs={{0,8},{8,0},{16,24},{24,16},{1,9},{9,1},{17,25},{25,17},{2,10},{10... | collective-permute-start | bytes 1572872 | tf_op jit(solution)/shard_map/ppermute | solution.py:284
  38.3 22.7 %collective-permute-start.12 = (bf16[256,512]{1,0:T(8,128)(2,1)}, bf16[256,512]{1,0:T(8,128)(2,1)S(1)}, u32[]{:S(2)}, u32[]{:S(2)}) collective-permute-start(bf16[256,512]{1,0:T(8,128)(2,1)} %slice.26), channel_id=1, source_target_pairs={{0,2},{2,0},{4,6},{6,4},{1,3},{3,1},{5,7},{7,5},{8,10},{10,8},{12,... | collective-permute-start | bytes 786440 | tf_op jit(solution)/shard_map/ppermute | solution.py:271
  50.7 10.3 %collective-permute-start.13 = (bf16[256,512]{1,0:T(8,128)(2,1)}, bf16[256,512]{1,0:T(8,128)(2,1)}, u32[]{:S(2)}, u32[]{:S(2)}) collective-permute-start(bf16[256,512]{1,0:T(8,128)(2,1)} %slice.27), channel_id=1, source_target_pairs={{0,4},{2,6},{4,0},{6,2},{1,5},{3,7},{5,1},{7,3},{8,12},{10,14},{12... | collective-permute-start | bytes 786440 | tf_op jit(solution)/shard_map/ppermute | solution.py:271
  66.9 13.8 %collective-permute-start.14 = (bf16[512,256]{1,0:T(8,128)(2,1)S(1)}, bf16[512,256]{1,0:T(8,128)(2,1)S(1)}, u32[]{:S(2)}, u32[]{:S(2)}) collective-permute-start(bf16[512,256]{1,0:T(8,128)(2,1)S(1)} %get-tuple-element.24), channel_id=1, source_target_pairs={{0,16},{8,24},{16,0},{24,8},{1,17},{9,25},{17,1},{25,9},{2,18},{10... | collective-permute-start | bytes 786440 | tf_op jit(solution)/shard_map/ppermute | solution.py:284
  69.0 27.1 %collective-permute-start.9 = (bf16[256,1024]{1,0:T(8,128)(2,1)}, bf16[256,1024]{1,0:T(8,128)(2,1)}, u32[]{:S(2)}, u32[]{:S(2)}) collective-permute-start(bf16[256,1024]{1,0:T(8,128)(2,1)} %slice.24), channel_id=1, source_target_pairs={{0,2},{2,0},{4,6},{6,4},{1,3},{3,1},{5,7},{7,5},{8,10},{10,8},{12,... | collective-permute-start | bytes 1572872 | tf_op jit(solution)/shard_map/ppermute | solution.py:271
  71.2 25.0 %collective-permute-start.10 = (bf16[256,1024]{1,0:T(8,128)(2,1)}, bf16[256,1024]{1,0:T(8,128)(2,1)}, u32[]{:S(2)}, u32[]{:S(2)}) collective-permute-start(bf16[256,1024]{1,0:T(8,128)(2,1)} %slice.25), channel_id=1, source_target_pairs={{0,4},{2,6},{4,0},{6,2},{1,5},{3,7},{5,1},{7,3},{8,12},{10,14},{12... | collective-permute-start | bytes 1572872 | tf_op jit(solution)/shard_map/ppermute | solution.py:271
  82.2 7.6 %collective-permute-start.17 = (bf16[512,256]{1,0:T(8,128)(2,1)}, bf16[512,256]{1,0:T(8,128)(2,1)}, u32[]{:S(2)}, u32[]{:S(2)}) collective-permute-start(bf16[512,256]{1,0:T(8,128)(2,1)} %shard_map.75.refs_2_), channel_id=1, source_target_pairs={{0,6},{2,4},{4,2},{6,0},{1,7},{3,5},{5,3},{7,1},{8,14},{10,12},{12... | collective-permute-start | bytes 786440 | tf_op jit(solution)/shard_map/ppermute | solution.py:271
  82.6 13.6 %collective-permute-start.16 = (bf16[512,256]{1,0:T(8,128)(2,1)}, bf16[512,256]{1,0:T(8,128)(2,1)}, u32[]{:S(2)}, u32[]{:S(2)}) collective-permute-start(bf16[512,256]{1,0:T(8,128)(2,1)} %shard_map.75.refs_2_), channel_id=1, source_target_pairs={{0,4},{2,6},{4,0},{6,2},{1,5},{3,7},{5,1},{7,3},{8,12},{10,14},{12... | collective-permute-start | bytes 786440 | tf_op jit(solution)/shard_map/ppermute | solution.py:271
  83.7 12.4 %collective-permute-start.15 = (bf16[512,256]{1,0:T(8,128)(2,1)}, bf16[512,256]{1,0:T(8,128)(2,1)}, u32[]{:S(2)}, u32[]{:S(2)}) collective-permute-start(bf16[512,256]{1,0:T(8,128)(2,1)} %shard_map.75.refs_2_), channel_id=1, source_target_pairs={{0,2},{2,0},{4,6},{6,4},{1,3},{3,1},{5,7},{7,5},{8,10},{10,8},{12,... | collective-permute-start | bytes 786440 | tf_op jit(solution)/shard_map/ppermute | solution.py:271
  96.1 32.4 %collective-permute-start.22 = (bf16[2048,256]{1,0:T(8,128)(2,1)}, bf16[2048,256]{1,0:T(8,128)(2,1)S(1)}, u32[]{:S(2)}, u32[]{:S(2)}) collective-permute-start(bf16[2048,256]{1,0:T(8,128)(2,1)} %refs_4_.1), channel_id=1, source_target_pairs={{0,4},{2,6},{4,0},{6,2},{1,5},{3,7},{5,1},{7,3},{8,12},{10,14},{12... | collective-permute-start | bytes 3145736 | tf_op jit(solution)/shard_map/ppermute | solution.py:271
  97.6 30.9 %collective-permute-start.21 = (bf16[2048,256]{1,0:T(8,128)(2,1)}, bf16[2048,256]{1,0:T(8,128)(2,1)S(1)}, u32[]{:S(2)}, u32[]{:S(2)}) collective-permute-start(bf16[2048,256]{1,0:T(8,128)(2,1)} %refs_4_.1), channel_id=1, source_target_pairs={{0,2},{2,0},{4,6},{6,4},{1,3},{3,1},{5,7},{7,5},{8,10},{10,8},{12,... | collective-permute-start | bytes 3145736 | tf_op jit(solution)/shard_map/ppermute | solution.py:271
  101.4 19.9 %collective-permute-start.11 = (bf16[512,256]{1,0:T(8,128)(2,1)S(1)}, bf16[512,256]{1,0:T(8,128)(2,1)S(1)}, u32[]{:S(2)}, u32[]{:S(2)}) collective-permute-start(bf16[512,256]{1,0:T(8,128)(2,1)S(1)} %get-tuple-element.22), channel_id=1, source_target_pairs={{0,16},{8,24},{16,0},{24,8},{1,17},{9,25},{17,1},{25,9},{2,18},{10... | collective-permute-start | bytes 786440 | tf_op jit(solution)/shard_map/ppermute | solution.py:284
  104.9 25.0 %collective-permute-start.25 = (bf16[512,256]{1,0:T(8,128)(2,1)S(1)}, bf16[512,256]{1,0:T(8,128)(2,1)S(1)}, u32[]{:S(2)}, u32[]{:S(2)}) collective-permute-start(bf16[512,256]{1,0:T(8,128)(2,1)S(1)} %get-tuple-element.30), channel_id=1, source_target_pairs={{0,16},{8,24},{16,0},{24,8},{1,17},{9,25},{17,1},{25,9},{2,18},{10... | collective-permute-start | bytes 786440 | tf_op jit(solution)/shard_map/ppermute | solution.py:284
  128.6 18.5 %collective-permute-start.23 = (bf16[1024,256]{1,0:T(8,128)(2,1)S(1)}, bf16[1024,256]{1,0:T(8,128)(2,1)S(1)}, u32[]{:S(2)}, u32[]{:S(2)}) collective-permute-start(bf16[1024,256]{1,0:T(8,128)(2,1)S(1)} %slice.22), channel_id=1, source_target_pairs={{0,2},{2,0},{4,6},{6,4},{1,3},{3,1},{5,7},{7,5},{8,10},{10,8},{12,... | collective-permute-start | bytes 1572872 | tf_op jit(solution)/shard_map/ppermute | solution.py:271
  129.1 18.0 %collective-permute-start.24 = (bf16[1024,256]{1,0:T(8,128)(2,1)S(1)}, bf16[1024,256]{1,0:T(8,128)(2,1)S(1)}, u32[]{:S(2)}, u32[]{:S(2)}) collective-permute-start(bf16[1024,256]{1,0:T(8,128)(2,1)S(1)} %slice.23), channel_id=1, source_target_pairs={{0,4},{2,6},{4,0},{6,2},{1,5},{3,7},{5,1},{7,3},{8,12},{10,14},{12... | collective-permute-start | bytes 1572872 | tf_op jit(solution)/shard_map/ppermute | solution.py:271
  136.9 6.2 %collective-permute-start.28 = (bf16[512,256]{1,0:T(8,128)(2,1)S(1)}, bf16[512,256]{1,0:T(8,128)(2,1)S(1)}, u32[]{:S(2)}, u32[]{:S(2)}) collective-permute-start(bf16[512,256]{1,0:T(8,128)(2,1)S(1)} %shard_map.78.refs_0_), channel_id=1, source_target_pairs={{0,24},{8,0},{16,8},{24,16},{1,25},{9,1},{17,9},{25,17},{2,26},{10... | collective-permute-start | bytes 786440 | tf_op jit(solution)/shard_map/ppermute | solution.py:289
  138.4 20.6 %collective-permute-start.27 = (bf16[512,256]{1,0:T(8,128)(2,1)S(1)}, bf16[512,256]{1,0:T(8,128)(2,1)S(1)}, u32[]{:S(2)}, u32[]{:S(2)}) collective-permute-start(bf16[512,256]{1,0:T(8,128)(2,1)S(1)} %shard_map.78.refs_0_), channel_id=1, source_target_pairs={{0,16},{8,24},{16,0},{24,8},{1,17},{9,25},{17,1},{25,9},{2,18},{10... | collective-permute-start | bytes 786440 | tf_op jit(solution)/shard_map/ppermute | solution.py:289
  138.4 20.6 %collective-permute-start.26 = (bf16[512,256]{1,0:T(8,128)(2,1)S(1)}, bf16[512,256]{1,0:T(8,128)(2,1)S(1)}, u32[]{:S(2)}, u32[]{:S(2)}) collective-permute-start(bf16[512,256]{1,0:T(8,128)(2,1)S(1)} %shard_map.78.refs_0_), channel_id=1, source_target_pairs={{0,8},{8,16},{16,24},{24,0},{1,9},{9,17},{17,25},{25,1},{2,10},{10... | collective-permute-start | bytes 786440 | tf_op jit(solution)/shard_map/ppermute | solution.py:289
  143.0 17.8 %collective-permute-start.20 = (bf16[512,256]{1,0:T(8,128)(2,1)S(1)}, bf16[512,256]{1,0:T(8,128)(2,1)S(1)}, u32[]{:S(2)}, u32[]{:S(2)}) collective-permute-start(bf16[512,256]{1,0:T(8,128)(2,1)S(1)} %shard_map.76.refs_0_), channel_id=1, source_target_pairs={{0,24},{8,0},{16,8},{24,16},{1,25},{9,1},{17,9},{25,17},{2,26},{10... | collective-permute-start | bytes 786440 | tf_op jit(solution)/shard_map/ppermute | solution.py:289
  147.1 34.4 %collective-permute-start.19 = (bf16[512,256]{1,0:T(8,128)(2,1)S(1)}, bf16[512,256]{1,0:T(8,128)(2,1)S(1)}, u32[]{:S(2)}, u32[]{:S(2)}) collective-permute-start(bf16[512,256]{1,0:T(8,128)(2,1)S(1)} %shard_map.76.refs_0_), channel_id=1, source_target_pairs={{0,16},{8,24},{16,0},{24,8},{1,17},{9,25},{17,1},{25,9},{2,18},{10... | collective-permute-start | bytes 786440 | tf_op jit(solution)/shard_map/ppermute | solution.py:289
  147.1 34.4 %collective-permute-start.18 = (bf16[512,256]{1,0:T(8,128)(2,1)S(1)}, bf16[512,256]{1,0:T(8,128)(2,1)S(1)}, u32[]{:S(2)}, u32[]{:S(2)}) collective-permute-start(bf16[512,256]{1,0:T(8,128)(2,1)S(1)} %shard_map.76.refs_0_), channel_id=1, source_target_pairs={{0,8},{8,16},{16,24},{24,0},{1,9},{9,17},{17,25},{25,1},{2,10},{10... | collective-permute-start | bytes 786440 | tf_op jit(solution)/shard_map/ppermute | solution.py:289
  183.3 3.6 %collective-permute-start.29 = (bf16[256,1024]{1,0:T(8,128)(2,1)S(1)}, bf16[256,1024]{1,0:T(8,128)(2,1)S(1)}, u32[]{:S(2)}, u32[]{:S(2)}) collective-permute-start(bf16[256,1024]{1,0:T(8,128)(2,1)S(1)} %get-tuple-element.34), channel_id=1, source_target_pairs={{0,1},{1,0},{2,3},{3,2},{4,5},{5,4},{6,7},{7,6},{8,9},{9,8},{10,11... | collective-permute-start | bytes 1572872 | tf_op jit(solution)/shard_map/ppermute | solution.py:353
  187.2 15.0 %collective-permute-start.30 = (bf16[128,1024]{1,0:T(8,128)(2,1)S(1)}, bf16[128,1024]{1,0:T(8,128)(2,1)S(1)}, u32[]{:S(2)}, u32[]{:S(2)}) collective-permute-start(bf16[128,1024]{1,0:T(8,128)(2,1)S(1)} %get-tuple-element.45), channel_id=1, source_target_pairs={{0,0},{1,16},{8,8},{9,24},{16,1},{17,17},{24,9},{25,25},{2,2},{3,1... | collective-permute-start | bytes 786440 | tf_op jit(solution)/shard_map/ppermute | solution.py:360
  192.5 9.7 %collective-permute-start.31 = (bf16[128,1024]{1,0:T(8,128)(2,1)S(1)}, bf16[128,1024]{1,0:T(8,128)(2,1)S(1)}, u32[]{:S(2)}, u32[]{:S(2)}) collective-permute-start(bf16[128,1024]{1,0:T(8,128)(2,1)S(1)} %get-tuple-element.46), channel_id=1, source_target_pairs={{0,8},{1,24},{8,0},{9,16},{16,9},{17,25},{24,1},{25,17},{2,10},{3,... | collective-permute-start | bytes 786440 | tf_op jit(solution)/shard_map/ppermute | solution.py:360
  (12 other events, 79.1 us)

commit v8 on v7

--- a/solution.py
+++ b/solution.py
@@ -143,16 +143,23 @@
 
 
 def product_kernel(place_ref, *refs):
-    token_refs, weight_refs, out_refs, gathered = refs[:4], refs[4:9], refs[9:11], refs[11]
+    own_ref, half_refs = refs[0], refs[1:3]
+    weight_refs, out_refs, gathered = refs[3:8], refs[8:10], refs[10]
     hi = place_ref[0]
     lo = place_ref[1]
-    rows = token_refs[0].shape[0]
+    rows, depth = own_ref.shape
     share = weight_refs[3].shape[0]
-    for d, token_ref in enumerate(token_refs):
-        gathered[pl.ds(pl.multiple_of((hi ^ d) * rows, rows), rows), :] = token_ref[...]
+    gathered[pl.ds(pl.multiple_of(hi * rows, rows), rows), :] = own_ref[...]
+    for side, half_ref in enumerate(half_refs):
+        first = lax.rem(place_ref[2] + side, 2) * (depth // 2)
+        features = pl.ds(pl.multiple_of(first, depth // 2), depth // 2)
+        for d in range(1, 4):
+            gathered[pl.ds(pl.multiple_of((hi ^ d) * rows, rows), rows), features] = half_ref[
+                pl.ds((d - 1) * rows, rows), :
+            ]
     for side, out_ref in enumerate(out_refs):
         width = out_ref.shape[1]
-        first = (lax.div(hi, 2) ^ side) * place_ref[2] + place_ref[3]
+        first = (lax.div(hi, 2) ^ side) * place_ref[3] + place_ref[4]
         columns = pl.ds(pl.multiple_of(first, width), width)
         total = 0.0
         for part in range(2):
@@ -170,11 +177,11 @@
         out_ref[...] = total.astype(jnp.bfloat16)
 
 
-def product(hi, lo, token_parts, weights, chunk, chunks):
+def product(index, token_parts, weights, chunk, chunks):
     rows, depth = token_parts[0].shape
     step = weights[0].shape[1] // 2
     width = step // chunks
-    place = jnp.stack([hi, lo, jnp.full((), step, jnp.int32), jnp.full((), chunk * width, jnp.int32)])
+    place = jnp.concatenate([index, jnp.array([step, chunk * width], jnp.int32)])
     shape = jax.ShapeDtypeStruct((4 * rows, width), jnp.bfloat16)
     return local_kernel(
         product_kernel,
@@ -316,26 +323,32 @@
     for sources, size in (((w_key, w_value), HD), ((w_query,), heads)):
         came = along(columns_for(1 - which, sources, size), 1)
         both = jnp.concatenate([columns_for(which, sources, size), came], axis=0)
-        stage = sides(after(both, *stage) if stage else both)
-        weights.append(corner(stage))
-        stage = stage[1:]
+        weights.append(corner(sides(after(both, *stage) if stage else both)))
+        stage = weights[-1][3:]
 
     normed = normalised(tokens, norm_gain)
     own = lax.dynamic_slice_in_dim(normed, which_half * depth, depth, 1)
-    other = along(lax.dynamic_slice_in_dim(normed, (1 - which_half) * depth, depth, 1), 2)
-    token_parts = [own, along(own, 1), other, along(other, 1)]
+
+    def core_half(z):
+        return lax.dynamic_slice_in_dim(normed, z * depth + core * (depth // 2), depth // 2, 1)
+
+    near = along(core_half(which_half), 1)
+    other = along(core_half(1 - which_half), 2)
+    halves = jnp.concatenate([near, other, along(after(other, near), 1)], axis=0)
+    token_parts = [own, halves, lax.ppermute(halves, "head", [(0, 1), (1, 0)])]
+    index = jnp.stack([hi, lo, core])
 
     row_index = jnp.arange(4 * rows, dtype=jnp.int32)
     cosine, sine = rotary_tables((row_index // rows * 4 + lo) * rows + row_index % rows)
 
-    kept, sent = product(hi, lo, token_parts, weights[0], 0, 1)
+    kept, sent = product(index, token_parts, weights[0], 0, 1)
     kv_own = finish_pair(cosine, sine, [kept, along(sent, 2)])
     kv_parts = [kv_own] + [beside(kv_own, r) for r in range(1, 4)]
 
     firsts = jnp.stack([lo, lo, lo ^ 1, lo ^ 2, lo ^ 3]) * rows
     seen = jnp.concatenate([firsts, doc_starts])
     out_sides = sides(after(w_out, *weights[1][3:], *kv_parts[1:]))
-    products = [product(hi, lo, token_parts, weights[1], c, 2) for c in range(2)]
+    products = [product(index, token_parts, weights[1], c, 2) for c in range(2)]
     products[0] = (after(products[0][0], products[1][0]), products[0][1])
     attended = [
         attention(seen, cosine, sine, [kept, along(sent, 2)], kv_parts, 4, 4 * rows)
@@ -346,7 +359,7 @@
     out_blocks[3:] = [jnp.concatenate(out_blocks[3:], axis=0)]
     totals = ()
     for c, kind in enumerate((jnp.float32, jnp.bfloat16)):
-        where = jnp.stack([hi, lo, core, jnp.full((), c * width, jnp.int32)])
+        where = jnp.concatenate([index, jnp.full((1,), c * width, jnp.int32)])
         totals = project(where, round_line(attended[c]), out_blocks, totals, kind)
 
     mine, theirs = totals

time: 205 us -> 194 us (0.946)
  waiting for transfers between devices: 120 us -> 104 us
  starting transfers between devices: 36.2 us -> 44.9 us
  local copies, waits for them, and re-layouts: 13.7 us -> 11.4 us
  Pallas kernels: 28 us -> 25.9 us
    ppermute x8, waiting for transfers between devices: 51.8 us -> 24.7 us  [along(): return lax.ppermute(block, 'hi', [(i, i ^ d) for i in range(4)])]
    ppermute x15, waiting for transfers between devices: 21.2 us -> 30.1 us  [beside(): return lax.ppermute(block, 'lo', [(i, i ^ r) for i in range(4)])]
    slice x6, local copies, waits for them, and re-layouts: 6.13 us -> 3.35 us  [corner(): return [*blocks, beside(blocks[2][:half], 1), beside(blocks[1][half:], 2)]]
    ppermute x8, starting transfers between devices: 9.4 us -> 12 us  [along(): return lax.ppermute(block, 'hi', [(i, i ^ d) for i in range(4)])]
    ppermute x0 -> x1, starting transfers between devices: none -> 2.45 us  [line_device(): token_parts = [own, halves, lax.ppermute(halves, 'head', [(0, 1), (1, 0)])]]
    pallas_call x8, Pallas kernels: 28 us -> 25.9 us  [local_kernel(): pl.pallas_call(body, in_specs=[pl.BlockSpec(memory_space=pltpu.SMEM)] + [...]
    unnamed x25 -> x53, local copies, waits for them, and re-layouts: 4.54 us -> 5.57 us
  transfers between devices with their start and end apart: 32 -> 33, of which waited for: 15 -> 14; matrix products, arithmetic and copies ran while one was open for 6% -> 6% of each run, Pallas kernels for 13% -> 12%
where the time goes in v8:
time: 194 us; the launch traced here: 192 us
  waiting for transfers between devices  104 us (54%)
  starting transfers between devices  44.9 us (23%)
  Pallas kernels  25.9 us (13%)
  local copies, waits for them, and re-layouts  11.4 us (6%)
  other arithmetic  5.43 us (3%)
    ppermute x6, waiting for transfers between devices, round_line(): lax.ppermute(block, 'hi', [(i, (i + d) % 4) for i in range(4)])  36.5 us
    ppermute x15, waiting for transfers between devices, beside(): return lax.ppermute(block, 'lo', [(i, i ^ r) for i in range(4)])  30.1 us
    pallas_call x8, Pallas kernels, local_kernel(): pl.pallas_call(body, in_specs=[pl.BlockSpec(memory_space=pltpu.SMEM)] + [...  25.9 us
    ppermute x8, waiting for transfers between devices, along(): return lax.ppermute(block, 'hi', [(i, i ^ d) for i in range(4)])  24.7 us
    ppermute x15, starting transfers between devices, beside(): return lax.ppermute(block, 'lo', [(i, i ^ r) for i in range(4)])  14.7 us
    ppermute x8, starting transfers between devices, along(): return lax.ppermute(block, 'hi', [(i, i ^ d) for i in range(4)])  12 us
    ppermute x2, waiting for transfers between devices, line_device(): arrived.append(lax.ppermute(piece, ('hi', 'head'), route))  9.45 us
    ppermute x6, starting transfers between devices, round_line(): lax.ppermute(block, 'hi', [(i, (i + d) % 4) for i in range(4)])  8.11 us
  transfers between devices with their start and end apart: 33, of which 14 were waited for; matrix products, arithmetic and copies ran while one was open for 6% of the time, Pallas kernels for 12%

profile of v8, /device:TPU:1, one launch (start us, length us, event | category | flops | bytes accessed | tf_op | source)
XLA Modules:
  0.0 192.1 jit_solution(2813790957085300163)
XLA Ops:
  1.2 2.2 %collective-permute-start.5 = (bf16[256,512]{1,0:T(8,128)(2,1)S(1)}, bf16[256,512]{1,0:T(8,128)(2,1)S(1)}, u32[]{:S(2)}, u32[]{:S(2)}) collective-permute-start(bf16[256,512]{1,0:T(8,128)(2,1)S(1)} %pad_maximum_fusion.6), channel_id=1, source_target_pairs={{0,8},{8,0},{16,24},{24,16},{1,9},{9,1},{17,25},{25,17},{2,10},{10... | collective-permute-start | bytes 786440 | tf_op jit(solution)/shard_map/ppermute | solution.py:291
  5.3 4.2 %collective-permute-done.5 = bf16[256,512]{1,0:T(8,128)(2,1)S(1)} collective-permute-done((bf16[256,512]{1,0:T(8,128)(2,1)S(1)}, bf16[256,512]{1,0:T(8,128)(2,1)S(1)}, u32[]{:S(2)}, u32[]{:S(2)}) %collective-permute-start.5) | collective-permute-done | bytes 262176 | tf_op jit(solution)/shard_map/ppermute | solution.py:291
  13.2 2.3 %collective-permute-start.1 = (bf16[128,1024]{1,0:T(8,128)(2,1)}, bf16[128,1024]{1,0:T(8,128)(2,1)}, u32[]{:S(2)}, u32[]{:S(2)}) collective-permute-start(bf16[128,1024]{1,0:T(8,128)(2,1)} %get-tuple-element.45), channel_id=1, source_target_pairs={{0,16},{8,24},{16,0},{24,8},{1,17},{9,25},{17,1},{25,9},{2,18},{10... | collective-permute-start | bytes 786440 | tf_op jit(solution)/shard_map/ppermute | solution.py:291
  15.5 1.3 collective-permute-start
  16.8 4.2 %collective-permute-done.8.refs_4_ = bf16[512,512]{1,0:T(8,128)(2,1)S(1)} collective-permute-done((bf16[512,512]{1,0:T(8,128)(2,1)S(1)}, bf16[512,512]{1,0:T(8,128)(2,1)S(1)}, u32[]{:S(2)}, u32[]{:S(2)}) %collective-permute-start.8) | collective-permute-done | bytes 524320 | tf_op jit(solution)/shard_map/ppermute | solution.py:278
  25.4 6.6 %collective-permute-done = bf16[128,1024]{1,0:T(8,128)(2,1)} collective-permute-done((bf16[128,1024]{1,0:T(8,128)(2,1)}, bf16[128,1024]{1,0:T(8,128)(2,1)}, u32[]{:S(2)}, u32[]{:S(2)}) %collective-permute-start) | collective-permute-done | bytes 262176 | tf_op jit(solution)/shard_map/ppermute | solution.py:291
  35.6 1.3 collective-permute-start.11
  39.1 2.5 %collective-permute-start.3 = (bf16[384,1024]{1,0:T(8,128)(2,1)S(1)}, bf16[384,1024]{1,0:T(8,128)(2,1)S(1)}, u32[]{:S(2)}, u32[]{:S(2)}) collective-permute-start(bf16[384,1024]{1,0:T(8,128)(2,1)S(1)} %constant_dynamic-update-slice_fusion.refs_1_), channel_id=1, source_target_pairs={{0,1},{1,0},{2,3},{3,2},{4,5},{5,4},{6,7},{7,6},{8,9},{9,8},{10,11... | collective-permute-start | bytes 2359304 | tf_op jit(solution)/shard_map/ppermute | solution.py:338
  41.8 1.7 collective-permute-done.3.refs_2_
  43.5 1.9 shard_map.101
  45.4 2.3 %collective-permute-start.15 = (bf16[512,256]{1,0:T(8,128)(2,1)S(1)}, bf16[512,256]{1,0:T(8,128)(2,1)S(1)}, u32[]{:S(2)}, u32[]{:S(2)}) collective-permute-start(bf16[512,256]{1,0:T(8,128)(2,1)S(1)} %get-tuple-element.26), channel_id=1, source_target_pairs={{0,16},{8,24},{16,0},{24,8},{1,17},{9,25},{17,1},{25,9},{2,18},{10... | collective-permute-start | bytes 786440 | tf_op jit(solution)/shard_map/ppermute | solution.py:291
  47.7 10.7 %collective-permute-done.11.refs_5_ = bf16[512,1024]{1,0:T(8,128)(2,1)S(1)} collective-permute-done((bf16[512,1024]{1,0:T(8,128)(2,1)S(1)}, bf16[512,1024]{1,0:T(8,128)(2,1)S(1)}, u32[]{:S(2)}, u32[]{:S(2)}) %collective-permute-start.11) | collective-permute-done | bytes 1048608 | tf_op jit(solution)/shard_map/ppermute | solution.py:278
  68.2 8.4 %collective-permute-done.18.refs_5_ = bf16[512,256]{1,0:T(8,128)(2,1)} collective-permute-done((bf16[512,256]{1,0:T(8,128)(2,1)}, bf16[512,256]{1,0:T(8,128)(2,1)}, u32[]{:S(2)}, u32[]{:S(2)}) %collective-permute-start.18) | collective-permute-done | bytes 262176 | tf_op jit(solution)/shard_map/ppermute | solution.py:278
  76.6 6.8 %collective-permute-done.17.refs_4_ = bf16[512,256]{1,0:T(8,128)(2,1)} collective-permute-done((bf16[512,256]{1,0:T(8,128)(2,1)}, bf16[512,256]{1,0:T(8,128)(2,1)}, u32[]{:S(2)}, u32[]{:S(2)}) %collective-permute-start.17) | collective-permute-done | bytes 262176 | tf_op jit(solution)/shard_map/ppermute | solution.py:278
  83.4 1.3 collective-permute-start.23
  87.4 2.7 %shard_map.100 = (bf16[512,256]{1,0:T(8,128)(2,1)S(1)}, bf16[512,256]{1,0:T(8,128)(2,1)S(1)}) custom-call(s32[5]{0:T(128)S(1)} %get-tuple-element.63.place_ref, bf16[128,2048]{1,0:T(8,128)(2,1)S(1)} %constant_dynamic-slice_fusion.16.refs_0_, bf16[384,1024]{1,0:T(8,128)(2,1)S(1)} %constant_dynamic-update-slice_fusion.refs_1_, ...), custom_call_target="tpu_custom_call" | custom-call | flops 1073741824 | bytes 6291476 | tf_op jit(solution)/shard_map/pallas_call | solution.py:18
  90.1 2.3 %collective-permute-start.14 = (bf16[512,256]{1,0:T(8,128)(2,1)S(1)}, bf16[512,256]{1,0:T(8,128)(2,1)S(1)}, u32[]{:S(2)}, u32[]{:S(2)}) collective-permute-start(bf16[512,256]{1,0:T(8,128)(2,1)S(1)} %get-tuple-element.24), channel_id=1, source_target_pairs={{0,16},{8,24},{16,0},{24,8},{1,17},{9,25},{17,1},{25,9},{2,18},{10... | collective-permute-start | bytes 786440 | tf_op jit(solution)/shard_map/ppermute | solution.py:291
  92.5 2.6 %shard_map.104 = (bf16[512,256]{1,0:T(8,128)(2,1)S(1)}, bf16[512,256]{1,0:T(8,128)(2,1)S(1)}) custom-call(s32[5]{0:T(128)S(1)} %get-tuple-element.37.place_ref, bf16[128,2048]{1,0:T(8,128)(2,1)S(1)} %constant_dynamic-slice_fusion.16.refs_0_, bf16[384,1024]{1,0:T(8,128)(2,1)S(1)} %constant_dynamic-update-slice_fusion.refs_1_, ...), custom_call_target="tpu_custom_call" | custom-call | flops 1073741824 | bytes 6291476 | tf_op jit(solution)/shard_map/pallas_call | solution.py:18
  95.3 12.7 %collective-permute-done.14.refs_1_ = bf16[512,256]{1,0:T(8,128)(2,1)S(1)} collective-permute-done((bf16[512,256]{1,0:T(8,128)(2,1)S(1)}, bf16[512,256]{1,0:T(8,128)(2,1)S(1)}, u32[]{:S(2)}, u32[]{:S(2)}) %collective-permute-start.14) | collective-permute-done | bytes 262176 | tf_op jit(solution)/shard_map/ppermute | solution.py:291
  108.0 7.1 %shard_map.103.refs_0_ = bf16[512,256]{1,0:T(8,128)(2,1)S(1)} custom-call(s32[21]{0:T(128)S(1)} %pad_add_fusion.2.place_ref, f32[512,128]{1,0:T(8,128)S(1)} %get-tuple-element.64.cos_ref, f32[512,128]{1,0:T(8,128)S(1)} %copy-done.13, bf16[512,256]{1,0:T(8,128)(2,1)S(1)} %get-tuple-element.23.refs_0_, bf16[512,256]{1,0:T(8,128)(2,1)S(1)} %collective-permute-done.14.refs_1_, ...), custom_call_target="tpu_custom_call" | custom-call | flops 8589934592 | bytes 2097236 | tf_op jit(solution)/shard_map/pallas_call | solution.py:18
  116.7 7.0 %shard_map.105.refs_0_ = bf16[512,256]{1,0:T(8,128)(2,1)S(1)} custom-call(s32[21]{0:T(128)S(1)} %pad_add_fusion.2.place_ref, f32[512,128]{1,0:T(8,128)S(1)} %get-tuple-element.64.cos_ref, f32[512,128]{1,0:T(8,128)S(1)} %copy-done.13, bf16[512,256]{1,0:T(8,128)(2,1)S(1)} %get-tuple-element.31.refs_0_, bf16[512,256]{1,0:T(8,128)(2,1)S(1)} %collective-permute-done.26.refs_1_, ...), custom_call_target="tpu_custom_call" | custom-call | flops 8589934592 | bytes 2097236 | tf_op jit(solution)/shard_map/pallas_call | solution.py:18
  123.7 3.7 %collective-permute-start.29 = (bf16[512,256]{1,0:T(8,128)(2,1)S(1)}, bf16[512,256]{1,0:T(8,128)(2,1)S(1)}, u32[]{:S(2)}, u32[]{:S(2)}) collective-permute-start(bf16[512,256]{1,0:T(8,128)(2,1)S(1)} %shard_map.105.refs_0_), channel_id=1, source_target_pairs={{0,24},{8,0},{16,8},{24,16},{1,25},{9,1},{17,9},{25,17},{2,26},{10... | collective-permute-start | bytes 786440 | tf_op jit(solution)/shard_map/ppermute | solution.py:296
  127.8 2.9 %collective-permute-done.29.refs_3_ = bf16[512,256]{1,0:T(8,128)(2,1)S(1)} collective-permute-done((bf16[512,256]{1,0:T(8,128)(2,1)S(1)}, bf16[512,256]{1,0:T(8,128)(2,1)S(1)}, u32[]{:S(2)}, u32[]{:S(2)}) %collective-permute-start.29) | collective-permute-done | bytes 262176 | tf_op jit(solution)/shard_map/ppermute | solution.py:296
  130.7 3.9 %collective-permute-start.21 = (bf16[512,256]{1,0:T(8,128)(2,1)S(1)}, bf16[512,256]{1,0:T(8,128)(2,1)S(1)}, u32[]{:S(2)}, u32[]{:S(2)}) collective-permute-start(bf16[512,256]{1,0:T(8,128)(2,1)S(1)} %shard_map.103.refs_0_), channel_id=1, source_target_pairs={{0,24},{8,0},{16,8},{24,16},{1,25},{9,1},{17,9},{25,17},{2,26},{10... | collective-permute-start | bytes 786440 | tf_op jit(solution)/shard_map/ppermute | solution.py:296
  135.0 11.8 %collective-permute-done.28.refs_2_ = bf16[512,256]{1,0:T(8,128)(2,1)S(1)} collective-permute-done((bf16[512,256]{1,0:T(8,128)(2,1)S(1)}, bf16[512,256]{1,0:T(8,128)(2,1)S(1)}, u32[]{:S(2)}, u32[]{:S(2)}) %collective-permute-start.28) | collective-permute-done | bytes 262176 | tf_op jit(solution)/shard_map/ppermute | solution.py:296
  146.8 1.8 shard_map.106
  148.6 21.7 %collective-permute-done.20.refs_2_ = bf16[512,256]{1,0:T(8,128)(2,1)S(1)} collective-permute-done((bf16[512,256]{1,0:T(8,128)(2,1)S(1)}, bf16[512,256]{1,0:T(8,128)(2,1)S(1)}, u32[]{:S(2)}, u32[]{:S(2)}) %collective-permute-start.20) | collective-permute-done | bytes 262176 | tf_op jit(solution)/shard_map/ppermute | solution.py:296
  170.4 1.9 shard_map.107
  172.3 2.9 %collective-permute-start.30 = (bf16[256,1024]{1,0:T(8,128)(2,1)S(1)}, bf16[256,1024]{1,0:T(8,128)(2,1)S(1)}, u32[]{:S(2)}, u32[]{:S(2)}) collective-permute-start(bf16[256,1024]{1,0:T(8,128)(2,1)S(1)} %get-tuple-element.36), channel_id=1, source_target_pairs={{0,1},{1,0},{2,3},{3,2},{4,5},{5,4},{6,7},{7,6},{8,9},{9,8},{10,11... | collective-permute-start | bytes 1572872 | tf_op jit(solution)/shard_map/ppermute | solution.py:366
  175.2 1.5 collective-permute-done.30
  177.0 4.5 %collective-permute-start.31 = (bf16[128,1024]{1,0:T(8,128)(2,1)S(1)}, bf16[128,1024]{1,0:T(8,128)(2,1)S(1)}, u32[]{:S(2)}, u32[]{:S(2)}) collective-permute-start(bf16[128,1024]{1,0:T(8,128)(2,1)S(1)} %get-tuple-element.49), channel_id=1, source_target_pairs={{0,0},{1,16},{8,8},{9,24},{16,1},{17,17},{24,9},{25,25},{2,2},{3,1... | collective-permute-start | bytes 786440 | tf_op jit(solution)/shard_map/ppermute | solution.py:373
  181.8 9.5 %collective-permute-done.31 = bf16[128,1024]{1,0:T(8,128)(2,1)S(1)} collective-permute-done((bf16[128,1024]{1,0:T(8,128)(2,1)S(1)}, bf16[128,1024]{1,0:T(8,128)(2,1)S(1)}, u32[]{:S(2)}, u32[]{:S(2)}) %collective-permute-start.31) | collective-permute-done | bytes 262176 | tf_op jit(solution)/shard_map/ppermute | solution.py:373
  (129 shorter events, 33.4 us)
Async XLA Ops:
  1.2 8.2 %collective-permute-start.5 = (bf16[256,512]{1,0:T(8,128)(2,1)S(1)}, bf16[256,512]{1,0:T(8,128)(2,1)S(1)}, u32[]{:S(2)}, u32[]{:S(2)}) collective-permute-start(bf16[256,512]{1,0:T(8,128)(2,1)S(1)} %pad_maximum_fusion.6), channel_id=1, source_target_pairs={{0,8},{8,0},{16,24},{24,16},{1,9},{9,1},{17,25},{25,17},{2,10},{10... | collective-permute-start | bytes 786440 | tf_op jit(solution)/shard_map/ppermute | solution.py:291
  4.4 29.8 %collective-permute-start.4 = (bf16[256,1024]{1,0:T(8,128)(2,1)}, bf16[256,1024]{1,0:T(8,128)(2,1)}, u32[]{:S(2)}, u32[]{:S(2)}) collective-permute-start(bf16[256,1024]{1,0:T(8,128)(2,1)} %pad_maximum_fusion.1), channel_id=1, source_target_pairs={{0,8},{8,0},{16,24},{24,16},{1,9},{9,1},{17,25},{25,17},{2,10},{10... | collective-permute-start | bytes 1572872 | tf_op jit(solution)/shard_map/ppermute | solution.py:291
  9.5 11.5 %collective-permute-start.8 = (bf16[512,512]{1,0:T(8,128)(2,1)S(1)}, bf16[512,512]{1,0:T(8,128)(2,1)S(1)}, u32[]{:S(2)}, u32[]{:S(2)}) collective-permute-start(bf16[512,512]{1,0:T(8,128)(2,1)S(1)} %pad_maximum_fusion.2.refs_3_), channel_id=1, source_target_pairs={{0,2},{2,0},{4,6},{6,4},{1,3},{3,1},{5,7},{7,5},{8,10},{10,8},{12,... | collective-permute-start | bytes 1572872 | tf_op jit(solution)/shard_map/ppermute | solution.py:278
  10.7 11.6 %collective-permute-start.6 = (bf16[512,512]{1,0:T(8,128)(2,1)S(1)}, bf16[512,512]{1,0:T(8,128)(2,1)S(1)}, u32[]{:S(2)}, u32[]{:S(2)}) collective-permute-start(bf16[512,512]{1,0:T(8,128)(2,1)S(1)} %pad_maximum_fusion.2.refs_3_), channel_id=1, source_target_pairs={{0,4},{2,6},{4,0},{6,2},{1,5},{3,7},{5,1},{7,3},{8,12},{10,14},{12... | collective-permute-start | bytes 1572872 | tf_op jit(solution)/shard_map/ppermute | solution.py:278
  13.2 12.2 %collective-permute-start.1 = (bf16[128,1024]{1,0:T(8,128)(2,1)}, bf16[128,1024]{1,0:T(8,128)(2,1)}, u32[]{:S(2)}, u32[]{:S(2)}) collective-permute-start(bf16[128,1024]{1,0:T(8,128)(2,1)} %get-tuple-element.45), channel_id=1, source_target_pairs={{0,16},{8,24},{16,0},{24,8},{1,17},{9,25},{17,1},{25,9},{2,18},{10... | collective-permute-start | bytes 786440 | tf_op jit(solution)/shard_map/ppermute | solution.py:291
  15.5 16.5 %collective-permute-start = (bf16[128,1024]{1,0:T(8,128)(2,1)}, bf16[128,1024]{1,0:T(8,128)(2,1)}, u32[]{:S(2)}, u32[]{:S(2)}) collective-permute-start(bf16[128,1024]{1,0:T(8,128)(2,1)} %get-tuple-element.46), channel_id=1, source_target_pairs={{0,8},{8,0},{16,24},{24,16},{1,9},{9,1},{17,25},{25,17},{2,10},{10... | collective-permute-start | bytes 786440 | tf_op jit(solution)/shard_map/ppermute | solution.py:291
  21.8 13.7 %collective-permute-start.9 = (bf16[256,512]{1,0:T(8,128)(2,1)}, bf16[256,512]{1,0:T(8,128)(2,1)S(1)}, u32[]{:S(2)}, u32[]{:S(2)}) collective-permute-start(bf16[256,512]{1,0:T(8,128)(2,1)} %slice.25), channel_id=1, source_target_pairs={{0,4},{2,6},{4,0},{6,2},{1,5},{3,7},{5,1},{7,3},{8,12},{10,14},{12... | collective-permute-start | bytes 786440 | tf_op jit(solution)/shard_map/ppermute | solution.py:278
  23.0 12.5 %collective-permute-start.7 = (bf16[256,512]{1,0:T(8,128)(2,1)}, bf16[256,512]{1,0:T(8,128)(2,1)S(1)}, u32[]{:S(2)}, u32[]{:S(2)}) collective-permute-start(bf16[256,512]{1,0:T(8,128)(2,1)} %slice.24), channel_id=1, source_target_pairs={{0,2},{2,0},{4,6},{6,4},{1,3},{3,1},{5,7},{7,5},{8,10},{10,8},{12,... | collective-permute-start | bytes 786440 | tf_op jit(solution)/shard_map/ppermute | solution.py:278
  32.0 7.0 %collective-permute-start.2 = (bf16[128,1024]{1,0:T(8,128)(2,1)}, bf16[128,1024]{1,0:T(8,128)(2,1)S(1)}, u32[]{:S(2)}, u32[]{:S(2)}) collective-permute-start(bf16[128,1024]{1,0:T(8,128)(2,1)} %collective-permute-done.1), channel_id=1, source_target_pairs={{0,8},{8,0},{16,24},{24,16},{1,9},{9,1},{17,25},{25,17},{2,10},{10... | collective-permute-start | bytes 786440 | tf_op jit(solution)/shard_map/ppermute | solution.py:291
  35.6 22.9 %collective-permute-start.11 = (bf16[512,1024]{1,0:T(8,128)(2,1)S(1)}, bf16[512,1024]{1,0:T(8,128)(2,1)S(1)}, u32[]{:S(2)}, u32[]{:S(2)}) collective-permute-start(bf16[512,1024]{1,0:T(8,128)(2,1)S(1)} %pad_maximum_fusion.refs_3_), channel_id=1, source_target_pairs={{0,4},{2,6},{4,0},{6,2},{1,5},{3,7},{5,1},{7,3},{8,12},{10,14},{12... | collective-permute-start | bytes 3145736 | tf_op jit(solution)/shard_map/ppermute | solution.py:278
  36.9 23.7 %collective-permute-start.10 = (bf16[512,1024]{1,0:T(8,128)(2,1)S(1)}, bf16[512,1024]{1,0:T(8,128)(2,1)S(1)}, u32[]{:S(2)}, u32[]{:S(2)}) collective-permute-start(bf16[512,1024]{1,0:T(8,128)(2,1)S(1)} %pad_maximum_fusion.refs_3_), channel_id=1, source_target_pairs={{0,2},{2,0},{4,6},{6,4},{1,3},{3,1},{5,7},{7,5},{8,10},{10,8},{12,... | collective-permute-start | bytes 3145736 | tf_op jit(solution)/shard_map/ppermute | solution.py:278
  45.4 18.5 %collective-permute-start.15 = (bf16[512,256]{1,0:T(8,128)(2,1)S(1)}, bf16[512,256]{1,0:T(8,128)(2,1)S(1)}, u32[]{:S(2)}, u32[]{:S(2)}) collective-permute-start(bf16[512,256]{1,0:T(8,128)(2,1)S(1)} %get-tuple-element.26), channel_id=1, source_target_pairs={{0,16},{8,24},{16,0},{24,8},{1,17},{9,25},{17,1},{25,9},{2,18},{10... | collective-permute-start | bytes 786440 | tf_op jit(solution)/shard_map/ppermute | solution.py:291
  59.3 24.0 %collective-permute-start.12 = (bf16[256,1024]{1,0:T(8,128)(2,1)}, bf16[256,1024]{1,0:T(8,128)(2,1)}, u32[]{:S(2)}, u32[]{:S(2)}) collective-permute-start(bf16[256,1024]{1,0:T(8,128)(2,1)} %slice.26), channel_id=1, source_target_pairs={{0,2},{2,0},{4,6},{6,4},{1,3},{3,1},{5,7},{7,5},{8,10},{10,8},{12,... | collective-permute-start | bytes 1572872 | tf_op jit(solution)/shard_map/ppermute | solution.py:278
  61.4 21.9 %collective-permute-start.13 = (bf16[256,1024]{1,0:T(8,128)(2,1)}, bf16[256,1024]{1,0:T(8,128)(2,1)}, u32[]{:S(2)}, u32[]{:S(2)}) collective-permute-start(bf16[256,1024]{1,0:T(8,128)(2,1)} %slice.27), channel_id=1, source_target_pairs={{0,4},{2,6},{4,0},{6,2},{1,5},{3,7},{5,1},{7,3},{8,12},{10,14},{12... | collective-permute-start | bytes 1572872 | tf_op jit(solution)/shard_map/ppermute | solution.py:278
  65.5 11.1 %collective-permute-start.18 = (bf16[512,256]{1,0:T(8,128)(2,1)}, bf16[512,256]{1,0:T(8,128)(2,1)}, u32[]{:S(2)}, u32[]{:S(2)}) collective-permute-start(bf16[512,256]{1,0:T(8,128)(2,1)} %shard_map.102.refs_2_), channel_id=1, source_target_pairs={{0,6},{2,4},{4,2},{6,0},{1,7},{3,5},{5,3},{7,1},{8,14},{10,12},{12... | collective-permute-start | bytes 786440 | tf_op jit(solution)/shard_map/ppermute | solution.py:278
  65.7 17.7 %collective-permute-start.17 = (bf16[512,256]{1,0:T(8,128)(2,1)}, bf16[512,256]{1,0:T(8,128)(2,1)}, u32[]{:S(2)}, u32[]{:S(2)}) collective-permute-start(bf16[512,256]{1,0:T(8,128)(2,1)} %shard_map.102.refs_2_), channel_id=1, source_target_pairs={{0,4},{2,6},{4,0},{6,2},{1,5},{3,7},{5,1},{7,3},{8,12},{10,14},{12... | collective-permute-start | bytes 786440 | tf_op jit(solution)/shard_map/ppermute | solution.py:278
  66.9 16.4 %collective-permute-start.16 = (bf16[512,256]{1,0:T(8,128)(2,1)}, bf16[512,256]{1,0:T(8,128)(2,1)}, u32[]{:S(2)}, u32[]{:S(2)}) collective-permute-start(bf16[512,256]{1,0:T(8,128)(2,1)} %shard_map.102.refs_2_), channel_id=1, source_target_pairs={{0,2},{2,0},{4,6},{6,4},{1,3},{3,1},{5,7},{7,5},{8,10},{10,8},{12,... | collective-permute-start | bytes 786440 | tf_op jit(solution)/shard_map/ppermute | solution.py:278
  83.4 31.7 %collective-permute-start.23 = (bf16[2048,256]{1,0:T(8,128)(2,1)}, bf16[2048,256]{1,0:T(8,128)(2,1)S(1)}, u32[]{:S(2)}, u32[]{:S(2)}) collective-permute-start(bf16[2048,256]{1,0:T(8,128)(2,1)} %refs_4_.1), channel_id=1, source_target_pairs={{0,4},{2,6},{4,0},{6,2},{1,5},{3,7},{5,1},{7,3},{8,12},{10,14},{12... | collective-permute-start | bytes 3145736 | tf_op jit(solution)/shard_map/ppermute | solution.py:278
  84.7 30.4 %collective-permute-start.22 = (bf16[2048,256]{1,0:T(8,128)(2,1)}, bf16[2048,256]{1,0:T(8,128)(2,1)S(1)}, u32[]{:S(2)}, u32[]{:S(2)}) collective-permute-start(bf16[2048,256]{1,0:T(8,128)(2,1)} %refs_4_.1), channel_id=1, source_target_pairs={{0,2},{2,0},{4,6},{6,4},{1,3},{3,1},{5,7},{7,5},{8,10},{10,8},{12,... | collective-permute-start | bytes 3145736 | tf_op jit(solution)/shard_map/ppermute | solution.py:278
  90.1 17.9 %collective-permute-start.14 = (bf16[512,256]{1,0:T(8,128)(2,1)S(1)}, bf16[512,256]{1,0:T(8,128)(2,1)S(1)}, u32[]{:S(2)}, u32[]{:S(2)}) collective-permute-start(bf16[512,256]{1,0:T(8,128)(2,1)S(1)} %get-tuple-element.24), channel_id=1, source_target_pairs={{0,16},{8,24},{16,0},{24,8},{1,17},{9,25},{17,1},{25,9},{2,18},{10... | collective-permute-start | bytes 786440 | tf_op jit(solution)/shard_map/ppermute | solution.py:291
  95.1 21.6 %collective-permute-start.26 = (bf16[512,256]{1,0:T(8,128)(2,1)S(1)}, bf16[512,256]{1,0:T(8,128)(2,1)S(1)}, u32[]{:S(2)}, u32[]{:S(2)}) collective-permute-start(bf16[512,256]{1,0:T(8,128)(2,1)S(1)} %get-tuple-element.32), channel_id=1, source_target_pairs={{0,16},{8,24},{16,0},{24,8},{1,17},{9,25},{17,1},{25,9},{2,18},{10... | collective-permute-start | bytes 786440 | tf_op jit(solution)/shard_map/ppermute | solution.py:291
  115.2 19.4 %collective-permute-start.24 = (bf16[1024,256]{1,0:T(8,128)(2,1)S(1)}, bf16[1024,256]{1,0:T(8,128)(2,1)S(1)}, u32[]{:S(2)}, u32[]{:S(2)}) collective-permute-start(bf16[1024,256]{1,0:T(8,128)(2,1)S(1)} %slice.22), channel_id=1, source_target_pairs={{0,2},{2,0},{4,6},{6,4},{1,3},{3,1},{5,7},{7,5},{8,10},{10,8},{12,... | collective-permute-start | bytes 1572872 | tf_op jit(solution)/shard_map/ppermute | solution.py:278
  116.5 18.1 %collective-permute-start.25 = (bf16[1024,256]{1,0:T(8,128)(2,1)S(1)}, bf16[1024,256]{1,0:T(8,128)(2,1)S(1)}, u32[]{:S(2)}, u32[]{:S(2)}) collective-permute-start(bf16[1024,256]{1,0:T(8,128)(2,1)S(1)} %slice.23), channel_id=1, source_target_pairs={{0,4},{2,6},{4,0},{6,2},{1,5},{3,7},{5,1},{7,3},{8,12},{10,14},{12... | collective-permute-start | bytes 1572872 | tf_op jit(solution)/shard_map/ppermute | solution.py:278
  123.7 7.0 %collective-permute-start.29 = (bf16[512,256]{1,0:T(8,128)(2,1)S(1)}, bf16[512,256]{1,0:T(8,128)(2,1)S(1)}, u32[]{:S(2)}, u32[]{:S(2)}) collective-permute-start(bf16[512,256]{1,0:T(8,128)(2,1)S(1)} %shard_map.105.refs_0_), channel_id=1, source_target_pairs={{0,24},{8,0},{16,8},{24,16},{1,25},{9,1},{17,9},{25,17},{2,26},{10... | collective-permute-start | bytes 786440 | tf_op jit(solution)/shard_map/ppermute | solution.py:296
  127.4 19.3 %collective-permute-start.28 = (bf16[512,256]{1,0:T(8,128)(2,1)S(1)}, bf16[512,256]{1,0:T(8,128)(2,1)S(1)}, u32[]{:S(2)}, u32[]{:S(2)}) collective-permute-start(bf16[512,256]{1,0:T(8,128)(2,1)S(1)} %shard_map.105.refs_0_), channel_id=1, source_target_pairs={{0,16},{8,24},{16,0},{24,8},{1,17},{9,25},{17,1},{25,9},{2,18},{10... | collective-permute-start | bytes 786440 | tf_op jit(solution)/shard_map/ppermute | solution.py:296
  127.5 19.3 %collective-permute-start.27 = (bf16[512,256]{1,0:T(8,128)(2,1)S(1)}, bf16[512,256]{1,0:T(8,128)(2,1)S(1)}, u32[]{:S(2)}, u32[]{:S(2)}) collective-permute-start(bf16[512,256]{1,0:T(8,128)(2,1)S(1)} %shard_map.105.refs_0_), channel_id=1, source_target_pairs={{0,8},{8,16},{16,24},{24,0},{1,9},{9,17},{17,25},{25,1},{2,10},{10... | collective-permute-start | bytes 786440 | tf_op jit(solution)/shard_map/ppermute | solution.py:296
  130.7 17.9 %collective-permute-start.21 = (bf16[512,256]{1,0:T(8,128)(2,1)S(1)}, bf16[512,256]{1,0:T(8,128)(2,1)S(1)}, u32[]{:S(2)}, u32[]{:S(2)}) collective-permute-start(bf16[512,256]{1,0:T(8,128)(2,1)S(1)} %shard_map.103.refs_0_), channel_id=1, source_target_pairs={{0,24},{8,0},{16,8},{24,16},{1,25},{9,1},{17,9},{25,17},{2,26},{10... | collective-permute-start | bytes 786440 | tf_op jit(solution)/shard_map/ppermute | solution.py:296
  134.6 35.8 %collective-permute-start.20 = (bf16[512,256]{1,0:T(8,128)(2,1)S(1)}, bf16[512,256]{1,0:T(8,128)(2,1)S(1)}, u32[]{:S(2)}, u32[]{:S(2)}) collective-permute-start(bf16[512,256]{1,0:T(8,128)(2,1)S(1)} %shard_map.103.refs_0_), channel_id=1, source_target_pairs={{0,16},{8,24},{16,0},{24,8},{1,17},{9,25},{17,1},{25,9},{2,18},{10... | collective-permute-start | bytes 786440 | tf_op jit(solution)/shard_map/ppermute | solution.py:296
  134.6 35.8 %collective-permute-start.19 = (bf16[512,256]{1,0:T(8,128)(2,1)S(1)}, bf16[512,256]{1,0:T(8,128)(2,1)S(1)}, u32[]{:S(2)}, u32[]{:S(2)}) collective-permute-start(bf16[512,256]{1,0:T(8,128)(2,1)S(1)} %shard_map.103.refs_0_), channel_id=1, source_target_pairs={{0,8},{8,16},{16,24},{24,0},{1,9},{9,17},{17,25},{25,1},{2,10},{10... | collective-permute-start | bytes 786440 | tf_op jit(solution)/shard_map/ppermute | solution.py:296
  172.3 4.5 %collective-permute-start.30 = (bf16[256,1024]{1,0:T(8,128)(2,1)S(1)}, bf16[256,1024]{1,0:T(8,128)(2,1)S(1)}, u32[]{:S(2)}, u32[]{:S(2)}) collective-permute-start(bf16[256,1024]{1,0:T(8,128)(2,1)S(1)} %get-tuple-element.36), channel_id=1, source_target_pairs={{0,1},{1,0},{2,3},{3,2},{4,5},{5,4},{6,7},{7,6},{8,9},{9,8},{10,11... | collective-permute-start | bytes 1572872 | tf_op jit(solution)/shard_map/ppermute | solution.py:366
  177.0 14.2 %collective-permute-start.31 = (bf16[128,1024]{1,0:T(8,128)(2,1)S(1)}, bf16[128,1024]{1,0:T(8,128)(2,1)S(1)}, u32[]{:S(2)}, u32[]{:S(2)}) collective-permute-start(bf16[128,1024]{1,0:T(8,128)(2,1)S(1)} %get-tuple-element.49), channel_id=1, source_target_pairs={{0,0},{1,16},{8,8},{9,24},{16,1},{17,17},{24,9},{25,25},{2,2},{3,1... | collective-permute-start | bytes 786440 | tf_op jit(solution)/shard_map/ppermute | solution.py:373
  181.5 9.7 %collective-permute-start.32 = (bf16[128,1024]{1,0:T(8,128)(2,1)S(1)}, bf16[128,1024]{1,0:T(8,128)(2,1)S(1)}, u32[]{:S(2)}, u32[]{:S(2)}) collective-permute-start(bf16[128,1024]{1,0:T(8,128)(2,1)S(1)} %get-tuple-element.50), channel_id=1, source_target_pairs={{0,8},{1,24},{8,0},{9,16},{16,9},{17,25},{24,1},{25,17},{2,10},{3,... | collective-permute-start | bytes 786440 | tf_op jit(solution)/shard_map/ppermute | solution.py:373
  (26 other events, 167.9 us)

commit v9 on v8

--- a/solution.py
+++ b/solution.py
@@ -193,40 +193,33 @@
 
 
 def project_kernel(place_ref, *refs):
-    attended_refs = refs[:4]
-    weight_refs = refs[4:8]
-    total_refs = refs[8:-2]
+    attended_refs, weight_refs, out_ref = refs[:4], refs[4:8], refs[8]
     hi = place_ref[0]
     lo = place_ref[1]
-    core = place_ref[2]
-    offset = place_ref[3]
+    side = lax.div(hi, 2) ^ place_ref[2]
     depth = attended_refs[0].shape[1]
-    width = weight_refs[0].shape[1]
-    span = weight_refs[0].shape[0] // 4
-    for side, out_ref in enumerate(refs[-2:]):
-        kept = out_ref.shape[0]
-        rows = pl.ds(pl.multiple_of(lax.rem(core + side, 2) * kept, kept), kept)
-        for r, weight_ref in enumerate(weight_refs):
-            columns = pl.ds(pl.multiple_of((lo ^ r) * width, width), width)
-            total = total_refs[side][:, columns] if total_refs else 0.0
-            for k, attended_ref in enumerate(attended_refs):
-                first = lax.rem(hi - k + 4, 4) * span + offset
-                total = total + jnp.dot(
-                    attended_ref[rows, :],
-                    weight_ref[pl.ds(pl.multiple_of(first, depth), depth), :],
-                    preferred_element_type=jnp.float32,
-                )
-            out_ref[:, columns] = total.astype(out_ref.dtype)
-
-
-def project(place, attended_parts, weights, totals, kind):
+    features, width = weight_refs[0].shape
+    span = features // 4
+    for r, weight_ref in enumerate(weight_refs):
+        total = 0.0
+        for k, attended_ref in enumerate(attended_refs):
+            first = side * (2 * span) + (lax.rem(hi, 2) ^ (k // 2)) * span + (k % 2) * depth
+            total = total + jnp.dot(
+                attended_ref[...],
+                weight_ref[pl.ds(pl.multiple_of(first, depth), depth), :],
+                preferred_element_type=jnp.float32,
+            )
+        columns = pl.ds(pl.multiple_of((lo ^ r) * width, width), width)
+        out_ref[:, columns] = total.astype(out_ref.dtype)
+
+
+def project(place, attended_parts, weights):
     tokens, depth = attended_parts[0].shape
     width = weights[0].shape[1]
-    shape = jax.ShapeDtypeStruct((tokens // 2, 4 * width), kind)
     return local_kernel(
         project_kernel,
-        (shape, shape),
-        (place, *attended_parts, *weights, *totals),
+        jax.ShapeDtypeStruct((tokens, 4 * width), jnp.bfloat16),
+        (place, *attended_parts, *weights),
         2 * tokens * 4 * depth * 4 * width,
     )
 
@@ -291,12 +284,6 @@
     return lax.ppermute(block, "hi", [(i, i ^ d) for i in range(4)])
 
 
-def round_line(block):
-    return [block] + [
-        lax.ppermute(block, "hi", [(i, (i + d) % 4) for i in range(4)]) for d in range(1, 4)
-    ]
-
-
 def line_device(tokens, norm_gain, w_query, w_key, w_value, w_out, doc_starts):
     rows, features = tokens.shape
     hi = lax.axis_index("hi")
@@ -342,12 +329,17 @@
     cosine, sine = rotary_tables((row_index // rows * 4 + lo) * rows + row_index % rows)
 
     kept, sent = product(index, token_parts, weights[0], 0, 1)
-    kv_own = finish_pair(cosine, sine, [kept, along(sent, 2)])
-    kv_parts = [kv_own] + [beside(kv_own, r) for r in range(1, 4)]
+    features_here = w_out.shape[0] // 2
+    out_own = lax.dynamic_slice_in_dim(w_out, which_half * features_here, features_here, 0)
+    out_other = lax.dynamic_slice_in_dim(w_out, (1 - which_half) * features_here, features_here, 0)
+    out_other = along(after(out_other, halves), 2)
+    kv_own = finish_pair(cosine, sine, [after(kept, out_other), along(sent, 2)])
+    kv_going = after(kv_own, *weights[1][3:])
+    kv_parts = [kv_own] + [beside(kv_going, r) for r in range(1, 4)]
 
     firsts = jnp.stack([lo, lo, lo ^ 1, lo ^ 2, lo ^ 3]) * rows
     seen = jnp.concatenate([firsts, doc_starts])
-    out_sides = sides(after(w_out, *weights[1][3:], *kv_parts[1:]))
+    out_sides = sides(after(jnp.concatenate([out_own, out_other], axis=0), *kv_parts[1:]))
     products = [product(index, token_parts, weights[1], c, 2) for c in range(2)]
     products[0] = (after(products[0][0], products[1][0]), products[0][1])
     attended = [
@@ -357,23 +349,30 @@
     out_sides[1:] = lax.optimization_barrier((*out_sides[1:], attended[1]))[:2]
     out_blocks = corner(out_sides)
     out_blocks[3:] = [jnp.concatenate(out_blocks[3:], axis=0)]
-    totals = ()
-    for c, kind in enumerate((jnp.float32, jnp.bfloat16)):
-        where = jnp.concatenate([index, jnp.full((1,), c * width, jnp.int32)])
-        totals = project(where, round_line(attended[c]), out_blocks, totals, kind)
-
-    mine, theirs = totals
+    attended += [along(chunk, 1) for chunk in attended]
+
+    theirs, mine = [
+        project(jnp.stack([hi, lo, group]), attended, out_blocks) for group in (1 - core, core)
+    ]
     theirs = lax.ppermute(theirs, "head", [(0, 1), (1, 0)])
-    summed = (mine.astype(jnp.float32) + theirs.astype(jnp.float32)).astype(jnp.bfloat16)
-    arrived = []
-    for e in range(2):
-        block = lax.rem(hi + e, 2)
-        piece = lax.dynamic_slice_in_dim(summed, block * rows, rows, 0)
-        route = [(z * 2 + g, (2 * g + (z + e) % 2) * 2 + z // 2) for z in range(4) for g in range(2)]
-        arrived.append(lax.ppermute(piece, ("hi", "head"), route))
-    even = lax.rem(hi, 2) == 0
+
+    def added(one, two):
+        return (one.astype(jnp.float32) + two.astype(jnp.float32)).astype(jnp.bfloat16)
+
+    kept = 2 * rows
+    shares = [
+        added(
+            lax.dynamic_slice_in_dim(mine, z * kept, kept, 0),
+            lax.dynamic_slice_in_dim(theirs, z * kept, kept, 0),
+        )
+        for z in (which_half, 1 - which_half)
+    ]
+    summed = added(shares[0], along(shares[1], 2))
+    here = lax.dynamic_slice_in_dim(summed, which * rows, rows, 0)
+    there = along(lax.dynamic_slice_in_dim(summed, (1 - which) * rows, rows, 0), 1)
+    first = which == 0
     return jnp.concatenate(
-        [jnp.where(even, arrived[0], arrived[1]), jnp.where(even, arrived[1], arrived[0])], axis=1
+        [jnp.where(first, here, there), jnp.where(first, there, here)], axis=1
     )
 
 

time: 194 us -> 191 us (0.985)
  waiting for transfers between devices: 104 us -> 87.7 us
  local copies, waits for them, and re-layouts: 11.4 us -> 21.4 us
  starting transfers between devices: 44.9 us -> 39.6 us
  Pallas kernels: 25.9 us -> 30.3 us
  other arithmetic: 5.43 us -> 8.96 us
    ppermute x8 -> x0, waiting for transfers between devices: 45.9 us -> none  [the longest x6 36.5 us: round_line(): lax.ppermute(block, 'hi', [(i, (i + d) % 4) for i in range(4)])]
    ppermute x8 -> x13, waiting for transfers between devices: 24.7 us -> 56.2 us  [along(): return lax.ppermute(block, 'hi', [(i, i ^ d) for i in range(4)])]
    ppermute x8 -> x0, starting transfers between devices: 12.9 us -> none  [the longest x6 8.11 us: round_line(): lax.ppermute(block, 'hi', [(i, (i + d) % 4) for i in range(4)])]
    ppermute x8 -> x13, starting transfers between devices: 12 us -> 19.7 us  [along(): return lax.ppermute(block, 'hi', [(i, i ^ d) for i in range(4)])]
    unnamed x53 -> x89, local copies, waits for them, and re-layouts: 5.57 us -> 10.1 us
    pallas_call x8, Pallas kernels: 25.9 us -> 30.3 us  [local_kernel(): pl.pallas_call(body, in_specs=[pl.BlockSpec(memory_space=pltpu.SMEM)] + [...]
    slice x6, local copies, waits for them, and re-layouts: 3.35 us -> 6.7 us  [corner(): return [*blocks, beside(blocks[2][:half], 1), beside(blocks[1][half:], 2)]]
    convert_element_type x1 -> x2, other arithmetic: 0.19 us -> 2.54 us  [added(): (one.astype(jnp.float32) + two.astype(jnp.float32)).astype(jnp.bfloat16)]
  transfers between devices with their start and end apart: 33 -> 30, of which waited for: 14 -> 16; matrix products, arithmetic and copies ran while one was open for 6% -> 9% of each run, Pallas kernels for 12% -> 14%
where the time goes in v9:
time: 191 us; the launch traced here: 189 us
  waiting for transfers between devices  87.7 us (46%)
  starting transfers between devices  39.6 us (21%)
  Pallas kernels  30.3 us (16%)
  local copies, waits for them, and re-layouts  21.4 us (11%)
  other arithmetic  8.96 us (5%)
    ppermute x13, waiting for transfers between devices, along(): return lax.ppermute(block, 'hi', [(i, i ^ d) for i in range(4)])  56.2 us
    ppermute x15, waiting for transfers between devices, beside(): return lax.ppermute(block, 'lo', [(i, i ^ r) for i in range(4)])  31.4 us
    pallas_call x8, Pallas kernels, local_kernel(): pl.pallas_call(body, in_specs=[pl.BlockSpec(memory_space=pltpu.SMEM)] + [...  30.3 us
    ppermute x13, starting transfers between devices, along(): return lax.ppermute(block, 'hi', [(i, i ^ d) for i in range(4)])  19.7 us
    ppermute x15, starting transfers between devices, beside(): return lax.ppermute(block, 'lo', [(i, i ^ r) for i in range(4)])  14.3 us
    unnamed x89, local copies, waits for them, and re-layouts  10.1 us
    slice x6, local copies, waits for them, and re-layouts, corner(): return [*blocks, beside(blocks[2][:half], 1), beside(blocks[1][half:], 2)]  6.7 us
  transfers between devices with their start and end apart: 30, of which 16 were waited for; matrix products, arithmetic and copies ran while one was open for 9% of the time, Pallas kernels for 14%

profile of v9, /device:TPU:1, one launch (start us, length us, event | category | flops | bytes accessed | tf_op | source)
XLA Modules:
  0.0 188.5 jit_solution(13223432341271739953)
XLA Ops:
  1.2 2.2 %collective-permute-start.5 = (bf16[256,512]{1,0:T(8,128)(2,1)S(1)}, bf16[256,512]{1,0:T(8,128)(2,1)S(1)}, u32[]{:S(2)}, u32[]{:S(2)}) collective-permute-start(bf16[256,512]{1,0:T(8,128)(2,1)S(1)} %pad_maximum_fusion.7), channel_id=1, source_target_pairs={{0,8},{8,0},{16,24},{24,16},{1,9},{9,1},{17,25},{25,17},{2,10},{10... | collective-permute-start | bytes 786440 | tf_op jit(solution)/shard_map/ppermute | solution.py:284
  5.3 4.2 %collective-permute-done.5 = bf16[256,512]{1,0:T(8,128)(2,1)S(1)} collective-permute-done((bf16[256,512]{1,0:T(8,128)(2,1)S(1)}, bf16[256,512]{1,0:T(8,128)(2,1)S(1)}, u32[]{:S(2)}, u32[]{:S(2)}) %collective-permute-start.5) | collective-permute-done | bytes 262176 | tf_op jit(solution)/shard_map/ppermute | solution.py:284
  13.1 2.3 %collective-permute-start.1 = (bf16[128,1024]{1,0:T(8,128)(2,1)}, bf16[128,1024]{1,0:T(8,128)(2,1)}, u32[]{:S(2)}, u32[]{:S(2)}) collective-permute-start(bf16[128,1024]{1,0:T(8,128)(2,1)} %get-tuple-element.43), channel_id=1, source_target_pairs={{0,16},{8,24},{16,0},{24,8},{1,17},{9,25},{17,1},{25,9},{2,18},{10... | collective-permute-start | bytes 786440 | tf_op jit(solution)/shard_map/ppermute | solution.py:284
  16.7 4.3 %collective-permute-done.8.refs_4_ = bf16[512,512]{1,0:T(8,128)(2,1)S(1)} collective-permute-done((bf16[512,512]{1,0:T(8,128)(2,1)S(1)}, bf16[512,512]{1,0:T(8,128)(2,1)S(1)}, u32[]{:S(2)}, u32[]{:S(2)}) %collective-permute-start.8) | collective-permute-done | bytes 524320 | tf_op jit(solution)/shard_map/ppermute | solution.py:271
  23.6 1.8 collective-permute-done.1
  25.4 6.6 %collective-permute-done = bf16[128,1024]{1,0:T(8,128)(2,1)} collective-permute-done((bf16[128,1024]{1,0:T(8,128)(2,1)S(1)}, bf16[128,1024]{1,0:T(8,128)(2,1)}, u32[]{:S(2)}, u32[]{:S(2)}) %collective-permute-start) | collective-permute-done | bytes 262176 | tf_op jit(solution)/shard_map/ppermute | solution.py:284
  34.4 1.3 collective-permute-start.11
  38.9 2.5 %collective-permute-start.3 = (bf16[384,1024]{1,0:T(8,128)(2,1)S(1)}, bf16[384,1024]{1,0:T(8,128)(2,1)S(1)}, u32[]{:S(2)}, u32[]{:S(2)}) collective-permute-start(bf16[384,1024]{1,0:T(8,128)(2,1)S(1)} %constant_dynamic-update-slice_fusion.refs_1_), channel_id=1, source_target_pairs={{0,1},{1,0},{2,3},{3,2},{4,5},{5,4},{6,7},{7,6},{8,9},{9,8},{10,11... | collective-permute-start | bytes 2359304 | tf_op jit(solution)/shard_map/ppermute | solution.py:325
  41.3 2.3 %constant_dynamic-slice_fusion.1 = (bf16[1024,256]{1,0:T(8,128)(2,1)}, bf16[1024,256]{1,0:T(8,128)(2,1)}) fusion(bf16[2048,256]{1,0:T(8,128)(2,1)} %param.15, s32[]{:T(128)S(6)} %select_n.104, s32[]{:T(128)S(6)} %select_n.103), kind=kLoop, calls=%fused_computation.27 | loop fusion | bytes 2097160 | tf_op jit(solution)/shard_map/dynamic_slice | solution.py:333
  44.8 2.4 %collective-permute-start.15 = (bf16[1024,256]{1,0:T(8,128)(2,1)}, bf16[1024,256]{1,0:T(8,128)(2,1)}, u32[]{:S(2)}, u32[]{:S(2)}) collective-permute-start(bf16[1024,256]{1,0:T(8,128)(2,1)} %get-tuple-element.27), channel_id=1, source_target_pairs={{0,16},{8,24},{16,0},{24,8},{1,17},{9,25},{17,1},{25,9},{2,18},{10... | collective-permute-start | bytes 1572872 | tf_op jit(solution)/shard_map/ppermute | solution.py:284
  47.1 10.3 %collective-permute-done.11.refs_5_ = bf16[512,1024]{1,0:T(8,128)(2,1)} collective-permute-done((bf16[512,1024]{1,0:T(8,128)(2,1)S(1)}, bf16[512,1024]{1,0:T(8,128)(2,1)}, u32[]{:S(2)}, u32[]{:S(2)}) %collective-permute-start.11) | collective-permute-done | bytes 1048608 | tf_op jit(solution)/shard_map/ppermute | solution.py:271
  57.4 1.9 slice.26
  60.5 1.9 slice.27
  63.7 2.6 %shard_map.102 = (bf16[512,256]{1,0:T(8,128)(2,1)S(1)}, bf16[512,256]{1,0:T(8,128)(2,1)}) custom-call(s32[5]{0:T(128)S(1)} %get-tuple-element.35.place_ref, bf16[128,2048]{1,0:T(8,128)(2,1)S(1)} %constant_dynamic-slice_fusion.17.refs_0_, bf16[384,1024]{1,0:T(8,128)(2,1)S(1)} %constant_dynamic-update-slice_fusion.refs_1_, ...), custom_call_target="tpu_custom_call" | custom-call | flops 1073741824 | bytes 4194324 | tf_op jit(solution)/shard_map/pallas_call | solution.py:18
  67.0 2.3 %collective-permute-start.16 = (bf16[512,256]{1,0:T(8,128)(2,1)}, bf16[512,256]{1,0:T(8,128)(2,1)S(1)}, u32[]{:S(2)}, u32[]{:S(2)}) collective-permute-start(bf16[512,256]{1,0:T(8,128)(2,1)} %get-tuple-element.29), channel_id=1, source_target_pairs={{0,16},{8,24},{16,0},{24,8},{1,17},{9,25},{17,1},{25,9},{2,18},{10... | collective-permute-start | bytes 786440 | tf_op jit(solution)/shard_map/ppermute | solution.py:284
  70.8 10.8 %collective-permute-done.16.refs_1_ = bf16[512,256]{1,0:T(8,128)(2,1)S(1)} collective-permute-done((bf16[512,256]{1,0:T(8,128)(2,1)}, bf16[512,256]{1,0:T(8,128)(2,1)S(1)}, u32[]{:S(2)}, u32[]{:S(2)}) %collective-permute-start.16) | collective-permute-done | bytes 262176 | tf_op jit(solution)/shard_map/ppermute | solution.py:284
  81.8 2.1 %collective-permute-start.19 = (bf16[512,256]{1,0:T(8,128)(2,1)S(1)}, bf16[512,256]{1,0:T(8,128)(2,1)S(1)}, u32[]{:S(2)}, u32[]{:S(2)}) collective-permute-start(bf16[512,256]{1,0:T(8,128)(2,1)S(1)} %shard_map.103.refs_2_), channel_id=1, source_target_pairs={{0,6},{2,4},{4,2},{6,0},{1,7},{3,5},{5,3},{7,1},{8,14},{10,12},{12... | collective-permute-start | bytes 786440 | tf_op jit(solution)/shard_map/ppermute | solution.py:271
  85.8 4.0 %shard_map.101 = (bf16[512,256]{1,0:T(8,128)(2,1)S(1)}, bf16[512,256]{1,0:T(8,128)(2,1)}) custom-call(s32[5]{0:T(128)S(1)} %get-tuple-element.58.place_ref, bf16[128,2048]{1,0:T(8,128)(2,1)S(1)} %constant_dynamic-slice_fusion.17.refs_0_, bf16[384,1024]{1,0:T(8,128)(2,1)S(1)} %constant_dynamic-update-slice_fusion.refs_1_, bf16[384,1024]{1,0:T(8,128)(2,1)S(1)} %copy-done.1, ...), custom_call_target="tpu_custom_call" | custom-call | flops 1073741824 | bytes 6291476 | tf_op jit(solution)/shard_map/pallas_call | solution.py:18
  91.2 5.4 %collective-permute-done.18.refs_4_ = bf16[512,256]{1,0:T(8,128)(2,1)S(1)} collective-permute-done((bf16[512,256]{1,0:T(8,128)(2,1)S(1)}, bf16[512,256]{1,0:T(8,128)(2,1)S(1)}, u32[]{:S(2)}, u32[]{:S(2)}) %collective-permute-start.18) | collective-permute-done | bytes 262176 | tf_op jit(solution)/shard_map/ppermute | solution.py:271
  100.4 3.3 %shard_map.100 = (bf16[512,256]{1,0:T(8,128)(2,1)S(1)}, bf16[512,256]{1,0:T(8,128)(2,1)S(1)}) custom-call(s32[5]{0:T(128)S(1)} %get-tuple-element.59.place_ref, bf16[128,2048]{1,0:T(8,128)(2,1)S(1)} %constant_dynamic-slice_fusion.17.refs_0_, bf16[384,1024]{1,0:T(8,128)(2,1)S(1)} %constant_dynamic-update-slice_fusion.refs_1_, ...), custom_call_target="tpu_custom_call" | custom-call | flops 1073741824 | bytes 6291476 | tf_op jit(solution)/shard_map/pallas_call | solution.py:18
  104.5 6.9 %shard_map.105.refs_1_ = bf16[512,256]{1,0:T(8,128)(2,1)S(1)} custom-call(s32[21]{0:T(128)S(1)} %pad_add_fusion.2.place_ref, f32[512,128]{1,0:T(8,128)S(1)} %copy-done.10, f32[512,128]{1,0:T(8,128)S(1)} %copy-done.12, bf16[512,256]{1,0:T(8,128)(2,1)S(1)} %copy-done.32, bf16[512,256]{1,0:T(8,128)(2,1)} %collective-permute-done.20.refs_1_, ...), custom_call_target="tpu_custom_call" | custom-call | flops 8589934592 | bytes 2097236 | tf_op jit(solution)/shard_map/pallas_call | solution.py:18
  111.5 3.3 %collective-permute-start.22 = (bf16[512,256]{1,0:T(8,128)(2,1)S(1)}, bf16[512,256]{1,0:T(8,128)(2,1)S(1)}, u32[]{:S(2)}, u32[]{:S(2)}) collective-permute-start(bf16[512,256]{1,0:T(8,128)(2,1)S(1)} %shard_map.105.refs_1_), channel_id=1, source_target_pairs={{0,8},{8,0},{16,24},{24,16},{1,9},{9,1},{17,25},{25,17},{2,10},{10... | collective-permute-start | bytes 786440 | tf_op jit(solution)/shard_map/ppermute | solution.py:284
  114.8 7.6 %collective-permute-done.24.refs_6_ = bf16[2048,256]{1,0:T(8,128)(2,1)} collective-permute-done((bf16[2048,256]{1,0:T(8,128)(2,1)S(1)}, bf16[2048,256]{1,0:T(8,128)(2,1)}, u32[]{:S(2)}, u32[]{:S(2)}) %collective-permute-start.24) | collective-permute-done | bytes 1048608 | tf_op jit(solution)/shard_map/ppermute | solution.py:271
  126.8 6.3 %shard_map.104.refs_0_ = bf16[512,256]{1,0:T(8,128)(2,1)S(1)} custom-call(s32[21]{0:T(128)S(1)} %pad_add_fusion.2.place_ref, f32[512,128]{1,0:T(8,128)S(1)} %copy-done.10, f32[512,128]{1,0:T(8,128)S(1)} %copy-done.12, bf16[512,256]{1,0:T(8,128)(2,1)S(1)} %get-tuple-element.24.refs_0_, bf16[512,256]{1,0:T(8,128)(2,1)S(1)} %collective-permute-done.14.refs_1_, ...), custom_call_target="tpu_custom_call" | custom-call | flops 8589934592 | bytes 2097236 | tf_op jit(solution)/shard_map/pallas_call | solution.py:18
  134.5 2.7 %collective-permute-done.25 = bf16[1024,256]{1,0:T(8,128)(2,1)S(1)} collective-permute-done((bf16[1024,256]{1,0:T(8,128)(2,1)S(1)}, bf16[1024,256]{1,0:T(8,128)(2,1)S(1)}, u32[]{:S(2)}, u32[]{:S(2)}) %collective-permute-start.25) | collective-permute-done | bytes 524320 | tf_op jit(solution)/shard_map/ppermute | solution.py:271
  137.5 1.3 collective-permute-done.21.refs_2_
  138.9 4.1 %shard_map.107 = bf16[512,1024]{1,0:T(8,128)(2,1)} custom-call(s32[3]{0:T(128)S(1)} %pad_add_fusion.7.place_ref, bf16[512,256]{1,0:T(8,128)(2,1)S(1)} %shard_map.104.refs_0_, bf16[512,256]{1,0:T(8,128)(2,1)S(1)} %shard_map.105.refs_1_, bf16[512,256]{1,0:T(8,128)(2,1)S(1)} %collective-permute-done.21.refs_2_, ...), custom_call_target="tpu_custom_call" | custom-call | flops 1073741824 | bytes 5242892 | tf_op jit(solution)/shard_map/pallas_call | solution.py:18
  143.0 3.1 %collective-permute-start.27 = (bf16[512,1024]{1,0:T(8,128)(2,1)}, bf16[512,1024]{1,0:T(8,128)(2,1)}, u32[]{:S(2)}, u32[]{:S(2)}) collective-permute-start(bf16[512,1024]{1,0:T(8,128)(2,1)} %shard_map.107), channel_id=1, source_target_pairs={{0,1},{1,0},{2,3},{3,2},{4,5},{5,4},{6,7},{7,6},{8,9},{9,8},{10,11... | collective-permute-start | bytes 3145736 | tf_op jit(solution)/shard_map/ppermute | solution.py:357
  149.0 2.9 %shard_map.106 = bf16[512,1024]{1,0:T(8,128)(2,1)S(1)} custom-call(s32[3]{0:T(128)S(1)} %pad_add_fusion.place_ref, bf16[512,256]{1,0:T(8,128)(2,1)S(1)} %copy-done.16, bf16[512,256]{1,0:T(8,128)(2,1)S(1)} %shard_map.105.refs_1_, bf16[512,256]{1,0:T(8,128)(2,1)S(1)} %copy-done.18, bf16[512,256]{1,0:T(8,128)(2,1)S(1)} %copy-done.14, ...), custom_call_target="tpu_custom_call" | custom-call | flops 1073741824 | bytes 5242892 | tf_op jit(solution)/shard_map/pallas_call | solution.py:18
  153.2 2.5 %collective-permute-start.28 = (bf16[256,1024]{1,0:T(8,128)(2,1)S(1)}, bf16[256,1024]{1,0:T(8,128)(2,1)S(1)}, u32[]{:S(2)}, u32[]{:S(2)}) collective-permute-start(bf16[256,1024]{1,0:T(8,128)(2,1)S(1)} %add_convert_fusion.1), channel_id=1, source_target_pairs={{0,16},{8,24},{16,0},{24,8},{1,17},{9,25},{17,1},{25,9},{2,18},{10... | collective-permute-start | bytes 1572872 | tf_op jit(solution)/shard_map/ppermute | solution.py:284
  155.7 23.4 %collective-permute-done.28 = bf16[256,1024]{1,0:T(8,128)(2,1)S(1)} collective-permute-done((bf16[256,1024]{1,0:T(8,128)(2,1)S(1)}, bf16[256,1024]{1,0:T(8,128)(2,1)S(1)}, u32[]{:S(2)}, u32[]{:S(2)}) %collective-permute-start.28) | collective-permute-done | bytes 524320 | tf_op jit(solution)/shard_map/ppermute | solution.py:284
  181.2 6.4 %collective-permute-done.29 = bf16[128,1024]{1,0:T(8,128)(2,1)S(1)} collective-permute-done((bf16[128,1024]{1,0:T(8,128)(2,1)S(1)}, bf16[128,1024]{1,0:T(8,128)(2,1)S(1)}, u32[]{:S(2)}, u32[]{:S(2)}) %collective-permute-start.29) | collective-permute-done | bytes 262176 | tf_op jit(solution)/shard_map/ppermute | solution.py:284
  (162 shorter events, 42.9 us)
Async XLA Ops:
  1.2 8.2 %collective-permute-start.5 = (bf16[256,512]{1,0:T(8,128)(2,1)S(1)}, bf16[256,512]{1,0:T(8,128)(2,1)S(1)}, u32[]{:S(2)}, u32[]{:S(2)}) collective-permute-start(bf16[256,512]{1,0:T(8,128)(2,1)S(1)} %pad_maximum_fusion.7), channel_id=1, source_target_pairs={{0,8},{8,0},{16,24},{24,16},{1,9},{9,1},{17,25},{25,17},{2,10},{10... | collective-permute-start | bytes 786440 | tf_op jit(solution)/shard_map/ppermute | solution.py:284
  4.4 28.8 %collective-permute-start.4 = (bf16[256,1024]{1,0:T(8,128)(2,1)}, bf16[256,1024]{1,0:T(8,128)(2,1)}, u32[]{:S(2)}, u32[]{:S(2)}) collective-permute-start(bf16[256,1024]{1,0:T(8,128)(2,1)} %pad_maximum_fusion.2), channel_id=1, source_target_pairs={{0,8},{8,0},{16,24},{24,16},{1,9},{9,1},{17,25},{25,17},{2,10},{10... | collective-permute-start | bytes 1572872 | tf_op jit(solution)/shard_map/ppermute | solution.py:284
  9.5 11.5 %collective-permute-start.8 = (bf16[512,512]{1,0:T(8,128)(2,1)S(1)}, bf16[512,512]{1,0:T(8,128)(2,1)S(1)}, u32[]{:S(2)}, u32[]{:S(2)}) collective-permute-start(bf16[512,512]{1,0:T(8,128)(2,1)S(1)} %pad_maximum_fusion.3.refs_3_), channel_id=1, source_target_pairs={{0,2},{2,0},{4,6},{6,4},{1,3},{3,1},{5,7},{7,5},{8,10},{10,8},{12,... | collective-permute-start | bytes 1572872 | tf_op jit(solution)/shard_map/ppermute | solution.py:271
  10.7 11.7 %collective-permute-start.6 = (bf16[512,512]{1,0:T(8,128)(2,1)S(1)}, bf16[512,512]{1,0:T(8,128)(2,1)S(1)}, u32[]{:S(2)}, u32[]{:S(2)}) collective-permute-start(bf16[512,512]{1,0:T(8,128)(2,1)S(1)} %pad_maximum_fusion.3.refs_3_), channel_id=1, source_target_pairs={{0,4},{2,6},{4,0},{6,2},{1,5},{3,7},{5,1},{7,3},{8,12},{10,14},{12... | collective-permute-start | bytes 1572872 | tf_op jit(solution)/shard_map/ppermute | solution.py:271
  13.1 12.3 %collective-permute-start.1 = (bf16[128,1024]{1,0:T(8,128)(2,1)}, bf16[128,1024]{1,0:T(8,128)(2,1)}, u32[]{:S(2)}, u32[]{:S(2)}) collective-permute-start(bf16[128,1024]{1,0:T(8,128)(2,1)} %get-tuple-element.43), channel_id=1, source_target_pairs={{0,16},{8,24},{16,0},{24,8},{1,17},{9,25},{17,1},{25,9},{2,18},{10... | collective-permute-start | bytes 786440 | tf_op jit(solution)/shard_map/ppermute | solution.py:284
  15.4 16.6 %collective-permute-start = (bf16[128,1024]{1,0:T(8,128)(2,1)S(1)}, bf16[128,1024]{1,0:T(8,128)(2,1)}, u32[]{:S(2)}, u32[]{:S(2)}) collective-permute-start(bf16[128,1024]{1,0:T(8,128)(2,1)S(1)} %get-tuple-element.44), channel_id=1, source_target_pairs={{0,8},{8,0},{16,24},{24,16},{1,9},{9,1},{17,25},{25,17},{2,10},{10... | collective-permute-start | bytes 786440 | tf_op jit(solution)/shard_map/ppermute | solution.py:284
  21.9 12.5 %collective-permute-start.9 = (bf16[256,512]{1,0:T(8,128)(2,1)}, bf16[256,512]{1,0:T(8,128)(2,1)S(1)}, u32[]{:S(2)}, u32[]{:S(2)}) collective-permute-start(bf16[256,512]{1,0:T(8,128)(2,1)} %slice.25), channel_id=1, source_target_pairs={{0,4},{2,6},{4,0},{6,2},{1,5},{3,7},{5,1},{7,3},{8,12},{10,14},{12... | collective-permute-start | bytes 786440 | tf_op jit(solution)/shard_map/ppermute | solution.py:271
  22.3 12.1 %collective-permute-start.7 = (bf16[256,512]{1,0:T(8,128)(2,1)S(1)}, bf16[256,512]{1,0:T(8,128)(2,1)S(1)}, u32[]{:S(2)}, u32[]{:S(2)}) collective-permute-start(bf16[256,512]{1,0:T(8,128)(2,1)S(1)} %slice.24), channel_id=1, source_target_pairs={{0,2},{2,0},{4,6},{6,4},{1,3},{3,1},{5,7},{7,5},{8,10},{10,8},{12,... | collective-permute-start | bytes 786440 | tf_op jit(solution)/shard_map/ppermute | solution.py:271
  32.0 6.8 %collective-permute-start.2 = (bf16[128,1024]{1,0:T(8,128)(2,1)}, bf16[128,1024]{1,0:T(8,128)(2,1)S(1)}, u32[]{:S(2)}, u32[]{:S(2)}) collective-permute-start(bf16[128,1024]{1,0:T(8,128)(2,1)} %collective-permute-done.1), channel_id=1, source_target_pairs={{0,8},{8,0},{16,24},{24,16},{1,9},{9,1},{17,25},{25,17},{2,10},{10... | collective-permute-start | bytes 786440 | tf_op jit(solution)/shard_map/ppermute | solution.py:284
  34.4 23.0 %collective-permute-start.11 = (bf16[512,1024]{1,0:T(8,128)(2,1)S(1)}, bf16[512,1024]{1,0:T(8,128)(2,1)}, u32[]{:S(2)}, u32[]{:S(2)}) collective-permute-start(bf16[512,1024]{1,0:T(8,128)(2,1)S(1)} %pad_maximum_fusion.refs_3_), channel_id=1, source_target_pairs={{0,4},{2,6},{4,0},{6,2},{1,5},{3,7},{5,1},{7,3},{8,12},{10,14},{12... | collective-permute-start | bytes 3145736 | tf_op jit(solution)/shard_map/ppermute | solution.py:271
  35.7 24.8 %collective-permute-start.10 = (bf16[512,1024]{1,0:T(8,128)(2,1)S(1)}, bf16[512,1024]{1,0:T(8,128)(2,1)}, u32[]{:S(2)}, u32[]{:S(2)}) collective-permute-start(bf16[512,1024]{1,0:T(8,128)(2,1)S(1)} %pad_maximum_fusion.refs_3_), channel_id=1, source_target_pairs={{0,2},{2,0},{4,6},{6,4},{1,3},{3,1},{5,7},{7,5},{8,10},{10,8},{12,... | collective-permute-start | bytes 3145736 | tf_op jit(solution)/shard_map/ppermute | solution.py:271
  38.9 24.8 %collective-permute-start.3 = (bf16[384,1024]{1,0:T(8,128)(2,1)S(1)}, bf16[384,1024]{1,0:T(8,128)(2,1)S(1)}, u32[]{:S(2)}, u32[]{:S(2)}) collective-permute-start(bf16[384,1024]{1,0:T(8,128)(2,1)S(1)} %constant_dynamic-update-slice_fusion.refs_1_), channel_id=1, source_target_pairs={{0,1},{1,0},{2,3},{3,2},{4,5},{5,4},{6,7},{7,6},{8,9},{9,8},{10,11... | collective-permute-start | bytes 2359304 | tf_op jit(solution)/shard_map/ppermute | solution.py:325
  44.7 18.9 %copy-start.4 = (bf16[512,512]{1,0:T(8,128)(2,1)S(1)}, bf16[512,512]{1,0:T(8,128)(2,1)}, u32[]{:S(2)}) copy-start(bf16[512,512]{1,0:T(8,128)(2,1)} %copy-done.3) | copy-start | bytes 1572868
  44.7 18.9 %copy-start.6 = (bf16[512,512]{1,0:T(8,128)(2,1)S(1)}, bf16[512,512]{1,0:T(8,128)(2,1)}, u32[]{:S(2)}) copy-start(bf16[512,512]{1,0:T(8,128)(2,1)} %copy-done.5) | copy-start | bytes 1572868
  44.8 26.0 %collective-permute-start.15 = (bf16[1024,256]{1,0:T(8,128)(2,1)}, bf16[1024,256]{1,0:T(8,128)(2,1)}, u32[]{:S(2)}, u32[]{:S(2)}) collective-permute-start(bf16[1024,256]{1,0:T(8,128)(2,1)} %get-tuple-element.27), channel_id=1, source_target_pairs={{0,16},{8,24},{16,0},{24,8},{1,17},{9,25},{17,1},{25,9},{2,18},{10... | collective-permute-start | bytes 1572872 | tf_op jit(solution)/shard_map/ppermute | solution.py:284
  59.3 22.5 %collective-permute-start.12 = (bf16[256,1024]{1,0:T(8,128)(2,1)}, bf16[256,1024]{1,0:T(8,128)(2,1)}, u32[]{:S(2)}, u32[]{:S(2)}) collective-permute-start(bf16[256,1024]{1,0:T(8,128)(2,1)} %slice.26), channel_id=1, source_target_pairs={{0,2},{2,0},{4,6},{6,4},{1,3},{3,1},{5,7},{7,5},{8,10},{10,8},{12,... | collective-permute-start | bytes 1572872 | tf_op jit(solution)/shard_map/ppermute | solution.py:271
  62.4 19.4 %collective-permute-start.13 = (bf16[256,1024]{1,0:T(8,128)(2,1)}, bf16[256,1024]{1,0:T(8,128)(2,1)}, u32[]{:S(2)}, u32[]{:S(2)}) collective-permute-start(bf16[256,1024]{1,0:T(8,128)(2,1)} %slice.27), channel_id=1, source_target_pairs={{0,4},{2,6},{4,0},{6,2},{1,5},{3,7},{5,1},{7,3},{8,12},{10,14},{12... | collective-permute-start | bytes 1572872 | tf_op jit(solution)/shard_map/ppermute | solution.py:271
  67.0 14.6 %collective-permute-start.16 = (bf16[512,256]{1,0:T(8,128)(2,1)}, bf16[512,256]{1,0:T(8,128)(2,1)S(1)}, u32[]{:S(2)}, u32[]{:S(2)}) collective-permute-start(bf16[512,256]{1,0:T(8,128)(2,1)} %get-tuple-element.29), channel_id=1, source_target_pairs={{0,16},{8,24},{16,0},{24,8},{1,17},{9,25},{17,1},{25,9},{2,18},{10... | collective-permute-start | bytes 786440 | tf_op jit(solution)/shard_map/ppermute | solution.py:284
  81.8 8.7 %collective-permute-start.19 = (bf16[512,256]{1,0:T(8,128)(2,1)S(1)}, bf16[512,256]{1,0:T(8,128)(2,1)S(1)}, u32[]{:S(2)}, u32[]{:S(2)}) collective-permute-start(bf16[512,256]{1,0:T(8,128)(2,1)S(1)} %shard_map.103.refs_2_), channel_id=1, source_target_pairs={{0,6},{2,4},{4,2},{6,0},{1,7},{3,5},{5,3},{7,1},{8,14},{10,12},{12... | collective-permute-start | bytes 786440 | tf_op jit(solution)/shard_map/ppermute | solution.py:271
  83.9 12.7 %collective-permute-start.18 = (bf16[512,256]{1,0:T(8,128)(2,1)S(1)}, bf16[512,256]{1,0:T(8,128)(2,1)S(1)}, u32[]{:S(2)}, u32[]{:S(2)}) collective-permute-start(bf16[512,256]{1,0:T(8,128)(2,1)S(1)} %shard_map.103.refs_2_), channel_id=1, source_target_pairs={{0,4},{2,6},{4,0},{6,2},{1,5},{3,7},{5,1},{7,3},{8,12},{10,14},{12... | collective-permute-start | bytes 786440 | tf_op jit(solution)/shard_map/ppermute | solution.py:271
  84.1 13.2 %collective-permute-start.17 = (bf16[512,256]{1,0:T(8,128)(2,1)S(1)}, bf16[512,256]{1,0:T(8,128)(2,1)S(1)}, u32[]{:S(2)}, u32[]{:S(2)}) collective-permute-start(bf16[512,256]{1,0:T(8,128)(2,1)S(1)} %shard_map.103.refs_2_), channel_id=1, source_target_pairs={{0,2},{2,0},{4,6},{6,4},{1,3},{3,1},{5,7},{7,5},{8,10},{10,8},{12,... | collective-permute-start | bytes 786440 | tf_op jit(solution)/shard_map/ppermute | solution.py:271
  90.5 14.0 %collective-permute-start.20 = (bf16[512,256]{1,0:T(8,128)(2,1)}, bf16[512,256]{1,0:T(8,128)(2,1)}, u32[]{:S(2)}, u32[]{:S(2)}) collective-permute-start(bf16[512,256]{1,0:T(8,128)(2,1)} %get-tuple-element.31), channel_id=1, source_target_pairs={{0,16},{8,24},{16,0},{24,8},{1,17},{9,25},{17,1},{25,9},{2,18},{10... | collective-permute-start | bytes 786440 | tf_op jit(solution)/shard_map/ppermute | solution.py:284
  98.0 24.3 %collective-permute-start.24 = (bf16[2048,256]{1,0:T(8,128)(2,1)S(1)}, bf16[2048,256]{1,0:T(8,128)(2,1)}, u32[]{:S(2)}, u32[]{:S(2)}) collective-permute-start(bf16[2048,256]{1,0:T(8,128)(2,1)S(1)} %pad_maximum_fusion.1.refs_4_), channel_id=1, source_target_pairs={{0,4},{2,6},{4,0},{6,2},{1,5},{3,7},{5,1},{7,3},{8,12},{10,14},{12... | collective-permute-start | bytes 3145736 | tf_op jit(solution)/shard_map/ppermute | solution.py:271
  99.2 24.0 %collective-permute-start.23 = (bf16[2048,256]{1,0:T(8,128)(2,1)S(1)}, bf16[2048,256]{1,0:T(8,128)(2,1)}, u32[]{:S(2)}, u32[]{:S(2)}) collective-permute-start(bf16[2048,256]{1,0:T(8,128)(2,1)S(1)} %pad_maximum_fusion.1.refs_4_), channel_id=1, source_target_pairs={{0,2},{2,0},{4,6},{6,4},{1,3},{3,1},{5,7},{7,5},{8,10},{10,8},{12,... | collective-permute-start | bytes 3145736 | tf_op jit(solution)/shard_map/ppermute | solution.py:271
  103.8 23.1 %collective-permute-start.14 = (bf16[512,256]{1,0:T(8,128)(2,1)S(1)}, bf16[512,256]{1,0:T(8,128)(2,1)S(1)}, u32[]{:S(2)}, u32[]{:S(2)}) collective-permute-start(bf16[512,256]{1,0:T(8,128)(2,1)S(1)} %get-tuple-element.25), channel_id=1, source_target_pairs={{0,16},{8,24},{16,0},{24,8},{1,17},{9,25},{17,1},{25,9},{2,18},{10... | collective-permute-start | bytes 786440 | tf_op jit(solution)/shard_map/ppermute | solution.py:284
  111.5 27.4 %collective-permute-start.22 = (bf16[512,256]{1,0:T(8,128)(2,1)S(1)}, bf16[512,256]{1,0:T(8,128)(2,1)S(1)}, u32[]{:S(2)}, u32[]{:S(2)}) collective-permute-start(bf16[512,256]{1,0:T(8,128)(2,1)S(1)} %shard_map.105.refs_1_), channel_id=1, source_target_pairs={{0,8},{8,0},{16,24},{24,16},{1,9},{9,1},{17,25},{25,17},{2,10},{10... | collective-permute-start | bytes 786440 | tf_op jit(solution)/shard_map/ppermute | solution.py:284
  125.3 11.8 %collective-permute-start.25 = (bf16[1024,256]{1,0:T(8,128)(2,1)S(1)}, bf16[1024,256]{1,0:T(8,128)(2,1)S(1)}, u32[]{:S(2)}, u32[]{:S(2)}) collective-permute-start(bf16[1024,256]{1,0:T(8,128)(2,1)S(1)} %slice.22), channel_id=1, source_target_pairs={{0,2},{2,0},{4,6},{6,4},{1,3},{3,1},{5,7},{7,5},{8,10},{10,8},{12,... | collective-permute-start | bytes 1572872 | tf_op jit(solution)/shard_map/ppermute | solution.py:271
  125.7 11.8 %collective-permute-start.26 = (bf16[1024,256]{1,0:T(8,128)(2,1)S(1)}, bf16[1024,256]{1,0:T(8,128)(2,1)S(1)}, u32[]{:S(2)}, u32[]{:S(2)}) collective-permute-start(bf16[1024,256]{1,0:T(8,128)(2,1)S(1)} %slice.23), channel_id=1, source_target_pairs={{0,4},{2,6},{4,0},{6,2},{1,5},{3,7},{5,1},{7,3},{8,12},{10,14},{12... | collective-permute-start | bytes 1572872 | tf_op jit(solution)/shard_map/ppermute | solution.py:271
  133.2 5.6 %collective-permute-start.21 = (bf16[512,256]{1,0:T(8,128)(2,1)S(1)}, bf16[512,256]{1,0:T(8,128)(2,1)S(1)}, u32[]{:S(2)}, u32[]{:S(2)}) collective-permute-start(bf16[512,256]{1,0:T(8,128)(2,1)S(1)} %shard_map.104.refs_0_), channel_id=1, source_target_pairs={{0,8},{8,0},{16,24},{24,16},{1,9},{9,1},{17,25},{25,17},{2,10},{10... | collective-permute-start | bytes 786440 | tf_op jit(solution)/shard_map/ppermute | solution.py:284
  143.0 9.0 %collective-permute-start.27 = (bf16[512,1024]{1,0:T(8,128)(2,1)}, bf16[512,1024]{1,0:T(8,128)(2,1)}, u32[]{:S(2)}, u32[]{:S(2)}) collective-permute-start(bf16[512,1024]{1,0:T(8,128)(2,1)} %shard_map.107), channel_id=1, source_target_pairs={{0,1},{1,0},{2,3},{3,2},{4,5},{5,4},{6,7},{7,6},{8,9},{9,8},{10,11... | collective-permute-start | bytes 3145736 | tf_op jit(solution)/shard_map/ppermute | solution.py:357
  153.2 25.9 %collective-permute-start.28 = (bf16[256,1024]{1,0:T(8,128)(2,1)S(1)}, bf16[256,1024]{1,0:T(8,128)(2,1)S(1)}, u32[]{:S(2)}, u32[]{:S(2)}) collective-permute-start(bf16[256,1024]{1,0:T(8,128)(2,1)S(1)} %add_convert_fusion.1), channel_id=1, source_target_pairs={{0,16},{8,24},{16,0},{24,8},{1,17},{9,25},{17,1},{25,9},{2,18},{10... | collective-permute-start | bytes 1572872 | tf_op jit(solution)/shard_map/ppermute | solution.py:284
  180.4 7.2 %collective-permute-start.29 = (bf16[128,1024]{1,0:T(8,128)(2,1)S(1)}, bf16[128,1024]{1,0:T(8,128)(2,1)S(1)}, u32[]{:S(2)}, u32[]{:S(2)}) collective-permute-start(bf16[128,1024]{1,0:T(8,128)(2,1)S(1)} %constant_dynamic-slice_fusion), channel_id=1, source_target_pairs={{0,8},{8,0},{16,24},{24,16},{1,9},{9,1},{17,25},{25,17},{2,10},{10... | collective-permute-start | bytes 786440 | tf_op jit(solution)/shard_map/ppermute | solution.py:284
  (41 other events, 247.9 us)

commit v10 on v9

--- a/solution.py
+++ b/solution.py
@@ -193,10 +193,9 @@
 
 
 def project_kernel(place_ref, *refs):
-    attended_refs, weight_refs, out_ref = refs[:4], refs[4:8], refs[8]
+    attended_refs, weight_refs, out_ref = refs[:4], refs[4:-1], refs[-1]
     hi = place_ref[0]
-    lo = place_ref[1]
-    side = lax.div(hi, 2) ^ place_ref[2]
+    side = lax.div(hi, 2) ^ place_ref[1]
     depth = attended_refs[0].shape[1]
     features, width = weight_refs[0].shape
     span = features // 4
@@ -209,8 +208,7 @@
                 weight_ref[pl.ds(pl.multiple_of(first, depth), depth), :],
                 preferred_element_type=jnp.float32,
             )
-        columns = pl.ds(pl.multiple_of((lo ^ r) * width, width), width)
-        out_ref[:, columns] = total.astype(out_ref.dtype)
+        out_ref[:, pl.ds(r * width, width)] = total.astype(out_ref.dtype)
 
 
 def project(place, attended_parts, weights):
@@ -218,10 +216,32 @@
     width = weights[0].shape[1]
     return local_kernel(
         project_kernel,
-        jax.ShapeDtypeStruct((tokens, 4 * width), jnp.bfloat16),
+        jax.ShapeDtypeStruct((tokens, len(weights) * width), jnp.bfloat16),
         (place, *attended_parts, *weights),
-        2 * tokens * 4 * depth * 4 * width,
+        2 * tokens * 4 * depth * len(weights) * width,
     )
+
+
+def assemble_kernel(place_ref, *refs):
+    piece_refs, out_ref = refs[:-1], refs[-1]
+    which = lax.rem(place_ref[0], 2)
+    lo = place_ref[1]
+    width = out_ref.shape[1] // 8
+    chunks = len(piece_refs) // 2
+    for d in range(2):
+        for r in range(4):
+            piece_ref = piece_refs[d * chunks + r * chunks // 4]
+            block = (which ^ d) * 4 + (lo ^ r)
+            out_ref[:, pl.ds(pl.multiple_of(block * width, width), width)] = piece_ref[
+                :, pl.ds(r % (4 // chunks) * width, width)
+            ]
+
+
+def assemble(place, pieces):
+    rows = pieces[0].shape[0]
+    width = sum(piece.shape[1] for piece in pieces)
+    shape = jax.ShapeDtypeStruct((rows, width), jnp.bfloat16)
+    return local_kernel(assemble_kernel, shape, (place, *pieces), rows * width)
 
 
 def normalised(tokens, norm_gain):
@@ -267,6 +287,10 @@
     return lax.optimization_barrier((value, *earlier))[0]
 
 
+def corner_after(blocks, *earlier):
+    return corner([blocks[0], *lax.optimization_barrier((*blocks[1:], *earlier))[:2]])
+
+
 def beside(block, r):
     return lax.ppermute(block, "lo", [(i, i ^ r) for i in range(4)])
 
@@ -305,13 +329,12 @@
             axis=1,
         )
 
-    stage = ()
-    weights = []
-    for sources, size in (((w_key, w_value), HD), ((w_query,), heads)):
-        came = along(columns_for(1 - which, sources, size), 1)
-        both = jnp.concatenate([columns_for(which, sources, size), came], axis=0)
-        weights.append(corner(sides(after(both, *stage) if stage else both)))
-        stage = weights[-1][3:]
+    def exchanged(sources, width):
+        came = along(columns_for(1 - which, sources, width), 1)
+        return jnp.concatenate([columns_for(which, sources, width), came], axis=0)
+
+    pair_weight = corner(sides(exchanged((w_key, w_value), HD)))
+    query_sides = sides(after(exchanged((w_query,), heads), *pair_weight[3:]))
 
     normed = normalised(tokens, norm_gain)
     own = lax.dynamic_slice_in_dim(normed, which_half * depth, depth, 1)
@@ -328,52 +351,52 @@
     row_index = jnp.arange(4 * rows, dtype=jnp.int32)
     cosine, sine = rotary_tables((row_index // rows * 4 + lo) * rows + row_index % rows)
 
-    kept, sent = product(index, token_parts, weights[0], 0, 1)
+    kept, sent = product(index, token_parts, pair_weight, 0, 1)
+    query_weight = corner_after(query_sides, sent)
+
     features_here = w_out.shape[0] // 2
     out_own = lax.dynamic_slice_in_dim(w_out, which_half * features_here, features_here, 0)
     out_other = lax.dynamic_slice_in_dim(w_out, (1 - which_half) * features_here, features_here, 0)
-    out_other = along(after(out_other, halves), 2)
+    out_other = along(after(out_other, sent), 2)
     kv_own = finish_pair(cosine, sine, [after(kept, out_other), along(sent, 2)])
-    kv_going = after(kv_own, *weights[1][3:])
+    kv_going = after(kv_own, *query_weight[3:])
     kv_parts = [kv_own] + [beside(kv_going, r) for r in range(1, 4)]
 
     firsts = jnp.stack([lo, lo, lo ^ 1, lo ^ 2, lo ^ 3]) * rows
     seen = jnp.concatenate([firsts, doc_starts])
     out_sides = sides(after(jnp.concatenate([out_own, out_other], axis=0), *kv_parts[1:]))
-    products = [product(index, token_parts, weights[1], c, 2) for c in range(2)]
+    products = [product(index, token_parts, query_weight, c, 2) for c in range(2)]
     products[0] = (after(products[0][0], products[1][0]), products[0][1])
     attended = [
         attention(seen, cosine, sine, [kept, along(sent, 2)], kv_parts, 4, 4 * rows)
         for kept, sent in products
     ]
-    out_sides[1:] = lax.optimization_barrier((*out_sides[1:], attended[1]))[:2]
-    out_blocks = corner(out_sides)
+    out_blocks = corner_after(out_sides, *attended)
     out_blocks[3:] = [jnp.concatenate(out_blocks[3:], axis=0)]
     attended += [along(chunk, 1) for chunk in attended]
 
-    theirs, mine = [
-        project(jnp.stack([hi, lo, group]), attended, out_blocks) for group in (1 - core, core)
-    ]
-    theirs = lax.ppermute(theirs, "head", [(0, 1), (1, 0)])
-
     def added(one, two):
         return (one.astype(jnp.float32) + two.astype(jnp.float32)).astype(jnp.bfloat16)
 
     kept = 2 * rows
-    shares = [
-        added(
-            lax.dynamic_slice_in_dim(mine, z * kept, kept, 0),
-            lax.dynamic_slice_in_dim(theirs, z * kept, kept, 0),
-        )
-        for z in (which_half, 1 - which_half)
-    ]
-    summed = added(shares[0], along(shares[1], 2))
-    here = lax.dynamic_slice_in_dim(summed, which * rows, rows, 0)
-    there = along(lax.dynamic_slice_in_dim(summed, (1 - which) * rows, rows, 0), 1)
-    first = which == 0
-    return jnp.concatenate(
-        [jnp.where(first, here, there), jnp.where(first, there, here)], axis=1
-    )
+    here, there, shares = [], [], []
+    for blocks in (out_blocks[:2], out_blocks[2:]):
+        blocks = [after(blocks[0], *shares[1:]), *blocks[1:]]
+        theirs, mine = [
+            project(jnp.stack([hi, group]), attended, blocks) for group in (1 - core, core)
+        ]
+        theirs = lax.ppermute(theirs, "head", [(0, 1), (1, 0)])
+        shares = [
+            added(
+                lax.dynamic_slice_in_dim(mine, z * kept, kept, 0),
+                lax.dynamic_slice_in_dim(theirs, z * kept, kept, 0),
+            )
+            for z in (which_half, 1 - which_half)
+        ]
+        summed = added(shares[0], along(shares[1], 2))
+        here.append(lax.dynamic_slice_in_dim(summed, which * rows, rows, 0))
+        there.append(along(lax.dynamic_slice_in_dim(summed, (1 - which) * rows, rows, 0), 1))
+    return assemble(index, here + there)
 
 
 def solution(mesh):

time: 191 us -> 198 us (1.037)
  local copies, waits for them, and re-layouts: 21.4 us -> 14.4 us
  waiting for transfers between devices: 87.7 us -> 94.5 us
  other arithmetic: 8.96 us -> 12.9 us
  starting transfers between devices: 39.6 us -> 42.3 us
    ppermute x13 -> x15, waiting for transfers between devices: 56.2 us -> 71 us  [along(): return lax.ppermute(block, 'hi', [(i, i ^ d) for i in range(4)])]
    ppermute x15, waiting for transfers between devices: 31.4 us -> 23.3 us  [beside(): return lax.ppermute(block, 'lo', [(i, i ^ r) for i in range(4)])]
    unnamed x89 -> x67, local copies, waits for them, and re-layouts: 10.1 us -> 4.94 us
    convert_element_type x2 -> x4, other arithmetic: 2.54 us -> 5.11 us  [added(): (one.astype(jnp.float32) + two.astype(jnp.float32)).astype(jnp.bfloat16)]
    ppermute x1 -> x2, starting transfers between devices: 3.15 us -> 5.42 us  [line_device(): theirs = lax.ppermute(theirs, 'head', [(0, 1), (1, 0)])]
    pallas_call x8 -> x11, Pallas kernels: 30.3 us -> 31.3 us  [local_kernel(): pl.pallas_call(body, in_specs=[pl.BlockSpec(memory_space=pltpu.SMEM)] + [...]
    ppermute x13 -> x15, starting transfers between devices: 19.7 us -> 18.8 us  [along(): return lax.ppermute(block, 'hi', [(i, i ^ d) for i in range(4)])]
  transfers between devices with their start and end apart: 30 -> 33, of which waited for: 16 -> 17; matrix products, arithmetic and copies ran while one was open for 9% -> 11% of each run, Pallas kernels for 14% -> 13%
where the time goes in v10:
time: 198 us; the launch traced here: 196 us
  waiting for transfers between devices  94.5 us (48%)
  starting transfers between devices  42.3 us (21%)
  Pallas kernels  31.3 us (16%)
  local copies, waits for them, and re-layouts  14.4 us (7%)
  other arithmetic  12.9 us (7%)
    ppermute x15, waiting for transfers between devices, along(): return lax.ppermute(block, 'hi', [(i, i ^ d) for i in range(4)])  71 us
    pallas_call x11, Pallas kernels, local_kernel(): pl.pallas_call(body, in_specs=[pl.BlockSpec(memory_space=pltpu.SMEM)] + [...  31.3 us
    ppermute x15, waiting for transfers between devices, beside(): return lax.ppermute(block, 'lo', [(i, i ^ r) for i in range(4)])  23.3 us
    ppermute x15, starting transfers between devices, along(): return lax.ppermute(block, 'hi', [(i, i ^ d) for i in range(4)])  18.8 us
    ppermute x15, starting transfers between devices, beside(): return lax.ppermute(block, 'lo', [(i, i ^ r) for i in range(4)])  14 us
    ppermute x2, starting transfers between devices, line_device(): theirs = lax.ppermute(theirs, 'head', [(0, 1), (1, 0)])  5.42 us
    convert_element_type x4, other arithmetic, added(): (one.astype(jnp.float32) + two.astype(jnp.float32)).astype(jnp.bfloat16)  5.11 us
    unnamed x67, local copies, waits for them, and re-layouts  4.94 us
  transfers between devices with their start and end apart: 33, of which 17 were waited for; matrix products, arithmetic and copies ran while one was open for 11% of the time, Pallas kernels for 13%

profile of v10, /device:TPU:1, one launch (start us, length us, event | category | flops | bytes accessed | tf_op | source)
XLA Modules:
  0.0 195.8 jit_solution(11044868554278111635)
XLA Ops:
  2.2 2.1 %collective-permute-start.4 = (bf16[256,1024]{1,0:T(8,128)(2,1)}, bf16[256,1024]{1,0:T(8,128)(2,1)}, u32[]{:S(2)}, u32[]{:S(2)}) collective-permute-start(bf16[256,1024]{1,0:T(8,128)(2,1)} %pad_maximum_fusion.2), channel_id=1, source_target_pairs={{0,8},{8,0},{16,24},{24,16},{1,9},{9,1},{17,25},{25,17},{2,10},{10... | collective-permute-start | bytes 1572872 | tf_op jit(solution)/shard_map/ppermute | solution.py:308
  5.1 16.7 %collective-permute-done.5 = bf16[256,512]{1,0:T(8,128)(2,1)S(1)} collective-permute-done((bf16[256,512]{1,0:T(8,128)(2,1)S(1)}, bf16[256,512]{1,0:T(8,128)(2,1)S(1)}, u32[]{:S(2)}, u32[]{:S(2)}) %collective-permute-start.5) | collective-permute-done | bytes 262176 | tf_op jit(solution)/shard_map/ppermute | solution.py:308
  26.7 2.3 %collective-permute-start.1 = (bf16[128,1024]{1,0:T(8,128)(2,1)S(1)}, bf16[128,1024]{1,0:T(8,128)(2,1)}, u32[]{:S(2)}, u32[]{:S(2)}) collective-permute-start(bf16[128,1024]{1,0:T(8,128)(2,1)S(1)} %get-tuple-element.49), channel_id=1, source_target_pairs={{0,16},{8,24},{16,0},{24,8},{1,17},{9,25},{17,1},{25,9},{2,18},{10... | collective-permute-start | bytes 786440 | tf_op jit(solution)/shard_map/ppermute | solution.py:308
  29.0 5.1 %collective-permute-done.6.refs_5_ = bf16[512,512]{1,0:T(8,128)(2,1)S(1)} collective-permute-done((bf16[512,512]{1,0:T(8,128)(2,1)S(1)}, bf16[512,512]{1,0:T(8,128)(2,1)S(1)}, u32[]{:S(2)}, u32[]{:S(2)}) %collective-permute-start.6) | collective-permute-done | bytes 524320 | tf_op jit(solution)/shard_map/ppermute | solution.py:295
  37.8 1.6 collective-permute-start.2
  44.7 4.1 %collective-permute-start.3 = (bf16[384,1024]{1,0:T(8,128)(2,1)S(1)}, bf16[384,1024]{1,0:T(8,128)(2,1)S(1)}, u32[]{:S(2)}, u32[]{:S(2)}) collective-permute-start(bf16[384,1024]{1,0:T(8,128)(2,1)S(1)} %constant_dynamic-update-slice_fusion.refs_1_), channel_id=1, source_target_pairs={{0,1},{1,0},{2,3},{3,2},{4,5},{5,4},{6,7},{7,6},{8,9},{9,8},{10,11... | collective-permute-start | bytes 2359304 | tf_op jit(solution)/shard_map/ppermute | solution.py:348
  51.3 1.9 shard_map.100
  53.9 2.3 %collective-permute-start.15 = (bf16[1024,256]{1,0:T(8,128)(2,1)}, bf16[1024,256]{1,0:T(8,128)(2,1)}, u32[]{:S(2)}, u32[]{:S(2)}) collective-permute-start(bf16[1024,256]{1,0:T(8,128)(2,1)} %get-tuple-element.33), channel_id=1, source_target_pairs={{0,16},{8,24},{16,0},{24,8},{1,17},{9,25},{17,1},{25,9},{2,18},{10... | collective-permute-start | bytes 1572872 | tf_op jit(solution)/shard_map/ppermute | solution.py:308
  56.2 7.2 %collective-permute-done.10.refs_4_ = bf16[512,1024]{1,0:T(8,128)(2,1)S(1)} collective-permute-done((bf16[512,1024]{1,0:T(8,128)(2,1)S(1)}, bf16[512,1024]{1,0:T(8,128)(2,1)S(1)}, u32[]{:S(2)}, u32[]{:S(2)}) %collective-permute-start.10) | collective-permute-done | bytes 1048608 | tf_op jit(solution)/shard_map/ppermute | solution.py:295
  67.5 1.9 fusion.3
  69.5 2.3 %collective-permute-start.16 = (bf16[512,256]{1,0:T(8,128)(2,1)}, bf16[512,256]{1,0:T(8,128)(2,1)S(1)}, u32[]{:S(2)}, u32[]{:S(2)}) collective-permute-start(bf16[512,256]{1,0:T(8,128)(2,1)} %copy-done.18), channel_id=1, source_target_pairs={{0,16},{8,24},{16,0},{24,8},{1,17},{9,25},{17,1},{25,9},{2,18},{10... | collective-permute-start | bytes 786440 | tf_op jit(solution)/shard_map/ppermute | solution.py:308
  73.4 12.1 %collective-permute-done.15 = bf16[1024,256]{1,0:T(8,128)(2,1)} collective-permute-done((bf16[1024,256]{1,0:T(8,128)(2,1)}, bf16[1024,256]{1,0:T(8,128)(2,1)}, u32[]{:S(2)}, u32[]{:S(2)}) %collective-permute-start.15) | collective-permute-done | bytes 524320 | tf_op jit(solution)/shard_map/ppermute | solution.py:308
  85.5 5.5 %collective-permute-done.16.refs_1_ = bf16[512,256]{1,0:T(8,128)(2,1)S(1)} collective-permute-done((bf16[512,256]{1,0:T(8,128)(2,1)}, bf16[512,256]{1,0:T(8,128)(2,1)S(1)}, u32[]{:S(2)}, u32[]{:S(2)}) %collective-permute-start.16) | collective-permute-done | bytes 262176 | tf_op jit(solution)/shard_map/ppermute | solution.py:308
  93.9 2.6 %shard_map.101 = (bf16[512,256]{1,0:T(8,128)(2,1)S(1)}, bf16[512,256]{1,0:T(8,128)(2,1)S(1)}) custom-call(s32[5]{0:T(128)S(1)} %get-tuple-element.67.place_ref, bf16[128,2048]{1,0:T(8,128)(2,1)S(1)} %constant_dynamic-slice_fusion.20.refs_0_, bf16[384,1024]{1,0:T(8,128)(2,1)S(1)} %constant_dynamic-update-slice_fusion.refs_1_, ...), custom_call_target="tpu_custom_call" | custom-call | flops 1073741824 | bytes 6291476 | tf_op jit(solution)/shard_map/pallas_call | solution.py:18
  98.0 2.6 %shard_map.102 = (bf16[512,256]{1,0:T(8,128)(2,1)S(1)}, bf16[512,256]{1,0:T(8,128)(2,1)S(1)}) custom-call(s32[5]{0:T(128)S(1)} %get-tuple-element.41.place_ref, bf16[128,2048]{1,0:T(8,128)(2,1)S(1)} %constant_dynamic-slice_fusion.20.refs_0_, bf16[384,1024]{1,0:T(8,128)(2,1)S(1)} %constant_dynamic-update-slice_fusion.refs_1_, ...), custom_call_target="tpu_custom_call" | custom-call | flops 1073741824 | bytes 6291476 | tf_op jit(solution)/shard_map/pallas_call | solution.py:18
  100.6 2.4 %collective-permute-start.20 = (bf16[512,256]{1,0:T(8,128)(2,1)S(1)}, bf16[512,256]{1,0:T(8,128)(2,1)S(1)}, u32[]{:S(2)}, u32[]{:S(2)}) collective-permute-start(bf16[512,256]{1,0:T(8,128)(2,1)S(1)} %get-tuple-element.36), channel_id=1, source_target_pairs={{0,16},{8,24},{16,0},{24,8},{1,17},{9,25},{17,1},{25,9},{2,18},{10... | collective-permute-start | bytes 786440 | tf_op jit(solution)/shard_map/ppermute | solution.py:308
  106.4 9.4 %collective-permute-done.14.refs_1_ = bf16[512,256]{1,0:T(8,128)(2,1)S(1)} collective-permute-done((bf16[512,256]{1,0:T(8,128)(2,1)S(1)}, bf16[512,256]{1,0:T(8,128)(2,1)S(1)}, u32[]{:S(2)}, u32[]{:S(2)}) %collective-permute-start.14) | collective-permute-done | bytes 262176 | tf_op jit(solution)/shard_map/ppermute | solution.py:308
  115.7 6.3 %shard_map.104.refs_0_ = bf16[512,256]{1,0:T(8,128)(2,1)S(1)} custom-call(s32[21]{0:T(128)S(1)} %pad_add_fusion.2.place_ref, f32[512,128]{1,0:T(8,128)S(1)} %get-tuple-element.68.cos_ref, f32[512,128]{1,0:T(8,128)S(1)} %get-tuple-element.69.sin_ref, bf16[512,256]{1,0:T(8,128)(2,1)S(1)} %get-tuple-element.30.refs_0_, ...), custom_call_target="tpu_custom_call" | custom-call | flops 8589934592 | bytes 2097236 | tf_op jit(solution)/shard_map/pallas_call | solution.py:18
  122.2 7.3 %shard_map.105.refs_1_ = bf16[512,256]{1,0:T(8,128)(2,1)} custom-call(s32[21]{0:T(128)S(1)} %pad_add_fusion.2.place_ref, f32[512,128]{1,0:T(8,128)S(1)} %get-tuple-element.68.cos_ref, f32[512,128]{1,0:T(8,128)S(1)} %get-tuple-element.69.sin_ref, bf16[512,256]{1,0:T(8,128)(2,1)S(1)} %get-tuple-element.29.refs_0_, ...), custom_call_target="tpu_custom_call" | custom-call | flops 8589934592 | bytes 2097236 | tf_op jit(solution)/shard_map/pallas_call | solution.py:18
  131.0 4.0 %collective-permute-done.22.refs_3_ = bf16[512,256]{1,0:T(8,128)(2,1)} collective-permute-done((bf16[512,256]{1,0:T(8,128)(2,1)}, bf16[512,256]{1,0:T(8,128)(2,1)}, u32[]{:S(2)}, u32[]{:S(2)}) %collective-permute-start.22) | collective-permute-done | bytes 262176 | tf_op jit(solution)/shard_map/ppermute | solution.py:308
  135.0 2.6 %shard_map.107 = bf16[512,512]{1,0:T(8,128)(2,1)} custom-call(s32[2]{0:T(128)S(1)} %pad_add_fusion.7.place_ref, bf16[512,256]{1,0:T(8,128)(2,1)S(1)} %shard_map.104.refs_0_, bf16[512,256]{1,0:T(8,128)(2,1)} %shard_map.105.refs_1_, bf16[512,256]{1,0:T(8,128)(2,1)} %collective-permute-done.21.refs_2_, bf16[512,256]{1,0:T(8,128)(2,1)} %collective-permute-done.22.refs_3_, ...), custom_call_target="tpu_custom_call" | custom-call | flops 536870912 | bytes 3145736 | tf_op jit(solution)/shard_map/pallas_call | solution.py:18
  137.6 4.3 %collective-permute-start.25 = (bf16[512,512]{1,0:T(8,128)(2,1)}, bf16[512,512]{1,0:T(8,128)(2,1)}, u32[]{:S(2)}, u32[]{:S(2)}) collective-permute-start(bf16[512,512]{1,0:T(8,128)(2,1)} %shard_map.107), channel_id=1, source_target_pairs={{0,1},{1,0},{2,3},{3,2},{4,5},{5,4},{6,7},{7,6},{8,9},{9,8},{10,11... | collective-permute-start | bytes 1572872 | tf_op jit(solution)/shard_map/ppermute | solution.py:388
  145.2 1.8 shard_map.106
  147.1 1.9 add_convert_fusion.4
  149.0 7.7 %collective-permute-done.27 = bf16[1024,256]{1,0:T(8,128)(2,1)} collective-permute-done((bf16[1024,256]{1,0:T(8,128)(2,1)}, bf16[1024,256]{1,0:T(8,128)(2,1)}, u32[]{:S(2)}, u32[]{:S(2)}) %collective-permute-start.27) | collective-permute-done | bytes 524320 | tf_op jit(solution)/shard_map/ppermute | solution.py:295
  159.5 2.6 %shard_map.109 = bf16[512,512]{1,0:T(8,128)(2,1)} custom-call(s32[2]{0:T(128)S(1)} %pad_add_fusion.7.place_ref, bf16[512,256]{1,0:T(8,128)(2,1)S(1)} %shard_map.104.refs_0_, bf16[512,256]{1,0:T(8,128)(2,1)} %shard_map.105.refs_1_, bf16[512,256]{1,0:T(8,128)(2,1)} %collective-permute-done.21.refs_2_, bf16[512,256]{1,0:T(8,128)(2,1)} %collective-permute-done.22.refs_3_, ...), custom_call_target="tpu_custom_call" | custom-call | flops 536870912 | bytes 3145736 | tf_op jit(solution)/shard_map/pallas_call | solution.py:18
  163.3 1.6 collective-permute-start.26
  164.9 1.9 shard_map.108
  168.6 15.0 %collective-permute-done.26 = bf16[256,512]{1,0:T(8,128)(2,1)} collective-permute-done((bf16[256,512]{1,0:T(8,128)(2,1)}, bf16[256,512]{1,0:T(8,128)(2,1)}, u32[]{:S(2)}, u32[]{:S(2)}) %collective-permute-start.26) | collective-permute-done | bytes 262176 | tf_op jit(solution)/shard_map/ppermute | solution.py:308
  184.9 4.3 %collective-permute-done.30 = bf16[256,512]{1,0:T(8,128)(2,1)S(1)} collective-permute-done((bf16[256,512]{1,0:T(8,128)(2,1)S(1)}, bf16[256,512]{1,0:T(8,128)(2,1)S(1)}, u32[]{:S(2)}, u32[]{:S(2)}) %collective-permute-start.30) | collective-permute-done | bytes 262176 | tf_op jit(solution)/shard_map/ppermute | solution.py:308
  190.4 1.8 collective-permute-done.31.refs_2_
  192.3 2.2 %collective-permute-done.32.refs_3_ = bf16[128,512]{1,0:T(8,128)(2,1)S(1)} collective-permute-done((bf16[128,512]{1,0:T(8,128)(2,1)S(1)}, bf16[128,512]{1,0:T(8,128)(2,1)S(1)}, u32[]{:S(2)}, u32[]{:S(2)}) %collective-permute-start.32) | collective-permute-done | bytes 131104 | tf_op jit(solution)/shard_map/ppermute | solution.py:308
  (151 shorter events, 47.7 us)
Async XLA Ops:
  2.2 38.2 %collective-permute-start.4 = (bf16[256,1024]{1,0:T(8,128)(2,1)}, bf16[256,1024]{1,0:T(8,128)(2,1)}, u32[]{:S(2)}, u32[]{:S(2)}) collective-permute-start(bf16[256,1024]{1,0:T(8,128)(2,1)} %pad_maximum_fusion.2), channel_id=1, source_target_pairs={{0,8},{8,0},{16,24},{24,16},{1,9},{9,1},{17,25},{25,17},{2,10},{10... | collective-permute-start | bytes 1572872 | tf_op jit(solution)/shard_map/ppermute | solution.py:308
  4.5 17.3 %collective-permute-start.5 = (bf16[256,512]{1,0:T(8,128)(2,1)S(1)}, bf16[256,512]{1,0:T(8,128)(2,1)S(1)}, u32[]{:S(2)}, u32[]{:S(2)}) collective-permute-start(bf16[256,512]{1,0:T(8,128)(2,1)S(1)} %pad_maximum_fusion.6), channel_id=1, source_target_pairs={{0,8},{8,0},{16,24},{24,16},{1,9},{9,1},{17,25},{25,17},{2,10},{10... | collective-permute-start | bytes 786440 | tf_op jit(solution)/shard_map/ppermute | solution.py:308
  21.8 12.4 %collective-permute-start.6 = (bf16[512,512]{1,0:T(8,128)(2,1)S(1)}, bf16[512,512]{1,0:T(8,128)(2,1)S(1)}, u32[]{:S(2)}, u32[]{:S(2)}) collective-permute-start(bf16[512,512]{1,0:T(8,128)(2,1)S(1)} %pad_maximum_fusion.3.refs_3_), channel_id=1, source_target_pairs={{0,4},{2,6},{4,0},{6,2},{1,5},{3,7},{5,1},{7,3},{8,12},{10,14},{12... | collective-permute-start | bytes 1572872 | tf_op jit(solution)/shard_map/ppermute | solution.py:295
  23.0 12.7 %collective-permute-start.8 = (bf16[512,512]{1,0:T(8,128)(2,1)S(1)}, bf16[512,512]{1,0:T(8,128)(2,1)S(1)}, u32[]{:S(2)}, u32[]{:S(2)}) collective-permute-start(bf16[512,512]{1,0:T(8,128)(2,1)S(1)} %pad_maximum_fusion.3.refs_3_), channel_id=1, source_target_pairs={{0,2},{2,0},{4,6},{6,4},{1,3},{3,1},{5,7},{7,5},{8,10},{10,8},{12,... | collective-permute-start | bytes 1572872 | tf_op jit(solution)/shard_map/ppermute | solution.py:295
  25.4 12.3 %collective-permute-start = (bf16[128,1024]{1,0:T(8,128)(2,1)}, bf16[128,1024]{1,0:T(8,128)(2,1)}, u32[]{:S(2)}, u32[]{:S(2)}) collective-permute-start(bf16[128,1024]{1,0:T(8,128)(2,1)} %get-tuple-element.50), channel_id=1, source_target_pairs={{0,8},{8,0},{16,24},{24,16},{1,9},{9,1},{17,25},{25,17},{2,10},{10... | collective-permute-start | bytes 786440 | tf_op jit(solution)/shard_map/ppermute | solution.py:308
  26.7 11.0 %collective-permute-start.1 = (bf16[128,1024]{1,0:T(8,128)(2,1)S(1)}, bf16[128,1024]{1,0:T(8,128)(2,1)}, u32[]{:S(2)}, u32[]{:S(2)}) collective-permute-start(bf16[128,1024]{1,0:T(8,128)(2,1)S(1)} %get-tuple-element.49), channel_id=1, source_target_pairs={{0,16},{8,24},{16,0},{24,8},{1,17},{9,25},{17,1},{25,9},{2,18},{10... | collective-permute-start | bytes 786440 | tf_op jit(solution)/shard_map/ppermute | solution.py:308
  34.9 6.6 %collective-permute-start.7 = (bf16[256,512]{1,0:T(8,128)(2,1)}, bf16[256,512]{1,0:T(8,128)(2,1)S(1)}, u32[]{:S(2)}, u32[]{:S(2)}) collective-permute-start(bf16[256,512]{1,0:T(8,128)(2,1)} %slice.24), channel_id=1, source_target_pairs={{0,2},{2,0},{4,6},{6,4},{1,3},{3,1},{5,7},{7,5},{8,10},{10,8},{12,... | collective-permute-start | bytes 786440 | tf_op jit(solution)/shard_map/ppermute | solution.py:295
  36.5 5.7 %collective-permute-start.9 = (bf16[256,512]{1,0:T(8,128)(2,1)}, bf16[256,512]{1,0:T(8,128)(2,1)S(1)}, u32[]{:S(2)}, u32[]{:S(2)}) collective-permute-start(bf16[256,512]{1,0:T(8,128)(2,1)} %slice.25), channel_id=1, source_target_pairs={{0,4},{2,6},{4,0},{6,2},{1,5},{3,7},{5,1},{7,3},{8,12},{10,14},{12... | collective-permute-start | bytes 786440 | tf_op jit(solution)/shard_map/ppermute | solution.py:295
  37.8 6.9 %collective-permute-start.2 = (bf16[128,1024]{1,0:T(8,128)(2,1)}, bf16[128,1024]{1,0:T(8,128)(2,1)S(1)}, u32[]{:S(2)}, u32[]{:S(2)}) collective-permute-start(bf16[128,1024]{1,0:T(8,128)(2,1)} %collective-permute-done.1), channel_id=1, source_target_pairs={{0,8},{8,0},{16,24},{24,16},{1,9},{9,1},{17,25},{25,17},{2,10},{10... | collective-permute-start | bytes 786440 | tf_op jit(solution)/shard_map/ppermute | solution.py:308
  42.2 21.3 %collective-permute-start.10 = (bf16[512,1024]{1,0:T(8,128)(2,1)S(1)}, bf16[512,1024]{1,0:T(8,128)(2,1)S(1)}, u32[]{:S(2)}, u32[]{:S(2)}) collective-permute-start(bf16[512,1024]{1,0:T(8,128)(2,1)S(1)} %pad_maximum_fusion.refs_3_), channel_id=1, source_target_pairs={{0,2},{2,0},{4,6},{6,4},{1,3},{3,1},{5,7},{7,5},{8,10},{10,8},{12,... | collective-permute-start | bytes 3145736 | tf_op jit(solution)/shard_map/ppermute | solution.py:295
  42.9 21.3 %collective-permute-start.11 = (bf16[512,1024]{1,0:T(8,128)(2,1)S(1)}, bf16[512,1024]{1,0:T(8,128)(2,1)S(1)}, u32[]{:S(2)}, u32[]{:S(2)}) collective-permute-start(bf16[512,1024]{1,0:T(8,128)(2,1)S(1)} %pad_maximum_fusion.refs_3_), channel_id=1, source_target_pairs={{0,4},{2,6},{4,0},{6,2},{1,5},{3,7},{5,1},{7,3},{8,12},{10,14},{12... | collective-permute-start | bytes 3145736 | tf_op jit(solution)/shard_map/ppermute | solution.py:295
  44.7 6.0 %collective-permute-start.3 = (bf16[384,1024]{1,0:T(8,128)(2,1)S(1)}, bf16[384,1024]{1,0:T(8,128)(2,1)S(1)}, u32[]{:S(2)}, u32[]{:S(2)}) collective-permute-start(bf16[384,1024]{1,0:T(8,128)(2,1)S(1)} %constant_dynamic-update-slice_fusion.refs_1_), channel_id=1, source_target_pairs={{0,1},{1,0},{2,3},{3,2},{4,5},{5,4},{6,7},{7,6},{8,9},{9,8},{10,11... | collective-permute-start | bytes 2359304 | tf_op jit(solution)/shard_map/ppermute | solution.py:348
  53.9 31.6 %collective-permute-start.15 = (bf16[1024,256]{1,0:T(8,128)(2,1)}, bf16[1024,256]{1,0:T(8,128)(2,1)}, u32[]{:S(2)}, u32[]{:S(2)}) collective-permute-start(bf16[1024,256]{1,0:T(8,128)(2,1)} %get-tuple-element.33), channel_id=1, source_target_pairs={{0,16},{8,24},{16,0},{24,8},{1,17},{9,25},{17,1},{25,9},{2,18},{10... | collective-permute-start | bytes 1572872 | tf_op jit(solution)/shard_map/ppermute | solution.py:308
  65.1 26.1 %collective-permute-start.12 = (bf16[256,1024]{1,0:T(8,128)(2,1)}, bf16[256,1024]{1,0:T(8,128)(2,1)}, u32[]{:S(2)}, u32[]{:S(2)}) collective-permute-start(bf16[256,1024]{1,0:T(8,128)(2,1)} %slice.20), channel_id=1, source_target_pairs={{0,2},{2,0},{4,6},{6,4},{1,3},{3,1},{5,7},{7,5},{8,10},{10,8},{12,... | collective-permute-start | bytes 1572872 | tf_op jit(solution)/shard_map/ppermute | solution.py:295
  66.5 24.7 %collective-permute-start.13 = (bf16[256,1024]{1,0:T(8,128)(2,1)}, bf16[256,1024]{1,0:T(8,128)(2,1)}, u32[]{:S(2)}, u32[]{:S(2)}) collective-permute-start(bf16[256,1024]{1,0:T(8,128)(2,1)} %slice.21), channel_id=1, source_target_pairs={{0,4},{2,6},{4,0},{6,2},{1,5},{3,7},{5,1},{7,3},{8,12},{10,14},{12... | collective-permute-start | bytes 1572872 | tf_op jit(solution)/shard_map/ppermute | solution.py:295
  69.5 21.5 %collective-permute-start.16 = (bf16[512,256]{1,0:T(8,128)(2,1)}, bf16[512,256]{1,0:T(8,128)(2,1)S(1)}, u32[]{:S(2)}, u32[]{:S(2)}) collective-permute-start(bf16[512,256]{1,0:T(8,128)(2,1)} %copy-done.18), channel_id=1, source_target_pairs={{0,16},{8,24},{16,0},{24,8},{1,17},{9,25},{17,1},{25,9},{2,18},{10... | collective-permute-start | bytes 786440 | tf_op jit(solution)/shard_map/ppermute | solution.py:308
  91.2 11.8 %collective-permute-start.17 = (bf16[512,256]{1,0:T(8,128)(2,1)S(1)}, bf16[512,256]{1,0:T(8,128)(2,1)S(1)}, u32[]{:S(2)}, u32[]{:S(2)}) collective-permute-start(bf16[512,256]{1,0:T(8,128)(2,1)S(1)} %shard_map.103.refs_2_), channel_id=1, source_target_pairs={{0,2},{2,0},{4,6},{6,4},{1,3},{3,1},{5,7},{7,5},{8,10},{10,8},{12,... | collective-permute-start | bytes 786440 | tf_op jit(solution)/shard_map/ppermute | solution.py:295
  92.6 10.4 %collective-permute-start.18 = (bf16[512,256]{1,0:T(8,128)(2,1)S(1)}, bf16[512,256]{1,0:T(8,128)(2,1)S(1)}, u32[]{:S(2)}, u32[]{:S(2)}) collective-permute-start(bf16[512,256]{1,0:T(8,128)(2,1)S(1)} %shard_map.103.refs_2_), channel_id=1, source_target_pairs={{0,4},{2,6},{4,0},{6,2},{1,5},{3,7},{5,1},{7,3},{8,12},{10,14},{12... | collective-permute-start | bytes 786440 | tf_op jit(solution)/shard_map/ppermute | solution.py:295
  92.8 11.3 %collective-permute-start.19 = (bf16[512,256]{1,0:T(8,128)(2,1)S(1)}, bf16[512,256]{1,0:T(8,128)(2,1)S(1)}, u32[]{:S(2)}, u32[]{:S(2)}) collective-permute-start(bf16[512,256]{1,0:T(8,128)(2,1)S(1)} %shard_map.103.refs_2_), channel_id=1, source_target_pairs={{0,6},{2,4},{4,2},{6,0},{1,7},{3,5},{5,3},{7,1},{8,14},{10,12},{12... | collective-permute-start | bytes 786440 | tf_op jit(solution)/shard_map/ppermute | solution.py:295
  96.6 19.1 %collective-permute-start.14 = (bf16[512,256]{1,0:T(8,128)(2,1)S(1)}, bf16[512,256]{1,0:T(8,128)(2,1)S(1)}, u32[]{:S(2)}, u32[]{:S(2)}) collective-permute-start(bf16[512,256]{1,0:T(8,128)(2,1)S(1)} %get-tuple-element.31), channel_id=1, source_target_pairs={{0,16},{8,24},{16,0},{24,8},{1,17},{9,25},{17,1},{25,9},{2,18},{10... | collective-permute-start | bytes 786440 | tf_op jit(solution)/shard_map/ppermute | solution.py:308
  100.6 21.6 %collective-permute-start.20 = (bf16[512,256]{1,0:T(8,128)(2,1)S(1)}, bf16[512,256]{1,0:T(8,128)(2,1)S(1)}, u32[]{:S(2)}, u32[]{:S(2)}) collective-permute-start(bf16[512,256]{1,0:T(8,128)(2,1)S(1)} %get-tuple-element.36), channel_id=1, source_target_pairs={{0,16},{8,24},{16,0},{24,8},{1,17},{9,25},{17,1},{25,9},{2,18},{10... | collective-permute-start | bytes 786440 | tf_op jit(solution)/shard_map/ppermute | solution.py:308
  104.1 26.9 %collective-permute-start.23 = (bf16[2048,256]{1,0:T(8,128)(2,1)S(1)}, bf16[2048,256]{1,0:T(8,128)(2,1)S(1)}, u32[]{:S(2)}, u32[]{:S(2)}) collective-permute-start(bf16[2048,256]{1,0:T(8,128)(2,1)S(1)} %pad_maximum_fusion.1.refs_4_), channel_id=1, source_target_pairs={{0,2},{2,0},{4,6},{6,4},{1,3},{3,1},{5,7},{7,5},{8,10},{10,8},{12,... | collective-permute-start | bytes 3145736 | tf_op jit(solution)/shard_map/ppermute | solution.py:295
  105.2 25.8 %collective-permute-start.24 = (bf16[2048,256]{1,0:T(8,128)(2,1)S(1)}, bf16[2048,256]{1,0:T(8,128)(2,1)S(1)}, u32[]{:S(2)}, u32[]{:S(2)}) collective-permute-start(bf16[2048,256]{1,0:T(8,128)(2,1)S(1)} %pad_maximum_fusion.1.refs_4_), channel_id=1, source_target_pairs={{0,4},{2,6},{4,0},{6,2},{1,5},{3,7},{5,1},{7,3},{8,12},{10,14},{12... | collective-permute-start | bytes 3145736 | tf_op jit(solution)/shard_map/ppermute | solution.py:295
  122.1 8.9 %collective-permute-start.21 = (bf16[512,256]{1,0:T(8,128)(2,1)S(1)}, bf16[512,256]{1,0:T(8,128)(2,1)}, u32[]{:S(2)}, u32[]{:S(2)}) collective-permute-start(bf16[512,256]{1,0:T(8,128)(2,1)S(1)} %shard_map.104.refs_0_), channel_id=1, source_target_pairs={{0,8},{8,0},{16,24},{24,16},{1,9},{9,1},{17,25},{25,17},{2,10},{10... | collective-permute-start | bytes 786440 | tf_op jit(solution)/shard_map/ppermute | solution.py:308
  129.4 5.5 %collective-permute-start.22 = (bf16[512,256]{1,0:T(8,128)(2,1)}, bf16[512,256]{1,0:T(8,128)(2,1)}, u32[]{:S(2)}, u32[]{:S(2)}) collective-permute-start(bf16[512,256]{1,0:T(8,128)(2,1)} %shard_map.105.refs_1_), channel_id=1, source_target_pairs={{0,8},{8,0},{16,24},{24,16},{1,9},{9,1},{17,25},{25,17},{2,10},{10... | collective-permute-start | bytes 786440 | tf_op jit(solution)/shard_map/ppermute | solution.py:308
  137.6 9.4 %collective-permute-start.25 = (bf16[512,512]{1,0:T(8,128)(2,1)}, bf16[512,512]{1,0:T(8,128)(2,1)}, u32[]{:S(2)}, u32[]{:S(2)}) collective-permute-start(bf16[512,512]{1,0:T(8,128)(2,1)} %shard_map.107), channel_id=1, source_target_pairs={{0,1},{1,0},{2,3},{3,2},{4,5},{5,4},{6,7},{7,6},{8,9},{9,8},{10,11... | collective-permute-start | bytes 1572872 | tf_op jit(solution)/shard_map/ppermute | solution.py:388
  142.8 13.9 %collective-permute-start.27 = (bf16[1024,256]{1,0:T(8,128)(2,1)}, bf16[1024,256]{1,0:T(8,128)(2,1)}, u32[]{:S(2)}, u32[]{:S(2)}) collective-permute-start(bf16[1024,256]{1,0:T(8,128)(2,1)} %slice.22), channel_id=1, source_target_pairs={{0,2},{2,0},{4,6},{6,4},{1,3},{3,1},{5,7},{7,5},{8,10},{10,8},{12,... | collective-permute-start | bytes 1572872 | tf_op jit(solution)/shard_map/ppermute | solution.py:295
  144.9 13.6 %collective-permute-start.28 = (bf16[1024,256]{1,0:T(8,128)(2,1)}, bf16[1024,256]{1,0:T(8,128)(2,1)}, u32[]{:S(2)}, u32[]{:S(2)}) collective-permute-start(bf16[1024,256]{1,0:T(8,128)(2,1)} %slice.23), channel_id=1, source_target_pairs={{0,4},{2,6},{4,0},{6,2},{1,5},{3,7},{5,1},{7,3},{8,12},{10,14},{12... | collective-permute-start | bytes 1572872 | tf_op jit(solution)/shard_map/ppermute | solution.py:295
  162.2 4.6 %collective-permute-start.29 = (bf16[512,512]{1,0:T(8,128)(2,1)}, bf16[512,512]{1,0:T(8,128)(2,1)}, u32[]{:S(2)}, u32[]{:S(2)}) collective-permute-start(bf16[512,512]{1,0:T(8,128)(2,1)} %shard_map.109), channel_id=1, source_target_pairs={{0,1},{1,0},{2,3},{3,2},{4,5},{5,4},{6,7},{7,6},{8,9},{9,8},{10,11... | collective-permute-start | bytes 1572872 | tf_op jit(solution)/shard_map/ppermute | solution.py:388
  163.3 20.4 %collective-permute-start.26 = (bf16[256,512]{1,0:T(8,128)(2,1)}, bf16[256,512]{1,0:T(8,128)(2,1)}, u32[]{:S(2)}, u32[]{:S(2)}) collective-permute-start(bf16[256,512]{1,0:T(8,128)(2,1)} %add_convert_fusion.4), channel_id=1, source_target_pairs={{0,16},{8,24},{16,0},{24,8},{1,17},{9,25},{17,1},{25,9},{2,18},{10... | collective-permute-start | bytes 786440 | tf_op jit(solution)/shard_map/ppermute | solution.py:308
  167.8 21.3 %collective-permute-start.30 = (bf16[256,512]{1,0:T(8,128)(2,1)S(1)}, bf16[256,512]{1,0:T(8,128)(2,1)S(1)}, u32[]{:S(2)}, u32[]{:S(2)}) collective-permute-start(bf16[256,512]{1,0:T(8,128)(2,1)S(1)} %add_convert_fusion.1), channel_id=1, source_target_pairs={{0,16},{8,24},{16,0},{24,8},{1,17},{9,25},{17,1},{25,9},{2,18},{10... | collective-permute-start | bytes 786440 | tf_op jit(solution)/shard_map/ppermute | solution.py:308
  184.8 7.4 %collective-permute-start.31 = (bf16[128,512]{1,0:T(8,128)(2,1)S(1)}, bf16[128,512]{1,0:T(8,128)(2,1)S(1)}, u32[]{:S(2)}, u32[]{:S(2)}) collective-permute-start(bf16[128,512]{1,0:T(8,128)(2,1)S(1)} %get-tuple-element.53), channel_id=1, source_target_pairs={{0,8},{8,0},{16,24},{24,16},{1,9},{9,1},{17,25},{25,17},{2,10},{10... | collective-permute-start | bytes 393224 | tf_op jit(solution)/shard_map/ppermute | solution.py:308
  (33 other events, 281.5 us)

commit v11 on v10

--- a/solution.py
+++ b/solution.py
@@ -329,12 +329,14 @@
             axis=1,
         )
 
-    def exchanged(sources, width):
-        came = along(columns_for(1 - which, sources, width), 1)
+    def exchanged(sources, width, *earlier):
+        came = along(after(columns_for(1 - which, sources, width), *earlier), 1)
         return jnp.concatenate([columns_for(which, sources, width), came], axis=0)
 
-    pair_weight = corner(sides(exchanged((w_key, w_value), HD)))
-    query_sides = sides(after(exchanged((w_query,), heads), *pair_weight[3:]))
+    pair_both = exchanged((w_key, w_value), HD)
+    pair_weight = corner(sides(pair_both))
+    query_both = exchanged((w_query,), heads, pair_both)
+    query_sides = sides(after(query_both, *pair_weight[3:]))
 
     normed = normalised(tokens, norm_gain)
     own = lax.dynamic_slice_in_dim(normed, which_half * depth, depth, 1)
@@ -345,20 +347,21 @@
     near = along(core_half(which_half), 1)
     other = along(core_half(1 - which_half), 2)
     halves = jnp.concatenate([near, other, along(after(other, near), 1)], axis=0)
-    token_parts = [own, halves, lax.ppermute(halves, "head", [(0, 1), (1, 0)])]
-    index = jnp.stack([hi, lo, core])
-
-    row_index = jnp.arange(4 * rows, dtype=jnp.int32)
-    cosine, sine = rotary_tables((row_index // rows * 4 + lo) * rows + row_index % rows)
-
-    kept, sent = product(index, token_parts, pair_weight, 0, 1)
-    query_weight = corner_after(query_sides, sent)
-
     features_here = w_out.shape[0] // 2
     out_own = lax.dynamic_slice_in_dim(w_out, which_half * features_here, features_here, 0)
     out_other = lax.dynamic_slice_in_dim(w_out, (1 - which_half) * features_here, features_here, 0)
-    out_other = along(after(out_other, sent), 2)
-    kv_own = finish_pair(cosine, sine, [after(kept, out_other), along(sent, 2)])
+    out_other = along(after(out_other, near, other), 2)
+    own = after(own, out_other)
+    token_parts = [own, halves, lax.ppermute(halves, "head", [(0, 1), (1, 0)])]
+    index = jnp.stack([hi, lo, core])
+
+    row_index = jnp.arange(4 * rows, dtype=jnp.int32)
+    cosine, sine = rotary_tables((row_index // rows * 4 + lo) * rows + row_index % rows)
+
+    kept, sent = product(index, token_parts, pair_weight, 0, 1)
+    query_weight = corner_after(query_sides, sent)
+
+    kv_own = finish_pair(cosine, sine, [kept, along(sent, 2)])
     kv_going = after(kv_own, *query_weight[3:])
     kv_parts = [kv_own] + [beside(kv_going, r) for r in range(1, 4)]
 
@@ -379,12 +382,12 @@
         return (one.astype(jnp.float32) + two.astype(jnp.float32)).astype(jnp.bfloat16)
 
     kept = 2 * rows
-    here, there, shares = [], [], []
+    here, there, shares, summed = [], [], [], None
     for blocks in (out_blocks[:2], out_blocks[2:]):
-        blocks = [after(blocks[0], *shares[1:]), *blocks[1:]]
-        theirs, mine = [
-            project(jnp.stack([hi, group]), attended, blocks) for group in (1 - core, core)
-        ]
+        first = [after(blocks[0], *shares[1:]), *blocks[1:]]
+        theirs = project(jnp.stack([hi, 1 - core]), attended, first)
+        last = first if summed is None else [after(first[0], summed), *first[1:]]
+        mine = project(jnp.stack([hi, core]), attended, last)
         theirs = lax.ppermute(theirs, "head", [(0, 1), (1, 0)])
         shares = [
             added(

time: 198 us -> 195 us (0.985)
  starting transfers between devices: 42.3 us -> 36.4 us
    ppermute x15, waiting for transfers between devices: 71 us -> 81.9 us  [along(): return lax.ppermute(block, 'hi', [(i, i ^ d) for i in range(4)])]
    ppermute x15, waiting for transfers between devices: 23.3 us -> 13.9 us  [beside(): return lax.ppermute(block, 'lo', [(i, i ^ r) for i in range(4)])]
    ppermute x2, starting transfers between devices: 5.42 us -> 2.29 us  [line_device(): theirs = lax.ppermute(theirs, 'head', [(0, 1), (1, 0)])]
    ppermute x15, starting transfers between devices: 14 us -> 11.9 us  [beside(): return lax.ppermute(block, 'lo', [(i, i ^ r) for i in range(4)])]
    unnamed x67 -> x69, local copies, waits for them, and re-layouts: 4.94 us -> 5.69 us
  transfers between devices with their start and end apart: 33 -> 33, of which waited for: 17 -> 13; matrix products, arithmetic and copies ran while one was open for 11% -> 12% of each run, Pallas kernels for 13% -> 14%
where the time goes in v11:
time: 195 us; the launch traced here: 192 us
  waiting for transfers between devices  95.8 us (49%)
  starting transfers between devices  36.4 us (19%)
  Pallas kernels  30.5 us (16%)
  local copies, waits for them, and re-layouts  15.9 us (8%)
  other arithmetic  12.5 us (6%)
    ppermute x15, waiting for transfers between devices, along(): return lax.ppermute(block, 'hi', [(i, i ^ d) for i in range(4)])  81.9 us
    pallas_call x11, Pallas kernels, local_kernel(): pl.pallas_call(body, in_specs=[pl.BlockSpec(memory_space=pltpu.SMEM)] + [...  30.5 us
    ppermute x15, starting transfers between devices, along(): return lax.ppermute(block, 'hi', [(i, i ^ d) for i in range(4)])  18.2 us
    ppermute x15, waiting for transfers between devices, beside(): return lax.ppermute(block, 'lo', [(i, i ^ r) for i in range(4)])  13.9 us
    ppermute x15, starting transfers between devices, beside(): return lax.ppermute(block, 'lo', [(i, i ^ r) for i in range(4)])  11.9 us
    convert_element_type x4, other arithmetic, added(): (one.astype(jnp.float32) + two.astype(jnp.float32)).astype(jnp.bfloat16)  5.81 us
    unnamed x69, local copies, waits for them, and re-layouts  5.69 us
    slice x6, local copies, waits for them, and re-layouts, corner(): return [*blocks, beside(blocks[2][:half], 1), beside(blocks[1][half:], 2)]  5 us
  transfers between devices with their start and end apart: 33, of which 13 were waited for; matrix products, arithmetic and copies ran while one was open for 12% of the time, Pallas kernels for 14%

profile of v11, /device:TPU:1, one launch (start us, length us, event | category | flops | bytes accessed | tf_op | source)
XLA Modules:
  0.0 191.7 jit_solution(807262815170800107)
XLA Ops:
  1.3 2.2 %collective-permute-start.5 = (bf16[256,512]{1,0:T(8,128)(2,1)S(1)}, bf16[256,512]{1,0:T(8,128)(2,1)S(1)}, u32[]{:S(2)}, u32[]{:S(2)}) collective-permute-start(bf16[256,512]{1,0:T(8,128)(2,1)S(1)} %pad_maximum_fusion.6), channel_id=1, source_target_pairs={{0,8},{8,0},{16,24},{24,16},{1,9},{9,1},{17,25},{25,17},{2,10},{10... | collective-permute-start | bytes 786440 | tf_op jit(solution)/shard_map/ppermute | solution.py:308
  4.8 4.7 %collective-permute-done.5 = bf16[256,512]{1,0:T(8,128)(2,1)S(1)} collective-permute-done((bf16[256,512]{1,0:T(8,128)(2,1)S(1)}, bf16[256,512]{1,0:T(8,128)(2,1)S(1)}, u32[]{:S(2)}, u32[]{:S(2)}) %collective-permute-start.5) | collective-permute-done | bytes 262176 | tf_op jit(solution)/shard_map/ppermute | solution.py:308
  14.6 2.3 %collective-permute-start.1 = (bf16[128,1024]{1,0:T(8,128)(2,1)S(1)}, bf16[128,1024]{1,0:T(8,128)(2,1)}, u32[]{:S(2)}, u32[]{:S(2)}) collective-permute-start(bf16[128,1024]{1,0:T(8,128)(2,1)S(1)} %get-tuple-element.53), channel_id=1, source_target_pairs={{0,16},{8,24},{16,0},{24,8},{1,17},{9,25},{17,1},{25,9},{2,18},{10... | collective-permute-start | bytes 786440 | tf_op jit(solution)/shard_map/ppermute | solution.py:308
  16.9 5.0 %collective-permute-done.7.refs_5_ = bf16[512,512]{1,0:T(8,128)(2,1)S(1)} collective-permute-done((bf16[512,512]{1,0:T(8,128)(2,1)S(1)}, bf16[512,512]{1,0:T(8,128)(2,1)S(1)}, u32[]{:S(2)}, u32[]{:S(2)}) %collective-permute-start.7) | collective-permute-done | bytes 524320 | tf_op jit(solution)/shard_map/ppermute | solution.py:295
  25.4 9.3 %collective-permute-done = bf16[128,1024]{1,0:T(8,128)(2,1)} collective-permute-done((bf16[128,1024]{1,0:T(8,128)(2,1)}, bf16[128,1024]{1,0:T(8,128)(2,1)}, u32[]{:S(2)}, u32[]{:S(2)}) %collective-permute-start) | collective-permute-done | bytes 262176 | tf_op jit(solution)/shard_map/ppermute | solution.py:308
  34.8 2.3 %collective-permute-start.3 = (bf16[128,1024]{1,0:T(8,128)(2,1)}, bf16[128,1024]{1,0:T(8,128)(2,1)S(1)}, u32[]{:S(2)}, u32[]{:S(2)}) collective-permute-start(bf16[128,1024]{1,0:T(8,128)(2,1)} %collective-permute-done.1), channel_id=1, source_target_pairs={{0,8},{8,0},{16,24},{24,16},{1,9},{9,1},{17,25},{25,17},{2,10},{10... | collective-permute-start | bytes 786440 | tf_op jit(solution)/shard_map/ppermute | solution.py:308
  41.1 4.0 %collective-permute-start.4 = (bf16[384,1024]{1,0:T(8,128)(2,1)S(1)}, bf16[384,1024]{1,0:T(8,128)(2,1)S(1)}, u32[]{:S(2)}, u32[]{:S(2)}) collective-permute-start(bf16[384,1024]{1,0:T(8,128)(2,1)S(1)} %constant_dynamic-update-slice_fusion.refs_1_), channel_id=1, source_target_pairs={{0,1},{1,0},{2,3},{3,2},{4,5},{5,4},{6,7},{7,6},{8,9},{9,8},{10,11... | collective-permute-start | bytes 2359304 | tf_op jit(solution)/shard_map/ppermute | solution.py:355
  46.0 1.6 collective-permute-start.2
  47.8 23.9 %collective-permute-done.2 = bf16[1024,256]{1,0:T(8,128)(2,1)S(1)} collective-permute-done((bf16[1024,256]{1,0:T(8,128)(2,1)S(1)}, bf16[1024,256]{1,0:T(8,128)(2,1)S(1)}, u32[]{:S(2)}, u32[]{:S(2)}) %collective-permute-start.2) | collective-permute-done | bytes 524320 | tf_op jit(solution)/shard_map/ppermute | solution.py:308
  72.5 1.9 shard_map.100
  79.2 1.9 fusion.3
  81.3 1.5 pad_maximum_fusion.4
  82.9 12.1 %collective-permute-done.16.refs_1_ = bf16[512,256]{1,0:T(8,128)(2,1)S(1)} collective-permute-done((bf16[512,256]{1,0:T(8,128)(2,1)}, bf16[512,256]{1,0:T(8,128)(2,1)S(1)}, u32[]{:S(2)}, u32[]{:S(2)}) %collective-permute-start.16) | collective-permute-done | bytes 262176 | tf_op jit(solution)/shard_map/ppermute | solution.py:308
  97.8 2.7 %shard_map.101 = (bf16[512,256]{1,0:T(8,128)(2,1)S(1)}, bf16[512,256]{1,0:T(8,128)(2,1)S(1)}) custom-call(s32[5]{0:T(128)S(1)} %get-tuple-element.71.place_ref, bf16[128,2048]{1,0:T(8,128)(2,1)S(1)} %constant_dynamic-slice_fusion.20.refs_0_, bf16[384,1024]{1,0:T(8,128)(2,1)S(1)} %constant_dynamic-update-slice_fusion.refs_1_, ...), custom_call_target="tpu_custom_call" | custom-call | flops 1073741824 | bytes 6291476 | tf_op jit(solution)/shard_map/pallas_call | solution.py:18
  101.8 2.6 %shard_map.102 = (bf16[512,256]{1,0:T(8,128)(2,1)S(1)}, bf16[512,256]{1,0:T(8,128)(2,1)S(1)}) custom-call(s32[5]{0:T(128)S(1)} %get-tuple-element.45.place_ref, bf16[128,2048]{1,0:T(8,128)(2,1)S(1)} %constant_dynamic-slice_fusion.20.refs_0_, bf16[384,1024]{1,0:T(8,128)(2,1)S(1)} %constant_dynamic-update-slice_fusion.refs_1_, ...), custom_call_target="tpu_custom_call" | custom-call | flops 1073741824 | bytes 6291476 | tf_op jit(solution)/shard_map/pallas_call | solution.py:18
  104.4 2.4 %collective-permute-start.20 = (bf16[512,256]{1,0:T(8,128)(2,1)S(1)}, bf16[512,256]{1,0:T(8,128)(2,1)S(1)}, u32[]{:S(2)}, u32[]{:S(2)}) collective-permute-start(bf16[512,256]{1,0:T(8,128)(2,1)S(1)} %get-tuple-element.39), channel_id=1, source_target_pairs={{0,16},{8,24},{16,0},{24,8},{1,17},{9,25},{17,1},{25,9},{2,18},{10... | collective-permute-start | bytes 786440 | tf_op jit(solution)/shard_map/ppermute | solution.py:308
  106.8 2.4 %collective-permute-done.19.refs_5_ = bf16[512,256]{1,0:T(8,128)(2,1)S(1)} collective-permute-done((bf16[512,256]{1,0:T(8,128)(2,1)S(1)}, bf16[512,256]{1,0:T(8,128)(2,1)S(1)}, u32[]{:S(2)}, u32[]{:S(2)}) %collective-permute-start.19) | collective-permute-done | bytes 262176 | tf_op jit(solution)/shard_map/ppermute | solution.py:295
  110.6 10.2 %collective-permute-done.15.refs_1_ = bf16[512,256]{1,0:T(8,128)(2,1)S(1)} collective-permute-done((bf16[512,256]{1,0:T(8,128)(2,1)S(1)}, bf16[512,256]{1,0:T(8,128)(2,1)S(1)}, u32[]{:S(2)}, u32[]{:S(2)}) %collective-permute-start.15) | collective-permute-done | bytes 262176 | tf_op jit(solution)/shard_map/ppermute | solution.py:308
  120.8 6.3 %shard_map.104.refs_0_ = bf16[512,256]{1,0:T(8,128)(2,1)S(1)} custom-call(s32[21]{0:T(128)S(1)} %pad_add_fusion.2.place_ref, f32[512,128]{1,0:T(8,128)S(1)} %get-tuple-element.72.cos_ref, f32[512,128]{1,0:T(8,128)S(1)} %get-tuple-element.73.sin_ref, bf16[512,256]{1,0:T(8,128)(2,1)S(1)} %get-tuple-element.35.refs_0_, ...), custom_call_target="tpu_custom_call" | custom-call | flops 8589934592 | bytes 2097236 | tf_op jit(solution)/shard_map/pallas_call | solution.py:18
  127.2 7.3 %shard_map.105.refs_1_ = bf16[512,256]{1,0:T(8,128)(2,1)} custom-call(s32[21]{0:T(128)S(1)} %pad_add_fusion.2.place_ref, f32[512,128]{1,0:T(8,128)S(1)} %get-tuple-element.72.cos_ref, f32[512,128]{1,0:T(8,128)S(1)} %get-tuple-element.73.sin_ref, bf16[512,256]{1,0:T(8,128)(2,1)S(1)} %get-tuple-element.34.refs_0_, ...), custom_call_target="tpu_custom_call" | custom-call | flops 8589934592 | bytes 2097236 | tf_op jit(solution)/shard_map/pallas_call | solution.py:18
  136.0 6.1 %collective-permute-done.22.refs_3_ = bf16[512,256]{1,0:T(8,128)(2,1)} collective-permute-done((bf16[512,256]{1,0:T(8,128)(2,1)}, bf16[512,256]{1,0:T(8,128)(2,1)}, u32[]{:S(2)}, u32[]{:S(2)}) %collective-permute-start.22) | collective-permute-done | bytes 262176 | tf_op jit(solution)/shard_map/ppermute | solution.py:308
  142.1 2.6 %shard_map.107 = bf16[512,512]{1,0:T(8,128)(2,1)} custom-call(s32[2]{0:T(128)S(1)} %pad_add_fusion.7.place_ref, bf16[512,256]{1,0:T(8,128)(2,1)S(1)} %shard_map.104.refs_0_, bf16[512,256]{1,0:T(8,128)(2,1)} %shard_map.105.refs_1_, bf16[512,256]{1,0:T(8,128)(2,1)} %collective-permute-done.21.refs_2_, bf16[512,256]{1,0:T(8,128)(2,1)} %collective-permute-done.22.refs_3_, ...), custom_call_target="tpu_custom_call" | custom-call | flops 536870912 | bytes 3145736 | tf_op jit(solution)/shard_map/pallas_call | solution.py:18
  148.5 1.8 shard_map.106
  150.4 1.9 add_convert_fusion.4
  152.3 2.1 %collective-permute-start.26 = (bf16[256,512]{1,0:T(8,128)(2,1)}, bf16[256,512]{1,0:T(8,128)(2,1)}, u32[]{:S(2)}, u32[]{:S(2)}) collective-permute-start(bf16[256,512]{1,0:T(8,128)(2,1)} %add_convert_fusion.4), channel_id=1, source_target_pairs={{0,16},{8,24},{16,0},{24,8},{1,17},{9,25},{17,1},{25,9},{2,18},{10... | collective-permute-start | bytes 786440 | tf_op jit(solution)/shard_map/ppermute | solution.py:308
  154.3 6.5 %collective-permute-done.27 = bf16[1024,256]{1,0:T(8,128)(2,1)} collective-permute-done((bf16[1024,256]{1,0:T(8,128)(2,1)}, bf16[1024,256]{1,0:T(8,128)(2,1)}, u32[]{:S(2)}, u32[]{:S(2)}) %collective-permute-start.27) | collective-permute-done | bytes 524320 | tf_op jit(solution)/shard_map/ppermute | solution.py:295
  163.0 1.9 shard_map.109
  166.4 1.8 add_convert_fusion.3
  168.3 1.8 shard_map.108
  171.1 1.7 collective-permute-start.30
  174.3 11.0 %collective-permute-done.30 = bf16[256,512]{1,0:T(8,128)(2,1)S(1)} collective-permute-done((bf16[256,512]{1,0:T(8,128)(2,1)S(1)}, bf16[256,512]{1,0:T(8,128)(2,1)S(1)}, u32[]{:S(2)}, u32[]{:S(2)}) %collective-permute-start.30) | collective-permute-done | bytes 262176 | tf_op jit(solution)/shard_map/ppermute | solution.py:308
  186.6 3.7 %collective-permute-done.32.refs_3_ = bf16[128,512]{1,0:T(8,128)(2,1)S(1)} collective-permute-done((bf16[128,512]{1,0:T(8,128)(2,1)S(1)}, bf16[128,512]{1,0:T(8,128)(2,1)S(1)}, u32[]{:S(2)}, u32[]{:S(2)}) %collective-permute-start.32) | collective-permute-done | bytes 131104 | tf_op jit(solution)/shard_map/ppermute | solution.py:308
  (153 shorter events, 41.6 us)
Async XLA Ops:
  1.3 8.2 %collective-permute-start.5 = (bf16[256,512]{1,0:T(8,128)(2,1)S(1)}, bf16[256,512]{1,0:T(8,128)(2,1)S(1)}, u32[]{:S(2)}, u32[]{:S(2)}) collective-permute-start(bf16[256,512]{1,0:T(8,128)(2,1)S(1)} %pad_maximum_fusion.6), channel_id=1, source_target_pairs={{0,8},{8,0},{16,24},{24,16},{1,9},{9,1},{17,25},{25,17},{2,10},{10... | collective-permute-start | bytes 786440 | tf_op jit(solution)/shard_map/ppermute | solution.py:308
  9.5 12.4 %collective-permute-start.7 = (bf16[512,512]{1,0:T(8,128)(2,1)S(1)}, bf16[512,512]{1,0:T(8,128)(2,1)S(1)}, u32[]{:S(2)}, u32[]{:S(2)}) collective-permute-start(bf16[512,512]{1,0:T(8,128)(2,1)S(1)} %pad_maximum_fusion.3.refs_3_), channel_id=1, source_target_pairs={{0,4},{2,6},{4,0},{6,2},{1,5},{3,7},{5,1},{7,3},{8,12},{10,14},{12... | collective-permute-start | bytes 1572872 | tf_op jit(solution)/shard_map/ppermute | solution.py:295
  10.7 12.7 %collective-permute-start.9 = (bf16[512,512]{1,0:T(8,128)(2,1)S(1)}, bf16[512,512]{1,0:T(8,128)(2,1)S(1)}, u32[]{:S(2)}, u32[]{:S(2)}) collective-permute-start(bf16[512,512]{1,0:T(8,128)(2,1)S(1)} %pad_maximum_fusion.3.refs_3_), channel_id=1, source_target_pairs={{0,2},{2,0},{4,6},{6,4},{1,3},{3,1},{5,7},{7,5},{8,10},{10,8},{12,... | collective-permute-start | bytes 1572872 | tf_op jit(solution)/shard_map/ppermute | solution.py:295
  11.9 26.1 %collective-permute-start.6 = (bf16[256,1024]{1,0:T(8,128)(2,1)}, bf16[256,1024]{1,0:T(8,128)(2,1)}, u32[]{:S(2)}, u32[]{:S(2)}) collective-permute-start(bf16[256,1024]{1,0:T(8,128)(2,1)} %pad_maximum_fusion.2), channel_id=1, source_target_pairs={{0,8},{8,0},{16,24},{24,16},{1,9},{9,1},{17,25},{25,17},{2,10},{10... | collective-permute-start | bytes 1572872 | tf_op jit(solution)/shard_map/ppermute | solution.py:308
  14.4 20.3 %collective-permute-start = (bf16[128,1024]{1,0:T(8,128)(2,1)}, bf16[128,1024]{1,0:T(8,128)(2,1)}, u32[]{:S(2)}, u32[]{:S(2)}) collective-permute-start(bf16[128,1024]{1,0:T(8,128)(2,1)} %get-tuple-element.54), channel_id=1, source_target_pairs={{0,8},{8,0},{16,24},{24,16},{1,9},{9,1},{17,25},{25,17},{2,10},{10... | collective-permute-start | bytes 786440 | tf_op jit(solution)/shard_map/ppermute | solution.py:308
  14.6 20.2 %collective-permute-start.1 = (bf16[128,1024]{1,0:T(8,128)(2,1)S(1)}, bf16[128,1024]{1,0:T(8,128)(2,1)}, u32[]{:S(2)}, u32[]{:S(2)}) collective-permute-start(bf16[128,1024]{1,0:T(8,128)(2,1)S(1)} %get-tuple-element.53), channel_id=1, source_target_pairs={{0,16},{8,24},{16,0},{24,8},{1,17},{9,25},{17,1},{25,9},{2,18},{10... | collective-permute-start | bytes 786440 | tf_op jit(solution)/shard_map/ppermute | solution.py:308
  22.7 16.6 %collective-permute-start.8 = (bf16[256,512]{1,0:T(8,128)(2,1)}, bf16[256,512]{1,0:T(8,128)(2,1)S(1)}, u32[]{:S(2)}, u32[]{:S(2)}) collective-permute-start(bf16[256,512]{1,0:T(8,128)(2,1)} %slice.24), channel_id=1, source_target_pairs={{0,2},{2,0},{4,6},{6,4},{1,3},{3,1},{5,7},{7,5},{8,10},{10,8},{12,... | collective-permute-start | bytes 786440 | tf_op jit(solution)/shard_map/ppermute | solution.py:295
  24.2 15.1 %collective-permute-start.10 = (bf16[256,512]{1,0:T(8,128)(2,1)}, bf16[256,512]{1,0:T(8,128)(2,1)S(1)}, u32[]{:S(2)}, u32[]{:S(2)}) collective-permute-start(bf16[256,512]{1,0:T(8,128)(2,1)} %slice.25), channel_id=1, source_target_pairs={{0,4},{2,6},{4,0},{6,2},{1,5},{3,7},{5,1},{7,3},{8,12},{10,14},{12... | collective-permute-start | bytes 786440 | tf_op jit(solution)/shard_map/ppermute | solution.py:295
  34.8 6.3 %collective-permute-start.3 = (bf16[128,1024]{1,0:T(8,128)(2,1)}, bf16[128,1024]{1,0:T(8,128)(2,1)S(1)}, u32[]{:S(2)}, u32[]{:S(2)}) collective-permute-start(bf16[128,1024]{1,0:T(8,128)(2,1)} %collective-permute-done.1), channel_id=1, source_target_pairs={{0,8},{8,0},{16,24},{24,16},{1,9},{9,1},{17,25},{25,17},{2,10},{10... | collective-permute-start | bytes 786440 | tf_op jit(solution)/shard_map/ppermute | solution.py:308
  39.3 35.9 %collective-permute-start.11 = (bf16[512,1024]{1,0:T(8,128)(2,1)S(1)}, bf16[512,1024]{1,0:T(8,128)(2,1)S(1)}, u32[]{:S(2)}, u32[]{:S(2)}) collective-permute-start(bf16[512,1024]{1,0:T(8,128)(2,1)S(1)} %pad_maximum_fusion.refs_3_), channel_id=1, source_target_pairs={{0,2},{2,0},{4,6},{6,4},{1,3},{3,1},{5,7},{7,5},{8,10},{10,8},{12,... | collective-permute-start | bytes 3145736 | tf_op jit(solution)/shard_map/ppermute | solution.py:295
  39.6 35.6 %collective-permute-start.12 = (bf16[512,1024]{1,0:T(8,128)(2,1)S(1)}, bf16[512,1024]{1,0:T(8,128)(2,1)S(1)}, u32[]{:S(2)}, u32[]{:S(2)}) collective-permute-start(bf16[512,1024]{1,0:T(8,128)(2,1)S(1)} %pad_maximum_fusion.refs_3_), channel_id=1, source_target_pairs={{0,4},{2,6},{4,0},{6,2},{1,5},{3,7},{5,1},{7,3},{8,12},{10,14},{12... | collective-permute-start | bytes 3145736 | tf_op jit(solution)/shard_map/ppermute | solution.py:295
  41.1 30.6 %collective-permute-start.4 = (bf16[384,1024]{1,0:T(8,128)(2,1)S(1)}, bf16[384,1024]{1,0:T(8,128)(2,1)S(1)}, u32[]{:S(2)}, u32[]{:S(2)}) collective-permute-start(bf16[384,1024]{1,0:T(8,128)(2,1)S(1)} %constant_dynamic-update-slice_fusion.refs_1_), channel_id=1, source_target_pairs={{0,1},{1,0},{2,3},{3,2},{4,5},{5,4},{6,7},{7,6},{8,9},{9,8},{10,11... | collective-permute-start | bytes 2359304 | tf_op jit(solution)/shard_map/ppermute | solution.py:355
  46.0 25.7 %collective-permute-start.2 = (bf16[1024,256]{1,0:T(8,128)(2,1)S(1)}, bf16[1024,256]{1,0:T(8,128)(2,1)S(1)}, u32[]{:S(2)}, u32[]{:S(2)}) collective-permute-start(bf16[1024,256]{1,0:T(8,128)(2,1)S(1)} %get-tuple-element.25), channel_id=1, source_target_pairs={{0,16},{8,24},{16,0},{24,8},{1,17},{9,25},{17,1},{25,9},{2,18},{10... | collective-permute-start | bytes 1572872 | tf_op jit(solution)/shard_map/ppermute | solution.py:308
  76.1 19.0 %collective-permute-start.13 = (bf16[256,1024]{1,0:T(8,128)(2,1)}, bf16[256,1024]{1,0:T(8,128)(2,1)}, u32[]{:S(2)}, u32[]{:S(2)}) collective-permute-start(bf16[256,1024]{1,0:T(8,128)(2,1)} %slice.20), channel_id=1, source_target_pairs={{0,2},{2,0},{4,6},{6,4},{1,3},{3,1},{5,7},{7,5},{8,10},{10,8},{12,... | collective-permute-start | bytes 1572872 | tf_op jit(solution)/shard_map/ppermute | solution.py:295
  77.9 17.2 %collective-permute-start.14 = (bf16[256,1024]{1,0:T(8,128)(2,1)}, bf16[256,1024]{1,0:T(8,128)(2,1)}, u32[]{:S(2)}, u32[]{:S(2)}) collective-permute-start(bf16[256,1024]{1,0:T(8,128)(2,1)} %slice.21), channel_id=1, source_target_pairs={{0,4},{2,6},{4,0},{6,2},{1,5},{3,7},{5,1},{7,3},{8,12},{10,14},{12... | collective-permute-start | bytes 1572872 | tf_op jit(solution)/shard_map/ppermute | solution.py:295
  81.2 13.7 %collective-permute-start.16 = (bf16[512,256]{1,0:T(8,128)(2,1)}, bf16[512,256]{1,0:T(8,128)(2,1)S(1)}, u32[]{:S(2)}, u32[]{:S(2)}) collective-permute-start(bf16[512,256]{1,0:T(8,128)(2,1)} %copy-done.18), channel_id=1, source_target_pairs={{0,16},{8,24},{16,0},{24,8},{1,17},{9,25},{17,1},{25,9},{2,18},{10... | collective-permute-start | bytes 786440 | tf_op jit(solution)/shard_map/ppermute | solution.py:308
  95.1 11.7 %collective-permute-start.17 = (bf16[512,256]{1,0:T(8,128)(2,1)S(1)}, bf16[512,256]{1,0:T(8,128)(2,1)S(1)}, u32[]{:S(2)}, u32[]{:S(2)}) collective-permute-start(bf16[512,256]{1,0:T(8,128)(2,1)S(1)} %shard_map.103.refs_2_), channel_id=1, source_target_pairs={{0,2},{2,0},{4,6},{6,4},{1,3},{3,1},{5,7},{7,5},{8,10},{10,8},{12,... | collective-permute-start | bytes 786440 | tf_op jit(solution)/shard_map/ppermute | solution.py:295
  96.3 10.4 %collective-permute-start.18 = (bf16[512,256]{1,0:T(8,128)(2,1)S(1)}, bf16[512,256]{1,0:T(8,128)(2,1)S(1)}, u32[]{:S(2)}, u32[]{:S(2)}) collective-permute-start(bf16[512,256]{1,0:T(8,128)(2,1)S(1)} %shard_map.103.refs_2_), channel_id=1, source_target_pairs={{0,4},{2,6},{4,0},{6,2},{1,5},{3,7},{5,1},{7,3},{8,12},{10,14},{12... | collective-permute-start | bytes 786440 | tf_op jit(solution)/shard_map/ppermute | solution.py:295
  96.5 12.7 %collective-permute-start.19 = (bf16[512,256]{1,0:T(8,128)(2,1)S(1)}, bf16[512,256]{1,0:T(8,128)(2,1)S(1)}, u32[]{:S(2)}, u32[]{:S(2)}) collective-permute-start(bf16[512,256]{1,0:T(8,128)(2,1)S(1)} %shard_map.103.refs_2_), channel_id=1, source_target_pairs={{0,6},{2,4},{4,2},{6,0},{1,7},{3,5},{5,3},{7,1},{8,14},{10,12},{12... | collective-permute-start | bytes 786440 | tf_op jit(solution)/shard_map/ppermute | solution.py:295
  100.5 20.2 %collective-permute-start.15 = (bf16[512,256]{1,0:T(8,128)(2,1)S(1)}, bf16[512,256]{1,0:T(8,128)(2,1)S(1)}, u32[]{:S(2)}, u32[]{:S(2)}) collective-permute-start(bf16[512,256]{1,0:T(8,128)(2,1)S(1)} %get-tuple-element.36), channel_id=1, source_target_pairs={{0,16},{8,24},{16,0},{24,8},{1,17},{9,25},{17,1},{25,9},{2,18},{10... | collective-permute-start | bytes 786440 | tf_op jit(solution)/shard_map/ppermute | solution.py:308
  104.4 22.8 %collective-permute-start.20 = (bf16[512,256]{1,0:T(8,128)(2,1)S(1)}, bf16[512,256]{1,0:T(8,128)(2,1)S(1)}, u32[]{:S(2)}, u32[]{:S(2)}) collective-permute-start(bf16[512,256]{1,0:T(8,128)(2,1)S(1)} %get-tuple-element.39), channel_id=1, source_target_pairs={{0,16},{8,24},{16,0},{24,8},{1,17},{9,25},{17,1},{25,9},{2,18},{10... | collective-permute-start | bytes 786440 | tf_op jit(solution)/shard_map/ppermute | solution.py:308
  109.2 26.8 %collective-permute-start.23 = (bf16[2048,256]{1,0:T(8,128)(2,1)S(1)}, bf16[2048,256]{1,0:T(8,128)(2,1)S(1)}, u32[]{:S(2)}, u32[]{:S(2)}) collective-permute-start(bf16[2048,256]{1,0:T(8,128)(2,1)S(1)} %pad_maximum_fusion.1.refs_4_), channel_id=1, source_target_pairs={{0,2},{2,0},{4,6},{6,4},{1,3},{3,1},{5,7},{7,5},{8,10},{10,8},{12,... | collective-permute-start | bytes 3145736 | tf_op jit(solution)/shard_map/ppermute | solution.py:295
  109.2 26.8 %collective-permute-start.24 = (bf16[2048,256]{1,0:T(8,128)(2,1)S(1)}, bf16[2048,256]{1,0:T(8,128)(2,1)S(1)}, u32[]{:S(2)}, u32[]{:S(2)}) collective-permute-start(bf16[2048,256]{1,0:T(8,128)(2,1)S(1)} %pad_maximum_fusion.1.refs_4_), channel_id=1, source_target_pairs={{0,4},{2,6},{4,0},{6,2},{1,5},{3,7},{5,1},{7,3},{8,12},{10,14},{12... | collective-permute-start | bytes 3145736 | tf_op jit(solution)/shard_map/ppermute | solution.py:295
  127.1 8.9 %collective-permute-start.21 = (bf16[512,256]{1,0:T(8,128)(2,1)S(1)}, bf16[512,256]{1,0:T(8,128)(2,1)}, u32[]{:S(2)}, u32[]{:S(2)}) collective-permute-start(bf16[512,256]{1,0:T(8,128)(2,1)S(1)} %shard_map.104.refs_0_), channel_id=1, source_target_pairs={{0,8},{8,0},{16,24},{24,16},{1,9},{9,1},{17,25},{25,17},{2,10},{10... | collective-permute-start | bytes 786440 | tf_op jit(solution)/shard_map/ppermute | solution.py:308
  134.5 7.6 %collective-permute-start.22 = (bf16[512,256]{1,0:T(8,128)(2,1)}, bf16[512,256]{1,0:T(8,128)(2,1)}, u32[]{:S(2)}, u32[]{:S(2)}) collective-permute-start(bf16[512,256]{1,0:T(8,128)(2,1)} %shard_map.105.refs_1_), channel_id=1, source_target_pairs={{0,8},{8,0},{16,24},{24,16},{1,9},{9,1},{17,25},{25,17},{2,10},{10... | collective-permute-start | bytes 786440 | tf_op jit(solution)/shard_map/ppermute | solution.py:308
  144.7 5.7 %collective-permute-start.25 = (bf16[512,512]{1,0:T(8,128)(2,1)}, bf16[512,512]{1,0:T(8,128)(2,1)}, u32[]{:S(2)}, u32[]{:S(2)}) collective-permute-start(bf16[512,512]{1,0:T(8,128)(2,1)} %shard_map.107), channel_id=1, source_target_pairs={{0,1},{1,0},{2,3},{3,2},{4,5},{5,4},{6,7},{7,6},{8,9},{9,8},{10,11... | collective-permute-start | bytes 1572872 | tf_op jit(solution)/shard_map/ppermute | solution.py:391
  147.0 13.9 %collective-permute-start.27 = (bf16[1024,256]{1,0:T(8,128)(2,1)}, bf16[1024,256]{1,0:T(8,128)(2,1)}, u32[]{:S(2)}, u32[]{:S(2)}) collective-permute-start(bf16[1024,256]{1,0:T(8,128)(2,1)} %slice.22), channel_id=1, source_target_pairs={{0,2},{2,0},{4,6},{6,4},{1,3},{3,1},{5,7},{7,5},{8,10},{10,8},{12,... | collective-permute-start | bytes 1572872 | tf_op jit(solution)/shard_map/ppermute | solution.py:295
  148.0 14.0 %collective-permute-start.28 = (bf16[1024,256]{1,0:T(8,128)(2,1)}, bf16[1024,256]{1,0:T(8,128)(2,1)}, u32[]{:S(2)}, u32[]{:S(2)}) collective-permute-start(bf16[1024,256]{1,0:T(8,128)(2,1)} %slice.23), channel_id=1, source_target_pairs={{0,4},{2,6},{4,0},{6,2},{1,5},{3,7},{5,1},{7,3},{8,12},{10,14},{12... | collective-permute-start | bytes 1572872 | tf_op jit(solution)/shard_map/ppermute | solution.py:295
  152.3 14.1 %collective-permute-start.26 = (bf16[256,512]{1,0:T(8,128)(2,1)}, bf16[256,512]{1,0:T(8,128)(2,1)}, u32[]{:S(2)}, u32[]{:S(2)}) collective-permute-start(bf16[256,512]{1,0:T(8,128)(2,1)} %add_convert_fusion.4), channel_id=1, source_target_pairs={{0,16},{8,24},{16,0},{24,8},{1,17},{9,25},{17,1},{25,9},{2,18},{10... | collective-permute-start | bytes 786440 | tf_op jit(solution)/shard_map/ppermute | solution.py:308
  164.9 5.2 %collective-permute-start.29 = (bf16[512,512]{1,0:T(8,128)(2,1)S(1)}, bf16[512,512]{1,0:T(8,128)(2,1)}, u32[]{:S(2)}, u32[]{:S(2)}) collective-permute-start(bf16[512,512]{1,0:T(8,128)(2,1)S(1)} %shard_map.109), channel_id=1, source_target_pairs={{0,1},{1,0},{2,3},{3,2},{4,5},{5,4},{6,7},{7,6},{8,9},{9,8},{10,11... | collective-permute-start | bytes 1572872 | tf_op jit(solution)/shard_map/ppermute | solution.py:391
  171.1 14.2 %collective-permute-start.30 = (bf16[256,512]{1,0:T(8,128)(2,1)S(1)}, bf16[256,512]{1,0:T(8,128)(2,1)S(1)}, u32[]{:S(2)}, u32[]{:S(2)}) collective-permute-start(bf16[256,512]{1,0:T(8,128)(2,1)S(1)} %add_convert_fusion.1), channel_id=1, source_target_pairs={{0,16},{8,24},{16,0},{24,8},{1,17},{9,25},{17,1},{25,9},{2,18},{10... | collective-permute-start | bytes 786440 | tf_op jit(solution)/shard_map/ppermute | solution.py:308
  173.8 12.8 %collective-permute-start.31 = (bf16[128,512]{1,0:T(8,128)(2,1)S(1)}, bf16[128,512]{1,0:T(8,128)(2,1)S(1)}, u32[]{:S(2)}, u32[]{:S(2)}) collective-permute-start(bf16[128,512]{1,0:T(8,128)(2,1)S(1)} %get-tuple-element.57), channel_id=1, source_target_pairs={{0,8},{8,0},{16,24},{24,16},{1,9},{9,1},{17,25},{25,17},{2,10},{10... | collective-permute-start | bytes 393224 | tf_op jit(solution)/shard_map/ppermute | solution.py:308
  (34 other events, 315.1 us)

commit v12 on v11

--- a/solution.py
+++ b/solution.py
@@ -195,46 +195,47 @@
 def project_kernel(place_ref, *refs):
     attended_refs, weight_refs, out_ref = refs[:4], refs[4:-1], refs[-1]
     hi = place_ref[0]
-    side = lax.div(hi, 2) ^ place_ref[1]
+    kept, columns = out_ref.shape
+    rows = pl.ds(pl.multiple_of(place_ref[1] * kept, kept), kept)
     depth = attended_refs[0].shape[1]
     features, width = weight_refs[0].shape
     span = features // 4
-    for r, weight_ref in enumerate(weight_refs):
-        total = 0.0
-        for k, attended_ref in enumerate(attended_refs):
-            first = side * (2 * span) + (lax.rem(hi, 2) ^ (k // 2)) * span + (k % 2) * depth
-            total = total + jnp.dot(
-                attended_ref[...],
-                weight_ref[pl.ds(pl.multiple_of(first, depth), depth), :],
-                preferred_element_type=jnp.float32,
-            )
-        out_ref[:, pl.ds(r * width, width)] = total.astype(out_ref.dtype)
+    for chip in range(2):
+        side = lax.rem(hi, 2) ^ chip
+        for r, weight_ref in enumerate(weight_refs):
+            total = 0.0
+            for k, attended_ref in enumerate(attended_refs):
+                first = side * (2 * span) + (lax.div(hi, 2) ^ (k // 2)) * span + (k % 2) * depth
+                total = total + jnp.dot(
+                    attended_ref[rows, :],
+                    weight_ref[pl.ds(pl.multiple_of(first, depth), depth), :],
+                    preferred_element_type=jnp.float32,
+                )
+            place = chip * (columns // 2) + r * width
+            out_ref[:, pl.ds(place, width)] = total.astype(out_ref.dtype)
 
 
 def project(place, attended_parts, weights):
     tokens, depth = attended_parts[0].shape
-    width = weights[0].shape[1]
+    width = 2 * len(weights) * weights[0].shape[1]
     return local_kernel(
         project_kernel,
-        jax.ShapeDtypeStruct((tokens, len(weights) * width), jnp.bfloat16),
+        jax.ShapeDtypeStruct((tokens // 2, width), jnp.bfloat16),
         (place, *attended_parts, *weights),
-        2 * tokens * 4 * depth * len(weights) * width,
+        2 * (tokens // 2) * 4 * depth * width,
     )
 
 
 def assemble_kernel(place_ref, *refs):
     piece_refs, out_ref = refs[:-1], refs[-1]
-    which = lax.rem(place_ref[0], 2)
     lo = place_ref[1]
     width = out_ref.shape[1] // 8
-    chunks = len(piece_refs) // 2
-    for d in range(2):
+    each = 4 // len(piece_refs)
+    for chip in range(2):
         for r in range(4):
-            piece_ref = piece_refs[d * chunks + r * chunks // 4]
-            block = (which ^ d) * 4 + (lo ^ r)
-            out_ref[:, pl.ds(pl.multiple_of(block * width, width), width)] = piece_ref[
-                :, pl.ds(r % (4 // chunks) * width, width)
-            ]
+            out_ref[:, pl.ds(pl.multiple_of((chip * 4 + (lo ^ r)) * width, width), width)] = (
+                piece_refs[r // each][:, pl.ds((chip * each + r % each) * width, width)]
+            )
 
 
 def assemble(place, pieces):
@@ -347,11 +348,6 @@
     near = along(core_half(which_half), 1)
     other = along(core_half(1 - which_half), 2)
     halves = jnp.concatenate([near, other, along(after(other, near), 1)], axis=0)
-    features_here = w_out.shape[0] // 2
-    out_own = lax.dynamic_slice_in_dim(w_out, which_half * features_here, features_here, 0)
-    out_other = lax.dynamic_slice_in_dim(w_out, (1 - which_half) * features_here, features_here, 0)
-    out_other = along(after(out_other, near, other), 2)
-    own = after(own, out_other)
     token_parts = [own, halves, lax.ppermute(halves, "head", [(0, 1), (1, 0)])]
     index = jnp.stack([hi, lo, core])
 
@@ -360,6 +356,16 @@
 
     kept, sent = product(index, token_parts, pair_weight, 0, 1)
     query_weight = corner_after(query_sides, sent)
+
+    def rows_for(chip):
+        return jnp.concatenate(
+            [lax.dynamic_slice_in_dim(w_out, (2 * z + chip) * heads, heads, 0) for z in range(2)],
+            axis=0,
+        )
+
+    out_both = jnp.concatenate(
+        [rows_for(which), along(after(rows_for(1 - which), sent), 1)], axis=0
+    )
 
     kv_own = finish_pair(cosine, sine, [kept, along(sent, 2)])
     kv_going = after(kv_own, *query_weight[3:])
@@ -367,7 +373,7 @@
 
     firsts = jnp.stack([lo, lo, lo ^ 1, lo ^ 2, lo ^ 3]) * rows
     seen = jnp.concatenate([firsts, doc_starts])
-    out_sides = sides(after(jnp.concatenate([out_own, out_other], axis=0), *kv_parts[1:]))
+    out_sides = sides(after(out_both, *kv_parts[1:]))
     products = [product(index, token_parts, query_weight, c, 2) for c in range(2)]
     products[0] = (after(products[0][0], products[1][0]), products[0][1])
     attended = [
@@ -376,13 +382,18 @@
     ]
     out_blocks = corner_after(out_sides, *attended)
     out_blocks[3:] = [jnp.concatenate(out_blocks[3:], axis=0)]
-    attended += [along(chunk, 1) for chunk in attended]
+    attended += [along(chunk, 2) for chunk in attended]
 
     def added(one, two):
         return (one.astype(jnp.float32) + two.astype(jnp.float32)).astype(jnp.bfloat16)
 
-    kept = 2 * rows
-    here, there, shares, summed = [], [], [], None
+    home = [
+        ((2 * half + chip) * 2 + group, (2 * group + chip) * 2 + half)
+        for half in range(2)
+        for chip in range(2)
+        for group in range(2)
+    ]
+    pieces, shares, summed = [], [], None
     for blocks in (out_blocks[:2], out_blocks[2:]):
         first = [after(blocks[0], *shares[1:]), *blocks[1:]]
         theirs = project(jnp.stack([hi, 1 - core]), attended, first)
@@ -391,15 +402,14 @@
         theirs = lax.ppermute(theirs, "head", [(0, 1), (1, 0)])
         shares = [
             added(
-                lax.dynamic_slice_in_dim(mine, z * kept, kept, 0),
-                lax.dynamic_slice_in_dim(theirs, z * kept, kept, 0),
+                lax.dynamic_slice_in_dim(mine, chip * rows, rows, 0),
+                lax.dynamic_slice_in_dim(theirs, chip * rows, rows, 0),
             )
-            for z in (which_half, 1 - which_half)
+            for chip in (which, 1 - which)
         ]
-        summed = added(shares[0], along(shares[1], 2))
-        here.append(lax.dynamic_slice_in_dim(summed, which * rows, rows, 0))
-        there.append(along(lax.dynamic_slice_in_dim(summed, (1 - which) * rows, rows, 0), 1))
-    return assemble(index, here + there)
+        summed = added(shares[0], along(shares[1], 1))
+        pieces.append(lax.ppermute(summed, ("hi", "head"), home))
+    return assemble(index, pieces)
 
 
 def solution(mesh):

time: 195 us -> 188 us (0.964); the launches traced: 192 us -> 187 us
  waiting for transfers between devices: 95.8 us -> 82 us
  starting transfers between devices: 36.4 us -> 43.4 us
  local copies, waits for them, and re-layouts: 15.9 us -> 17.9 us
    ppermute x15 -> x13, waiting for transfers between devices: 81.9 us -> 54.8 us  [along(): return lax.ppermute(block, 'hi', [(i, i ^ d) for i in range(4)])]
    ppermute x0 -> x2, waiting for transfers between devices: none -> 8.67 us  [line_device(): pieces.append(lax.ppermute(summed, ('hi', 'head'), home))]
    ppermute x0 -> x2, starting transfers between devices: none -> 7.38 us  [line_device(): pieces.append(lax.ppermute(summed, ('hi', 'head'), home))]
    ppermute x15 -> x13, starting transfers between devices: 18.2 us -> 12.7 us  [along(): return lax.ppermute(block, 'hi', [(i, i ^ d) for i in range(4)])]
    ppermute x2, starting transfers between devices: 2.29 us -> 7.08 us  [line_device(): theirs = lax.ppermute(theirs, 'head', [(0, 1), (1, 0)])]
    ppermute x15, waiting for transfers between devices: 13.9 us -> 18.4 us  [beside(): return lax.ppermute(block, 'lo', [(i, i ^ r) for i in range(4)])]
    dynamic_slice x2, local copies, waits for them, and re-layouts: 1.31 us -> 3.29 us  [columns_for(): lax.dynamic_slice_in_dim(w, (2 * z + chip) * width, width, 1)]
    unnamed x69 -> x71, local copies, waits for them, and re-layouts: 5.69 us -> 6.28 us
  transfers between devices with their start and end apart: 33 -> 33, of which waited for: 13 -> 12; matrix products, arithmetic and copies ran while one was open for 12% -> 13% of each run, Pallas kernels for 14% -> 14%
where the time goes in v12:
time: 188 us; the launch traced here: 187 us
  waiting for transfers between devices  82 us (44%)
  starting transfers between devices  43.4 us (23%)
  Pallas kernels  30.4 us (16%)
  local copies, waits for them, and re-layouts  17.9 us (10%)
  other arithmetic  12.9 us (7%)
    ppermute x13, waiting for transfers between devices, along(): return lax.ppermute(block, 'hi', [(i, i ^ d) for i in range(4)])  54.8 us
    pallas_call x11, Pallas kernels, local_kernel(): pl.pallas_call(body, in_specs=[pl.BlockSpec(memory_space=pltpu.SMEM)] + [...  30.4 us
    ppermute x15, waiting for transfers between devices, beside(): return lax.ppermute(block, 'lo', [(i, i ^ r) for i in range(4)])  18.4 us
    ppermute x13, starting transfers between devices, along(): return lax.ppermute(block, 'hi', [(i, i ^ d) for i in range(4)])  12.7 us
    ppermute x15, starting transfers between devices, beside(): return lax.ppermute(block, 'lo', [(i, i ^ r) for i in range(4)])  12.2 us
    ppermute x2, waiting for transfers between devices, line_device(): pieces.append(lax.ppermute(summed, ('hi', 'head'), home))  8.67 us
    ppermute x2, starting transfers between devices, line_device(): pieces.append(lax.ppermute(summed, ('hi', 'head'), home))  7.38 us
    ppermute x2, starting transfers between devices, line_device(): theirs = lax.ppermute(theirs, 'head', [(0, 1), (1, 0)])  7.08 us
  transfers between devices with their start and end apart: 33, of which 12 were waited for; matrix products, arithmetic and copies ran while one was open for 13% of the time, Pallas kernels for 14%

profile of v12, /device:TPU:1, one launch (start us, length us, event | category | flops | bytes accessed | tf_op | source)
XLA Modules:
  0.0 187.1 jit_solution(7208640086183779927)
XLA Ops:
  1.3 2.2 %collective-permute-start.4 = (bf16[256,512]{1,0:T(8,128)(2,1)S(1)}, bf16[256,512]{1,0:T(8,128)(2,1)S(1)}, u32[]{:S(2)}, u32[]{:S(2)}) collective-permute-start(bf16[256,512]{1,0:T(8,128)(2,1)S(1)} %pad_maximum_fusion.7), channel_id=1, source_target_pairs={{0,8},{8,0},{16,24},{24,16},{1,9},{9,1},{17,25},{25,17},{2,10},{10... | collective-permute-start | bytes 786440 | tf_op jit(solution)/shard_map/ppermute | solution.py:309
  4.1 5.3 %collective-permute-done.4 = bf16[256,512]{1,0:T(8,128)(2,1)S(1)} collective-permute-done((bf16[256,512]{1,0:T(8,128)(2,1)S(1)}, bf16[256,512]{1,0:T(8,128)(2,1)S(1)}, u32[]{:S(2)}, u32[]{:S(2)}) %collective-permute-start.4) | collective-permute-done | bytes 262176 | tf_op jit(solution)/shard_map/ppermute | solution.py:309
  11.9 2.1 %constant_dynamic-slice_fusion.15 = (bf16[256,512]{1,0:T(8,128)(2,1)}, bf16[256,512]{1,0:T(8,128)(2,1)}, bf16[256,512]{1,0:T(8,128)(2,1)S(1)}, bf16[256,512]{1,0:T(8,128)(2,1)S(1)}) fusion(bf16[256,2048]{1,0:T(8,128)(2,1)} %param.12, s32[]{:T(128)S(6)} %select_n.78, s32[]{:T(128)S(6)} %select_n.79, s32[]{:T(128)S(6)} %select_n.81, s32[]{:T(128)S(6)} %select_n.80), kind=kLoop, calls=%fused_computation.42 | loop fusion | bytes 2097168 | tf_op jit(solution)/shard_map/dynamic_slice | solution.py:326
  16.4 2.3 %collective-permute-start.1 = (bf16[128,1024]{1,0:T(8,128)(2,1)S(1)}, bf16[128,1024]{1,0:T(8,128)(2,1)}, u32[]{:S(2)}, u32[]{:S(2)}) collective-permute-start(bf16[128,1024]{1,0:T(8,128)(2,1)S(1)} %get-tuple-element.53), channel_id=1, source_target_pairs={{0,16},{8,24},{16,0},{24,8},{1,17},{9,25},{17,1},{25,9},{2,18},{10... | collective-permute-start | bytes 786440 | tf_op jit(solution)/shard_map/ppermute | solution.py:309
  18.8 2.2 %constant_dynamic-slice_fusion.3 = (bf16[512,256]{1,0:T(8,128)(2,1)}, bf16[512,256]{1,0:T(8,128)(2,1)}, bf16[512,256]{1,0:T(8,128)(2,1)}, bf16[512,256]{1,0:T(8,128)(2,1)}) fusion(bf16[2048,256]{1,0:T(8,128)(2,1)} %param.15, s32[]{:T(128)S(6)} %select_n.78, s32[]{:T(128)S(6)} %select_n.79, s32[]{:T(128)S(6)} %select_n.81, s32[]{:T(128)S(6)} %select_n.80), kind=kLoop, calls=%fused_computation.30 | loop fusion | bytes 2097168 | tf_op jit(solution)/shard_map/dynamic_slice | solution.py:362
  25.5 12.3 %collective-permute-done = bf16[128,1024]{1,0:T(8,128)(2,1)S(1)} collective-permute-done((bf16[128,1024]{1,0:T(8,128)(2,1)S(1)}, bf16[128,1024]{1,0:T(8,128)(2,1)S(1)}, u32[]{:S(2)}, u32[]{:S(2)}) %collective-permute-start) | collective-permute-done | bytes 262176 | tf_op jit(solution)/shard_map/ppermute | solution.py:309
  44.1 4.0 %collective-permute-start.3 = (bf16[384,1024]{1,0:T(8,128)(2,1)S(1)}, bf16[384,1024]{1,0:T(8,128)(2,1)S(1)}, u32[]{:S(2)}, u32[]{:S(2)}) collective-permute-start(bf16[384,1024]{1,0:T(8,128)(2,1)S(1)} %constant_dynamic-update-slice_fusion.refs_1_), channel_id=1, source_target_pairs={{0,1},{1,0},{2,3},{3,2},{4,5},{5,4},{6,7},{7,6},{8,9},{9,8},{10,11... | collective-permute-start | bytes 2359304 | tf_op jit(solution)/shard_map/ppermute | solution.py:351
  48.2 2.1 %fusion.3 = (f32[512,64]{1,0:T(8,128)}, f32[512,64]{1,0:T(8,128)}, f32[512,64]{1,0:T(8,128)}) fusion(f32[64]{0:T(128)S(1)} %negate_power_fusion, f32[512]{0:T(512)S(1)} %fusion.12), kind=kLoop, calls=%fused_computation.21 | loop fusion | flops 65536 | bytes 395520 | tf_op jit(solution)/shard_map/neg | solution.py:36
  50.3 1.9 %shard_map.100 = (bf16[512,256]{1,0:T(8,128)(2,1)S(1)}, bf16[512,256]{1,0:T(8,128)(2,1)S(1)}) custom-call(s32[5]{0:T(128)S(1)} %get-tuple-element.66.place_ref, bf16[128,2048]{1,0:T(8,128)(2,1)S(1)} %constant_dynamic-slice_fusion.18.refs_0_, bf16[384,1024]{1,0:T(8,128)(2,1)S(1)} %constant_dynamic-update-slice_fusion.refs_1_, ...), custom_call_target="tpu_custom_call" | custom-call | flops 1073741824 | bytes 4194324 | tf_op jit(solution)/shard_map/pallas_call | solution.py:18
  53.6 10.0 %collective-permute-done.10.refs_4_ = bf16[512,1024]{1,0:T(8,128)(2,1)S(1)} collective-permute-done((bf16[512,1024]{1,0:T(8,128)(2,1)S(1)}, bf16[512,1024]{1,0:T(8,128)(2,1)S(1)}, u32[]{:S(2)}, u32[]{:S(2)}) %collective-permute-start.10) | collective-permute-done | bytes 1048608 | tf_op jit(solution)/shard_map/ppermute | solution.py:296
  67.7 2.3 %collective-permute-start.15 = (bf16[512,256]{1,0:T(8,128)(2,1)}, bf16[512,256]{1,0:T(8,128)(2,1)S(1)}, u32[]{:S(2)}, u32[]{:S(2)}) collective-permute-start(bf16[512,256]{1,0:T(8,128)(2,1)} %copy-done.18), channel_id=1, source_target_pairs={{0,16},{8,24},{16,0},{24,8},{1,17},{9,25},{17,1},{25,9},{2,18},{10... | collective-permute-start | bytes 786440 | tf_op jit(solution)/shard_map/ppermute | solution.py:309
  71.9 5.9 %collective-permute-done.15.refs_1_ = bf16[512,256]{1,0:T(8,128)(2,1)S(1)} collective-permute-done((bf16[512,256]{1,0:T(8,128)(2,1)}, bf16[512,256]{1,0:T(8,128)(2,1)S(1)}, u32[]{:S(2)}, u32[]{:S(2)}) %collective-permute-start.15) | collective-permute-done | bytes 262176 | tf_op jit(solution)/shard_map/ppermute | solution.py:309
  78.1 1.6 collective-permute-start.17
  80.7 2.6 %shard_map.101 = (bf16[512,256]{1,0:T(8,128)(2,1)S(1)}, bf16[512,256]{1,0:T(8,128)(2,1)S(1)}) custom-call(s32[5]{0:T(128)S(1)} %get-tuple-element.67.place_ref, bf16[128,2048]{1,0:T(8,128)(2,1)S(1)} %constant_dynamic-slice_fusion.18.refs_0_, bf16[384,1024]{1,0:T(8,128)(2,1)S(1)} %constant_dynamic-update-slice_fusion.refs_1_, ...), custom_call_target="tpu_custom_call" | custom-call | flops 1073741824 | bytes 6291476 | tf_op jit(solution)/shard_map/pallas_call | solution.py:18
  83.4 4.0 %collective-permute-done.22 = bf16[1024,256]{1,0:T(8,128)(2,1)S(1)} collective-permute-done((bf16[1024,256]{1,0:T(8,128)(2,1)}, bf16[1024,256]{1,0:T(8,128)(2,1)S(1)}, u32[]{:S(2)}, u32[]{:S(2)}) %collective-permute-start.22) | collective-permute-done | bytes 524320 | tf_op jit(solution)/shard_map/ppermute | solution.py:309
  88.6 2.6 %shard_map.102 = (bf16[512,256]{1,0:T(8,128)(2,1)S(1)}, bf16[512,256]{1,0:T(8,128)(2,1)S(1)}) custom-call(s32[5]{0:T(128)S(1)} %get-tuple-element.43.place_ref, bf16[128,2048]{1,0:T(8,128)(2,1)S(1)} %constant_dynamic-slice_fusion.18.refs_0_, bf16[384,1024]{1,0:T(8,128)(2,1)S(1)} %constant_dynamic-update-slice_fusion.refs_1_, ...), custom_call_target="tpu_custom_call" | custom-call | flops 1073741824 | bytes 6291476 | tf_op jit(solution)/shard_map/pallas_call | solution.py:18
  92.7 6.3 %shard_map.104.refs_0_ = bf16[512,256]{1,0:T(8,128)(2,1)S(1)} custom-call(s32[21]{0:T(128)S(1)} %pad_add_fusion.2.place_ref, f32[512,128]{1,0:T(8,128)S(1)} %get-tuple-element.68.cos_ref, f32[512,128]{1,0:T(8,128)S(1)} %get-tuple-element.69.sin_ref, bf16[512,256]{1,0:T(8,128)(2,1)S(1)} %get-tuple-element.32.refs_0_, ...), custom_call_target="tpu_custom_call" | custom-call | flops 8589934592 | bytes 2097236 | tf_op jit(solution)/shard_map/pallas_call | solution.py:18
  99.0 2.4 %collective-permute-start.20 = (bf16[512,256]{1,0:T(8,128)(2,1)S(1)}, bf16[512,256]{1,0:T(8,128)(2,1)}, u32[]{:S(2)}, u32[]{:S(2)}) collective-permute-start(bf16[512,256]{1,0:T(8,128)(2,1)S(1)} %shard_map.104.refs_0_), channel_id=1, source_target_pairs={{0,16},{8,24},{16,0},{24,8},{1,17},{9,25},{17,1},{25,9},{2,18},{10... | collective-permute-start | bytes 786440 | tf_op jit(solution)/shard_map/ppermute | solution.py:309
  101.4 8.7 %collective-permute-done.19.refs_1_ = bf16[512,256]{1,0:T(8,128)(2,1)S(1)} collective-permute-done((bf16[512,256]{1,0:T(8,128)(2,1)S(1)}, bf16[512,256]{1,0:T(8,128)(2,1)S(1)}, u32[]{:S(2)}, u32[]{:S(2)}) %collective-permute-start.19) | collective-permute-done | bytes 262176 | tf_op jit(solution)/shard_map/ppermute | solution.py:309
  110.2 7.2 %shard_map.105.refs_1_ = bf16[512,256]{1,0:T(8,128)(2,1)} custom-call(s32[21]{0:T(128)S(1)} %pad_add_fusion.2.place_ref, f32[512,128]{1,0:T(8,128)S(1)} %get-tuple-element.68.cos_ref, f32[512,128]{1,0:T(8,128)S(1)} %get-tuple-element.69.sin_ref, bf16[512,256]{1,0:T(8,128)(2,1)S(1)} %get-tuple-element.31.refs_0_, ...), custom_call_target="tpu_custom_call" | custom-call | flops 8589934592 | bytes 2097236 | tf_op jit(solution)/shard_map/pallas_call | solution.py:18
  117.5 12.4 %collective-permute-done.21.refs_3_ = bf16[512,256]{1,0:T(8,128)(2,1)} collective-permute-done((bf16[512,256]{1,0:T(8,128)(2,1)}, bf16[512,256]{1,0:T(8,128)(2,1)}, u32[]{:S(2)}, u32[]{:S(2)}) %collective-permute-start.21) | collective-permute-done | bytes 262176 | tf_op jit(solution)/shard_map/ppermute | solution.py:309
  129.9 2.6 %shard_map.107 = bf16[256,1024]{1,0:T(8,128)(2,1)} custom-call(s32[2]{0:T(128)S(1)} %pad_add_fusion.7.place_ref, bf16[512,256]{1,0:T(8,128)(2,1)S(1)} %shard_map.104.refs_0_, bf16[512,256]{1,0:T(8,128)(2,1)} %shard_map.105.refs_1_, bf16[512,256]{1,0:T(8,128)(2,1)} %collective-permute-done.20.refs_2_, bf16[512,256]{1,0:T(8,128)(2,1)} %collective-permute-done.21.refs_3_, ...), custom_call_target="tpu_custom_call" | custom-call | flops 536870912 | bytes 3145736 | tf_op jit(solution)/shard_map/pallas_call | solution.py:18
  132.5 6.0 %collective-permute-start.25 = (bf16[256,1024]{1,0:T(8,128)(2,1)}, bf16[256,1024]{1,0:T(8,128)(2,1)}, u32[]{:S(2)}, u32[]{:S(2)}) collective-permute-start(bf16[256,1024]{1,0:T(8,128)(2,1)} %shard_map.107), channel_id=1, source_target_pairs={{0,1},{1,0},{2,3},{3,2},{4,5},{5,4},{6,7},{7,6},{8,9},{9,8},{10,11... | collective-permute-start | bytes 1572872 | tf_op jit(solution)/shard_map/ppermute | solution.py:402
  142.0 1.8 shard_map.106
  143.8 1.9 %add_convert_fusion.4 = bf16[128,1024]{1,0:T(8,128)(2,1)} fusion(bf16[256,1024]{1,0:T(8,128)(2,1)} %collective-permute-done.25, s32[]{:T(128)S(6)} %select_n.87, bf16[256,1024]{1,0:T(8,128)(2,1)S(1)} %shard_map.106), kind=kLoop, calls=%fused_computation.14 | loop fusion | flops 524288 | bytes 786436 | tf_op jit(solution)/shard_map/convert_element_type | solution.py:388
  145.7 7.5 %collective-permute-done.28 = bf16[1024,256]{1,0:T(8,128)(2,1)} collective-permute-done((bf16[1024,256]{1,0:T(8,128)(2,1)}, bf16[1024,256]{1,0:T(8,128)(2,1)}, u32[]{:S(2)}, u32[]{:S(2)}) %collective-permute-start.28) | collective-permute-done | bytes 524320 | tf_op jit(solution)/shard_map/ppermute | solution.py:296
  155.4 1.9 %shard_map.109 = bf16[256,1024]{1,0:T(8,128)(2,1)S(1)} custom-call(s32[2]{0:T(128)S(1)} %pad_add_fusion.7.place_ref, bf16[512,256]{1,0:T(8,128)(2,1)S(1)} %shard_map.104.refs_0_, bf16[512,256]{1,0:T(8,128)(2,1)} %shard_map.105.refs_1_, bf16[512,256]{1,0:T(8,128)(2,1)} %collective-permute-done.20.refs_2_, bf16[512,256]{1,0:T(8,128)(2,1)} %collective-permute-done.21.refs_3_, ...), custom_call_target="tpu_custom_call" | custom-call | flops 536870912 | bytes 3145736 | tf_op jit(solution)/shard_map/pallas_call | solution.py:18
  159.6 1.8 shard_map.108
  162.5 4.7 %collective-permute-start.27 = (bf16[128,1024]{1,0:T(8,128)(2,1)S(1)}, bf16[128,1024]{1,0:T(8,128)(2,1)S(1)}, u32[]{:S(2)}, u32[]{:S(2)}) collective-permute-start(bf16[128,1024]{1,0:T(8,128)(2,1)S(1)} %add_convert_fusion.3), channel_id=1, source_target_pairs={{0,0},{1,16},{8,8},{9,24},{16,1},{17,17},{24,9},{25,25},{2,2},{3,1... | collective-permute-start | bytes 786440 | tf_op jit(solution)/shard_map/ppermute | solution.py:411
  167.3 5.9 %collective-permute-done.31 = bf16[128,1024]{1,0:T(8,128)(2,1)S(1)} collective-permute-done((bf16[128,1024]{1,0:T(8,128)(2,1)S(1)}, bf16[128,1024]{1,0:T(8,128)(2,1)S(1)}, u32[]{:S(2)}, u32[]{:S(2)}) %collective-permute-start.31) | collective-permute-done | bytes 262176 | tf_op jit(solution)/shard_map/ppermute | solution.py:309
  174.3 2.6 %collective-permute-start.32 = (bf16[128,1024]{1,0:T(8,128)(2,1)S(1)}, bf16[128,1024]{1,0:T(8,128)(2,1)S(1)}, u32[]{:S(2)}, u32[]{:S(2)}) collective-permute-start(bf16[128,1024]{1,0:T(8,128)(2,1)S(1)} %add_convert_fusion), channel_id=1, source_target_pairs={{0,0},{1,16},{8,8},{9,24},{16,1},{17,17},{24,9},{25,25},{2,2},{3,1... | collective-permute-start | bytes 786440 | tf_op jit(solution)/shard_map/ppermute | solution.py:411
  177.0 8.7 %collective-permute-done.32.refs_1_ = bf16[128,1024]{1,0:T(8,128)(2,1)S(1)} collective-permute-done((bf16[128,1024]{1,0:T(8,128)(2,1)S(1)}, bf16[128,1024]{1,0:T(8,128)(2,1)S(1)}, u32[]{:S(2)}, u32[]{:S(2)}) %collective-permute-start.32) | collective-permute-done | bytes 262176 | tf_op jit(solution)/shard_map/ppermute | solution.py:411
  (154 shorter events, 40.4 us)
Async XLA Ops:
  1.3 8.2 %collective-permute-start.4 = (bf16[256,512]{1,0:T(8,128)(2,1)S(1)}, bf16[256,512]{1,0:T(8,128)(2,1)S(1)}, u32[]{:S(2)}, u32[]{:S(2)}) collective-permute-start(bf16[256,512]{1,0:T(8,128)(2,1)S(1)} %pad_maximum_fusion.7), channel_id=1, source_target_pairs={{0,8},{8,0},{16,24},{24,16},{1,9},{9,1},{17,25},{25,17},{2,10},{10... | collective-permute-start | bytes 786440 | tf_op jit(solution)/shard_map/ppermute | solution.py:309
  9.5 12.3 %collective-permute-start.6 = (bf16[512,512]{1,0:T(8,128)(2,1)S(1)}, bf16[512,512]{1,0:T(8,128)(2,1)S(1)}, u32[]{:S(2)}, u32[]{:S(2)}) collective-permute-start(bf16[512,512]{1,0:T(8,128)(2,1)S(1)} %pad_maximum_fusion.3.refs_3_), channel_id=1, source_target_pairs={{0,4},{2,6},{4,0},{6,2},{1,5},{3,7},{5,1},{7,3},{8,12},{10,14},{12... | collective-permute-start | bytes 1572872 | tf_op jit(solution)/shard_map/ppermute | solution.py:296
  10.7 12.6 %collective-permute-start.8 = (bf16[512,512]{1,0:T(8,128)(2,1)S(1)}, bf16[512,512]{1,0:T(8,128)(2,1)S(1)}, u32[]{:S(2)}, u32[]{:S(2)}) collective-permute-start(bf16[512,512]{1,0:T(8,128)(2,1)S(1)} %pad_maximum_fusion.3.refs_3_), channel_id=1, source_target_pairs={{0,2},{2,0},{4,6},{6,4},{1,3},{3,1},{5,7},{7,5},{8,10},{10,8},{12,... | collective-permute-start | bytes 1572872 | tf_op jit(solution)/shard_map/ppermute | solution.py:296
  14.9 26.1 %collective-permute-start.5 = (bf16[256,1024]{1,0:T(8,128)(2,1)}, bf16[256,1024]{1,0:T(8,128)(2,1)}, u32[]{:S(2)}, u32[]{:S(2)}) collective-permute-start(bf16[256,1024]{1,0:T(8,128)(2,1)} %pad_maximum_fusion.2), channel_id=1, source_target_pairs={{0,8},{8,0},{16,24},{24,16},{1,9},{9,1},{17,25},{25,17},{2,10},{10... | collective-permute-start | bytes 1572872 | tf_op jit(solution)/shard_map/ppermute | solution.py:309
  16.2 21.6 %collective-permute-start = (bf16[128,1024]{1,0:T(8,128)(2,1)S(1)}, bf16[128,1024]{1,0:T(8,128)(2,1)S(1)}, u32[]{:S(2)}, u32[]{:S(2)}) collective-permute-start(bf16[128,1024]{1,0:T(8,128)(2,1)S(1)} %get-tuple-element.54), channel_id=1, source_target_pairs={{0,8},{8,0},{16,24},{24,16},{1,9},{9,1},{17,25},{25,17},{2,10},{10... | collective-permute-start | bytes 786440 | tf_op jit(solution)/shard_map/ppermute | solution.py:309
  16.4 21.4 %collective-permute-start.1 = (bf16[128,1024]{1,0:T(8,128)(2,1)S(1)}, bf16[128,1024]{1,0:T(8,128)(2,1)}, u32[]{:S(2)}, u32[]{:S(2)}) collective-permute-start(bf16[128,1024]{1,0:T(8,128)(2,1)S(1)} %get-tuple-element.53), channel_id=1, source_target_pairs={{0,16},{8,24},{16,0},{24,8},{1,17},{9,25},{17,1},{25,9},{2,18},{10... | collective-permute-start | bytes 786440 | tf_op jit(solution)/shard_map/ppermute | solution.py:309
  22.5 19.7 %collective-permute-start.7 = (bf16[256,512]{1,0:T(8,128)(2,1)}, bf16[256,512]{1,0:T(8,128)(2,1)S(1)}, u32[]{:S(2)}, u32[]{:S(2)}) collective-permute-start(bf16[256,512]{1,0:T(8,128)(2,1)} %slice.24), channel_id=1, source_target_pairs={{0,2},{2,0},{4,6},{6,4},{1,3},{3,1},{5,7},{7,5},{8,10},{10,8},{12,... | collective-permute-start | bytes 786440 | tf_op jit(solution)/shard_map/ppermute | solution.py:296
  24.1 18.2 %collective-permute-start.9 = (bf16[256,512]{1,0:T(8,128)(2,1)}, bf16[256,512]{1,0:T(8,128)(2,1)S(1)}, u32[]{:S(2)}, u32[]{:S(2)}) collective-permute-start(bf16[256,512]{1,0:T(8,128)(2,1)} %slice.25), channel_id=1, source_target_pairs={{0,4},{2,6},{4,0},{6,2},{1,5},{3,7},{5,1},{7,3},{8,12},{10,14},{12... | collective-permute-start | bytes 786440 | tf_op jit(solution)/shard_map/ppermute | solution.py:296
  38.5 5.5 %collective-permute-start.2 = (bf16[128,1024]{1,0:T(8,128)(2,1)}, bf16[128,1024]{1,0:T(8,128)(2,1)S(1)}, u32[]{:S(2)}, u32[]{:S(2)}) collective-permute-start(bf16[128,1024]{1,0:T(8,128)(2,1)} %collective-permute-done.1), channel_id=1, source_target_pairs={{0,8},{8,0},{16,24},{24,16},{1,9},{9,1},{17,25},{25,17},{2,10},{10... | collective-permute-start | bytes 786440 | tf_op jit(solution)/shard_map/ppermute | solution.py:309
  42.3 21.4 %collective-permute-start.10 = (bf16[512,1024]{1,0:T(8,128)(2,1)S(1)}, bf16[512,1024]{1,0:T(8,128)(2,1)S(1)}, u32[]{:S(2)}, u32[]{:S(2)}) collective-permute-start(bf16[512,1024]{1,0:T(8,128)(2,1)S(1)} %pad_maximum_fusion.refs_3_), channel_id=1, source_target_pairs={{0,2},{2,0},{4,6},{6,4},{1,3},{3,1},{5,7},{7,5},{8,10},{10,8},{12,... | collective-permute-start | bytes 3145736 | tf_op jit(solution)/shard_map/ppermute | solution.py:296
  42.6 21.1 %collective-permute-start.11 = (bf16[512,1024]{1,0:T(8,128)(2,1)S(1)}, bf16[512,1024]{1,0:T(8,128)(2,1)S(1)}, u32[]{:S(2)}, u32[]{:S(2)}) collective-permute-start(bf16[512,1024]{1,0:T(8,128)(2,1)S(1)} %pad_maximum_fusion.refs_3_), channel_id=1, source_target_pairs={{0,4},{2,6},{4,0},{6,2},{1,5},{3,7},{5,1},{7,3},{8,12},{10,14},{12... | collective-permute-start | bytes 3145736 | tf_op jit(solution)/shard_map/ppermute | solution.py:296
  44.1 6.2 %collective-permute-start.3 = (bf16[384,1024]{1,0:T(8,128)(2,1)S(1)}, bf16[384,1024]{1,0:T(8,128)(2,1)S(1)}, u32[]{:S(2)}, u32[]{:S(2)}) collective-permute-start(bf16[384,1024]{1,0:T(8,128)(2,1)S(1)} %constant_dynamic-update-slice_fusion.refs_1_), channel_id=1, source_target_pairs={{0,1},{1,0},{2,3},{3,2},{4,5},{5,4},{6,7},{7,6},{8,9},{9,8},{10,11... | collective-permute-start | bytes 2359304 | tf_op jit(solution)/shard_map/ppermute | solution.py:351
  64.5 13.4 %collective-permute-start.12 = (bf16[256,1024]{1,0:T(8,128)(2,1)}, bf16[256,1024]{1,0:T(8,128)(2,1)}, u32[]{:S(2)}, u32[]{:S(2)}) collective-permute-start(bf16[256,1024]{1,0:T(8,128)(2,1)} %slice.20), channel_id=1, source_target_pairs={{0,2},{2,0},{4,6},{6,4},{1,3},{3,1},{5,7},{7,5},{8,10},{10,8},{12,... | collective-permute-start | bytes 1572872 | tf_op jit(solution)/shard_map/ppermute | solution.py:296
  66.6 11.4 %collective-permute-start.13 = (bf16[256,1024]{1,0:T(8,128)(2,1)}, bf16[256,1024]{1,0:T(8,128)(2,1)}, u32[]{:S(2)}, u32[]{:S(2)}) collective-permute-start(bf16[256,1024]{1,0:T(8,128)(2,1)} %slice.21), channel_id=1, source_target_pairs={{0,4},{2,6},{4,0},{6,2},{1,5},{3,7},{5,1},{7,3},{8,12},{10,14},{12... | collective-permute-start | bytes 1572872 | tf_op jit(solution)/shard_map/ppermute | solution.py:296
  67.7 10.1 %collective-permute-start.15 = (bf16[512,256]{1,0:T(8,128)(2,1)}, bf16[512,256]{1,0:T(8,128)(2,1)S(1)}, u32[]{:S(2)}, u32[]{:S(2)}) collective-permute-start(bf16[512,256]{1,0:T(8,128)(2,1)} %copy-done.18), channel_id=1, source_target_pairs={{0,16},{8,24},{16,0},{24,8},{1,17},{9,25},{17,1},{25,9},{2,18},{10... | collective-permute-start | bytes 786440 | tf_op jit(solution)/shard_map/ppermute | solution.py:309
  70.0 17.4 %collective-permute-start.22 = (bf16[1024,256]{1,0:T(8,128)(2,1)}, bf16[1024,256]{1,0:T(8,128)(2,1)S(1)}, u32[]{:S(2)}, u32[]{:S(2)}) collective-permute-start(bf16[1024,256]{1,0:T(8,128)(2,1)} %pad_maximum_fusion.4), channel_id=1, source_target_pairs={{0,8},{8,0},{16,24},{24,16},{1,9},{9,1},{17,25},{25,17},{2,10},{10... | collective-permute-start | bytes 1572872 | tf_op jit(solution)/shard_map/ppermute | solution.py:309
  78.0 13.3 %collective-permute-start.16 = (bf16[512,256]{1,0:T(8,128)(2,1)S(1)}, bf16[512,256]{1,0:T(8,128)(2,1)S(1)}, u32[]{:S(2)}, u32[]{:S(2)}) collective-permute-start(bf16[512,256]{1,0:T(8,128)(2,1)S(1)} %shard_map.103.refs_2_), channel_id=1, source_target_pairs={{0,2},{2,0},{4,6},{6,4},{1,3},{3,1},{5,7},{7,5},{8,10},{10,8},{12,... | collective-permute-start | bytes 786440 | tf_op jit(solution)/shard_map/ppermute | solution.py:296
  78.1 13.1 %collective-permute-start.17 = (bf16[512,256]{1,0:T(8,128)(2,1)S(1)}, bf16[512,256]{1,0:T(8,128)(2,1)S(1)}, u32[]{:S(2)}, u32[]{:S(2)}) collective-permute-start(bf16[512,256]{1,0:T(8,128)(2,1)S(1)} %shard_map.103.refs_2_), channel_id=1, source_target_pairs={{0,4},{2,6},{4,0},{6,2},{1,5},{3,7},{5,1},{7,3},{8,12},{10,14},{12... | collective-permute-start | bytes 786440 | tf_op jit(solution)/shard_map/ppermute | solution.py:296
  79.7 11.6 %collective-permute-start.18 = (bf16[512,256]{1,0:T(8,128)(2,1)S(1)}, bf16[512,256]{1,0:T(8,128)(2,1)S(1)}, u32[]{:S(2)}, u32[]{:S(2)}) collective-permute-start(bf16[512,256]{1,0:T(8,128)(2,1)S(1)} %shard_map.103.refs_2_), channel_id=1, source_target_pairs={{0,6},{2,4},{4,2},{6,0},{1,7},{3,5},{5,3},{7,1},{8,14},{10,12},{12... | collective-permute-start | bytes 786440 | tf_op jit(solution)/shard_map/ppermute | solution.py:296
  83.3 9.4 %collective-permute-start.14 = (bf16[512,256]{1,0:T(8,128)(2,1)S(1)}, bf16[512,256]{1,0:T(8,128)(2,1)S(1)}, u32[]{:S(2)}, u32[]{:S(2)}) collective-permute-start(bf16[512,256]{1,0:T(8,128)(2,1)S(1)} %get-tuple-element.33), channel_id=1, source_target_pairs={{0,16},{8,24},{16,0},{24,8},{1,17},{9,25},{17,1},{25,9},{2,18},{10... | collective-permute-start | bytes 786440 | tf_op jit(solution)/shard_map/ppermute | solution.py:309
  91.2 19.0 %collective-permute-start.19 = (bf16[512,256]{1,0:T(8,128)(2,1)S(1)}, bf16[512,256]{1,0:T(8,128)(2,1)S(1)}, u32[]{:S(2)}, u32[]{:S(2)}) collective-permute-start(bf16[512,256]{1,0:T(8,128)(2,1)S(1)} %get-tuple-element.36), channel_id=1, source_target_pairs={{0,16},{8,24},{16,0},{24,8},{1,17},{9,25},{17,1},{25,9},{2,18},{10... | collective-permute-start | bytes 786440 | tf_op jit(solution)/shard_map/ppermute | solution.py:309
  91.3 26.2 %collective-permute-start.23 = (bf16[2048,256]{1,0:T(8,128)(2,1)S(1)}, bf16[2048,256]{1,0:T(8,128)(2,1)S(1)}, u32[]{:S(2)}, u32[]{:S(2)}) collective-permute-start(bf16[2048,256]{1,0:T(8,128)(2,1)S(1)} %pad_maximum_fusion.1.refs_4_), channel_id=1, source_target_pairs={{0,2},{2,0},{4,6},{6,4},{1,3},{3,1},{5,7},{7,5},{8,10},{10,8},{12,... | collective-permute-start | bytes 3145736 | tf_op jit(solution)/shard_map/ppermute | solution.py:296
  91.3 26.1 %collective-permute-start.24 = (bf16[2048,256]{1,0:T(8,128)(2,1)S(1)}, bf16[2048,256]{1,0:T(8,128)(2,1)S(1)}, u32[]{:S(2)}, u32[]{:S(2)}) collective-permute-start(bf16[2048,256]{1,0:T(8,128)(2,1)S(1)} %pad_maximum_fusion.1.refs_4_), channel_id=1, source_target_pairs={{0,4},{2,6},{4,0},{6,2},{1,5},{3,7},{5,1},{7,3},{8,12},{10,14},{12... | collective-permute-start | bytes 3145736 | tf_op jit(solution)/shard_map/ppermute | solution.py:296
  99.0 18.4 %collective-permute-start.20 = (bf16[512,256]{1,0:T(8,128)(2,1)S(1)}, bf16[512,256]{1,0:T(8,128)(2,1)}, u32[]{:S(2)}, u32[]{:S(2)}) collective-permute-start(bf16[512,256]{1,0:T(8,128)(2,1)S(1)} %shard_map.104.refs_0_), channel_id=1, source_target_pairs={{0,16},{8,24},{16,0},{24,8},{1,17},{9,25},{17,1},{25,9},{2,18},{10... | collective-permute-start | bytes 786440 | tf_op jit(solution)/shard_map/ppermute | solution.py:309
  117.4 12.5 %collective-permute-start.21 = (bf16[512,256]{1,0:T(8,128)(2,1)}, bf16[512,256]{1,0:T(8,128)(2,1)}, u32[]{:S(2)}, u32[]{:S(2)}) collective-permute-start(bf16[512,256]{1,0:T(8,128)(2,1)} %shard_map.105.refs_1_), channel_id=1, source_target_pairs={{0,16},{8,24},{16,0},{24,8},{1,17},{9,25},{17,1},{25,9},{2,18},{10... | collective-permute-start | bytes 786440 | tf_op jit(solution)/shard_map/ppermute | solution.py:309
  132.5 11.3 %collective-permute-start.25 = (bf16[256,1024]{1,0:T(8,128)(2,1)}, bf16[256,1024]{1,0:T(8,128)(2,1)}, u32[]{:S(2)}, u32[]{:S(2)}) collective-permute-start(bf16[256,1024]{1,0:T(8,128)(2,1)} %shard_map.107), channel_id=1, source_target_pairs={{0,1},{1,0},{2,3},{3,2},{4,5},{5,4},{6,7},{7,6},{8,9},{9,8},{10,11... | collective-permute-start | bytes 1572872 | tf_op jit(solution)/shard_map/ppermute | solution.py:402
  139.4 13.9 %collective-permute-start.28 = (bf16[1024,256]{1,0:T(8,128)(2,1)}, bf16[1024,256]{1,0:T(8,128)(2,1)}, u32[]{:S(2)}, u32[]{:S(2)}) collective-permute-start(bf16[1024,256]{1,0:T(8,128)(2,1)} %slice.22), channel_id=1, source_target_pairs={{0,2},{2,0},{4,6},{6,4},{1,3},{3,1},{5,7},{7,5},{8,10},{10,8},{12,... | collective-permute-start | bytes 1572872 | tf_op jit(solution)/shard_map/ppermute | solution.py:296
  140.7 13.6 %collective-permute-start.29 = (bf16[1024,256]{1,0:T(8,128)(2,1)}, bf16[1024,256]{1,0:T(8,128)(2,1)}, u32[]{:S(2)}, u32[]{:S(2)}) collective-permute-start(bf16[1024,256]{1,0:T(8,128)(2,1)} %slice.23), channel_id=1, source_target_pairs={{0,4},{2,6},{4,0},{6,2},{1,5},{3,7},{5,1},{7,3},{8,12},{10,14},{12... | collective-permute-start | bytes 1572872 | tf_op jit(solution)/shard_map/ppermute | solution.py:296
  145.7 12.7 %collective-permute-start.26 = (bf16[128,1024]{1,0:T(8,128)(2,1)}, bf16[128,1024]{1,0:T(8,128)(2,1)}, u32[]{:S(2)}, u32[]{:S(2)}) collective-permute-start(bf16[128,1024]{1,0:T(8,128)(2,1)} %add_convert_fusion.4), channel_id=1, source_target_pairs={{0,8},{8,0},{16,24},{24,16},{1,9},{9,1},{17,25},{25,17},{2,10},{10... | collective-permute-start | bytes 786440 | tf_op jit(solution)/shard_map/ppermute | solution.py:309
  162.4 10.8 %collective-permute-start.31 = (bf16[128,1024]{1,0:T(8,128)(2,1)S(1)}, bf16[128,1024]{1,0:T(8,128)(2,1)S(1)}, u32[]{:S(2)}, u32[]{:S(2)}) collective-permute-start(bf16[128,1024]{1,0:T(8,128)(2,1)S(1)} %add_convert_fusion.1), channel_id=1, source_target_pairs={{0,8},{8,0},{16,24},{24,16},{1,9},{9,1},{17,25},{25,17},{2,10},{10... | collective-permute-start | bytes 786440 | tf_op jit(solution)/shard_map/ppermute | solution.py:309
  162.5 14.5 %collective-permute-start.27 = (bf16[128,1024]{1,0:T(8,128)(2,1)S(1)}, bf16[128,1024]{1,0:T(8,128)(2,1)S(1)}, u32[]{:S(2)}, u32[]{:S(2)}) collective-permute-start(bf16[128,1024]{1,0:T(8,128)(2,1)S(1)} %add_convert_fusion.3), channel_id=1, source_target_pairs={{0,0},{1,16},{8,8},{9,24},{16,1},{17,17},{24,9},{25,25},{2,2},{3,1... | collective-permute-start | bytes 786440 | tf_op jit(solution)/shard_map/ppermute | solution.py:411
  174.3 11.4 %collective-permute-start.32 = (bf16[128,1024]{1,0:T(8,128)(2,1)S(1)}, bf16[128,1024]{1,0:T(8,128)(2,1)S(1)}, u32[]{:S(2)}, u32[]{:S(2)}) collective-permute-start(bf16[128,1024]{1,0:T(8,128)(2,1)S(1)} %add_convert_fusion), channel_id=1, source_target_pairs={{0,0},{1,16},{8,8},{9,24},{16,1},{17,17},{24,9},{25,25},{2,2},{3,1... | collective-permute-start | bytes 786440 | tf_op jit(solution)/shard_map/ppermute | solution.py:411
  (35 other events, 263.6 us)

commit v13 on v12

--- a/solution.py
+++ b/solution.py
@@ -334,11 +334,6 @@
         came = along(after(columns_for(1 - which, sources, width), *earlier), 1)
         return jnp.concatenate([columns_for(which, sources, width), came], axis=0)
 
-    pair_both = exchanged((w_key, w_value), HD)
-    pair_weight = corner(sides(pair_both))
-    query_both = exchanged((w_query,), heads, pair_both)
-    query_sides = sides(after(query_both, *pair_weight[3:]))
-
     normed = normalised(tokens, norm_gain)
     own = lax.dynamic_slice_in_dim(normed, which_half * depth, depth, 1)
 
@@ -351,6 +346,11 @@
     token_parts = [own, halves, lax.ppermute(halves, "head", [(0, 1), (1, 0)])]
     index = jnp.stack([hi, lo, core])
 
+    pair_both = exchanged((w_key, w_value), HD)
+    pair_weight = corner(sides(pair_both))
+    query_both = exchanged((w_query,), heads, pair_both, near)
+    query_sides = sides(after(query_both, *pair_weight[3:]))
+
     row_index = jnp.arange(4 * rows, dtype=jnp.int32)
     cosine, sine = rotary_tables((row_index // rows * 4 + lo) * rows + row_index % rows)
 
@@ -374,15 +374,17 @@
     firsts = jnp.stack([lo, lo, lo ^ 1, lo ^ 2, lo ^ 3]) * rows
     seen = jnp.concatenate([firsts, doc_starts])
     out_sides = sides(after(out_both, *kv_parts[1:]))
-    products = [product(index, token_parts, query_weight, c, 2) for c in range(2)]
-    products[0] = (after(products[0][0], products[1][0]), products[0][1])
-    attended = [
-        attention(seen, cosine, sine, [kept, along(sent, 2)], kv_parts, 4, 4 * rows)
-        for kept, sent in products
-    ]
-    out_blocks = corner_after(out_sides, *attended)
+    one = product(index, token_parts, query_weight, 0, 2)
+    two = product(index, token_parts, [after(query_weight[0], *one), *query_weight[1:]], 1, 2)
+    attended = []
+    for kept, sent in ((after(one[0], two[0]), one[1]), two):
+        query_parts = [after(kept, *attended[1:]), along(sent, 2)]
+        attended.append(attention(seen, cosine, sine, query_parts, kv_parts, 4, 4 * rows))
+        attended.append(along(attended[-1], 2))
+    attended = [attended[0], attended[2], attended[1], attended[3]]
+    out_blocks = corner_after(out_sides, *attended[:2])
     out_blocks[3:] = [jnp.concatenate(out_blocks[3:], axis=0)]
-    attended += [along(chunk, 2) for chunk in attended]
+    out_blocks[0] = after(out_blocks[0], out_blocks[3])
 
     def added(one, two):
         return (one.astype(jnp.float32) + two.astype(jnp.float32)).astype(jnp.bfloat16)

time: 188 us -> 195 us (1.037)
  starting transfers between devices: 43.4 us -> 48 us
  local copies, waits for them, and re-layouts: 17.9 us -> 20.7 us
  waiting for transfers between devices: 82 us -> 84.5 us
  other arithmetic: 12.9 us -> 10.6 us
    unnamed x71 -> x101, local copies, waits for them, and re-layouts: 6.28 us -> 11.5 us
    ppermute x15, waiting for transfers between devices: 18.4 us -> 23.4 us  [beside(): return lax.ppermute(block, 'lo', [(i, i ^ r) for i in range(4)])]
    ppermute x13, starting transfers between devices: 12.7 us -> 16.6 us  [along(): return lax.ppermute(block, 'hi', [(i, i ^ d) for i in range(4)])]
    ppermute x2, starting transfers between devices: 7.38 us -> 11.2 us  [line_device(): pieces.append(lax.ppermute(summed, ('hi', 'head'), home))]
    ppermute x2, starting transfers between devices: 7.08 us -> 3.94 us  [line_device(): theirs = lax.ppermute(theirs, 'head', [(0, 1), (1, 0)])]
    ppermute x13, waiting for transfers between devices: 54.8 us -> 52.6 us  [along(): return lax.ppermute(block, 'hi', [(i, i ^ d) for i in range(4)])]
    dynamic_slice x2, local copies, waits for them, and re-layouts: 3.29 us -> 1.3 us  [columns_for(): lax.dynamic_slice_in_dim(w, (2 * z + chip) * width, width, 1)]
  transfers between devices with their start and end apart: 33 -> 33, of which waited for: 12 -> 16; matrix products, arithmetic and copies ran while one was open for 13% -> 9% of each run, Pallas kernels for 14% -> 14%
where the time goes in v13:
time: 195 us; the launch traced here: 194 us
  waiting for transfers between devices  84.5 us (43%)
  starting transfers between devices  48 us (25%)
  Pallas kernels  29.9 us (15%)
  local copies, waits for them, and re-layouts  20.7 us (11%)
  other arithmetic  10.6 us (5%)
    ppermute x13, waiting for transfers between devices, along(): return lax.ppermute(block, 'hi', [(i, i ^ d) for i in range(4)])  52.6 us
    pallas_call x11, Pallas kernels, local_kernel(): pl.pallas_call(body, in_specs=[pl.BlockSpec(memory_space=pltpu.SMEM)] + [...  29.9 us
    ppermute x15, waiting for transfers between devices, beside(): return lax.ppermute(block, 'lo', [(i, i ^ r) for i in range(4)])  23.4 us
    ppermute x13, starting transfers between devices, along(): return lax.ppermute(block, 'hi', [(i, i ^ d) for i in range(4)])  16.6 us
    ppermute x15, starting transfers between devices, beside(): return lax.ppermute(block, 'lo', [(i, i ^ r) for i in range(4)])  12.8 us
    unnamed x101, local copies, waits for them, and re-layouts  11.5 us
    ppermute x2, starting transfers between devices, line_device(): pieces.append(lax.ppermute(summed, ('hi', 'head'), home))  11.2 us
    ppermute x2, waiting for transfers between devices, line_device(): pieces.append(lax.ppermute(summed, ('hi', 'head'), home))  6.77 us
  transfers between devices with their start and end apart: 33, of which 16 were waited for; matrix products, arithmetic and copies ran while one was open for 9% of the time, Pallas kernels for 14%

profile of v13, /device:TPU:1, one launch (start us, length us, event | category | flops | bytes accessed | tf_op | source)
XLA Modules:
  0.0 194.3 jit_solution(16035741706585726223)
XLA Ops:
  1.3 2.2 %collective-permute-start.4 = (bf16[256,512]{1,0:T(8,128)(2,1)S(1)}, bf16[256,512]{1,0:T(8,128)(2,1)}, u32[]{:S(2)}, u32[]{:S(2)}) collective-permute-start(bf16[256,512]{1,0:T(8,128)(2,1)S(1)} %pad_maximum_fusion.7), channel_id=1, source_target_pairs={{0,8},{8,0},{16,24},{24,16},{1,9},{9,1},{17,25},{25,17},{2,10},{10... | collective-permute-start | bytes 786440 | tf_op jit(solution)/shard_map/ppermute | solution.py:309
  5.9 3.7 %collective-permute-done.4 = bf16[256,512]{1,0:T(8,128)(2,1)} collective-permute-done((bf16[256,512]{1,0:T(8,128)(2,1)S(1)}, bf16[256,512]{1,0:T(8,128)(2,1)}, u32[]{:S(2)}, u32[]{:S(2)}) %collective-permute-start.4) | collective-permute-done | bytes 262176 | tf_op jit(solution)/shard_map/ppermute | solution.py:309
  13.0 2.2 %collective-permute-done = bf16[128,1024]{1,0:T(8,128)(2,1)} collective-permute-done((bf16[128,1024]{1,0:T(8,128)(2,1)S(1)}, bf16[128,1024]{1,0:T(8,128)(2,1)}, u32[]{:S(2)}, u32[]{:S(2)}) %collective-permute-start) | collective-permute-done | bytes 262176 | tf_op jit(solution)/shard_map/ppermute | solution.py:309
  16.3 2.3 %collective-permute-start.1 = (bf16[128,1024]{1,0:T(8,128)(2,1)}, bf16[128,1024]{1,0:T(8,128)(2,1)}, u32[]{:S(2)}, u32[]{:S(2)}) collective-permute-start(bf16[128,1024]{1,0:T(8,128)(2,1)} %get-tuple-element.59), channel_id=1, source_target_pairs={{0,16},{8,24},{16,0},{24,8},{1,17},{9,25},{17,1},{25,9},{2,18},{10... | collective-permute-start | bytes 786440 | tf_op jit(solution)/shard_map/ppermute | solution.py:309
  18.7 3.5 %collective-permute-done.6.refs_5_ = bf16[512,512]{1,0:T(8,128)(2,1)S(1)} collective-permute-done((bf16[512,512]{1,0:T(8,128)(2,1)S(1)}, bf16[512,512]{1,0:T(8,128)(2,1)S(1)}, u32[]{:S(2)}, u32[]{:S(2)}) %collective-permute-start.6) | collective-permute-done | bytes 524320 | tf_op jit(solution)/shard_map/ppermute | solution.py:296
  25.5 6.3 %collective-permute-done.1 = bf16[128,1024]{1,0:T(8,128)(2,1)} collective-permute-done((bf16[128,1024]{1,0:T(8,128)(2,1)}, bf16[128,1024]{1,0:T(8,128)(2,1)}, u32[]{:S(2)}, u32[]{:S(2)}) %collective-permute-start.1) | collective-permute-done | bytes 262176 | tf_op jit(solution)/shard_map/ppermute | solution.py:309
  31.7 3.2 %collective-permute-start.2 = (bf16[128,1024]{1,0:T(8,128)(2,1)}, bf16[128,1024]{1,0:T(8,128)(2,1)S(1)}, u32[]{:S(2)}, u32[]{:S(2)}) collective-permute-start(bf16[128,1024]{1,0:T(8,128)(2,1)} %collective-permute-done.1), channel_id=1, source_target_pairs={{0,8},{8,0},{16,24},{24,16},{1,9},{9,1},{17,25},{25,17},{2,10},{10... | collective-permute-start | bytes 786440 | tf_op jit(solution)/shard_map/ppermute | solution.py:309
  40.8 3.4 %collective-permute-start.3 = (bf16[384,1024]{1,0:T(8,128)(2,1)S(1)}, bf16[384,1024]{1,0:T(8,128)(2,1)S(1)}, u32[]{:S(2)}, u32[]{:S(2)}) collective-permute-start(bf16[384,1024]{1,0:T(8,128)(2,1)S(1)} %constant_dynamic-update-slice_fusion.refs_1_), channel_id=1, source_target_pairs={{0,1},{1,0},{2,3},{3,2},{4,5},{5,4},{6,7},{7,6},{8,9},{9,8},{10,11... | collective-permute-start | bytes 2359304 | tf_op jit(solution)/shard_map/ppermute | solution.py:346
  44.4 1.7 collective-permute-done.3.refs_2_
  46.1 2.6 %shard_map.100 = (bf16[512,256]{1,0:T(8,128)(2,1)S(1)}, bf16[512,256]{1,0:T(8,128)(2,1)}) custom-call(s32[5]{0:T(128)S(1)} %get-tuple-element.72.place_ref, bf16[128,2048]{1,0:T(8,128)(2,1)S(1)} %constant_dynamic-slice_fusion.18.refs_0_, bf16[384,1024]{1,0:T(8,128)(2,1)S(1)} %constant_dynamic-update-slice_fusion.refs_1_, ...), custom_call_target="tpu_custom_call" | custom-call | flops 1073741824 | bytes 4194324 | tf_op jit(solution)/shard_map/pallas_call | solution.py:18
  49.4 9.8 %collective-permute-done.10.refs_4_ = bf16[512,1024]{1,0:T(8,128)(2,1)S(1)} collective-permute-done((bf16[512,1024]{1,0:T(8,128)(2,1)S(1)}, bf16[512,1024]{1,0:T(8,128)(2,1)S(1)}, u32[]{:S(2)}, u32[]{:S(2)}) %collective-permute-start.10) | collective-permute-done | bytes 1048608 | tf_op jit(solution)/shard_map/ppermute | solution.py:296
  66.6 11.9 %collective-permute-done.15.refs_1_ = bf16[512,256]{1,0:T(8,128)(2,1)} collective-permute-done((bf16[512,256]{1,0:T(8,128)(2,1)}, bf16[512,256]{1,0:T(8,128)(2,1)}, u32[]{:S(2)}, u32[]{:S(2)}) %collective-permute-start.15) | collective-permute-done | bytes 262176 | tf_op jit(solution)/shard_map/ppermute | solution.py:309
  85.6 2.6 %shard_map.101 = (bf16[512,256]{1,0:T(8,128)(2,1)S(1)}, bf16[512,256]{1,0:T(8,128)(2,1)S(1)}) custom-call(s32[5]{0:T(128)S(1)} %get-tuple-element.73.place_ref, bf16[128,2048]{1,0:T(8,128)(2,1)S(1)} %constant_dynamic-slice_fusion.18.refs_0_, bf16[384,1024]{1,0:T(8,128)(2,1)S(1)} %constant_dynamic-update-slice_fusion.refs_1_, ...), custom_call_target="tpu_custom_call" | custom-call | flops 1073741824 | bytes 6291476 | tf_op jit(solution)/shard_map/pallas_call | solution.py:18
  88.4 1.4 collective-permute-start.22
  89.8 2.6 %shard_map.102 = (bf16[512,256]{1,0:T(8,128)(2,1)S(1)}, bf16[512,256]{1,0:T(8,128)(2,1)S(1)}) custom-call(s32[5]{0:T(128)S(1)} %get-tuple-element.49.place_ref, bf16[128,2048]{1,0:T(8,128)(2,1)S(1)} %constant_dynamic-slice_fusion.18.refs_0_, bf16[384,1024]{1,0:T(8,128)(2,1)S(1)} %constant_dynamic-update-slice_fusion.refs_1_, ...), custom_call_target="tpu_custom_call" | custom-call | flops 1073741824 | bytes 6291476 | tf_op jit(solution)/shard_map/pallas_call | solution.py:18
  92.5 7.8 %collective-permute-done.14.refs_1_ = bf16[512,256]{1,0:T(8,128)(2,1)S(1)} collective-permute-done((bf16[512,256]{1,0:T(8,128)(2,1)S(1)}, bf16[512,256]{1,0:T(8,128)(2,1)S(1)}, u32[]{:S(2)}, u32[]{:S(2)}) %collective-permute-start.14) | collective-permute-done | bytes 262176 | tf_op jit(solution)/shard_map/ppermute | solution.py:309
  100.3 6.5 %shard_map.104.refs_0_ = bf16[512,256]{1,0:T(8,128)(2,1)S(1)} custom-call(s32[21]{0:T(128)S(1)} %pad_add_fusion.2.place_ref, f32[512,128]{1,0:T(8,128)S(1)} %get-tuple-element.74.cos_ref, f32[512,128]{1,0:T(8,128)S(1)} %copy-done.30, bf16[512,256]{1,0:T(8,128)(2,1)S(1)} %get-tuple-element.37.refs_0_, bf16[512,256]{1,0:T(8,128)(2,1)S(1)} %collective-permute-done.14.refs_1_, ...), custom_call_target="tpu_custom_call" | custom-call | flops 8589934592 | bytes 2097236 | tf_op jit(solution)/shard_map/pallas_call | solution.py:18
  106.8 2.4 %collective-permute-start.19 = (bf16[512,256]{1,0:T(8,128)(2,1)S(1)}, bf16[512,256]{1,0:T(8,128)(2,1)S(1)}, u32[]{:S(2)}, u32[]{:S(2)}) collective-permute-start(bf16[512,256]{1,0:T(8,128)(2,1)S(1)} %shard_map.104.refs_0_), channel_id=1, source_target_pairs={{0,16},{8,24},{16,0},{24,8},{1,17},{9,25},{17,1},{25,9},{2,18},{10... | collective-permute-start | bytes 786440 | tf_op jit(solution)/shard_map/ppermute | solution.py:309
  109.3 1.3 collective-permute-start.23
  110.9 13.9 %collective-permute-done.19.refs_2_ = bf16[512,256]{1,0:T(8,128)(2,1)S(1)} collective-permute-done((bf16[512,256]{1,0:T(8,128)(2,1)S(1)}, bf16[512,256]{1,0:T(8,128)(2,1)S(1)}, u32[]{:S(2)}, u32[]{:S(2)}) %collective-permute-start.19) | collective-permute-done | bytes 262176 | tf_op jit(solution)/shard_map/ppermute | solution.py:309
  124.8 6.3 %shard_map.105.refs_1_ = bf16[512,256]{1,0:T(8,128)(2,1)S(1)} custom-call(s32[21]{0:T(128)S(1)} %pad_add_fusion.2.place_ref, f32[512,128]{1,0:T(8,128)S(1)} %copy-done.28, f32[512,128]{1,0:T(8,128)S(1)} %copy-done.30, bf16[512,256]{1,0:T(8,128)(2,1)S(1)} %get-tuple-element.40.refs_0_, bf16[512,256]{1,0:T(8,128)(2,1)S(1)} %collective-permute-done.20.refs_1_, ...), custom_call_target="tpu_custom_call" | custom-call | flops 8589934592 | bytes 2097236 | tf_op jit(solution)/shard_map/pallas_call | solution.py:18
  134.7 8.1 %collective-permute-done.25 = bf16[1024,256]{1,0:T(8,128)(2,1)} collective-permute-done((bf16[1024,256]{1,0:T(8,128)(2,1)}, bf16[1024,256]{1,0:T(8,128)(2,1)}, u32[]{:S(2)}, u32[]{:S(2)}) %collective-permute-start.25) | collective-permute-done | bytes 524320 | tf_op jit(solution)/shard_map/ppermute | solution.py:296
  147.3 2.1 %shard_map.107 = bf16[256,1024]{1,0:T(8,128)(2,1)} custom-call(s32[2]{0:T(128)S(1)} %pad_add_fusion.7.place_ref, bf16[512,256]{1,0:T(8,128)(2,1)S(1)} %shard_map.104.refs_0_, bf16[512,256]{1,0:T(8,128)(2,1)S(1)} %copy-done.14, bf16[512,256]{1,0:T(8,128)(2,1)S(1)} %copy-done.9, bf16[512,256]{1,0:T(8,128)(2,1)S(1)} %collective-permute-done.21.refs_3_, ...), custom_call_target="tpu_custom_call" | custom-call | flops 536870912 | bytes 3145736 | tf_op jit(solution)/shard_map/pallas_call | solution.py:18
  149.3 3.7 %collective-permute-start.27 = (bf16[256,1024]{1,0:T(8,128)(2,1)}, bf16[256,1024]{1,0:T(8,128)(2,1)}, u32[]{:S(2)}, u32[]{:S(2)}) collective-permute-start(bf16[256,1024]{1,0:T(8,128)(2,1)} %shard_map.107), channel_id=1, source_target_pairs={{0,1},{1,0},{2,3},{3,2},{4,5},{5,4},{6,7},{7,6},{8,9},{9,8},{10,11... | collective-permute-start | bytes 1572872 | tf_op jit(solution)/shard_map/ppermute | solution.py:404
  157.2 1.9 add_convert_fusion.4
  159.1 1.8 collective-permute-start.28
  160.9 2.1 %shard_map.109 = bf16[256,1024]{1,0:T(8,128)(2,1)} custom-call(s32[2]{0:T(128)S(1)} %pad_add_fusion.7.place_ref, bf16[512,256]{1,0:T(8,128)(2,1)S(1)} %shard_map.104.refs_0_, bf16[512,256]{1,0:T(8,128)(2,1)S(1)} %copy-done.15, bf16[512,256]{1,0:T(8,128)(2,1)S(1)} %copy-done.11, bf16[512,256]{1,0:T(8,128)(2,1)S(1)} %copy-done.18, ...), custom_call_target="tpu_custom_call" | custom-call | flops 536870912 | bytes 3145736 | tf_op jit(solution)/shard_map/pallas_call | solution.py:18
  163.3 4.5 %collective-permute-done.28 = bf16[128,1024]{1,0:T(8,128)(2,1)S(1)} collective-permute-done((bf16[128,1024]{1,0:T(8,128)(2,1)}, bf16[128,1024]{1,0:T(8,128)(2,1)S(1)}, u32[]{:S(2)}, u32[]{:S(2)}) %collective-permute-start.28) | collective-permute-done | bytes 262176 | tf_op jit(solution)/shard_map/ppermute | solution.py:309
  172.6 4.9 %collective-permute-start.29 = (bf16[128,1024]{1,0:T(8,128)(2,1)S(1)}, bf16[128,1024]{1,0:T(8,128)(2,1)S(1)}, u32[]{:S(2)}, u32[]{:S(2)}) collective-permute-start(bf16[128,1024]{1,0:T(8,128)(2,1)S(1)} %add_convert_fusion.3), channel_id=1, source_target_pairs={{0,0},{1,16},{8,8},{9,24},{16,1},{17,17},{24,9},{25,25},{2,2},{3,1... | collective-permute-start | bytes 786440 | tf_op jit(solution)/shard_map/ppermute | solution.py:413
  179.7 6.3 %collective-permute-start.32 = (bf16[128,1024]{1,0:T(8,128)(2,1)S(1)}, bf16[128,1024]{1,0:T(8,128)(2,1)S(1)}, u32[]{:S(2)}, u32[]{:S(2)}) collective-permute-start(bf16[128,1024]{1,0:T(8,128)(2,1)S(1)} %add_convert_fusion), channel_id=1, source_target_pairs={{0,0},{1,16},{8,8},{9,24},{16,1},{17,17},{24,9},{25,25},{2,2},{3,1... | collective-permute-start | bytes 786440 | tf_op jit(solution)/shard_map/ppermute | solution.py:413
  186.1 6.8 %collective-permute-done.32.refs_1_ = bf16[128,1024]{1,0:T(8,128)(2,1)S(1)} collective-permute-done((bf16[128,1024]{1,0:T(8,128)(2,1)S(1)}, bf16[128,1024]{1,0:T(8,128)(2,1)S(1)}, u32[]{:S(2)}, u32[]{:S(2)}) %collective-permute-start.32) | collective-permute-done | bytes 262176 | tf_op jit(solution)/shard_map/ppermute | solution.py:413
  192.9 1.4 shard_map.110
  (184 shorter events, 52.6 us)
Async XLA Ops:
  1.3 8.3 %collective-permute-start.4 = (bf16[256,512]{1,0:T(8,128)(2,1)S(1)}, bf16[256,512]{1,0:T(8,128)(2,1)}, u32[]{:S(2)}, u32[]{:S(2)}) collective-permute-start(bf16[256,512]{1,0:T(8,128)(2,1)S(1)} %pad_maximum_fusion.7), channel_id=1, source_target_pairs={{0,8},{8,0},{16,24},{24,16},{1,9},{9,1},{17,25},{25,17},{2,10},{10... | collective-permute-start | bytes 786440 | tf_op jit(solution)/shard_map/ppermute | solution.py:309
  4.9 10.3 %collective-permute-start = (bf16[128,1024]{1,0:T(8,128)(2,1)S(1)}, bf16[128,1024]{1,0:T(8,128)(2,1)}, u32[]{:S(2)}, u32[]{:S(2)}) collective-permute-start(bf16[128,1024]{1,0:T(8,128)(2,1)S(1)} %get-tuple-element.60), channel_id=1, source_target_pairs={{0,8},{8,0},{16,24},{24,16},{1,9},{9,1},{17,25},{25,17},{2,10},{10... | collective-permute-start | bytes 786440 | tf_op jit(solution)/shard_map/ppermute | solution.py:309
  10.6 11.5 %collective-permute-start.6 = (bf16[512,512]{1,0:T(8,128)(2,1)S(1)}, bf16[512,512]{1,0:T(8,128)(2,1)S(1)}, u32[]{:S(2)}, u32[]{:S(2)}) collective-permute-start(bf16[512,512]{1,0:T(8,128)(2,1)S(1)} %pad_maximum_fusion.3.refs_3_), channel_id=1, source_target_pairs={{0,4},{2,6},{4,0},{6,2},{1,5},{3,7},{5,1},{7,3},{8,12},{10,14},{12... | collective-permute-start | bytes 1572872 | tf_op jit(solution)/shard_map/ppermute | solution.py:296
  11.8 11.6 %collective-permute-start.8 = (bf16[512,512]{1,0:T(8,128)(2,1)S(1)}, bf16[512,512]{1,0:T(8,128)(2,1)S(1)}, u32[]{:S(2)}, u32[]{:S(2)}) collective-permute-start(bf16[512,512]{1,0:T(8,128)(2,1)S(1)} %pad_maximum_fusion.3.refs_3_), channel_id=1, source_target_pairs={{0,2},{2,0},{4,6},{6,4},{1,3},{3,1},{5,7},{7,5},{8,10},{10,8},{12,... | collective-permute-start | bytes 1572872 | tf_op jit(solution)/shard_map/ppermute | solution.py:296
  15.2 20.7 %collective-permute-start.5 = (bf16[256,1024]{1,0:T(8,128)(2,1)S(1)}, bf16[256,1024]{1,0:T(8,128)(2,1)}, u32[]{:S(2)}, u32[]{:S(2)}) collective-permute-start(bf16[256,1024]{1,0:T(8,128)(2,1)S(1)} %pad_maximum_fusion.2), channel_id=1, source_target_pairs={{0,8},{8,0},{16,24},{24,16},{1,9},{9,1},{17,25},{25,17},{2,10},{10... | collective-permute-start | bytes 1572872 | tf_op jit(solution)/shard_map/ppermute | solution.py:309
  16.3 15.4 %collective-permute-start.1 = (bf16[128,1024]{1,0:T(8,128)(2,1)}, bf16[128,1024]{1,0:T(8,128)(2,1)}, u32[]{:S(2)}, u32[]{:S(2)}) collective-permute-start(bf16[128,1024]{1,0:T(8,128)(2,1)} %get-tuple-element.59), channel_id=1, source_target_pairs={{0,16},{8,24},{16,0},{24,8},{1,17},{9,25},{17,1},{25,9},{2,18},{10... | collective-permute-start | bytes 786440 | tf_op jit(solution)/shard_map/ppermute | solution.py:309
  22.9 14.3 %collective-permute-start.7 = (bf16[256,512]{1,0:T(8,128)(2,1)}, bf16[256,512]{1,0:T(8,128)(2,1)S(1)}, u32[]{:S(2)}, u32[]{:S(2)}) collective-permute-start(bf16[256,512]{1,0:T(8,128)(2,1)} %slice.24), channel_id=1, source_target_pairs={{0,2},{2,0},{4,6},{6,4},{1,3},{3,1},{5,7},{7,5},{8,10},{10,8},{12,... | collective-permute-start | bytes 786440 | tf_op jit(solution)/shard_map/ppermute | solution.py:296
  24.2 13.0 %collective-permute-start.9 = (bf16[256,512]{1,0:T(8,128)(2,1)}, bf16[256,512]{1,0:T(8,128)(2,1)S(1)}, u32[]{:S(2)}, u32[]{:S(2)}) collective-permute-start(bf16[256,512]{1,0:T(8,128)(2,1)} %slice.25), channel_id=1, source_target_pairs={{0,4},{2,6},{4,0},{6,2},{1,5},{3,7},{5,1},{7,3},{8,12},{10,14},{12... | collective-permute-start | bytes 786440 | tf_op jit(solution)/shard_map/ppermute | solution.py:296
  31.7 9.0 %collective-permute-start.2 = (bf16[128,1024]{1,0:T(8,128)(2,1)}, bf16[128,1024]{1,0:T(8,128)(2,1)S(1)}, u32[]{:S(2)}, u32[]{:S(2)}) collective-permute-start(bf16[128,1024]{1,0:T(8,128)(2,1)} %collective-permute-done.1), channel_id=1, source_target_pairs={{0,8},{8,0},{16,24},{24,16},{1,9},{9,1},{17,25},{25,17},{2,10},{10... | collective-permute-start | bytes 786440 | tf_op jit(solution)/shard_map/ppermute | solution.py:309
  37.3 22.0 %collective-permute-start.10 = (bf16[512,1024]{1,0:T(8,128)(2,1)S(1)}, bf16[512,1024]{1,0:T(8,128)(2,1)S(1)}, u32[]{:S(2)}, u32[]{:S(2)}) collective-permute-start(bf16[512,1024]{1,0:T(8,128)(2,1)S(1)} %pad_maximum_fusion.refs_3_), channel_id=1, source_target_pairs={{0,2},{2,0},{4,6},{6,4},{1,3},{3,1},{5,7},{7,5},{8,10},{10,8},{12,... | collective-permute-start | bytes 3145736 | tf_op jit(solution)/shard_map/ppermute | solution.py:296
  38.6 21.6 %collective-permute-start.11 = (bf16[512,1024]{1,0:T(8,128)(2,1)S(1)}, bf16[512,1024]{1,0:T(8,128)(2,1)S(1)}, u32[]{:S(2)}, u32[]{:S(2)}) collective-permute-start(bf16[512,1024]{1,0:T(8,128)(2,1)S(1)} %pad_maximum_fusion.refs_3_), channel_id=1, source_target_pairs={{0,4},{2,6},{4,0},{6,2},{1,5},{3,7},{5,1},{7,3},{8,12},{10,14},{12... | collective-permute-start | bytes 3145736 | tf_op jit(solution)/shard_map/ppermute | solution.py:296
  61.1 20.5 %collective-permute-start.12 = (bf16[256,1024]{1,0:T(8,128)(2,1)}, bf16[256,1024]{1,0:T(8,128)(2,1)}, u32[]{:S(2)}, u32[]{:S(2)}) collective-permute-start(bf16[256,1024]{1,0:T(8,128)(2,1)} %slice.20), channel_id=1, source_target_pairs={{0,2},{2,0},{4,6},{6,4},{1,3},{3,1},{5,7},{7,5},{8,10},{10,8},{12,... | collective-permute-start | bytes 1572872 | tf_op jit(solution)/shard_map/ppermute | solution.py:296
  62.2 19.4 %collective-permute-start.13 = (bf16[256,1024]{1,0:T(8,128)(2,1)}, bf16[256,1024]{1,0:T(8,128)(2,1)}, u32[]{:S(2)}, u32[]{:S(2)}) collective-permute-start(bf16[256,1024]{1,0:T(8,128)(2,1)} %slice.21), channel_id=1, source_target_pairs={{0,4},{2,6},{4,0},{6,2},{1,5},{3,7},{5,1},{7,3},{8,12},{10,14},{12... | collective-permute-start | bytes 1572872 | tf_op jit(solution)/shard_map/ppermute | solution.py:296
  65.5 13.1 %collective-permute-start.15 = (bf16[512,256]{1,0:T(8,128)(2,1)}, bf16[512,256]{1,0:T(8,128)(2,1)}, u32[]{:S(2)}, u32[]{:S(2)}) collective-permute-start(bf16[512,256]{1,0:T(8,128)(2,1)} %get-tuple-element.30), channel_id=1, source_target_pairs={{0,16},{8,24},{16,0},{24,8},{1,17},{9,25},{17,1},{25,9},{2,18},{10... | collective-permute-start | bytes 786440 | tf_op jit(solution)/shard_map/ppermute | solution.py:309
  81.6 18.6 %collective-permute-start.16 = (bf16[512,256]{1,0:T(8,128)(2,1)S(1)}, bf16[512,256]{1,0:T(8,128)(2,1)S(1)}, u32[]{:S(2)}, u32[]{:S(2)}) collective-permute-start(bf16[512,256]{1,0:T(8,128)(2,1)S(1)} %shard_map.103.refs_2_), channel_id=1, source_target_pairs={{0,2},{2,0},{4,6},{6,4},{1,3},{3,1},{5,7},{7,5},{8,10},{10,8},{12,... | collective-permute-start | bytes 786440 | tf_op jit(solution)/shard_map/ppermute | solution.py:296
  82.9 17.4 %collective-permute-start.17 = (bf16[512,256]{1,0:T(8,128)(2,1)S(1)}, bf16[512,256]{1,0:T(8,128)(2,1)S(1)}, u32[]{:S(2)}, u32[]{:S(2)}) collective-permute-start(bf16[512,256]{1,0:T(8,128)(2,1)S(1)} %shard_map.103.refs_2_), channel_id=1, source_target_pairs={{0,4},{2,6},{4,0},{6,2},{1,5},{3,7},{5,1},{7,3},{8,12},{10,14},{12... | collective-permute-start | bytes 786440 | tf_op jit(solution)/shard_map/ppermute | solution.py:296
  83.1 17.2 %collective-permute-start.18 = (bf16[512,256]{1,0:T(8,128)(2,1)S(1)}, bf16[512,256]{1,0:T(8,128)(2,1)S(1)}, u32[]{:S(2)}, u32[]{:S(2)}) collective-permute-start(bf16[512,256]{1,0:T(8,128)(2,1)S(1)} %shard_map.103.refs_2_), channel_id=1, source_target_pairs={{0,6},{2,4},{4,2},{6,0},{1,7},{3,5},{5,3},{7,1},{8,14},{10,12},{12... | collective-permute-start | bytes 786440 | tf_op jit(solution)/shard_map/ppermute | solution.py:296
  88.2 12.0 %collective-permute-start.14 = (bf16[512,256]{1,0:T(8,128)(2,1)S(1)}, bf16[512,256]{1,0:T(8,128)(2,1)S(1)}, u32[]{:S(2)}, u32[]{:S(2)}) collective-permute-start(bf16[512,256]{1,0:T(8,128)(2,1)S(1)} %get-tuple-element.34), channel_id=1, source_target_pairs={{0,16},{8,24},{16,0},{24,8},{1,17},{9,25},{17,1},{25,9},{2,18},{10... | collective-permute-start | bytes 786440 | tf_op jit(solution)/shard_map/ppermute | solution.py:309
  88.4 20.8 %collective-permute-start.22 = (bf16[1024,256]{1,0:T(8,128)(2,1)S(1)}, bf16[1024,256]{1,0:T(8,128)(2,1)S(1)}, u32[]{:S(2)}, u32[]{:S(2)}) collective-permute-start(bf16[1024,256]{1,0:T(8,128)(2,1)S(1)} %pad_maximum_fusion.4), channel_id=1, source_target_pairs={{0,8},{8,0},{16,24},{24,16},{1,9},{9,1},{17,25},{25,17},{2,10},{10... | collective-permute-start | bytes 1572872 | tf_op jit(solution)/shard_map/ppermute | solution.py:309
  100.3 24.5 %collective-permute-start.20 = (bf16[512,256]{1,0:T(8,128)(2,1)S(1)}, bf16[512,256]{1,0:T(8,128)(2,1)S(1)}, u32[]{:S(2)}, u32[]{:S(2)}) collective-permute-start(bf16[512,256]{1,0:T(8,128)(2,1)S(1)} %get-tuple-element.41), channel_id=1, source_target_pairs={{0,16},{8,24},{16,0},{24,8},{1,17},{9,25},{17,1},{25,9},{2,18},{10... | collective-permute-start | bytes 786440 | tf_op jit(solution)/shard_map/ppermute | solution.py:309
  106.8 18.0 %collective-permute-start.19 = (bf16[512,256]{1,0:T(8,128)(2,1)S(1)}, bf16[512,256]{1,0:T(8,128)(2,1)S(1)}, u32[]{:S(2)}, u32[]{:S(2)}) collective-permute-start(bf16[512,256]{1,0:T(8,128)(2,1)S(1)} %shard_map.104.refs_0_), channel_id=1, source_target_pairs={{0,16},{8,24},{16,0},{24,8},{1,17},{9,25},{17,1},{25,9},{2,18},{10... | collective-permute-start | bytes 786440 | tf_op jit(solution)/shard_map/ppermute | solution.py:309
  109.3 21.8 %collective-permute-start.23 = (bf16[2048,256]{1,0:T(8,128)(2,1)S(1)}, bf16[2048,256]{1,0:T(8,128)(2,1)S(1)}, u32[]{:S(2)}, u32[]{:S(2)}) collective-permute-start(bf16[2048,256]{1,0:T(8,128)(2,1)S(1)} %pad_maximum_fusion.1.refs_4_), channel_id=1, source_target_pairs={{0,2},{2,0},{4,6},{6,4},{1,3},{3,1},{5,7},{7,5},{8,10},{10,8},{12,... | collective-permute-start | bytes 3145736 | tf_op jit(solution)/shard_map/ppermute | solution.py:296
  110.7 21.6 %collective-permute-start.24 = (bf16[2048,256]{1,0:T(8,128)(2,1)S(1)}, bf16[2048,256]{1,0:T(8,128)(2,1)S(1)}, u32[]{:S(2)}, u32[]{:S(2)}) collective-permute-start(bf16[2048,256]{1,0:T(8,128)(2,1)S(1)} %pad_maximum_fusion.1.refs_4_), channel_id=1, source_target_pairs={{0,4},{2,6},{4,0},{6,2},{1,5},{3,7},{5,1},{7,3},{8,12},{10,14},{12... | collective-permute-start | bytes 3145736 | tf_op jit(solution)/shard_map/ppermute | solution.py:296
  133.1 9.7 %collective-permute-start.25 = (bf16[1024,256]{1,0:T(8,128)(2,1)}, bf16[1024,256]{1,0:T(8,128)(2,1)}, u32[]{:S(2)}, u32[]{:S(2)}) collective-permute-start(bf16[1024,256]{1,0:T(8,128)(2,1)} %slice.22), channel_id=1, source_target_pairs={{0,2},{2,0},{4,6},{6,4},{1,3},{3,1},{5,7},{7,5},{8,10},{10,8},{12,... | collective-permute-start | bytes 1572872 | tf_op jit(solution)/shard_map/ppermute | solution.py:296
  134.2 9.7 %collective-permute-start.26 = (bf16[1024,256]{1,0:T(8,128)(2,1)}, bf16[1024,256]{1,0:T(8,128)(2,1)}, u32[]{:S(2)}, u32[]{:S(2)}) collective-permute-start(bf16[1024,256]{1,0:T(8,128)(2,1)} %slice.23), channel_id=1, source_target_pairs={{0,4},{2,6},{4,0},{6,2},{1,5},{3,7},{5,1},{7,3},{8,12},{10,14},{12... | collective-permute-start | bytes 1572872 | tf_op jit(solution)/shard_map/ppermute | solution.py:296
  134.4 12.8 %collective-permute-start.21 = (bf16[512,256]{1,0:T(8,128)(2,1)}, bf16[512,256]{1,0:T(8,128)(2,1)S(1)}, u32[]{:S(2)}, u32[]{:S(2)}) collective-permute-start(bf16[512,256]{1,0:T(8,128)(2,1)} %copy-done.13), channel_id=1, source_target_pairs={{0,16},{8,24},{16,0},{24,8},{1,17},{9,25},{17,1},{25,9},{2,18},{10... | collective-permute-start | bytes 786440 | tf_op jit(solution)/shard_map/ppermute | solution.py:309
  149.3 7.9 %collective-permute-start.27 = (bf16[256,1024]{1,0:T(8,128)(2,1)}, bf16[256,1024]{1,0:T(8,128)(2,1)}, u32[]{:S(2)}, u32[]{:S(2)}) collective-permute-start(bf16[256,1024]{1,0:T(8,128)(2,1)} %shard_map.107), channel_id=1, source_target_pairs={{0,1},{1,0},{2,3},{3,2},{4,5},{5,4},{6,7},{7,6},{8,9},{9,8},{10,11... | collective-permute-start | bytes 1572872 | tf_op jit(solution)/shard_map/ppermute | solution.py:404
  159.1 8.7 %collective-permute-start.28 = (bf16[128,1024]{1,0:T(8,128)(2,1)}, bf16[128,1024]{1,0:T(8,128)(2,1)S(1)}, u32[]{:S(2)}, u32[]{:S(2)}) collective-permute-start(bf16[128,1024]{1,0:T(8,128)(2,1)} %add_convert_fusion.4), channel_id=1, source_target_pairs={{0,8},{8,0},{16,24},{24,16},{1,9},{9,1},{17,25},{25,17},{2,10},{10... | collective-permute-start | bytes 786440 | tf_op jit(solution)/shard_map/ppermute | solution.py:309
  163.0 7.3 %collective-permute-start.30 = (bf16[256,1024]{1,0:T(8,128)(2,1)}, bf16[256,1024]{1,0:T(8,128)(2,1)}, u32[]{:S(2)}, u32[]{:S(2)}) collective-permute-start(bf16[256,1024]{1,0:T(8,128)(2,1)} %shard_map.109), channel_id=1, source_target_pairs={{0,1},{1,0},{2,3},{3,2},{4,5},{5,4},{6,7},{7,6},{8,9},{9,8},{10,11... | collective-permute-start | bytes 1572872 | tf_op jit(solution)/shard_map/ppermute | solution.py:404
  171.3 7.3 %collective-permute-start.31 = (bf16[128,1024]{1,0:T(8,128)(2,1)S(1)}, bf16[128,1024]{1,0:T(8,128)(2,1)S(1)}, u32[]{:S(2)}, u32[]{:S(2)}) collective-permute-start(bf16[128,1024]{1,0:T(8,128)(2,1)S(1)} %add_convert_fusion.1), channel_id=1, source_target_pairs={{0,8},{8,0},{16,24},{24,16},{1,9},{9,1},{17,25},{25,17},{2,10},{10... | collective-permute-start | bytes 786440 | tf_op jit(solution)/shard_map/ppermute | solution.py:309
  172.6 13.5 %collective-permute-start.29 = (bf16[128,1024]{1,0:T(8,128)(2,1)S(1)}, bf16[128,1024]{1,0:T(8,128)(2,1)S(1)}, u32[]{:S(2)}, u32[]{:S(2)}) collective-permute-start(bf16[128,1024]{1,0:T(8,128)(2,1)S(1)} %add_convert_fusion.3), channel_id=1, source_target_pairs={{0,0},{1,16},{8,8},{9,24},{16,1},{17,17},{24,9},{25,25},{2,2},{3,1... | collective-permute-start | bytes 786440 | tf_op jit(solution)/shard_map/ppermute | solution.py:413
  179.7 13.2 %collective-permute-start.32 = (bf16[128,1024]{1,0:T(8,128)(2,1)S(1)}, bf16[128,1024]{1,0:T(8,128)(2,1)S(1)}, u32[]{:S(2)}, u32[]{:S(2)}) collective-permute-start(bf16[128,1024]{1,0:T(8,128)(2,1)S(1)} %add_convert_fusion), channel_id=1, source_target_pairs={{0,0},{1,16},{8,8},{9,24},{16,1},{17,17},{24,9},{25,25},{2,2},{3,1... | collective-permute-start | bytes 786440 | tf_op jit(solution)/shard_map/ppermute | solution.py:413
  (50 other events, 299.4 us)

commit v14 on v12

--- a/solution.py
+++ b/solution.py
@@ -382,6 +382,7 @@
     ]
     out_blocks = corner_after(out_sides, *attended)
     out_blocks[3:] = [jnp.concatenate(out_blocks[3:], axis=0)]
+    out_blocks[0] = after(out_blocks[0], out_blocks[3])
     attended += [along(chunk, 2) for chunk in attended]
 
     def added(one, two):
@@ -393,12 +394,11 @@
         for chip in range(2)
         for group in range(2)
     ]
-    pieces, shares, summed = [], [], None
+    pieces, shares = [], []
     for blocks in (out_blocks[:2], out_blocks[2:]):
-        first = [after(blocks[0], *shares[1:]), *blocks[1:]]
-        theirs = project(jnp.stack([hi, 1 - core]), attended, first)
-        last = first if summed is None else [after(first[0], summed), *first[1:]]
-        mine = project(jnp.stack([hi, core]), attended, last)
+        blocks = [after(blocks[0], *shares[1:]), *blocks[1:]]
+        theirs = project(jnp.stack([hi, 1 - core]), attended, blocks)
+        mine = project(jnp.stack([hi, core]), attended, blocks)
         theirs = lax.ppermute(theirs, "head", [(0, 1), (1, 0)])
         shares = [
             added(

time: 188 us -> 178 us (0.947)
  waiting for transfers between devices: 82 us -> 77 us
  local copies, waits for them, and re-layouts: 17.9 us -> 21 us
  Pallas kernels: 30.4 us -> 27.3 us
  other arithmetic: 12.9 us -> 10 us
  starting transfers between devices: 43.4 us -> 41.3 us
    ppermute x15, waiting for transfers between devices: 18.4 us -> 13.1 us  [beside(): return lax.ppermute(block, 'lo', [(i, i ^ r) for i in range(4)])]
    ppermute x2, starting transfers between devices: 7.08 us -> 3.51 us  [line_device(): theirs = lax.ppermute(theirs, 'head', [(0, 1), (1, 0)])]
    pallas_call x11, Pallas kernels: 30.4 us -> 27.3 us  [local_kernel(): pl.pallas_call(body, in_specs=[pl.BlockSpec(memory_space=pltpu.SMEM)] + [...]
    unnamed x71 -> x85, local copies, waits for them, and re-layouts: 6.28 us -> 9.27 us
    convert_element_type x4, other arithmetic: 5.16 us -> 2.27 us  [added(): (one.astype(jnp.float32) + two.astype(jnp.float32)).astype(jnp.bfloat16)]
  transfers between devices with their start and end apart: 33 -> 33, of which waited for: 12 -> 18; matrix products, arithmetic and copies ran while one was open for 13% -> 11% of each run, Pallas kernels for 14% -> 13%
where the time goes in v14:
time: 178 us; the launch traced here: 177 us
  waiting for transfers between devices  77 us (43%)
  starting transfers between devices  41.3 us (23%)
  Pallas kernels  27.3 us (15%)
  local copies, waits for them, and re-layouts  21 us (12%)
  other arithmetic  10 us (6%)
    ppermute x13, waiting for transfers between devices, along(): return lax.ppermute(block, 'hi', [(i, i ^ d) for i in range(4)])  54.8 us
    pallas_call x11, Pallas kernels, local_kernel(): pl.pallas_call(body, in_specs=[pl.BlockSpec(memory_space=pltpu.SMEM)] + [...  27.3 us
    ppermute x13, starting transfers between devices, along(): return lax.ppermute(block, 'hi', [(i, i ^ d) for i in range(4)])  13.6 us
    ppermute x15, waiting for transfers between devices, beside(): return lax.ppermute(block, 'lo', [(i, i ^ r) for i in range(4)])  13.1 us
    ppermute x15, starting transfers between devices, beside(): return lax.ppermute(block, 'lo', [(i, i ^ r) for i in range(4)])  12.3 us
    unnamed x85, local copies, waits for them, and re-layouts  9.27 us
    ppermute x2, waiting for transfers between devices, line_device(): pieces.append(lax.ppermute(summed, ('hi', 'head'), home))  8.6 us
    ppermute x2, starting transfers between devices, line_device(): pieces.append(lax.ppermute(summed, ('hi', 'head'), home))  7.89 us
  transfers between devices with their start and end apart: 33, of which 18 were waited for; matrix products, arithmetic and copies ran while one was open for 11% of the time, Pallas kernels for 13%

profile of v14, /device:TPU:1, one launch (start us, length us, event | category | flops | bytes accessed | tf_op | source)
XLA Modules:
  0.0 177.2 jit_solution(3315733388659307793)
XLA Ops:
  1.3 2.2 %collective-permute-start.4 = (bf16[256,512]{1,0:T(8,128)(2,1)S(1)}, bf16[256,512]{1,0:T(8,128)(2,1)S(1)}, u32[]{:S(2)}, u32[]{:S(2)}) collective-permute-start(bf16[256,512]{1,0:T(8,128)(2,1)S(1)} %pad_maximum_fusion.7), channel_id=1, source_target_pairs={{0,8},{8,0},{16,24},{24,16},{1,9},{9,1},{17,25},{25,17},{2,10},{10... | collective-permute-start | bytes 786440 | tf_op jit(solution)/shard_map/ppermute | solution.py:309
  4.1 5.3 %collective-permute-done.4 = bf16[256,512]{1,0:T(8,128)(2,1)S(1)} collective-permute-done((bf16[256,512]{1,0:T(8,128)(2,1)S(1)}, bf16[256,512]{1,0:T(8,128)(2,1)S(1)}, u32[]{:S(2)}, u32[]{:S(2)}) %collective-permute-start.4) | collective-permute-done | bytes 262176 | tf_op jit(solution)/shard_map/ppermute | solution.py:309
  11.9 2.1 %constant_dynamic-slice_fusion.15 = (bf16[256,512]{1,0:T(8,128)(2,1)}, bf16[256,512]{1,0:T(8,128)(2,1)}, bf16[256,512]{1,0:T(8,128)(2,1)S(1)}, bf16[256,512]{1,0:T(8,128)(2,1)S(1)}) fusion(bf16[256,2048]{1,0:T(8,128)(2,1)} %param.12, s32[]{:T(128)S(6)} %select_n.78, s32[]{:T(128)S(6)} %select_n.79, s32[]{:T(128)S(6)} %select_n.81, s32[]{:T(128)S(6)} %select_n.80), kind=kLoop, calls=%fused_computation.42 | loop fusion | bytes 2097168 | tf_op jit(solution)/shard_map/dynamic_slice | solution.py:326
  17.1 2.3 %collective-permute-start.1 = (bf16[128,1024]{1,0:T(8,128)(2,1)S(1)}, bf16[128,1024]{1,0:T(8,128)(2,1)}, u32[]{:S(2)}, u32[]{:S(2)}) collective-permute-start(bf16[128,1024]{1,0:T(8,128)(2,1)S(1)} %get-tuple-element.53), channel_id=1, source_target_pairs={{0,16},{8,24},{16,0},{24,8},{1,17},{9,25},{17,1},{25,9},{2,18},{10... | collective-permute-start | bytes 786440 | tf_op jit(solution)/shard_map/ppermute | solution.py:309
  19.4 2.2 %constant_dynamic-slice_fusion.3 = (bf16[512,256]{1,0:T(8,128)(2,1)}, bf16[512,256]{1,0:T(8,128)(2,1)}, bf16[512,256]{1,0:T(8,128)(2,1)}, bf16[512,256]{1,0:T(8,128)(2,1)}) fusion(bf16[2048,256]{1,0:T(8,128)(2,1)} %param.15, s32[]{:T(128)S(6)} %select_n.78, s32[]{:T(128)S(6)} %select_n.79, s32[]{:T(128)S(6)} %select_n.81, s32[]{:T(128)S(6)} %select_n.80), kind=kLoop, calls=%fused_computation.30 | loop fusion | bytes 2097168 | tf_op jit(solution)/shard_map/dynamic_slice | solution.py:362
  23.5 1.3 collective-permute-start.9
  24.9 12.7 %collective-permute-done = bf16[128,1024]{1,0:T(8,128)(2,1)S(1)} collective-permute-done((bf16[128,1024]{1,0:T(8,128)(2,1)}, bf16[128,1024]{1,0:T(8,128)(2,1)S(1)}, u32[]{:S(2)}, u32[]{:S(2)}) %collective-permute-start) | collective-permute-done | bytes 262176 | tf_op jit(solution)/shard_map/ppermute | solution.py:309
  37.6 2.4 %collective-permute-start.2 = (bf16[128,1024]{1,0:T(8,128)(2,1)}, bf16[128,1024]{1,0:T(8,128)(2,1)S(1)}, u32[]{:S(2)}, u32[]{:S(2)}) collective-permute-start(bf16[128,1024]{1,0:T(8,128)(2,1)} %collective-permute-done.1), channel_id=1, source_target_pairs={{0,8},{8,0},{16,24},{24,16},{1,9},{9,1},{17,25},{25,17},{2,10},{10... | collective-permute-start | bytes 786440 | tf_op jit(solution)/shard_map/ppermute | solution.py:309
  44.0 4.0 %collective-permute-start.3 = (bf16[384,1024]{1,0:T(8,128)(2,1)S(1)}, bf16[384,1024]{1,0:T(8,128)(2,1)S(1)}, u32[]{:S(2)}, u32[]{:S(2)}) collective-permute-start(bf16[384,1024]{1,0:T(8,128)(2,1)S(1)} %constant_dynamic-update-slice_fusion.refs_1_), channel_id=1, source_target_pairs={{0,1},{1,0},{2,3},{3,2},{4,5},{5,4},{6,7},{7,6},{8,9},{9,8},{10,11... | collective-permute-start | bytes 2359304 | tf_op jit(solution)/shard_map/ppermute | solution.py:351
  48.2 2.1 %fusion.3 = (f32[512,64]{1,0:T(8,128)}, f32[512,64]{1,0:T(8,128)}, f32[512,64]{1,0:T(8,128)}) fusion(f32[64]{0:T(128)S(1)} %negate_power_fusion, f32[512]{0:T(512)S(1)} %fusion.12), kind=kLoop, calls=%fused_computation.21 | loop fusion | flops 65536 | bytes 395520 | tf_op jit(solution)/shard_map/neg | solution.py:36
  50.3 1.9 %shard_map.100 = (bf16[512,256]{1,0:T(8,128)(2,1)S(1)}, bf16[512,256]{1,0:T(8,128)(2,1)S(1)}) custom-call(s32[5]{0:T(128)S(1)} %get-tuple-element.66.place_ref, bf16[128,2048]{1,0:T(8,128)(2,1)S(1)} %constant_dynamic-slice_fusion.18.refs_0_, bf16[384,1024]{1,0:T(8,128)(2,1)S(1)} %constant_dynamic-update-slice_fusion.refs_1_, ...), custom_call_target="tpu_custom_call" | custom-call | flops 1073741824 | bytes 4194324 | tf_op jit(solution)/shard_map/pallas_call | solution.py:18
  53.6 9.2 %collective-permute-done.10.refs_4_ = bf16[512,1024]{1,0:T(8,128)(2,1)S(1)} collective-permute-done((bf16[512,1024]{1,0:T(8,128)(2,1)S(1)}, bf16[512,1024]{1,0:T(8,128)(2,1)S(1)}, u32[]{:S(2)}, u32[]{:S(2)}) %collective-permute-start.10) | collective-permute-done | bytes 1048608 | tf_op jit(solution)/shard_map/ppermute | solution.py:296
  68.2 1.5 pad_maximum_fusion.5
  69.8 7.2 %collective-permute-done.15.refs_1_ = bf16[512,256]{1,0:T(8,128)(2,1)S(1)} collective-permute-done((bf16[512,256]{1,0:T(8,128)(2,1)}, bf16[512,256]{1,0:T(8,128)(2,1)S(1)}, u32[]{:S(2)}, u32[]{:S(2)}) %collective-permute-start.15) | collective-permute-done | bytes 262176 | tf_op jit(solution)/shard_map/ppermute | solution.py:309
  79.9 2.6 %shard_map.102 = (bf16[512,256]{1,0:T(8,128)(2,1)S(1)}, bf16[512,256]{1,0:T(8,128)(2,1)S(1)}) custom-call(s32[5]{0:T(128)S(1)} %get-tuple-element.43.place_ref, bf16[128,2048]{1,0:T(8,128)(2,1)S(1)} %constant_dynamic-slice_fusion.18.refs_0_, bf16[384,1024]{1,0:T(8,128)(2,1)S(1)} %constant_dynamic-update-slice_fusion.refs_1_, ...), custom_call_target="tpu_custom_call" | custom-call | flops 1073741824 | bytes 6291476 | tf_op jit(solution)/shard_map/pallas_call | solution.py:18
  82.6 2.1 %collective-permute-done.22 = bf16[1024,256]{1,0:T(8,128)(2,1)S(1)} collective-permute-done((bf16[1024,256]{1,0:T(8,128)(2,1)}, bf16[1024,256]{1,0:T(8,128)(2,1)S(1)}, u32[]{:S(2)}, u32[]{:S(2)}) %collective-permute-start.22) | collective-permute-done | bytes 524320 | tf_op jit(solution)/shard_map/ppermute | solution.py:309
  85.8 2.6 %shard_map.101 = (bf16[512,256]{1,0:T(8,128)(2,1)S(1)}, bf16[512,256]{1,0:T(8,128)(2,1)S(1)}) custom-call(s32[5]{0:T(128)S(1)} %get-tuple-element.67.place_ref, bf16[128,2048]{1,0:T(8,128)(2,1)S(1)} %constant_dynamic-slice_fusion.18.refs_0_, bf16[384,1024]{1,0:T(8,128)(2,1)S(1)} %constant_dynamic-update-slice_fusion.refs_1_, ...), custom_call_target="tpu_custom_call" | custom-call | flops 1073741824 | bytes 6291476 | tf_op jit(solution)/shard_map/pallas_call | solution.py:18
  90.9 6.3 %shard_map.105.refs_1_ = bf16[512,256]{1,0:T(8,128)(2,1)S(1)} custom-call(s32[21]{0:T(128)S(1)} %pad_add_fusion.2.place_ref, f32[512,128]{1,0:T(8,128)S(1)} %get-tuple-element.68.cos_ref, f32[512,128]{1,0:T(8,128)S(1)} %get-tuple-element.69.sin_ref, bf16[512,256]{1,0:T(8,128)(2,1)S(1)} %get-tuple-element.31.refs_0_, ...), custom_call_target="tpu_custom_call" | custom-call | flops 8589934592 | bytes 2097236 | tf_op jit(solution)/shard_map/pallas_call | solution.py:18
  97.2 7.9 %collective-permute-done.14.refs_1_ = bf16[512,256]{1,0:T(8,128)(2,1)S(1)} collective-permute-done((bf16[512,256]{1,0:T(8,128)(2,1)S(1)}, bf16[512,256]{1,0:T(8,128)(2,1)S(1)}, u32[]{:S(2)}, u32[]{:S(2)}) %collective-permute-start.14) | collective-permute-done | bytes 262176 | tf_op jit(solution)/shard_map/ppermute | solution.py:309
  105.1 6.5 %shard_map.104.refs_0_ = bf16[512,256]{1,0:T(8,128)(2,1)S(1)} custom-call(s32[21]{0:T(128)S(1)} %pad_add_fusion.2.place_ref, f32[512,128]{1,0:T(8,128)S(1)} %get-tuple-element.68.cos_ref, f32[512,128]{1,0:T(8,128)S(1)} %get-tuple-element.69.sin_ref, bf16[512,256]{1,0:T(8,128)(2,1)S(1)} %get-tuple-element.32.refs_0_, ...), custom_call_target="tpu_custom_call" | custom-call | flops 8589934592 | bytes 2097236 | tf_op jit(solution)/shard_map/pallas_call | solution.py:18
  114.9 2.4 %collective-permute-start.21 = (bf16[512,256]{1,0:T(8,128)(2,1)S(1)}, bf16[512,256]{1,0:T(8,128)(2,1)S(1)}, u32[]{:S(2)}, u32[]{:S(2)}) collective-permute-start(bf16[512,256]{1,0:T(8,128)(2,1)S(1)} %shard_map.105.refs_1_), channel_id=1, source_target_pairs={{0,16},{8,24},{16,0},{24,8},{1,17},{9,25},{17,1},{25,9},{2,18},{10... | collective-permute-start | bytes 786440 | tf_op jit(solution)/shard_map/ppermute | solution.py:309
  117.4 3.5 %collective-permute-done.25 = bf16[1024,256]{1,0:T(8,128)(2,1)} collective-permute-done((bf16[1024,256]{1,0:T(8,128)(2,1)}, bf16[1024,256]{1,0:T(8,128)(2,1)}, u32[]{:S(2)}, u32[]{:S(2)}) %collective-permute-start.25) | collective-permute-done | bytes 524320 | tf_op jit(solution)/shard_map/ppermute | solution.py:296
  124.1 1.9 %collective-permute-done.20.refs_2_ = bf16[512,256]{1,0:T(8,128)(2,1)S(1)} collective-permute-done((bf16[512,256]{1,0:T(8,128)(2,1)}, bf16[512,256]{1,0:T(8,128)(2,1)S(1)}, u32[]{:S(2)}, u32[]{:S(2)}) %collective-permute-start.20) | collective-permute-done | bytes 262176 | tf_op jit(solution)/shard_map/ppermute | solution.py:309
  126.0 11.3 %collective-permute-done.21.refs_3_ = bf16[512,256]{1,0:T(8,128)(2,1)S(1)} collective-permute-done((bf16[512,256]{1,0:T(8,128)(2,1)S(1)}, bf16[512,256]{1,0:T(8,128)(2,1)S(1)}, u32[]{:S(2)}, u32[]{:S(2)}) %collective-permute-start.21) | collective-permute-done | bytes 262176 | tf_op jit(solution)/shard_map/ppermute | solution.py:309
  137.3 2.1 %shard_map.107 = bf16[256,1024]{1,0:T(8,128)(2,1)} custom-call(s32[2]{0:T(128)S(1)} %pad_add_fusion.7.place_ref, bf16[512,256]{1,0:T(8,128)(2,1)S(1)} %copy-done.9, bf16[512,256]{1,0:T(8,128)(2,1)S(1)} %shard_map.105.refs_1_, bf16[512,256]{1,0:T(8,128)(2,1)S(1)} %collective-permute-done.20.refs_2_, bf16[512,256]{1,0:T(8,128)(2,1)S(1)} %collective-permute-done.21.refs_3_, ...), custom_call_target="tpu_custom_call" | custom-call | flops 536870912 | bytes 3145736 | tf_op jit(solution)/shard_map/pallas_call | solution.py:18
  139.4 3.4 %collective-permute-start.27 = (bf16[256,1024]{1,0:T(8,128)(2,1)}, bf16[256,1024]{1,0:T(8,128)(2,1)}, u32[]{:S(2)}, u32[]{:S(2)}) collective-permute-start(bf16[256,1024]{1,0:T(8,128)(2,1)} %shard_map.107), channel_id=1, source_target_pairs={{0,1},{1,0},{2,3},{3,2},{4,5},{5,4},{6,7},{7,6},{8,9},{9,8},{10,11... | collective-permute-start | bytes 1572872 | tf_op jit(solution)/shard_map/ppermute | solution.py:402
  153.1 4.6 %collective-permute-done.28 = bf16[128,1024]{1,0:T(8,128)(2,1)S(1)} collective-permute-done((bf16[128,1024]{1,0:T(8,128)(2,1)S(1)}, bf16[128,1024]{1,0:T(8,128)(2,1)S(1)}, u32[]{:S(2)}, u32[]{:S(2)}) %collective-permute-start.28) | collective-permute-done | bytes 262176 | tf_op jit(solution)/shard_map/ppermute | solution.py:309
  158.8 4.2 %collective-permute-start.29 = (bf16[128,1024]{1,0:T(8,128)(2,1)S(1)}, bf16[128,1024]{1,0:T(8,128)(2,1)S(1)}, u32[]{:S(2)}, u32[]{:S(2)}) collective-permute-start(bf16[128,1024]{1,0:T(8,128)(2,1)S(1)} %add_convert_fusion.3), channel_id=1, source_target_pairs={{0,0},{1,16},{8,8},{9,24},{16,1},{17,17},{24,9},{25,25},{2,2},{3,1... | collective-permute-start | bytes 786440 | tf_op jit(solution)/shard_map/ppermute | solution.py:411
  163.4 3.7 %collective-permute-start.32 = (bf16[128,1024]{1,0:T(8,128)(2,1)S(1)}, bf16[128,1024]{1,0:T(8,128)(2,1)S(1)}, u32[]{:S(2)}, u32[]{:S(2)}) collective-permute-start(bf16[128,1024]{1,0:T(8,128)(2,1)S(1)} %add_convert_fusion), channel_id=1, source_target_pairs={{0,0},{1,16},{8,8},{9,24},{16,1},{17,17},{24,9},{25,25},{2,2},{3,1... | collective-permute-start | bytes 786440 | tf_op jit(solution)/shard_map/ppermute | solution.py:411
  167.2 3.0 %collective-permute-done.29.refs_0_ = bf16[128,1024]{1,0:T(8,128)(2,1)S(1)} collective-permute-done((bf16[128,1024]{1,0:T(8,128)(2,1)S(1)}, bf16[128,1024]{1,0:T(8,128)(2,1)S(1)}, u32[]{:S(2)}, u32[]{:S(2)}) %collective-permute-start.29) | collective-permute-done | bytes 262176 | tf_op jit(solution)/shard_map/ppermute | solution.py:411
  170.2 5.6 %collective-permute-done.32.refs_1_ = bf16[128,1024]{1,0:T(8,128)(2,1)S(1)} collective-permute-done((bf16[128,1024]{1,0:T(8,128)(2,1)S(1)}, bf16[128,1024]{1,0:T(8,128)(2,1)S(1)}, u32[]{:S(2)}, u32[]{:S(2)}) %collective-permute-start.32) | collective-permute-done | bytes 262176 | tf_op jit(solution)/shard_map/ppermute | solution.py:411
  175.8 1.4 shard_map.110
  (168 shorter events, 45.3 us)
Async XLA Ops:
  1.3 8.2 %collective-permute-start.4 = (bf16[256,512]{1,0:T(8,128)(2,1)S(1)}, bf16[256,512]{1,0:T(8,128)(2,1)S(1)}, u32[]{:S(2)}, u32[]{:S(2)}) collective-permute-start(bf16[256,512]{1,0:T(8,128)(2,1)S(1)} %pad_maximum_fusion.7), channel_id=1, source_target_pairs={{0,8},{8,0},{16,24},{24,16},{1,9},{9,1},{17,25},{25,17},{2,10},{10... | collective-permute-start | bytes 786440 | tf_op jit(solution)/shard_map/ppermute | solution.py:309
  9.5 12.4 %collective-permute-start.6 = (bf16[512,512]{1,0:T(8,128)(2,1)S(1)}, bf16[512,512]{1,0:T(8,128)(2,1)S(1)}, u32[]{:S(2)}, u32[]{:S(2)}) collective-permute-start(bf16[512,512]{1,0:T(8,128)(2,1)S(1)} %pad_maximum_fusion.3.refs_3_), channel_id=1, source_target_pairs={{0,4},{2,6},{4,0},{6,2},{1,5},{3,7},{5,1},{7,3},{8,12},{10,14},{12... | collective-permute-start | bytes 1572872 | tf_op jit(solution)/shard_map/ppermute | solution.py:296
  10.7 12.8 %collective-permute-start.8 = (bf16[512,512]{1,0:T(8,128)(2,1)S(1)}, bf16[512,512]{1,0:T(8,128)(2,1)S(1)}, u32[]{:S(2)}, u32[]{:S(2)}) collective-permute-start(bf16[512,512]{1,0:T(8,128)(2,1)S(1)} %pad_maximum_fusion.3.refs_3_), channel_id=1, source_target_pairs={{0,2},{2,0},{4,6},{6,4},{1,3},{3,1},{5,7},{7,5},{8,10},{10,8},{12,... | collective-permute-start | bytes 1572872 | tf_op jit(solution)/shard_map/ppermute | solution.py:296
  14.8 25.2 %collective-permute-start.5 = (bf16[256,1024]{1,0:T(8,128)(2,1)}, bf16[256,1024]{1,0:T(8,128)(2,1)}, u32[]{:S(2)}, u32[]{:S(2)}) collective-permute-start(bf16[256,1024]{1,0:T(8,128)(2,1)} %pad_maximum_fusion.2), channel_id=1, source_target_pairs={{0,8},{8,0},{16,24},{24,16},{1,9},{9,1},{17,25},{25,17},{2,10},{10... | collective-permute-start | bytes 1572872 | tf_op jit(solution)/shard_map/ppermute | solution.py:309
  16.9 20.7 %collective-permute-start = (bf16[128,1024]{1,0:T(8,128)(2,1)}, bf16[128,1024]{1,0:T(8,128)(2,1)S(1)}, u32[]{:S(2)}, u32[]{:S(2)}) collective-permute-start(bf16[128,1024]{1,0:T(8,128)(2,1)} %get-tuple-element.54), channel_id=1, source_target_pairs={{0,8},{8,0},{16,24},{24,16},{1,9},{9,1},{17,25},{25,17},{2,10},{10... | collective-permute-start | bytes 786440 | tf_op jit(solution)/shard_map/ppermute | solution.py:309
  17.1 20.5 %collective-permute-start.1 = (bf16[128,1024]{1,0:T(8,128)(2,1)S(1)}, bf16[128,1024]{1,0:T(8,128)(2,1)}, u32[]{:S(2)}, u32[]{:S(2)}) collective-permute-start(bf16[128,1024]{1,0:T(8,128)(2,1)S(1)} %get-tuple-element.53), channel_id=1, source_target_pairs={{0,16},{8,24},{16,0},{24,8},{1,17},{9,25},{17,1},{25,9},{2,18},{10... | collective-permute-start | bytes 786440 | tf_op jit(solution)/shard_map/ppermute | solution.py:309
  22.7 18.6 %collective-permute-start.7 = (bf16[256,512]{1,0:T(8,128)(2,1)}, bf16[256,512]{1,0:T(8,128)(2,1)S(1)}, u32[]{:S(2)}, u32[]{:S(2)}) collective-permute-start(bf16[256,512]{1,0:T(8,128)(2,1)} %slice.24), channel_id=1, source_target_pairs={{0,2},{2,0},{4,6},{6,4},{1,3},{3,1},{5,7},{7,5},{8,10},{10,8},{12,... | collective-permute-start | bytes 786440 | tf_op jit(solution)/shard_map/ppermute | solution.py:296
  23.5 17.8 %collective-permute-start.9 = (bf16[256,512]{1,0:T(8,128)(2,1)S(1)}, bf16[256,512]{1,0:T(8,128)(2,1)S(1)}, u32[]{:S(2)}, u32[]{:S(2)}) collective-permute-start(bf16[256,512]{1,0:T(8,128)(2,1)S(1)} %slice.25), channel_id=1, source_target_pairs={{0,4},{2,6},{4,0},{6,2},{1,5},{3,7},{5,1},{7,3},{8,12},{10,14},{12... | collective-permute-start | bytes 786440 | tf_op jit(solution)/shard_map/ppermute | solution.py:296
  37.6 6.4 %collective-permute-start.2 = (bf16[128,1024]{1,0:T(8,128)(2,1)}, bf16[128,1024]{1,0:T(8,128)(2,1)S(1)}, u32[]{:S(2)}, u32[]{:S(2)}) collective-permute-start(bf16[128,1024]{1,0:T(8,128)(2,1)} %collective-permute-done.1), channel_id=1, source_target_pairs={{0,8},{8,0},{16,24},{24,16},{1,9},{9,1},{17,25},{25,17},{2,10},{10... | collective-permute-start | bytes 786440 | tf_op jit(solution)/shard_map/ppermute | solution.py:309
  41.3 21.4 %collective-permute-start.10 = (bf16[512,1024]{1,0:T(8,128)(2,1)S(1)}, bf16[512,1024]{1,0:T(8,128)(2,1)S(1)}, u32[]{:S(2)}, u32[]{:S(2)}) collective-permute-start(bf16[512,1024]{1,0:T(8,128)(2,1)S(1)} %pad_maximum_fusion.refs_3_), channel_id=1, source_target_pairs={{0,2},{2,0},{4,6},{6,4},{1,3},{3,1},{5,7},{7,5},{8,10},{10,8},{12,... | collective-permute-start | bytes 3145736 | tf_op jit(solution)/shard_map/ppermute | solution.py:296
  41.7 21.1 %collective-permute-start.11 = (bf16[512,1024]{1,0:T(8,128)(2,1)S(1)}, bf16[512,1024]{1,0:T(8,128)(2,1)S(1)}, u32[]{:S(2)}, u32[]{:S(2)}) collective-permute-start(bf16[512,1024]{1,0:T(8,128)(2,1)S(1)} %pad_maximum_fusion.refs_3_), channel_id=1, source_target_pairs={{0,4},{2,6},{4,0},{6,2},{1,5},{3,7},{5,1},{7,3},{8,12},{10,14},{12... | collective-permute-start | bytes 3145736 | tf_op jit(solution)/shard_map/ppermute | solution.py:296
  44.0 6.2 %collective-permute-start.3 = (bf16[384,1024]{1,0:T(8,128)(2,1)S(1)}, bf16[384,1024]{1,0:T(8,128)(2,1)S(1)}, u32[]{:S(2)}, u32[]{:S(2)}) collective-permute-start(bf16[384,1024]{1,0:T(8,128)(2,1)S(1)} %constant_dynamic-update-slice_fusion.refs_1_), channel_id=1, source_target_pairs={{0,1},{1,0},{2,3},{3,2},{4,5},{5,4},{6,7},{7,6},{8,9},{9,8},{10,11... | collective-permute-start | bytes 2359304 | tf_op jit(solution)/shard_map/ppermute | solution.py:351
  63.6 13.5 %collective-permute-start.12 = (bf16[256,1024]{1,0:T(8,128)(2,1)}, bf16[256,1024]{1,0:T(8,128)(2,1)}, u32[]{:S(2)}, u32[]{:S(2)}) collective-permute-start(bf16[256,1024]{1,0:T(8,128)(2,1)} %slice.20), channel_id=1, source_target_pairs={{0,2},{2,0},{4,6},{6,4},{1,3},{3,1},{5,7},{7,5},{8,10},{10,8},{12,... | collective-permute-start | bytes 1572872 | tf_op jit(solution)/shard_map/ppermute | solution.py:296
  65.6 11.5 %collective-permute-start.13 = (bf16[256,1024]{1,0:T(8,128)(2,1)}, bf16[256,1024]{1,0:T(8,128)(2,1)}, u32[]{:S(2)}, u32[]{:S(2)}) collective-permute-start(bf16[256,1024]{1,0:T(8,128)(2,1)} %slice.21), channel_id=1, source_target_pairs={{0,4},{2,6},{4,0},{6,2},{1,5},{3,7},{5,1},{7,3},{8,12},{10,14},{12... | collective-permute-start | bytes 1572872 | tf_op jit(solution)/shard_map/ppermute | solution.py:296
  66.8 10.2 %collective-permute-start.15 = (bf16[512,256]{1,0:T(8,128)(2,1)}, bf16[512,256]{1,0:T(8,128)(2,1)S(1)}, u32[]{:S(2)}, u32[]{:S(2)}) collective-permute-start(bf16[512,256]{1,0:T(8,128)(2,1)} %copy-done.27), channel_id=1, source_target_pairs={{0,16},{8,24},{16,0},{24,8},{1,17},{9,25},{17,1},{25,9},{2,18},{10... | collective-permute-start | bytes 786440 | tf_op jit(solution)/shard_map/ppermute | solution.py:309
  68.0 16.7 %collective-permute-start.22 = (bf16[1024,256]{1,0:T(8,128)(2,1)}, bf16[1024,256]{1,0:T(8,128)(2,1)S(1)}, u32[]{:S(2)}, u32[]{:S(2)}) collective-permute-start(bf16[1024,256]{1,0:T(8,128)(2,1)} %pad_maximum_fusion.4), channel_id=1, source_target_pairs={{0,8},{8,0},{16,24},{24,16},{1,9},{9,1},{17,25},{25,17},{2,10},{10... | collective-permute-start | bytes 1572872 | tf_op jit(solution)/shard_map/ppermute | solution.py:309
  77.1 11.6 %collective-permute-start.16 = (bf16[512,256]{1,0:T(8,128)(2,1)S(1)}, bf16[512,256]{1,0:T(8,128)(2,1)S(1)}, u32[]{:S(2)}, u32[]{:S(2)}) collective-permute-start(bf16[512,256]{1,0:T(8,128)(2,1)S(1)} %shard_map.103.refs_2_), channel_id=1, source_target_pairs={{0,2},{2,0},{4,6},{6,4},{1,3},{3,1},{5,7},{7,5},{8,10},{10,8},{12,... | collective-permute-start | bytes 786440 | tf_op jit(solution)/shard_map/ppermute | solution.py:296
  77.6 11.1 %collective-permute-start.17 = (bf16[512,256]{1,0:T(8,128)(2,1)S(1)}, bf16[512,256]{1,0:T(8,128)(2,1)S(1)}, u32[]{:S(2)}, u32[]{:S(2)}) collective-permute-start(bf16[512,256]{1,0:T(8,128)(2,1)S(1)} %shard_map.103.refs_2_), channel_id=1, source_target_pairs={{0,4},{2,6},{4,0},{6,2},{1,5},{3,7},{5,1},{7,3},{8,12},{10,14},{12... | collective-permute-start | bytes 786440 | tf_op jit(solution)/shard_map/ppermute | solution.py:296
  78.9 9.9 %collective-permute-start.18 = (bf16[512,256]{1,0:T(8,128)(2,1)S(1)}, bf16[512,256]{1,0:T(8,128)(2,1)S(1)}, u32[]{:S(2)}, u32[]{:S(2)}) collective-permute-start(bf16[512,256]{1,0:T(8,128)(2,1)S(1)} %shard_map.103.refs_2_), channel_id=1, source_target_pairs={{0,6},{2,4},{4,2},{6,0},{1,7},{3,5},{5,3},{7,1},{8,14},{10,12},{12... | collective-permute-start | bytes 786440 | tf_op jit(solution)/shard_map/ppermute | solution.py:296
  82.5 8.4 %collective-permute-start.19 = (bf16[512,256]{1,0:T(8,128)(2,1)S(1)}, bf16[512,256]{1,0:T(8,128)(2,1)S(1)}, u32[]{:S(2)}, u32[]{:S(2)}) collective-permute-start(bf16[512,256]{1,0:T(8,128)(2,1)S(1)} %get-tuple-element.36), channel_id=1, source_target_pairs={{0,16},{8,24},{16,0},{24,8},{1,17},{9,25},{17,1},{25,9},{2,18},{10... | collective-permute-start | bytes 786440 | tf_op jit(solution)/shard_map/ppermute | solution.py:309
  88.4 16.7 %collective-permute-start.14 = (bf16[512,256]{1,0:T(8,128)(2,1)S(1)}, bf16[512,256]{1,0:T(8,128)(2,1)S(1)}, u32[]{:S(2)}, u32[]{:S(2)}) collective-permute-start(bf16[512,256]{1,0:T(8,128)(2,1)S(1)} %get-tuple-element.33), channel_id=1, source_target_pairs={{0,16},{8,24},{16,0},{24,8},{1,17},{9,25},{17,1},{25,9},{2,18},{10... | collective-permute-start | bytes 786440 | tf_op jit(solution)/shard_map/ppermute | solution.py:309
  88.8 22.9 %collective-permute-start.23 = (bf16[2048,256]{1,0:T(8,128)(2,1)S(1)}, bf16[2048,256]{1,0:T(8,128)(2,1)S(1)}, u32[]{:S(2)}, u32[]{:S(2)}) collective-permute-start(bf16[2048,256]{1,0:T(8,128)(2,1)S(1)} %pad_maximum_fusion.1.refs_4_), channel_id=1, source_target_pairs={{0,2},{2,0},{4,6},{6,4},{1,3},{3,1},{5,7},{7,5},{8,10},{10,8},{12,... | collective-permute-start | bytes 3145736 | tf_op jit(solution)/shard_map/ppermute | solution.py:296
  89.3 22.4 %collective-permute-start.24 = (bf16[2048,256]{1,0:T(8,128)(2,1)S(1)}, bf16[2048,256]{1,0:T(8,128)(2,1)S(1)}, u32[]{:S(2)}, u32[]{:S(2)}) collective-permute-start(bf16[2048,256]{1,0:T(8,128)(2,1)S(1)} %pad_maximum_fusion.1.refs_4_), channel_id=1, source_target_pairs={{0,4},{2,6},{4,0},{6,2},{1,5},{3,7},{5,1},{7,3},{8,12},{10,14},{12... | collective-permute-start | bytes 3145736 | tf_op jit(solution)/shard_map/ppermute | solution.py:296
  112.5 8.3 %collective-permute-start.25 = (bf16[1024,256]{1,0:T(8,128)(2,1)}, bf16[1024,256]{1,0:T(8,128)(2,1)}, u32[]{:S(2)}, u32[]{:S(2)}) collective-permute-start(bf16[1024,256]{1,0:T(8,128)(2,1)} %slice.22), channel_id=1, source_target_pairs={{0,2},{2,0},{4,6},{6,4},{1,3},{3,1},{5,7},{7,5},{8,10},{10,8},{12,... | collective-permute-start | bytes 1572872 | tf_op jit(solution)/shard_map/ppermute | solution.py:296
  113.7 8.3 %collective-permute-start.26 = (bf16[1024,256]{1,0:T(8,128)(2,1)}, bf16[1024,256]{1,0:T(8,128)(2,1)}, u32[]{:S(2)}, u32[]{:S(2)}) collective-permute-start(bf16[1024,256]{1,0:T(8,128)(2,1)} %slice.23), channel_id=1, source_target_pairs={{0,4},{2,6},{4,0},{6,2},{1,5},{3,7},{5,1},{7,3},{8,12},{10,14},{12... | collective-permute-start | bytes 1572872 | tf_op jit(solution)/shard_map/ppermute | solution.py:296
  114.9 11.1 %collective-permute-start.20 = (bf16[512,256]{1,0:T(8,128)(2,1)}, bf16[512,256]{1,0:T(8,128)(2,1)S(1)}, u32[]{:S(2)}, u32[]{:S(2)}) collective-permute-start(bf16[512,256]{1,0:T(8,128)(2,1)} %copy-done.8), channel_id=1, source_target_pairs={{0,16},{8,24},{16,0},{24,8},{1,17},{9,25},{17,1},{25,9},{2,18},{10... | collective-permute-start | bytes 786440 | tf_op jit(solution)/shard_map/ppermute | solution.py:309
  114.9 22.4 %collective-permute-start.21 = (bf16[512,256]{1,0:T(8,128)(2,1)S(1)}, bf16[512,256]{1,0:T(8,128)(2,1)S(1)}, u32[]{:S(2)}, u32[]{:S(2)}) collective-permute-start(bf16[512,256]{1,0:T(8,128)(2,1)S(1)} %shard_map.105.refs_1_), channel_id=1, source_target_pairs={{0,16},{8,24},{16,0},{24,8},{1,17},{9,25},{17,1},{25,9},{2,18},{10... | collective-permute-start | bytes 786440 | tf_op jit(solution)/shard_map/ppermute | solution.py:309
  139.4 7.6 %collective-permute-start.27 = (bf16[256,1024]{1,0:T(8,128)(2,1)}, bf16[256,1024]{1,0:T(8,128)(2,1)}, u32[]{:S(2)}, u32[]{:S(2)}) collective-permute-start(bf16[256,1024]{1,0:T(8,128)(2,1)} %shard_map.107), channel_id=1, source_target_pairs={{0,1},{1,0},{2,3},{3,2},{4,5},{5,4},{6,7},{7,6},{8,9},{9,8},{10,11... | collective-permute-start | bytes 1572872 | tf_op jit(solution)/shard_map/ppermute | solution.py:402
  150.2 7.5 %collective-permute-start.28 = (bf16[128,1024]{1,0:T(8,128)(2,1)S(1)}, bf16[128,1024]{1,0:T(8,128)(2,1)S(1)}, u32[]{:S(2)}, u32[]{:S(2)}) collective-permute-start(bf16[128,1024]{1,0:T(8,128)(2,1)S(1)} %add_convert_fusion.4), channel_id=1, source_target_pairs={{0,8},{8,0},{16,24},{24,16},{1,9},{9,1},{17,25},{25,17},{2,10},{10... | collective-permute-start | bytes 786440 | tf_op jit(solution)/shard_map/ppermute | solution.py:309
  152.2 11.2 %collective-permute-start.31 = (bf16[128,1024]{1,0:T(8,128)(2,1)S(1)}, bf16[128,1024]{1,0:T(8,128)(2,1)S(1)}, u32[]{:S(2)}, u32[]{:S(2)}) collective-permute-start(bf16[128,1024]{1,0:T(8,128)(2,1)S(1)} %add_convert_fusion.1), channel_id=1, source_target_pairs={{0,8},{8,0},{16,24},{24,16},{1,9},{9,1},{17,25},{25,17},{2,10},{10... | collective-permute-start | bytes 786440 | tf_op jit(solution)/shard_map/ppermute | solution.py:309
  158.8 11.4 %collective-permute-start.29 = (bf16[128,1024]{1,0:T(8,128)(2,1)S(1)}, bf16[128,1024]{1,0:T(8,128)(2,1)S(1)}, u32[]{:S(2)}, u32[]{:S(2)}) collective-permute-start(bf16[128,1024]{1,0:T(8,128)(2,1)S(1)} %add_convert_fusion.3), channel_id=1, source_target_pairs={{0,0},{1,16},{8,8},{9,24},{16,1},{17,17},{24,9},{25,25},{2,2},{3,1... | collective-permute-start | bytes 786440 | tf_op jit(solution)/shard_map/ppermute | solution.py:411
  163.4 12.4 %collective-permute-start.32 = (bf16[128,1024]{1,0:T(8,128)(2,1)S(1)}, bf16[128,1024]{1,0:T(8,128)(2,1)S(1)}, u32[]{:S(2)}, u32[]{:S(2)}) collective-permute-start(bf16[128,1024]{1,0:T(8,128)(2,1)S(1)} %add_convert_fusion), channel_id=1, source_target_pairs={{0,0},{1,16},{8,8},{9,24},{16,1},{17,17},{24,9},{25,25},{2,2},{3,1... | collective-permute-start | bytes 786440 | tf_op jit(solution)/shard_map/ppermute | solution.py:411
  (42 other events, 271.6 us)

commit v15 on v14

--- a/solution.py
+++ b/solution.py
@@ -13,7 +13,7 @@
 MIB = 1024 * 1024
 
 
-def local_kernel(body, out_shape, operands, flops, scratch=(), exps=0):
+def local_kernel(body, out_shape, operands, flops, scratch=(), exps=0, limit=12):
     size = sum(x.size * x.dtype.itemsize for x in operands)
     return pl.pallas_call(
         body,
@@ -21,7 +21,7 @@
         + [pl.BlockSpec(memory_space=pltpu.VMEM)] * (len(operands) - 1),
         out_shape=out_shape,
         scratch_shapes=scratch,
-        compiler_params=pltpu.CompilerParams(vmem_limit_bytes=12 * MIB),
+        compiler_params=pltpu.CompilerParams(vmem_limit_bytes=limit * MIB),
         cost_estimate=pl.CostEstimate(flops=flops, bytes_accessed=size, transcendentals=exps),
     )(*operands)
 
@@ -139,6 +139,7 @@
             pltpu.VMEM((tokens // blocks, keys), jnp.float32),
         ],
         tokens * heads * keys,
+        limit=8 if len(kv_parts) > 1 else 12,
     )
 
 
@@ -223,6 +224,7 @@
         jax.ShapeDtypeStruct((tokens // 2, width), jnp.bfloat16),
         (place, *attended_parts, *weights),
         2 * (tokens // 2) * 4 * depth * width,
+        limit=6,
     )
 
 

time: 178 us -> 178 us (level)
    unnamed x85 -> x91, local copies, waits for them, and re-layouts: 9.27 us -> 8.19 us
where the time goes in v15:
time: 178 us; the launch traced here: 177 us
  waiting for transfers between devices  78.7 us (44%)
  starting transfers between devices  40.7 us (23%)
  Pallas kernels  27.3 us (15%)
  local copies, waits for them, and re-layouts  19.8 us (11%)
  other arithmetic  10.2 us (6%)
    ppermute x13, waiting for transfers between devices, along(): return lax.ppermute(block, 'hi', [(i, i ^ d) for i in range(4)])  56.5 us
    pallas_call x11, Pallas kernels, local_kernel(): pl.pallas_call(body, in_specs=[pl.BlockSpec(memory_space=pltpu.SMEM)] + [...  27.3 us
    ppermute x13, starting transfers between devices, along(): return lax.ppermute(block, 'hi', [(i, i ^ d) for i in range(4)])  13.6 us
    ppermute x15, waiting for transfers between devices, beside(): return lax.ppermute(block, 'lo', [(i, i ^ r) for i in range(4)])  13.1 us
    ppermute x15, starting transfers between devices, beside(): return lax.ppermute(block, 'lo', [(i, i ^ r) for i in range(4)])  12.3 us
    ppermute x2, waiting for transfers between devices, line_device(): pieces.append(lax.ppermute(summed, ('hi', 'head'), home))  8.59 us
    unnamed x91, local copies, waits for them, and re-layouts  8.19 us
    ppermute x2, starting transfers between devices, line_device(): pieces.append(lax.ppermute(summed, ('hi', 'head'), home))  7.91 us
  transfers between devices with their start and end apart: 33, of which 18 were waited for; matrix products, arithmetic and copies ran while one was open for 11% of the time, Pallas kernels for 13%

profile of v15, /device:TPU:1, one launch (start us, length us, event | category | flops | bytes accessed | tf_op | source)
XLA Modules:
  0.0 177.3 jit_solution(10072510959540190250)
XLA Ops:
  1.3 2.2 %collective-permute-start.4 = (bf16[256,512]{1,0:T(8,128)(2,1)S(1)}, bf16[256,512]{1,0:T(8,128)(2,1)S(1)}, u32[]{:S(2)}, u32[]{:S(2)}) collective-permute-start(bf16[256,512]{1,0:T(8,128)(2,1)S(1)} %pad_maximum_fusion.7), channel_id=1, source_target_pairs={{0,8},{8,0},{16,24},{24,16},{1,9},{9,1},{17,25},{25,17},{2,10},{10... | collective-permute-start | bytes 786440 | tf_op jit(solution)/shard_map/ppermute | solution.py:311
  4.1 5.3 %collective-permute-done.4 = bf16[256,512]{1,0:T(8,128)(2,1)S(1)} collective-permute-done((bf16[256,512]{1,0:T(8,128)(2,1)S(1)}, bf16[256,512]{1,0:T(8,128)(2,1)S(1)}, u32[]{:S(2)}, u32[]{:S(2)}) %collective-permute-start.4) | collective-permute-done | bytes 262176 | tf_op jit(solution)/shard_map/ppermute | solution.py:311
  11.9 2.1 %constant_dynamic-slice_fusion.15 = (bf16[256,512]{1,0:T(8,128)(2,1)}, bf16[256,512]{1,0:T(8,128)(2,1)}, bf16[256,512]{1,0:T(8,128)(2,1)S(1)}, bf16[256,512]{1,0:T(8,128)(2,1)S(1)}) fusion(bf16[256,2048]{1,0:T(8,128)(2,1)} %param.12, s32[]{:T(128)S(6)} %select_n.78, s32[]{:T(128)S(6)} %select_n.79, s32[]{:T(128)S(6)} %select_n.81, s32[]{:T(128)S(6)} %select_n.80), kind=kLoop, calls=%fused_computation.42 | loop fusion | bytes 2097168 | tf_op jit(solution)/shard_map/dynamic_slice | solution.py:328
  17.0 2.3 %collective-permute-start.1 = (bf16[128,1024]{1,0:T(8,128)(2,1)S(1)}, bf16[128,1024]{1,0:T(8,128)(2,1)}, u32[]{:S(2)}, u32[]{:S(2)}) collective-permute-start(bf16[128,1024]{1,0:T(8,128)(2,1)S(1)} %get-tuple-element.53), channel_id=1, source_target_pairs={{0,16},{8,24},{16,0},{24,8},{1,17},{9,25},{17,1},{25,9},{2,18},{10... | collective-permute-start | bytes 786440 | tf_op jit(solution)/shard_map/ppermute | solution.py:311
  19.4 2.2 %constant_dynamic-slice_fusion.3 = (bf16[512,256]{1,0:T(8,128)(2,1)}, bf16[512,256]{1,0:T(8,128)(2,1)}, bf16[512,256]{1,0:T(8,128)(2,1)}, bf16[512,256]{1,0:T(8,128)(2,1)}) fusion(bf16[2048,256]{1,0:T(8,128)(2,1)} %param.15, s32[]{:T(128)S(6)} %select_n.78, s32[]{:T(128)S(6)} %select_n.79, s32[]{:T(128)S(6)} %select_n.81, s32[]{:T(128)S(6)} %select_n.80), kind=kLoop, calls=%fused_computation.30 | loop fusion | bytes 2097168 | tf_op jit(solution)/shard_map/dynamic_slice | solution.py:364
  23.5 1.3 collective-permute-start.9
  24.9 12.7 %collective-permute-done = bf16[128,1024]{1,0:T(8,128)(2,1)S(1)} collective-permute-done((bf16[128,1024]{1,0:T(8,128)(2,1)}, bf16[128,1024]{1,0:T(8,128)(2,1)S(1)}, u32[]{:S(2)}, u32[]{:S(2)}) %collective-permute-start) | collective-permute-done | bytes 262176 | tf_op jit(solution)/shard_map/ppermute | solution.py:311
  37.6 2.4 %collective-permute-start.2 = (bf16[128,1024]{1,0:T(8,128)(2,1)}, bf16[128,1024]{1,0:T(8,128)(2,1)S(1)}, u32[]{:S(2)}, u32[]{:S(2)}) collective-permute-start(bf16[128,1024]{1,0:T(8,128)(2,1)} %collective-permute-done.1), channel_id=1, source_target_pairs={{0,8},{8,0},{16,24},{24,16},{1,9},{9,1},{17,25},{25,17},{2,10},{10... | collective-permute-start | bytes 786440 | tf_op jit(solution)/shard_map/ppermute | solution.py:311
  44.0 4.0 %collective-permute-start.3 = (bf16[384,1024]{1,0:T(8,128)(2,1)S(1)}, bf16[384,1024]{1,0:T(8,128)(2,1)S(1)}, u32[]{:S(2)}, u32[]{:S(2)}) collective-permute-start(bf16[384,1024]{1,0:T(8,128)(2,1)S(1)} %constant_dynamic-update-slice_fusion.refs_1_), channel_id=1, source_target_pairs={{0,1},{1,0},{2,3},{3,2},{4,5},{5,4},{6,7},{7,6},{8,9},{9,8},{10,11... | collective-permute-start | bytes 2359304 | tf_op jit(solution)/shard_map/ppermute | solution.py:353
  48.2 2.1 %fusion.3 = (f32[512,64]{1,0:T(8,128)}, f32[512,64]{1,0:T(8,128)}, f32[512,64]{1,0:T(8,128)}) fusion(f32[64]{0:T(128)S(1)} %negate_power_fusion, f32[512]{0:T(512)S(1)} %fusion.12), kind=kLoop, calls=%fused_computation.21 | loop fusion | flops 65536 | bytes 395520 | tf_op jit(solution)/shard_map/neg | solution.py:36
  50.3 1.9 %shard_map.100 = (bf16[512,256]{1,0:T(8,128)(2,1)S(1)}, bf16[512,256]{1,0:T(8,128)(2,1)S(1)}) custom-call(s32[5]{0:T(128)S(1)} %get-tuple-element.66.place_ref, bf16[128,2048]{1,0:T(8,128)(2,1)S(1)} %constant_dynamic-slice_fusion.18.refs_0_, bf16[384,1024]{1,0:T(8,128)(2,1)S(1)} %constant_dynamic-update-slice_fusion.refs_1_, ...), custom_call_target="tpu_custom_call" | custom-call | flops 1073741824 | bytes 4194324 | tf_op jit(solution)/shard_map/pallas_call | solution.py:18
  53.6 9.2 %collective-permute-done.10.refs_4_ = bf16[512,1024]{1,0:T(8,128)(2,1)S(1)} collective-permute-done((bf16[512,1024]{1,0:T(8,128)(2,1)S(1)}, bf16[512,1024]{1,0:T(8,128)(2,1)S(1)}, u32[]{:S(2)}, u32[]{:S(2)}) %collective-permute-start.10) | collective-permute-done | bytes 1048608 | tf_op jit(solution)/shard_map/ppermute | solution.py:298
  68.2 1.5 pad_maximum_fusion.5
  69.7 7.2 %collective-permute-done.15.refs_1_ = bf16[512,256]{1,0:T(8,128)(2,1)S(1)} collective-permute-done((bf16[512,256]{1,0:T(8,128)(2,1)}, bf16[512,256]{1,0:T(8,128)(2,1)S(1)}, u32[]{:S(2)}, u32[]{:S(2)}) %collective-permute-start.15) | collective-permute-done | bytes 262176 | tf_op jit(solution)/shard_map/ppermute | solution.py:311
  79.9 2.6 %shard_map.102 = (bf16[512,256]{1,0:T(8,128)(2,1)S(1)}, bf16[512,256]{1,0:T(8,128)(2,1)S(1)}) custom-call(s32[5]{0:T(128)S(1)} %get-tuple-element.43.place_ref, bf16[128,2048]{1,0:T(8,128)(2,1)S(1)} %constant_dynamic-slice_fusion.18.refs_0_, bf16[384,1024]{1,0:T(8,128)(2,1)S(1)} %constant_dynamic-update-slice_fusion.refs_1_, ...), custom_call_target="tpu_custom_call" | custom-call | flops 1073741824 | bytes 6291476 | tf_op jit(solution)/shard_map/pallas_call | solution.py:18
  82.6 2.1 %collective-permute-done.22 = bf16[1024,256]{1,0:T(8,128)(2,1)S(1)} collective-permute-done((bf16[1024,256]{1,0:T(8,128)(2,1)}, bf16[1024,256]{1,0:T(8,128)(2,1)S(1)}, u32[]{:S(2)}, u32[]{:S(2)}) %collective-permute-start.22) | collective-permute-done | bytes 524320 | tf_op jit(solution)/shard_map/ppermute | solution.py:311
  85.8 2.6 %shard_map.101 = (bf16[512,256]{1,0:T(8,128)(2,1)S(1)}, bf16[512,256]{1,0:T(8,128)(2,1)S(1)}) custom-call(s32[5]{0:T(128)S(1)} %get-tuple-element.67.place_ref, bf16[128,2048]{1,0:T(8,128)(2,1)S(1)} %constant_dynamic-slice_fusion.18.refs_0_, bf16[384,1024]{1,0:T(8,128)(2,1)S(1)} %constant_dynamic-update-slice_fusion.refs_1_, ...), custom_call_target="tpu_custom_call" | custom-call | flops 1073741824 | bytes 6291476 | tf_op jit(solution)/shard_map/pallas_call | solution.py:18
  90.9 6.3 %shard_map.105.refs_1_ = bf16[512,256]{1,0:T(8,128)(2,1)S(1)} custom-call(s32[21]{0:T(128)S(1)} %pad_add_fusion.2.place_ref, f32[512,128]{1,0:T(8,128)S(1)} %get-tuple-element.68.cos_ref, f32[512,128]{1,0:T(8,128)S(1)} %get-tuple-element.69.sin_ref, bf16[512,256]{1,0:T(8,128)(2,1)S(1)} %get-tuple-element.31.refs_0_, ...), custom_call_target="tpu_custom_call" | custom-call | flops 8589934592 | bytes 2097236 | tf_op jit(solution)/shard_map/pallas_call | solution.py:18
  97.2 7.9 %collective-permute-done.14.refs_1_ = bf16[512,256]{1,0:T(8,128)(2,1)S(1)} collective-permute-done((bf16[512,256]{1,0:T(8,128)(2,1)S(1)}, bf16[512,256]{1,0:T(8,128)(2,1)S(1)}, u32[]{:S(2)}, u32[]{:S(2)}) %collective-permute-start.14) | collective-permute-done | bytes 262176 | tf_op jit(solution)/shard_map/ppermute | solution.py:311
  105.1 6.5 %shard_map.104.refs_0_ = bf16[512,256]{1,0:T(8,128)(2,1)S(1)} custom-call(s32[21]{0:T(128)S(1)} %pad_add_fusion.2.place_ref, f32[512,128]{1,0:T(8,128)S(1)} %get-tuple-element.68.cos_ref, f32[512,128]{1,0:T(8,128)S(1)} %get-tuple-element.69.sin_ref, bf16[512,256]{1,0:T(8,128)(2,1)S(1)} %get-tuple-element.32.refs_0_, ...), custom_call_target="tpu_custom_call" | custom-call | flops 8589934592 | bytes 2097236 | tf_op jit(solution)/shard_map/pallas_call | solution.py:18
  115.5 2.4 %collective-permute-start.21 = (bf16[512,256]{1,0:T(8,128)(2,1)S(1)}, bf16[512,256]{1,0:T(8,128)(2,1)S(1)}, u32[]{:S(2)}, u32[]{:S(2)}) collective-permute-start(bf16[512,256]{1,0:T(8,128)(2,1)S(1)} %shard_map.105.refs_1_), channel_id=1, source_target_pairs={{0,16},{8,24},{16,0},{24,8},{1,17},{9,25},{17,1},{25,9},{2,18},{10... | collective-permute-start | bytes 786440 | tf_op jit(solution)/shard_map/ppermute | solution.py:311
  118.0 3.5 %collective-permute-done.25 = bf16[1024,256]{1,0:T(8,128)(2,1)} collective-permute-done((bf16[1024,256]{1,0:T(8,128)(2,1)}, bf16[1024,256]{1,0:T(8,128)(2,1)}, u32[]{:S(2)}, u32[]{:S(2)}) %collective-permute-start.25) | collective-permute-done | bytes 524320 | tf_op jit(solution)/shard_map/ppermute | solution.py:298
  123.7 9.2 %collective-permute-done.20.refs_2_ = bf16[512,256]{1,0:T(8,128)(2,1)S(1)} collective-permute-done((bf16[512,256]{1,0:T(8,128)(2,1)}, bf16[512,256]{1,0:T(8,128)(2,1)S(1)}, u32[]{:S(2)}, u32[]{:S(2)}) %collective-permute-start.20) | collective-permute-done | bytes 262176 | tf_op jit(solution)/shard_map/ppermute | solution.py:311
  132.9 5.6 %collective-permute-done.21.refs_3_ = bf16[512,256]{1,0:T(8,128)(2,1)S(1)} collective-permute-done((bf16[512,256]{1,0:T(8,128)(2,1)S(1)}, bf16[512,256]{1,0:T(8,128)(2,1)S(1)}, u32[]{:S(2)}, u32[]{:S(2)}) %collective-permute-start.21) | collective-permute-done | bytes 262176 | tf_op jit(solution)/shard_map/ppermute | solution.py:311
  138.6 2.1 %shard_map.107 = bf16[256,1024]{1,0:T(8,128)(2,1)} custom-call(s32[2]{0:T(128)S(1)} %pad_add_fusion.7.place_ref, bf16[512,256]{1,0:T(8,128)(2,1)S(1)} %copy-done.9, bf16[512,256]{1,0:T(8,128)(2,1)S(1)} %shard_map.105.refs_1_, bf16[512,256]{1,0:T(8,128)(2,1)S(1)} %collective-permute-done.20.refs_2_, bf16[512,256]{1,0:T(8,128)(2,1)S(1)} %collective-permute-done.21.refs_3_, ...), custom_call_target="tpu_custom_call" | custom-call | flops 536870912 | bytes 3145736 | tf_op jit(solution)/shard_map/pallas_call | solution.py:18
  140.6 2.8 %collective-permute-start.27 = (bf16[256,1024]{1,0:T(8,128)(2,1)}, bf16[256,1024]{1,0:T(8,128)(2,1)}, u32[]{:S(2)}, u32[]{:S(2)}) collective-permute-start(bf16[256,1024]{1,0:T(8,128)(2,1)} %shard_map.107), channel_id=1, source_target_pairs={{0,1},{1,0},{2,3},{3,2},{4,5},{5,4},{6,7},{7,6},{8,9},{9,8},{10,11... | collective-permute-start | bytes 1572872 | tf_op jit(solution)/shard_map/ppermute | solution.py:404
  153.3 4.6 %collective-permute-done.28 = bf16[128,1024]{1,0:T(8,128)(2,1)S(1)} collective-permute-done((bf16[128,1024]{1,0:T(8,128)(2,1)S(1)}, bf16[128,1024]{1,0:T(8,128)(2,1)S(1)}, u32[]{:S(2)}, u32[]{:S(2)}) %collective-permute-start.28) | collective-permute-done | bytes 262176 | tf_op jit(solution)/shard_map/ppermute | solution.py:311
  158.9 4.2 %collective-permute-start.29 = (bf16[128,1024]{1,0:T(8,128)(2,1)S(1)}, bf16[128,1024]{1,0:T(8,128)(2,1)S(1)}, u32[]{:S(2)}, u32[]{:S(2)}) collective-permute-start(bf16[128,1024]{1,0:T(8,128)(2,1)S(1)} %add_convert_fusion.3), channel_id=1, source_target_pairs={{0,0},{1,16},{8,8},{9,24},{16,1},{17,17},{24,9},{25,25},{2,2},{3,1... | collective-permute-start | bytes 786440 | tf_op jit(solution)/shard_map/ppermute | solution.py:413
  163.6 3.7 %collective-permute-start.32 = (bf16[128,1024]{1,0:T(8,128)(2,1)S(1)}, bf16[128,1024]{1,0:T(8,128)(2,1)S(1)}, u32[]{:S(2)}, u32[]{:S(2)}) collective-permute-start(bf16[128,1024]{1,0:T(8,128)(2,1)S(1)} %add_convert_fusion), channel_id=1, source_target_pairs={{0,0},{1,16},{8,8},{9,24},{16,1},{17,17},{24,9},{25,25},{2,2},{3,1... | collective-permute-start | bytes 786440 | tf_op jit(solution)/shard_map/ppermute | solution.py:413
  167.3 3.0 %collective-permute-done.29.refs_0_ = bf16[128,1024]{1,0:T(8,128)(2,1)S(1)} collective-permute-done((bf16[128,1024]{1,0:T(8,128)(2,1)S(1)}, bf16[128,1024]{1,0:T(8,128)(2,1)S(1)}, u32[]{:S(2)}, u32[]{:S(2)}) %collective-permute-start.29) | collective-permute-done | bytes 262176 | tf_op jit(solution)/shard_map/ppermute | solution.py:413
  170.3 5.6 %collective-permute-done.32.refs_1_ = bf16[128,1024]{1,0:T(8,128)(2,1)S(1)} collective-permute-done((bf16[128,1024]{1,0:T(8,128)(2,1)S(1)}, bf16[128,1024]{1,0:T(8,128)(2,1)S(1)}, u32[]{:S(2)}, u32[]{:S(2)}) %collective-permute-start.32) | collective-permute-done | bytes 262176 | tf_op jit(solution)/shard_map/ppermute | solution.py:413
  175.9 1.4 shard_map.110
  (174 shorter events, 44.3 us)
Async XLA Ops:
  1.3 8.2 %collective-permute-start.4 = (bf16[256,512]{1,0:T(8,128)(2,1)S(1)}, bf16[256,512]{1,0:T(8,128)(2,1)S(1)}, u32[]{:S(2)}, u32[]{:S(2)}) collective-permute-start(bf16[256,512]{1,0:T(8,128)(2,1)S(1)} %pad_maximum_fusion.7), channel_id=1, source_target_pairs={{0,8},{8,0},{16,24},{24,16},{1,9},{9,1},{17,25},{25,17},{2,10},{10... | collective-permute-start | bytes 786440 | tf_op jit(solution)/shard_map/ppermute | solution.py:311
  9.5 12.4 %collective-permute-start.6 = (bf16[512,512]{1,0:T(8,128)(2,1)S(1)}, bf16[512,512]{1,0:T(8,128)(2,1)S(1)}, u32[]{:S(2)}, u32[]{:S(2)}) collective-permute-start(bf16[512,512]{1,0:T(8,128)(2,1)S(1)} %pad_maximum_fusion.3.refs_3_), channel_id=1, source_target_pairs={{0,4},{2,6},{4,0},{6,2},{1,5},{3,7},{5,1},{7,3},{8,12},{10,14},{12... | collective-permute-start | bytes 1572872 | tf_op jit(solution)/shard_map/ppermute | solution.py:298
  10.7 12.8 %collective-permute-start.8 = (bf16[512,512]{1,0:T(8,128)(2,1)S(1)}, bf16[512,512]{1,0:T(8,128)(2,1)S(1)}, u32[]{:S(2)}, u32[]{:S(2)}) collective-permute-start(bf16[512,512]{1,0:T(8,128)(2,1)S(1)} %pad_maximum_fusion.3.refs_3_), channel_id=1, source_target_pairs={{0,2},{2,0},{4,6},{6,4},{1,3},{3,1},{5,7},{7,5},{8,10},{10,8},{12,... | collective-permute-start | bytes 1572872 | tf_op jit(solution)/shard_map/ppermute | solution.py:298
  14.8 25.2 %collective-permute-start.5 = (bf16[256,1024]{1,0:T(8,128)(2,1)}, bf16[256,1024]{1,0:T(8,128)(2,1)}, u32[]{:S(2)}, u32[]{:S(2)}) collective-permute-start(bf16[256,1024]{1,0:T(8,128)(2,1)} %pad_maximum_fusion.2), channel_id=1, source_target_pairs={{0,8},{8,0},{16,24},{24,16},{1,9},{9,1},{17,25},{25,17},{2,10},{10... | collective-permute-start | bytes 1572872 | tf_op jit(solution)/shard_map/ppermute | solution.py:311
  16.9 20.7 %collective-permute-start = (bf16[128,1024]{1,0:T(8,128)(2,1)}, bf16[128,1024]{1,0:T(8,128)(2,1)S(1)}, u32[]{:S(2)}, u32[]{:S(2)}) collective-permute-start(bf16[128,1024]{1,0:T(8,128)(2,1)} %get-tuple-element.54), channel_id=1, source_target_pairs={{0,8},{8,0},{16,24},{24,16},{1,9},{9,1},{17,25},{25,17},{2,10},{10... | collective-permute-start | bytes 786440 | tf_op jit(solution)/shard_map/ppermute | solution.py:311
  17.0 20.5 %collective-permute-start.1 = (bf16[128,1024]{1,0:T(8,128)(2,1)S(1)}, bf16[128,1024]{1,0:T(8,128)(2,1)}, u32[]{:S(2)}, u32[]{:S(2)}) collective-permute-start(bf16[128,1024]{1,0:T(8,128)(2,1)S(1)} %get-tuple-element.53), channel_id=1, source_target_pairs={{0,16},{8,24},{16,0},{24,8},{1,17},{9,25},{17,1},{25,9},{2,18},{10... | collective-permute-start | bytes 786440 | tf_op jit(solution)/shard_map/ppermute | solution.py:311
  22.7 18.6 %collective-permute-start.7 = (bf16[256,512]{1,0:T(8,128)(2,1)}, bf16[256,512]{1,0:T(8,128)(2,1)S(1)}, u32[]{:S(2)}, u32[]{:S(2)}) collective-permute-start(bf16[256,512]{1,0:T(8,128)(2,1)} %slice.24), channel_id=1, source_target_pairs={{0,2},{2,0},{4,6},{6,4},{1,3},{3,1},{5,7},{7,5},{8,10},{10,8},{12,... | collective-permute-start | bytes 786440 | tf_op jit(solution)/shard_map/ppermute | solution.py:298
  23.5 17.9 %collective-permute-start.9 = (bf16[256,512]{1,0:T(8,128)(2,1)S(1)}, bf16[256,512]{1,0:T(8,128)(2,1)S(1)}, u32[]{:S(2)}, u32[]{:S(2)}) collective-permute-start(bf16[256,512]{1,0:T(8,128)(2,1)S(1)} %slice.25), channel_id=1, source_target_pairs={{0,4},{2,6},{4,0},{6,2},{1,5},{3,7},{5,1},{7,3},{8,12},{10,14},{12... | collective-permute-start | bytes 786440 | tf_op jit(solution)/shard_map/ppermute | solution.py:298
  37.6 6.4 %collective-permute-start.2 = (bf16[128,1024]{1,0:T(8,128)(2,1)}, bf16[128,1024]{1,0:T(8,128)(2,1)S(1)}, u32[]{:S(2)}, u32[]{:S(2)}) collective-permute-start(bf16[128,1024]{1,0:T(8,128)(2,1)} %collective-permute-done.1), channel_id=1, source_target_pairs={{0,8},{8,0},{16,24},{24,16},{1,9},{9,1},{17,25},{25,17},{2,10},{10... | collective-permute-start | bytes 786440 | tf_op jit(solution)/shard_map/ppermute | solution.py:311
  41.3 21.4 %collective-permute-start.10 = (bf16[512,1024]{1,0:T(8,128)(2,1)S(1)}, bf16[512,1024]{1,0:T(8,128)(2,1)S(1)}, u32[]{:S(2)}, u32[]{:S(2)}) collective-permute-start(bf16[512,1024]{1,0:T(8,128)(2,1)S(1)} %pad_maximum_fusion.refs_3_), channel_id=1, source_target_pairs={{0,2},{2,0},{4,6},{6,4},{1,3},{3,1},{5,7},{7,5},{8,10},{10,8},{12,... | collective-permute-start | bytes 3145736 | tf_op jit(solution)/shard_map/ppermute | solution.py:298
  41.7 21.1 %collective-permute-start.11 = (bf16[512,1024]{1,0:T(8,128)(2,1)S(1)}, bf16[512,1024]{1,0:T(8,128)(2,1)S(1)}, u32[]{:S(2)}, u32[]{:S(2)}) collective-permute-start(bf16[512,1024]{1,0:T(8,128)(2,1)S(1)} %pad_maximum_fusion.refs_3_), channel_id=1, source_target_pairs={{0,4},{2,6},{4,0},{6,2},{1,5},{3,7},{5,1},{7,3},{8,12},{10,14},{12... | collective-permute-start | bytes 3145736 | tf_op jit(solution)/shard_map/ppermute | solution.py:298
  44.0 6.2 %collective-permute-start.3 = (bf16[384,1024]{1,0:T(8,128)(2,1)S(1)}, bf16[384,1024]{1,0:T(8,128)(2,1)S(1)}, u32[]{:S(2)}, u32[]{:S(2)}) collective-permute-start(bf16[384,1024]{1,0:T(8,128)(2,1)S(1)} %constant_dynamic-update-slice_fusion.refs_1_), channel_id=1, source_target_pairs={{0,1},{1,0},{2,3},{3,2},{4,5},{5,4},{6,7},{7,6},{8,9},{9,8},{10,11... | collective-permute-start | bytes 2359304 | tf_op jit(solution)/shard_map/ppermute | solution.py:353
  63.6 13.5 %collective-permute-start.12 = (bf16[256,1024]{1,0:T(8,128)(2,1)}, bf16[256,1024]{1,0:T(8,128)(2,1)}, u32[]{:S(2)}, u32[]{:S(2)}) collective-permute-start(bf16[256,1024]{1,0:T(8,128)(2,1)} %slice.20), channel_id=1, source_target_pairs={{0,2},{2,0},{4,6},{6,4},{1,3},{3,1},{5,7},{7,5},{8,10},{10,8},{12,... | collective-permute-start | bytes 1572872 | tf_op jit(solution)/shard_map/ppermute | solution.py:298
  65.6 11.5 %collective-permute-start.13 = (bf16[256,1024]{1,0:T(8,128)(2,1)}, bf16[256,1024]{1,0:T(8,128)(2,1)}, u32[]{:S(2)}, u32[]{:S(2)}) collective-permute-start(bf16[256,1024]{1,0:T(8,128)(2,1)} %slice.21), channel_id=1, source_target_pairs={{0,4},{2,6},{4,0},{6,2},{1,5},{3,7},{5,1},{7,3},{8,12},{10,14},{12... | collective-permute-start | bytes 1572872 | tf_op jit(solution)/shard_map/ppermute | solution.py:298
  66.8 10.2 %collective-permute-start.15 = (bf16[512,256]{1,0:T(8,128)(2,1)}, bf16[512,256]{1,0:T(8,128)(2,1)S(1)}, u32[]{:S(2)}, u32[]{:S(2)}) collective-permute-start(bf16[512,256]{1,0:T(8,128)(2,1)} %copy-done.30), channel_id=1, source_target_pairs={{0,16},{8,24},{16,0},{24,8},{1,17},{9,25},{17,1},{25,9},{2,18},{10... | collective-permute-start | bytes 786440 | tf_op jit(solution)/shard_map/ppermute | solution.py:311
  68.0 16.7 %collective-permute-start.22 = (bf16[1024,256]{1,0:T(8,128)(2,1)}, bf16[1024,256]{1,0:T(8,128)(2,1)S(1)}, u32[]{:S(2)}, u32[]{:S(2)}) collective-permute-start(bf16[1024,256]{1,0:T(8,128)(2,1)} %pad_maximum_fusion.4), channel_id=1, source_target_pairs={{0,8},{8,0},{16,24},{24,16},{1,9},{9,1},{17,25},{25,17},{2,10},{10... | collective-permute-start | bytes 1572872 | tf_op jit(solution)/shard_map/ppermute | solution.py:311
  77.1 11.6 %collective-permute-start.16 = (bf16[512,256]{1,0:T(8,128)(2,1)S(1)}, bf16[512,256]{1,0:T(8,128)(2,1)S(1)}, u32[]{:S(2)}, u32[]{:S(2)}) collective-permute-start(bf16[512,256]{1,0:T(8,128)(2,1)S(1)} %shard_map.103.refs_2_), channel_id=1, source_target_pairs={{0,2},{2,0},{4,6},{6,4},{1,3},{3,1},{5,7},{7,5},{8,10},{10,8},{12,... | collective-permute-start | bytes 786440 | tf_op jit(solution)/shard_map/ppermute | solution.py:298
  77.6 11.1 %collective-permute-start.17 = (bf16[512,256]{1,0:T(8,128)(2,1)S(1)}, bf16[512,256]{1,0:T(8,128)(2,1)S(1)}, u32[]{:S(2)}, u32[]{:S(2)}) collective-permute-start(bf16[512,256]{1,0:T(8,128)(2,1)S(1)} %shard_map.103.refs_2_), channel_id=1, source_target_pairs={{0,4},{2,6},{4,0},{6,2},{1,5},{3,7},{5,1},{7,3},{8,12},{10,14},{12... | collective-permute-start | bytes 786440 | tf_op jit(solution)/shard_map/ppermute | solution.py:298
  78.8 9.9 %collective-permute-start.18 = (bf16[512,256]{1,0:T(8,128)(2,1)S(1)}, bf16[512,256]{1,0:T(8,128)(2,1)S(1)}, u32[]{:S(2)}, u32[]{:S(2)}) collective-permute-start(bf16[512,256]{1,0:T(8,128)(2,1)S(1)} %shard_map.103.refs_2_), channel_id=1, source_target_pairs={{0,6},{2,4},{4,2},{6,0},{1,7},{3,5},{5,3},{7,1},{8,14},{10,12},{12... | collective-permute-start | bytes 786440 | tf_op jit(solution)/shard_map/ppermute | solution.py:298
  82.5 8.4 %collective-permute-start.19 = (bf16[512,256]{1,0:T(8,128)(2,1)S(1)}, bf16[512,256]{1,0:T(8,128)(2,1)S(1)}, u32[]{:S(2)}, u32[]{:S(2)}) collective-permute-start(bf16[512,256]{1,0:T(8,128)(2,1)S(1)} %get-tuple-element.36), channel_id=1, source_target_pairs={{0,16},{8,24},{16,0},{24,8},{1,17},{9,25},{17,1},{25,9},{2,18},{10... | collective-permute-start | bytes 786440 | tf_op jit(solution)/shard_map/ppermute | solution.py:311
  88.4 16.7 %collective-permute-start.14 = (bf16[512,256]{1,0:T(8,128)(2,1)S(1)}, bf16[512,256]{1,0:T(8,128)(2,1)S(1)}, u32[]{:S(2)}, u32[]{:S(2)}) collective-permute-start(bf16[512,256]{1,0:T(8,128)(2,1)S(1)} %get-tuple-element.33), channel_id=1, source_target_pairs={{0,16},{8,24},{16,0},{24,8},{1,17},{9,25},{17,1},{25,9},{2,18},{10... | collective-permute-start | bytes 786440 | tf_op jit(solution)/shard_map/ppermute | solution.py:311
  88.8 23.6 %collective-permute-start.23 = (bf16[2048,256]{1,0:T(8,128)(2,1)S(1)}, bf16[2048,256]{1,0:T(8,128)(2,1)S(1)}, u32[]{:S(2)}, u32[]{:S(2)}) collective-permute-start(bf16[2048,256]{1,0:T(8,128)(2,1)S(1)} %pad_maximum_fusion.1.refs_4_), channel_id=1, source_target_pairs={{0,2},{2,0},{4,6},{6,4},{1,3},{3,1},{5,7},{7,5},{8,10},{10,8},{12,... | collective-permute-start | bytes 3145736 | tf_op jit(solution)/shard_map/ppermute | solution.py:298
  89.2 23.1 %collective-permute-start.24 = (bf16[2048,256]{1,0:T(8,128)(2,1)S(1)}, bf16[2048,256]{1,0:T(8,128)(2,1)S(1)}, u32[]{:S(2)}, u32[]{:S(2)}) collective-permute-start(bf16[2048,256]{1,0:T(8,128)(2,1)S(1)} %pad_maximum_fusion.1.refs_4_), channel_id=1, source_target_pairs={{0,4},{2,6},{4,0},{6,2},{1,5},{3,7},{5,1},{7,3},{8,12},{10,14},{12... | collective-permute-start | bytes 3145736 | tf_op jit(solution)/shard_map/ppermute | solution.py:298
  113.1 8.3 %collective-permute-start.25 = (bf16[1024,256]{1,0:T(8,128)(2,1)}, bf16[1024,256]{1,0:T(8,128)(2,1)}, u32[]{:S(2)}, u32[]{:S(2)}) collective-permute-start(bf16[1024,256]{1,0:T(8,128)(2,1)} %slice.22), channel_id=1, source_target_pairs={{0,2},{2,0},{4,6},{6,4},{1,3},{3,1},{5,7},{7,5},{8,10},{10,8},{12,... | collective-permute-start | bytes 1572872 | tf_op jit(solution)/shard_map/ppermute | solution.py:298
  114.3 8.3 %collective-permute-start.26 = (bf16[1024,256]{1,0:T(8,128)(2,1)}, bf16[1024,256]{1,0:T(8,128)(2,1)}, u32[]{:S(2)}, u32[]{:S(2)}) collective-permute-start(bf16[1024,256]{1,0:T(8,128)(2,1)} %slice.23), channel_id=1, source_target_pairs={{0,4},{2,6},{4,0},{6,2},{1,5},{3,7},{5,1},{7,3},{8,12},{10,14},{12... | collective-permute-start | bytes 1572872 | tf_op jit(solution)/shard_map/ppermute | solution.py:298
  115.5 17.4 %collective-permute-start.20 = (bf16[512,256]{1,0:T(8,128)(2,1)}, bf16[512,256]{1,0:T(8,128)(2,1)S(1)}, u32[]{:S(2)}, u32[]{:S(2)}) collective-permute-start(bf16[512,256]{1,0:T(8,128)(2,1)} %copy-done.8), channel_id=1, source_target_pairs={{0,16},{8,24},{16,0},{24,8},{1,17},{9,25},{17,1},{25,9},{2,18},{10... | collective-permute-start | bytes 786440 | tf_op jit(solution)/shard_map/ppermute | solution.py:311
  115.5 23.0 %collective-permute-start.21 = (bf16[512,256]{1,0:T(8,128)(2,1)S(1)}, bf16[512,256]{1,0:T(8,128)(2,1)S(1)}, u32[]{:S(2)}, u32[]{:S(2)}) collective-permute-start(bf16[512,256]{1,0:T(8,128)(2,1)S(1)} %shard_map.105.refs_1_), channel_id=1, source_target_pairs={{0,16},{8,24},{16,0},{24,8},{1,17},{9,25},{17,1},{25,9},{2,18},{10... | collective-permute-start | bytes 786440 | tf_op jit(solution)/shard_map/ppermute | solution.py:311
  140.6 7.1 %collective-permute-start.27 = (bf16[256,1024]{1,0:T(8,128)(2,1)}, bf16[256,1024]{1,0:T(8,128)(2,1)}, u32[]{:S(2)}, u32[]{:S(2)}) collective-permute-start(bf16[256,1024]{1,0:T(8,128)(2,1)} %shard_map.107), channel_id=1, source_target_pairs={{0,1},{1,0},{2,3},{3,2},{4,5},{5,4},{6,7},{7,6},{8,9},{9,8},{10,11... | collective-permute-start | bytes 1572872 | tf_op jit(solution)/shard_map/ppermute | solution.py:404
  150.3 7.5 %collective-permute-start.28 = (bf16[128,1024]{1,0:T(8,128)(2,1)S(1)}, bf16[128,1024]{1,0:T(8,128)(2,1)S(1)}, u32[]{:S(2)}, u32[]{:S(2)}) collective-permute-start(bf16[128,1024]{1,0:T(8,128)(2,1)S(1)} %add_convert_fusion.4), channel_id=1, source_target_pairs={{0,8},{8,0},{16,24},{24,16},{1,9},{9,1},{17,25},{25,17},{2,10},{10... | collective-permute-start | bytes 786440 | tf_op jit(solution)/shard_map/ppermute | solution.py:311
  152.3 11.2 %collective-permute-start.31 = (bf16[128,1024]{1,0:T(8,128)(2,1)S(1)}, bf16[128,1024]{1,0:T(8,128)(2,1)S(1)}, u32[]{:S(2)}, u32[]{:S(2)}) collective-permute-start(bf16[128,1024]{1,0:T(8,128)(2,1)S(1)} %add_convert_fusion.1), channel_id=1, source_target_pairs={{0,8},{8,0},{16,24},{24,16},{1,9},{9,1},{17,25},{25,17},{2,10},{10... | collective-permute-start | bytes 786440 | tf_op jit(solution)/shard_map/ppermute | solution.py:311
  158.9 11.4 %collective-permute-start.29 = (bf16[128,1024]{1,0:T(8,128)(2,1)S(1)}, bf16[128,1024]{1,0:T(8,128)(2,1)S(1)}, u32[]{:S(2)}, u32[]{:S(2)}) collective-permute-start(bf16[128,1024]{1,0:T(8,128)(2,1)S(1)} %add_convert_fusion.3), channel_id=1, source_target_pairs={{0,0},{1,16},{8,8},{9,24},{16,1},{17,17},{24,9},{25,25},{2,2},{3,1... | collective-permute-start | bytes 786440 | tf_op jit(solution)/shard_map/ppermute | solution.py:413
  163.6 12.4 %collective-permute-start.32 = (bf16[128,1024]{1,0:T(8,128)(2,1)S(1)}, bf16[128,1024]{1,0:T(8,128)(2,1)S(1)}, u32[]{:S(2)}, u32[]{:S(2)}) collective-permute-start(bf16[128,1024]{1,0:T(8,128)(2,1)S(1)} %add_convert_fusion), channel_id=1, source_target_pairs={{0,0},{1,16},{8,8},{9,24},{16,1},{17,17},{24,9},{25,25},{2,2},{3,1... | collective-permute-start | bytes 786440 | tf_op jit(solution)/shard_map/ppermute | solution.py:413
  (45 other events, 289.7 us)
